TPU v7x, 32 devices: a whole 2x2x4 slice. The times are simulated.
32 devices in a mesh: groups: 2 (over y), shard: 4 (over z), sub: 4 (over x, core).
Axes of the slice: x: 2, y: 2, z: 4, core: 2. Of those that a mesh axis runs over, the one named last changes fastest.
Arguments:
- points: bfloat16 [49152, 1024], P(('groups', 'shard', 'sub')), parts along dimension 0, may hold values from -6 to 6
- block_ids: int32 [384], P(('groups', 'shard', 'sub')), parts along dimension 0, may hold values from 0 to 3
- slot_ids: int32 [49152], P(('groups', 'shard', 'sub')), parts along dimension 0, may hold values from 0 to 127
- live_blocks: int32 [32], P(('groups', 'shard', 'sub')), parts along dimension 0, may hold values from 6 to 12, as said below
- old_centroids: bfloat16 [1024, 1024], P(('groups', 'shard'), 'sub'), parts along dimension 0, may hold values from -6 to 6
Outputs:
- new_centroids: bfloat16 [1024, 1024], P(('groups', 'shard'), 'sub'), parts along dimension 0
- margin: float32 [49152], P(('groups', 'shard', 'sub')), parts along dimension 0
There are 2 independent parts, one for each index of `groups`. A program takes and returns all parts, laid end to end along the dimension named above; each array names one. Nothing has to cross between parts.
Inputs may be any that keep to these rules, and one draw needn't show every extreme that they name: `live_blocks`: some device holds 12 live blocks in every draw.
All inputs are finite; a program needn't handle non-finite values.
Results may differ from a plain program's by a relative error of at most 0.0026.
Values may be sent and summed in bfloat16 or wider, within the bound.
No kernel may reach another device: no remote copies, remote signals or barrier semaphores. Data moves between devices by JAX's collectives and lax.ppermute only.
A program may use at most 128 MiB of HBM per device.

v0:
```python
import math

import jax
import jax.numpy as jnp
from jax import lax
from jax.sharding import PartitionSpec as P

SLOT = 128


prior_weight = 4.0
norm_eps = 1e-06


def local(points, block_ids, slot_ids, live_blocks, old_centroids):
    row_count, feat_width = points.shape
    block_count = row_count // SLOT
    shard_count = lax.axis_size("shard")
    sub_count = lax.axis_size("sub")
    owned_rows = old_centroids.shape[0]
    total_cents = owned_rows * shard_count
    cent_blocks = total_cents // SLOT
    slot_table = slot_ids.reshape(block_count, SLOT)
    live_mask = jnp.arange(block_count) < live_blocks[0]
    onehot_rows = (
        (slot_table[:, :, None] == jnp.arange(SLOT)[None, None, :]) & live_mask[:, None, None]
    ).astype(jnp.bfloat16)
    partial_value = jnp.einsum(
        "bpc,bpd->bcd",
        onehot_rows,
        points.reshape(block_count, SLOT, feat_width),
        preferred_element_type=jnp.float32,
    )
    block_hot = (block_ids[:, None] == jnp.arange(cent_blocks)[None, :]).astype(jnp.float32)
    dense_sums = jnp.einsum(
        "bk,bcd->kcd", block_hot, partial_value, precision=lax.Precision.HIGHEST
    )
    dense_sums = dense_sums.reshape(total_cents, feat_width)
    arranged = dense_sums.reshape(shard_count, owned_rows, sub_count, feat_width // sub_count)
    arranged = arranged.transpose(0, 2, 1, 3).reshape(
        shard_count * sub_count * owned_rows, feat_width // sub_count
    )
    sums = lax.psum_scatter(arranged, ("shard", "sub"), scatter_dimension=0, tiled=True)
    combined = sums + prior_weight * old_centroids.astype(jnp.float32)
    squares = lax.psum(jnp.sum(combined * combined, axis=1), "sub")
    new_centroids = (combined * lax.rsqrt(squares + norm_eps)[:, None]).astype(jnp.bfloat16)
    wide_owned = lax.all_gather(new_centroids, "sub", axis=1, tiled=True)
    own_ids = (block_ids[:, None] * SLOT + slot_table).reshape(row_count)

    def fold_scores(running, part_rows, first_row):
        own_score, rival = running
        score_block = jnp.einsum("rd,kd->rk", points, part_rows, preferred_element_type=jnp.float32)
        cent_index = first_row + jnp.arange(part_rows.shape[0], dtype=jnp.int32)
        own_hit = own_ids[:, None] == cent_index[None, :]
        own_score = own_score + jnp.sum(jnp.where(own_hit, score_block, 0.0), axis=1)
        rival = jnp.maximum(rival, jnp.max(jnp.where(own_hit, -jnp.inf, score_block), axis=1))
        return (own_score, rival)

    initial = (jnp.zeros((row_count,), jnp.float32), jnp.full((row_count,), -jnp.inf, jnp.float32))
    every_cent = lax.all_gather(wide_owned, "shard", axis=0, tiled=True)
    block_len = math.gcd(total_cents, 512)

    def scan_step(cursor, running):
        first_row = (cursor * block_len).astype(jnp.int32)
        part_rows = lax.dynamic_slice_in_dim(every_cent, first_row, block_len, 0)
        return fold_scores(running, part_rows, first_row)

    own_score, rival = lax.fori_loop(0, total_cents // block_len, scan_step, initial)
    return (new_centroids, own_score - rival)


def solution(mesh):
    return jax.shard_map(
        local,
        mesh=mesh,
        in_specs=(
            P(("groups", "shard", "sub"), None),
            P(("groups", "shard", "sub")),
            P(("groups", "shard", "sub")),
            P(("groups", "shard", "sub")),
            P(("groups", "shard"), "sub"),
        ),
        out_specs=(P(("groups", "shard"), "sub"), P(("groups", "shard", "sub"))),
        check_vma=False,
    )
```

profile of v0, /device:TPU:0, one launch (start us, length us, event | category | flops | bytes accessed | tf_op | source)
XLA Modules:
  0.0 143.7 jit_solution(13679760393497403148)
XLA Ops:
  7.2 0.0 copy-start
  7.2 0.0 reduce-scatter.2.cloned.1.call-start
  8.0 1.0 copy-done
  9.1 0.0 copy-start.4
  9.1 2.1 %fusion.3 = f32[12,128,1024]{2,1,0:T(8,128)S(1)} fusion(bf16[12,128,1024]{2,1,0:T(8,128)(2,1)S(1)} %bitcast.18, s32[12,128]{1,0:T(8,128)} %bitcast.21, pred[12]{0:T(512)(128)(4,1)S(1)} %iota_compare_fusion.3), kind=kOutput, calls=%fused_computation.8 | convolution fusion | flops 403046400 | bytes 9443340 | tf_op jit(solution)/shard_map/bpc,bpd->bcd/dot_general | solution.py:28
  11.2 0.0 copy-done.4
  11.2 8.1 %fusion = f32[4,128,1024]{2,0,1:T(4,128)} fusion(f32[12,128,1024]{2,1,0:T(8,128)S(1)} %fusion.3, s32[12]{0:T(128)S(1)} %copy-done.4), kind=kOutput, calls=%fused_computation | convolution fusion | flops 75497520 | bytes 8388656 | tf_op jit(solution)/shard_map/bk,bcd->kcd/dot_general | solution.py:35
  19.3 3.7 %reshape_reshape.3 = f32[4,128,4,256]{3,2,0,1:T(4,128)} reshape(f32[4,128,1024]{2,0,1:T(4,128)} %fusion) | data formatting | bytes 4194304 | tf_op jit(solution)/shard_map/reshape;reshape | solution.py:39
  23.0 0.0 copy-start.1
  23.0 0.0 copy-start.3
  23.0 4.1 %copy.7 = f32[4,4,128,256]{3,2,1,0:T(8,128)} copy(f32[4,4,128,256]{3,1,0,2:T(4,128)} %bitcast.20) | data formatting | bytes 4194304 | tf_op jit(solution)/shard_map/transpose | solution.py:40
  27.1 0.0 reduce-scatter.2.cloned.1.call-update
  27.2 0.0 all-gather.2.cloned.1.call-start
  27.2 64.3 %reduce-scatter.2.cloned.1.call-done = f32[128,256]{1,0:T(8,128)} async-done(((f32[2048,256]{1,0:T(8,128)}), f32[128,256]{1,0:T(8,128)}) %reduce-scatter.2.cloned.1.call-update) | async-done | bytes 131088 | tf_op jit(solution)/shard_map/reduce_scatter | solution.py:43
  91.5 0.0 copy-done.1
  91.5 1.0 multiply_reduce_fusion
  92.6 5.7 %psum.7 = f32[128]{0:T(128)S(1)} all-reduce(f32[128]{0:T(128)S(1)} %multiply_reduce_fusion), channel_id=1, replica_groups=mesh['groups'=2,'shard'=4,'sub'=4] {'sub'}, use_global_device_ids=true, to_apply=%region_2.0 | all-reduce | flops 128 | bytes 1024 | tf_op jit(solution)/shard_map/psum | solution.py:45
  98.2 1.0 multiply_convert_fusion
  99.2 0.0 copy-start.2
  99.2 6.3 %all_gather.6 = bf16[128,1024]{1,0:T(8,128)(2,1)} all-gather(bf16[128,256]{1,0:T(8,128)(2,1)S(1)} %multiply_convert_fusion), channel_id=1, replica_groups=mesh['groups'=2,'shard'=4,'sub'=4] {'sub'}, dimensions={1}, use_global_device_ids=true | all-gather | bytes 327680 | tf_op jit(solution)/shard_map/all_gather | solution.py:47
  105.5 0.0 all-gather.2.cloned.1.call-update
  105.5 0.0 copy-done.3
  105.5 0.1 bitcast_add_fusion
  105.6 27.3 %all-gather.2.cloned.1.call-done = bf16[512,1024]{1,0:T(8,128)(2,1)} async-done(((bf16[128,1024]{1,0:T(8,128)(2,1)}), bf16[512,1024]{1,0:T(8,128)(2,1)}) %all-gather.2.cloned.1.call-update) | async-done | bytes 1048592 | tf_op jit(solution)/shard_map/all_gather | solution.py:60
  132.9 3.3 %select_reduce_fusion = (f32[1536]{0:T(1024)S(1)}, f32[1536]{0:T(1024)S(1)}) fusion(s32[1536]{0:T(1024)S(1)} %bitcast_add_fusion, bf16[512,1024]{1,0:T(8,128)(2,1)} %all-gather.2.cloned.1.call-done, bf16[1536,1024]{1,0:T(8,128)(2,1)S(1)} %copy-done), kind=kOutput, calls=%fused_computation.3 | convolution fusion | flops 1614541824 | bytes 4212736 | tf_op jit(solution)/shard_map/while/body/eval_jaxpr/rd,kd->rk/dot_general | solution.py:52
  136.3 0.0 copy-done.2
  136.3 0.6 sub.3
  (3 shorter events, 0.0 us)
Async XLA Ops:
  7.2 1.9 %copy-start = (bf16[1536,1024]{1,0:T(8,128)(2,1)S(1)}, bf16[1536,1024]{1,0:T(8,128)(2,1)}, u32[]{:S(2)}) copy-start(bf16[1536,1024]{1,0:T(8,128)(2,1)} %param.5) | copy-start | bytes 9437188
  7.2 84.4 %reduce-scatter.2.cloned.1.call-start = ((), (), s32[]{:S(2)}) async-start(), calls=%async_computation.1 | async-start | bytes 2228224 | tf_op jit(solution)/shard_map/reduce_scatter | solution.py:43
  9.1 2.1 %copy-start.4 = (s32[12]{0:T(128)S(1)}, s32[12]{0:T(128)}, u32[]{:S(2)}) copy-start(s32[12]{0:T(128)} %param.6) | copy-start | bytes 148
  23.0 68.5 %copy-start.1 = (bf16[128,256]{1,0:T(8,128)(2,1)S(1)}, bf16[128,256]{1,0:T(8,128)(2,1)}, u32[]{:S(2)}) copy-start(bf16[128,256]{1,0:T(8,128)(2,1)} %param.9) | copy-start | bytes 196612
  23.0 82.5 %copy-start.3 = (s32[1536]{0:T(1024)S(1)}, s32[1536]{0:T(1024)}, u32[]{:S(2)}) copy-start(s32[1536]{0:T(1024)} %param.7) | copy-start | bytes 18436
  27.2 105.8 %all-gather.2.cloned.1.call-start = ((), (), s32[]{:S(2)}) async-start(), calls=%async_computation.2 | async-start | bytes 1310720 | tf_op jit(solution)/shard_map/all_gather | solution.py:60
  99.2 37.0 %copy-start.2 = (bf16[128,256]{1,0:T(8,128)(2,1)}, bf16[128,256]{1,0:T(8,128)(2,1)S(1)}, u32[]{:S(2)}) copy-start(bf16[128,256]{1,0:T(8,128)(2,1)S(1)} %multiply_convert_fusion) | copy-start | bytes 196612
Sparse Core Ops, SparseCore 0:
  27.3 64.1 reduce-scatter.1
  105.6 27.2 all-gather.1
where the time goes:
time: 144 us
  waiting for transfers between devices  91.7 us (64%)
  between operations  14.9 us (10%)
  matrix products  13.5 us (9%)
  blocking collectives  11.9 us (8%)
  local copies, waits for them, and re-layouts  8.91 us (6%)
  other arithmetic  2.7 us (2%)
    reduce_scatter x1, waiting for transfers between devices, local(): lax.psum_scatter(arranged, ('shard', 'sub'), scatter_dimension=0, tiled=T...  64.3 us
    all_gather x1, waiting for transfers between devices, local(): every_cent = lax.all_gather(wide_owned, 'shard', axis=0, tiled=True)  27.3 us
    dot_general x1, matrix products, local(): jnp.einsum('bk,bcd->kcd', block_hot, partial_value, precision=lax.Precisi...  8.06 us
    all_gather x1, blocking collectives, local(): wide_owned = lax.all_gather(new_centroids, 'sub', axis=1, tiled=True)  6.26 us
    psum x1, blocking collectives, local(): squares = lax.psum(jnp.sum(combined * combined, axis=1), 'sub')  5.67 us
    transpose x1, local copies, waits for them, and re-layouts, local(): arranged.transpose(0, 2, 1, 3)  4.13 us
    another operation x1, local copies, waits for them, and re-layouts, local(): dense_sums.reshape(shard_count, owned_rows, sub_count, feat_width // sub_...  3.71 us
    dot_general x1, matrix products, fold_scores(): jnp.einsum('rd,kd->rk', points, part_rows, preferred_element_type=jnp.flo...  3.33 us
  transfers between devices with their start and end apart: 2, of which 2 were waited for; matrix products, arithmetic and copies ran while one was open for 0% of the time, Pallas kernels for 0%

commit v1 on v0

v1 whole, which is shorter than its diff:
```python
import functools
import math

import jax
import jax.numpy as jnp
from jax import lax
from jax.experimental import pallas as pl
from jax.experimental.pallas import tpu as pltpu
from jax.sharding import PartitionSpec as P

SLOT = 128
POINT_LIMIT = 6.0

prior_weight = 4.0
norm_eps = 1e-06

LOW_EXP = -32
MIB = 1 << 20


def code_rate(top_exp):
    return 32767.0 / (top_exp - LOW_EXP)


def encode(value, rate):
    size = jnp.maximum(jnp.abs(value), 2.0**LOW_EXP)
    level = jnp.floor((jnp.log2(size) - LOW_EXP) * rate + 0.5)
    return jnp.where(value < 0.0, -level, level).astype(jnp.int32).astype(jnp.int16)


def decode(code, rate):
    level = code.astype(jnp.int32).astype(jnp.float32)
    size = jnp.exp2(jnp.abs(level) * (1.0 / rate) + LOW_EXP)
    return jnp.where(level == 0.0, 0.0, jnp.where(level < 0.0, -size, size))


def sums_kernel(place, bids, slots, points, send, keep, held, acc, arrived, *, blocks, shards, halves, rows, width):
    sub, shard, live = place[0], place[1], place[2]
    copies = []
    for block in range(blocks):
        span = pl.ds(block * SLOT, SLOT)
        copies.append(pltpu.make_async_copy(points.at[span], held.at[span], arrived.at[block]))
        copies[-1].start()
    acc[...] = jnp.zeros_like(acc)
    for block in range(blocks):
        copies[block].wait()

        @pl.when(block < live)
        def _(block=block):
            hot = slots[block : block + 1, :] == lax.broadcasted_iota(jnp.int32, (SLOT, SLOT), 0)
            part = jnp.dot(
                hot.astype(jnp.bfloat16),
                held[block * SLOT : (block + 1) * SLOT, :],
                preferred_element_type=jnp.float32,
            )
            first = pl.multiple_of(bids[block] * SLOT, SLOT)
            acc[pl.ds(first, SLOT), :] += part

    for half in range(halves):
        for step in range(shards):
            row = pl.ds(pl.multiple_of((shard ^ step) * rows, rows), rows)
            near = pl.multiple_of((sub ^ (2 * half)) * width, width)
            far = pl.multiple_of((sub ^ 1 ^ (2 * half)) * width, width)
            keep[half, step] = acc[row, pl.ds(near, width)]
            send[half, step] = acc[row, pl.ds(far, width)]


def score_kernel(
    place, bids, slots, own, points, *refs, blocks, shards, subs, rows, width, rate, group
):
    codes, (fresh, margin, cents) = refs[:subs], refs[subs:]
    sub, shard = place[0], place[1]
    def normalise(step, _):
        pieces = [decode(code[step], rate) for code in codes]
        squares = sum(jnp.sum(piece * piece, axis=1, keepdims=True) for piece in pieces)
        scale = lax.rsqrt(squares + norm_eps)
        row = pl.ds(pl.multiple_of(step * rows, rows), rows)
        for index, piece in enumerate(pieces):
            column = pl.ds(pl.multiple_of((sub ^ index) * width, width), width)
            cents[row, column] = (piece * scale).astype(jnp.bfloat16)

        @pl.when(step == 0)
        def _():
            fresh[...] = (own[...] * scale).astype(jnp.bfloat16)

        return 0

    lax.fori_loop(0, shards, normalise, 0)
    for block in range(blocks // group):
        score = lax.dot_general(
            cents[...],
            points[block * group * SLOT : (block + 1) * group * SLOT, :],
            (((1,), (1,)), ((), ())),
            preferred_element_type=jnp.float32,
        )
        for inner in range(group):
            at = block * group + inner
            part = score[:, inner * SLOT : (inner + 1) * SLOT]
            row = (bids[at] ^ shard) * SLOT + slots[at : at + 1, :]
            hit = lax.broadcasted_iota(jnp.int32, part.shape, 0) == row
            mine = jnp.sum(jnp.where(hit, part, 0.0), axis=0, keepdims=True)
            rival = jnp.max(jnp.where(hit, -jnp.inf, part), axis=0, keepdims=True)
            margin[at : at + 1, :] = mine - rival


def local(points, block_ids, slot_ids, live_blocks, old_centroids):
    row_count, feat_width = points.shape
    blocks = row_count // SLOT
    shards = lax.axis_size("shard")
    subs = lax.axis_size("sub")
    rows, width = old_centroids.shape
    total = rows * shards
    halves = subs // 2
    top = POINT_LIMIT * (row_count * shards * subs + prior_weight)
    rate = code_rate(math.ceil(math.log2(top)))
    place = jnp.stack([lax.axis_index("sub"), lax.axis_index("shard"), live_blocks[0]]).astype(jnp.int32)
    slots = slot_ids.reshape(blocks, SLOT)
    smem = pl.BlockSpec(memory_space=pltpu.SMEM)
    vmem = pl.BlockSpec(memory_space=pltpu.VMEM)
    hbm = pl.BlockSpec(memory_space=pltpu.HBM)

    def swap(value, axis, count, bits):
        return lax.ppermute(value, axis, [(i, i ^ bits) for i in range(count)])

    piece = jax.ShapeDtypeStruct((halves, shards, rows, width), jnp.float32)
    send, keep = pl.pallas_call(
        functools.partial(
            sums_kernel, blocks=blocks, shards=shards, halves=halves, rows=rows, width=width
        ),
        out_shape=(piece, piece),
        in_specs=[smem, smem, vmem, hbm],
        out_specs=(vmem, vmem),
        scratch_shapes=[
            pltpu.VMEM((row_count, feat_width), jnp.bfloat16),
            pltpu.VMEM((total, feat_width), jnp.float32),
            pltpu.SemaphoreType.DMA((blocks,)),
        ],
        compiler_params=pltpu.CompilerParams(vmem_limit_bytes=8 * MIB + 8 * total * feat_width),
        name="sums",
    )(place, block_ids, slots, points)

    mine = keep + swap(send, "sub", subs, 1)
    span = halves
    bits = 2
    while span > 1:
        split = mine.reshape((span // 2, 2) + mine.shape[1:])
        there = swap(encode(split[:, 1], rate), "sub", subs, bits)
        mine = split[:, 0] + decode(there, rate)
        span //= 2
        bits *= 2
    mine = mine[0]
    combined = mine[0] + prior_weight * old_centroids.astype(jnp.float32)
    for step in range(1, shards):
        there = swap(encode(mine[step], rate), "shard", shards, step)
        combined = combined + decode(there, rate)

    code = encode(combined, rate)
    gathered = [jnp.stack([code] + [swap(code, "shard", shards, step) for step in range(1, shards)])]
    bits = subs // 2
    held = {0: gathered[0]}
    while bits >= 1:
        for index in list(held):
            held[index ^ bits] = swap(held[index], "sub", subs, bits)
        bits //= 2

    group = 2 if blocks % 2 == 0 else 1
    fresh, margin = pl.pallas_call(
        functools.partial(
            score_kernel,
            blocks=blocks,
            shards=shards,
            subs=subs,
            rows=rows,
            width=width,
            rate=rate,
            group=group,
        ),
        out_shape=(
            jax.ShapeDtypeStruct((rows, width), jnp.bfloat16),
            jax.ShapeDtypeStruct((blocks, SLOT), jnp.float32),
        ),
        in_specs=[smem, smem, vmem, vmem, vmem] + [vmem] * subs,
        out_specs=(vmem, vmem),
        scratch_shapes=[
            pltpu.VMEM((total, feat_width), jnp.bfloat16),
        ],
        compiler_params=pltpu.CompilerParams(vmem_limit_bytes=12 * MIB + 6 * total * feat_width),
        name="scores",
    )(place, block_ids, slots, combined, points, *[held[index] for index in range(subs)])
    return fresh, margin.reshape(row_count)


def solution(mesh):
    return jax.shard_map(
        local,
        mesh=mesh,
        in_specs=(
            P(("groups", "shard", "sub"), None),
            P(("groups", "shard", "sub")),
            P(("groups", "shard", "sub")),
            P(("groups", "shard", "sub")),
            P(("groups", "shard"), "sub"),
        ),
        out_specs=(P(("groups", "shard"), "sub"), P(("groups", "shard", "sub"))),
        check_vma=False,
    )
```

time: 144 us -> 54.7 us (0.38)
  waiting for transfers between devices: 91.7 us -> 25.9 us
  starting transfers between devices: 0.08 us -> 15.2 us
  between operations: 14.9 us -> 1.34 us
  matrix products: 13.5 us -> 0 us
  blocking collectives: 11.9 us -> 0 us
  Pallas kernels: 0 us -> 7.26 us
  local copies, waits for them, and re-layouts: 8.91 us -> 3.26 us
  other arithmetic: 2.7 us -> 1.25 us
    reduce_scatter x1 -> x0, waiting for transfers between devices: 64.3 us -> none  [local(): lax.psum_scatter(arranged, ('shard', 'sub'), scatter_dimension=0, tiled=T...]
    all_gather x1 -> x0, waiting for transfers between devices: 27.3 us -> none  [local(): every_cent = lax.all_gather(wide_owned, 'shard', axis=0, tiled=True)]
    ppermute x0 -> x11, waiting for transfers between devices: none -> 25.9 us  [swap(): return lax.ppermute(value, axis, [(i, i ^ bits) for i in range(count)])]
    ppermute x0 -> x11, starting transfers between devices: none -> 15.2 us  [swap(): return lax.ppermute(value, axis, [(i, i ^ bits) for i in range(count)])]
    dot_general x3 -> x0, matrix products: 13.5 us -> none  [the longest x1 8.06 us: local(): jnp.einsum('bk,bcd->kcd', block_hot, partial_value, precision=lax.Precisi...]
    pallas_call x0 -> x2, Pallas kernels: none -> 7.26 us  [the longest x1 4.56 us: local(): pl.pallas_call(functools.partial(score_kernel, blocks=blocks, shards=shar...]
    all_gather x1 -> x0, blocking collectives: 6.26 us -> none  [local(): wide_owned = lax.all_gather(new_centroids, 'sub', axis=1, tiled=True)]
    psum x1 -> x0, blocking collectives: 5.67 us -> none  [local(): squares = lax.psum(jnp.sum(combined * combined, axis=1), 'sub')]
  transfers between devices with their start and end apart: 2 -> 11, of which waited for: 2 -> 8; matrix products, arithmetic and copies ran while one was open for 0% -> 0% of each run, Pallas kernels for 0% -> 0%
where the time goes in v1:
time: 54.7 us; the launch traced here: 54.3 us
  waiting for transfers between devices  25.9 us (47%)
  starting transfers between devices  15.2 us (28%)
  Pallas kernels  7.26 us (13%)
  local copies, waits for them, and re-layouts  3.26 us (6%)
  between operations  1.34 us (2%)
  other arithmetic  1.25 us (2%)
    ppermute x11, waiting for transfers between devices, swap(): return lax.ppermute(value, axis, [(i, i ^ bits) for i in range(count)])  25.9 us
    ppermute x11, starting transfers between devices, swap(): return lax.ppermute(value, axis, [(i, i ^ bits) for i in range(count)])  15.2 us
    pallas_call x1, Pallas kernels, local(): pl.pallas_call(functools.partial(score_kernel, blocks=blocks, shards=shar...  4.56 us
    unnamed x14, local copies, waits for them, and re-layouts  3.26 us
    pallas_call x1, Pallas kernels, local(): pl.pallas_call(functools.partial(sums_kernel, blocks=blocks, shards=shard...  2.7 us
  transfers between devices with their start and end apart: 11, of which 8 were waited for; matrix products, arithmetic and copies ran while one was open for 0% of the time, Pallas kernels for 0%

profile of v1, /device:TPU:0, one launch (start us, length us, event | category | flops | bytes accessed | tf_op | source)
XLA Modules:
  0.0 54.3 jit_solution(12105795445305875174)
XLA Ops:
  1.3 0.1 pad_add_fusion.1.place
  1.4 0.0 copy-start
  1.4 1.9 %copy-done = bf16[1536,1024]{1,0:T(8,128)(2,1)S(1)} copy-done((bf16[1536,1024]{1,0:T(8,128)(2,1)S(1)}, bf16[1536,1024]{1,0:T(8,128)(2,1)}, u32[]{:S(2)}) %copy-start) | copy-done | bytes 3145752
  3.2 0.0 copy-start.2
  3.2 0.7 %copy-done.2 = s32[1536]{0:T(1024)S(1)} copy-done((s32[1536]{0:T(1024)S(1)}, s32[1536]{0:T(1024)}, u32[]{:S(2)}) %copy-start.2) | copy-done | bytes 6168
  3.9 0.0 copy-start.4
  3.9 0.7 %copy-done.4 = s32[12]{0:T(128)S(1)} copy-done((s32[12]{0:T(128)S(1)}, s32[12]{0:T(128)}, u32[]{:S(2)}) %copy-start.4) | copy-done | bytes 72
  4.6 2.7 %sums.1 = (f32[2,4,128,256]{3,2,1,0:T(8,128)S(1)}, f32[2,4,128,256]{3,2,1,0:T(8,128)S(1)}) custom-call(s32[3]{0:T(128)S(1)} %pad_add_fusion.1.place, s32[12]{0:T(128)S(1)} %copy-done.4, s32[12,128]{1,0:T(8,128)S(1)} %bitcast.37, bf16[1536,1024]{1,0:T(8,128)(2,1)S(1)} %copy-done), custom_call_target="tpu_custom_call" | custom-call | tf_op jit(solution)/shard_map/sums/pallas_call | solution.py:126
  7.3 0.0 copy-start.6
  7.3 1.6 %collective-permute-start = (f32[2,4,128,256]{3,2,1,0:T(8,128)S(1)}, f32[2,4,128,256]{3,2,1,0:T(8,128)S(1)}, u32[]{:S(2)}, u32[]{:S(2)}) collective-permute-start(f32[2,4,128,256]{3,2,1,0:T(8,128)S(1)} %get-tuple-element.7), channel_id=1, source_target_pairs={{0,1},{1,0},{2,3},{3,2},{4,5},{5,4},{6,7},{7,6},{8,9},{9,8},{10,11... | collective-permute-start | bytes 3145736 | tf_op jit(solution)/shard_map/ppermute | solution.py:123
  8.9 2.3 %collective-permute-done = f32[2,4,128,256]{3,2,1,0:T(8,128)S(1)} collective-permute-done((f32[2,4,128,256]{3,2,1,0:T(8,128)S(1)}, f32[2,4,128,256]{3,2,1,0:T(8,128)S(1)}, u32[]{:S(2)}, u32[]{:S(2)}) %collective-permute-start) | collective-permute-done | bytes 1048608 | tf_op jit(solution)/shard_map/ppermute | solution.py:123
  11.2 0.0 copy-start.1
  11.2 0.0 copy-start.3
  11.2 0.0 copy-start.5
  11.2 0.1 add_bitcast_fusion
  11.3 0.3 fusion.1
  11.6 2.3 %collective-permute-start.1 = (s16[1,4,128,256]{3,2,1,0:T(8,128)(2,1)S(1)}, s16[1,4,128,256]{3,2,1,0:T(8,128)(2,1)S(1)}, u32[]{:S(2)}, u32[]{:S(2)}) collective-permute-start(s16[1,4,128,256]{3,2,1,0:T(8,128)(2,1)S(1)} %fusion.1), channel_id=1, source_target_pairs={{0,2},{1,3},{2,0},{3,1},{4,6},{5,7},{6,4},{7,5},{8,10},{9,11},{10,... | collective-permute-start | bytes 786440 | tf_op jit(solution)/shard_map/ppermute | solution.py:123
  13.9 6.6 %collective-permute-done.1 = s16[1,4,128,256]{3,2,1,0:T(8,128)(2,1)S(1)} collective-permute-done((s16[1,4,128,256]{3,2,1,0:T(8,128)(2,1)S(1)}, s16[1,4,128,256]{3,2,1,0:T(8,128)(2,1)S(1)}, u32[]{:S(2)}, u32[]{:S(2)}) %collective-permute-start.1) | collective-permute-done | bytes 262176 | tf_op jit(solution)/shard_map/ppermute | solution.py:123
  20.5 0.3 fusion.3
  20.8 0.2 fusion.5
  21.0 1.9 %collective-permute-start.2 = (s16[128,256]{1,0:T(8,128)(2,1)S(1)}, s16[128,256]{1,0:T(8,128)(2,1)S(1)}, u32[]{:S(2)}, u32[]{:S(2)}) collective-permute-start(s16[128,256]{1,0:T(8,128)(2,1)S(1)} %get-tuple-element.12), channel_id=1, source_target_pairs={{0,4},{4,0},{8,12},{12,8},{1,5},{5,1},{9,13},{13,9},{2,6},{6,2},{1... | collective-permute-start | bytes 196616 | tf_op jit(solution)/shard_map/ppermute | solution.py:123
  22.9 2.8 %collective-permute-start.4 = (s16[128,256]{1,0:T(8,128)(2,1)S(1)}, s16[128,256]{1,0:T(8,128)(2,1)S(1)}, u32[]{:S(2)}, u32[]{:S(2)}) collective-permute-start(s16[128,256]{1,0:T(8,128)(2,1)S(1)} %get-tuple-element.13), channel_id=1, source_target_pairs={{0,12},{4,8},{8,4},{12,0},{1,13},{5,9},{9,5},{13,1},{2,14},{6,10},... | collective-permute-start | bytes 196616 | tf_op jit(solution)/shard_map/ppermute | solution.py:123
  25.7 0.2 collective-permute-start.3
  25.9 0.0 collective-permute-done.2
  25.9 3.7 %collective-permute-done.4 = s16[128,256]{1,0:T(8,128)(2,1)S(1)} collective-permute-done((s16[128,256]{1,0:T(8,128)(2,1)S(1)}, s16[128,256]{1,0:T(8,128)(2,1)S(1)}, u32[]{:S(2)}, u32[]{:S(2)}) %collective-permute-start.4) | collective-permute-done | bytes 65568 | tf_op jit(solution)/shard_map/ppermute | solution.py:123
  29.6 2.0 %collective-permute-done.3 = s16[128,256]{1,0:T(8,128)(2,1)S(1)} collective-permute-done((s16[128,256]{1,0:T(8,128)(2,1)S(1)}, s16[128,256]{1,0:T(8,128)(2,1)S(1)}, u32[]{:S(2)}, u32[]{:S(2)}) %collective-permute-start.3) | collective-permute-done | bytes 65568 | tf_op jit(solution)/shard_map/ppermute | solution.py:123
  31.6 0.0 copy-done.6
  31.6 0.3 fusion.17
  31.9 2.7 %collective-permute-start.7 = (s16[128,256]{1,0:T(8,128)(2,1)S(1)}, s16[128,256]{1,0:T(8,128)(2,1)S(1)}, u32[]{:S(2)}, u32[]{:S(2)}) collective-permute-start(s16[128,256]{1,0:T(8,128)(2,1)S(1)} %get-tuple-element.10), channel_id=1, source_target_pairs={{0,12},{4,8},{8,4},{12,0},{1,13},{5,9},{9,5},{13,1},{2,14},{6,10},... | collective-permute-start | bytes 196616 | tf_op jit(solution)/shard_map/ppermute | solution.py:123
  34.7 0.0 collective-permute-start.6
  34.7 1.7 %collective-permute-start.5 = (s16[128,256]{1,0:T(8,128)(2,1)S(1)}, s16[128,256]{1,0:T(8,128)(2,1)S(1)}, u32[]{:S(2)}, u32[]{:S(2)}) collective-permute-start(s16[128,256]{1,0:T(8,128)(2,1)S(1)} %get-tuple-element.10), channel_id=1, source_target_pairs={{0,4},{4,0},{8,12},{12,8},{1,5},{5,1},{9,13},{13,9},{2,6},{6,2},{1... | collective-permute-start | bytes 196616 | tf_op jit(solution)/shard_map/ppermute | solution.py:123
  36.4 2.3 %collective-permute-done.7 = s16[128,256]{1,0:T(8,128)(2,1)S(1)} collective-permute-done((s16[128,256]{1,0:T(8,128)(2,1)S(1)}, s16[128,256]{1,0:T(8,128)(2,1)S(1)}, u32[]{:S(2)}, u32[]{:S(2)}) %collective-permute-start.7) | collective-permute-done | bytes 65568 | tf_op jit(solution)/shard_map/ppermute | solution.py:123
  38.7 1.5 %collective-permute-done.6 = s16[128,256]{1,0:T(8,128)(2,1)S(1)} collective-permute-done((s16[128,256]{1,0:T(8,128)(2,1)S(1)}, s16[128,256]{1,0:T(8,128)(2,1)S(1)}, u32[]{:S(2)}, u32[]{:S(2)}) %collective-permute-start.6) | collective-permute-done | bytes 65568 | tf_op jit(solution)/shard_map/ppermute | solution.py:123
  40.2 0.0 collective-permute-done.5
  40.2 2.0 %collective-permute-start.9 = (s16[4,128,256]{2,1,0:T(8,128)(2,1)S(1)}, s16[4,128,256]{2,1,0:T(8,128)(2,1)S(1)}, u32[]{:S(2)}, u32[]{:S(2)}) collective-permute-start(s16[4,128,256]{2,1,0:T(8,128)(2,1)S(1)} %pad_add_fusion.refs_0_), channel_id=1, source_target_pairs={{0,2},{1,3},{2,0},{3,1},{4,6},{5,7},{6,4},{7,5},{8,10},{9,11},{10,... | collective-permute-start | bytes 786440 | tf_op jit(solution)/shard_map/ppermute | solution.py:123
  42.2 0.0 collective-permute-start.8
  42.2 6.0 %collective-permute-done.9.refs_2_ = s16[4,128,256]{2,1,0:T(8,128)(2,1)S(1)} collective-permute-done((s16[4,128,256]{2,1,0:T(8,128)(2,1)S(1)}, s16[4,128,256]{2,1,0:T(8,128)(2,1)S(1)}, u32[]{:S(2)}, u32[]{:S(2)}) %collective-permute-start.9) | collective-permute-done | bytes 262176 | tf_op jit(solution)/shard_map/ppermute | solution.py:123
  48.2 0.0 collective-permute-start.10
  48.2 0.0 collective-permute-done.8.refs_1_
  48.2 1.5 %collective-permute-done.10.refs_3_ = s16[4,128,256]{2,1,0:T(8,128)(2,1)S(1)} collective-permute-done((s16[4,128,256]{2,1,0:T(8,128)(2,1)S(1)}, s16[4,128,256]{2,1,0:T(8,128)(2,1)S(1)}, u32[]{:S(2)}, u32[]{:S(2)}) %collective-permute-start.10) | collective-permute-done | bytes 262176 | tf_op jit(solution)/shard_map/ppermute | solution.py:123
  49.7 0.0 copy-done.1
  49.7 0.0 copy-done.3
  49.7 0.0 copy-done.5
  49.7 4.6 %scores.1 = (bf16[128,256]{1,0:T(8,128)(2,1)}, f32[12,128]{1,0:T(8,128)}) custom-call(s32[3]{0:T(128)S(1)} %pad_add_fusion.1.place, s32[12]{0:T(128)S(1)} %copy-done.5, s32[12,128]{1,0:T(8,128)S(1)} %bitcast.38, f32[128,256]{1,0:T(8,128)S(1)} %get-tuple-element.11.own, bf16[1536,1024]{1,0:T(8,128)(2,1)S(1)} %copy-done.1, ...), custom_call_target="tpu_custom_call" | custom-call | tf_op jit(solution)/shard_map/scores/pallas_call | solution.py:167
  (1 shorter events, 0.0 us)
Async XLA Ops:
  1.4 1.9 %copy-start = (bf16[1536,1024]{1,0:T(8,128)(2,1)S(1)}, bf16[1536,1024]{1,0:T(8,128)(2,1)}, u32[]{:S(2)}) copy-start(bf16[1536,1024]{1,0:T(8,128)(2,1)} %points.3) | copy-start | bytes 9437188
  3.2 0.7 %copy-start.2 = (s32[1536]{0:T(1024)S(1)}, s32[1536]{0:T(1024)}, u32[]{:S(2)}) copy-start(s32[1536]{0:T(1024)} %param.7) | copy-start | bytes 18436
  3.9 0.7 %copy-start.4 = (s32[12]{0:T(128)S(1)}, s32[12]{0:T(128)}, u32[]{:S(2)}) copy-start(s32[12]{0:T(128)} %bids.3) | copy-start | bytes 148
  7.3 24.3 %copy-start.6 = (bf16[128,256]{1,0:T(8,128)(2,1)S(1)}, bf16[128,256]{1,0:T(8,128)(2,1)}, u32[]{:S(2)}) copy-start(bf16[128,256]{1,0:T(8,128)(2,1)} %param.9) | copy-start | bytes 196612
  7.3 3.9 %collective-permute-start = (f32[2,4,128,256]{3,2,1,0:T(8,128)S(1)}, f32[2,4,128,256]{3,2,1,0:T(8,128)S(1)}, u32[]{:S(2)}, u32[]{:S(2)}) collective-permute-start(f32[2,4,128,256]{3,2,1,0:T(8,128)S(1)} %get-tuple-element.7), channel_id=1, source_target_pairs={{0,1},{1,0},{2,3},{3,2},{4,5},{5,4},{6,7},{7,6},{8,9},{9,8},{10,11... | collective-permute-start | bytes 3145736 | tf_op jit(solution)/shard_map/ppermute | solution.py:123
  11.2 38.5 %copy-start.1 = (bf16[1536,1024]{1,0:T(8,128)(2,1)S(1)}, bf16[1536,1024]{1,0:T(8,128)(2,1)}, u32[]{:S(2)}) copy-start(bf16[1536,1024]{1,0:T(8,128)(2,1)} %points.3) | copy-start | bytes 9437188
  11.2 38.5 %copy-start.3 = (s32[1536]{0:T(1024)S(1)}, s32[1536]{0:T(1024)}, u32[]{:S(2)}) copy-start(s32[1536]{0:T(1024)} %param.7) | copy-start | bytes 18436
  11.2 38.5 %copy-start.5 = (s32[12]{0:T(128)S(1)}, s32[12]{0:T(128)}, u32[]{:S(2)}) copy-start(s32[12]{0:T(128)} %bids.3) | copy-start | bytes 148
  11.6 8.9 %collective-permute-start.1 = (s16[1,4,128,256]{3,2,1,0:T(8,128)(2,1)S(1)}, s16[1,4,128,256]{3,2,1,0:T(8,128)(2,1)S(1)}, u32[]{:S(2)}, u32[]{:S(2)}) collective-permute-start(s16[1,4,128,256]{3,2,1,0:T(8,128)(2,1)S(1)} %fusion.1), channel_id=1, source_target_pairs={{0,2},{1,3},{2,0},{3,1},{4,6},{5,7},{6,4},{7,5},{8,10},{9,11},{10,... | collective-permute-start | bytes 786440 | tf_op jit(solution)/shard_map/ppermute | solution.py:123
  21.0 4.9 %collective-permute-start.2 = (s16[128,256]{1,0:T(8,128)(2,1)S(1)}, s16[128,256]{1,0:T(8,128)(2,1)S(1)}, u32[]{:S(2)}, u32[]{:S(2)}) collective-permute-start(s16[128,256]{1,0:T(8,128)(2,1)S(1)} %get-tuple-element.12), channel_id=1, source_target_pairs={{0,4},{4,0},{8,12},{12,8},{1,5},{5,1},{9,13},{13,9},{2,6},{6,2},{1... | collective-permute-start | bytes 196616 | tf_op jit(solution)/shard_map/ppermute | solution.py:123
  22.9 6.8 %collective-permute-start.4 = (s16[128,256]{1,0:T(8,128)(2,1)S(1)}, s16[128,256]{1,0:T(8,128)(2,1)S(1)}, u32[]{:S(2)}, u32[]{:S(2)}) collective-permute-start(s16[128,256]{1,0:T(8,128)(2,1)S(1)} %get-tuple-element.13), channel_id=1, source_target_pairs={{0,12},{4,8},{8,4},{12,0},{1,13},{5,9},{9,5},{13,1},{2,14},{6,10},... | collective-permute-start | bytes 196616 | tf_op jit(solution)/shard_map/ppermute | solution.py:123
  25.7 6.0 %collective-permute-start.3 = (s16[128,256]{1,0:T(8,128)(2,1)S(1)}, s16[128,256]{1,0:T(8,128)(2,1)S(1)}, u32[]{:S(2)}, u32[]{:S(2)}) collective-permute-start(s16[128,256]{1,0:T(8,128)(2,1)S(1)} %get-tuple-element.14), channel_id=1, source_target_pairs={{0,8},{4,12},{8,0},{12,4},{1,9},{5,13},{9,1},{13,5},{2,10},{6,14},... | collective-permute-start | bytes 196616 | tf_op jit(solution)/shard_map/ppermute | solution.py:123
  31.9 6.7 %collective-permute-start.7 = (s16[128,256]{1,0:T(8,128)(2,1)S(1)}, s16[128,256]{1,0:T(8,128)(2,1)S(1)}, u32[]{:S(2)}, u32[]{:S(2)}) collective-permute-start(s16[128,256]{1,0:T(8,128)(2,1)S(1)} %get-tuple-element.10), channel_id=1, source_target_pairs={{0,12},{4,8},{8,4},{12,0},{1,13},{5,9},{9,5},{13,1},{2,14},{6,10},... | collective-permute-start | bytes 196616 | tf_op jit(solution)/shard_map/ppermute | solution.py:123
  34.7 5.5 %collective-permute-start.6 = (s16[128,256]{1,0:T(8,128)(2,1)S(1)}, s16[128,256]{1,0:T(8,128)(2,1)S(1)}, u32[]{:S(2)}, u32[]{:S(2)}) collective-permute-start(s16[128,256]{1,0:T(8,128)(2,1)S(1)} %get-tuple-element.10), channel_id=1, source_target_pairs={{0,8},{4,12},{8,0},{12,4},{1,9},{5,13},{9,1},{13,5},{2,10},{6,14},... | collective-permute-start | bytes 196616 | tf_op jit(solution)/shard_map/ppermute | solution.py:123
  34.7 5.5 %collective-permute-start.5 = (s16[128,256]{1,0:T(8,128)(2,1)S(1)}, s16[128,256]{1,0:T(8,128)(2,1)S(1)}, u32[]{:S(2)}, u32[]{:S(2)}) collective-permute-start(s16[128,256]{1,0:T(8,128)(2,1)S(1)} %get-tuple-element.10), channel_id=1, source_target_pairs={{0,4},{4,0},{8,12},{12,8},{1,5},{5,1},{9,13},{13,9},{2,6},{6,2},{1... | collective-permute-start | bytes 196616 | tf_op jit(solution)/shard_map/ppermute | solution.py:123
  40.2 8.0 %collective-permute-start.9 = (s16[4,128,256]{2,1,0:T(8,128)(2,1)S(1)}, s16[4,128,256]{2,1,0:T(8,128)(2,1)S(1)}, u32[]{:S(2)}, u32[]{:S(2)}) collective-permute-start(s16[4,128,256]{2,1,0:T(8,128)(2,1)S(1)} %pad_add_fusion.refs_0_), channel_id=1, source_target_pairs={{0,2},{1,3},{2,0},{3,1},{4,6},{5,7},{6,4},{7,5},{8,10},{9,11},{10,... | collective-permute-start | bytes 786440 | tf_op jit(solution)/shard_map/ppermute | solution.py:123
  42.2 6.0 %collective-permute-start.8 = (s16[4,128,256]{2,1,0:T(8,128)(2,1)S(1)}, s16[4,128,256]{2,1,0:T(8,128)(2,1)S(1)}, u32[]{:S(2)}, u32[]{:S(2)}) collective-permute-start(s16[4,128,256]{2,1,0:T(8,128)(2,1)S(1)} %pad_add_fusion.refs_0_), channel_id=1, source_target_pairs={{0,1},{1,0},{2,3},{3,2},{4,5},{5,4},{6,7},{7,6},{8,9},{9,8},{10,11... | collective-permute-start | bytes 786440 | tf_op jit(solution)/shard_map/ppermute | solution.py:123
  48.2 1.5 %collective-permute-start.10 = (s16[4,128,256]{2,1,0:T(8,128)(2,1)S(1)}, s16[4,128,256]{2,1,0:T(8,128)(2,1)S(1)}, u32[]{:S(2)}, u32[]{:S(2)}) collective-permute-start(s16[4,128,256]{2,1,0:T(8,128)(2,1)S(1)} %collective-permute-done.9.refs_2_), channel_id=1, source_target_pairs={{0,1},{1,0},{2,3},{3,2},{4,5},{5,4},{6,7},{7,6},{8,9},{9,8},{10,11... | collective-permute-start | bytes 786440 | tf_op jit(solution)/shard_map/ppermute | solution.py:123

commit v2 on v1

--- a/solution.py
+++ b/solution.py
@@ -34,18 +34,29 @@
     return jnp.where(level == 0.0, 0.0, jnp.where(level < 0.0, -size, size))
 
 
-def sums_kernel(place, bids, slots, points, send, keep, held, acc, arrived, *, blocks, shards, halves, rows, width):
-    sub, shard, live = place[0], place[1], place[2]
+def sums_kernel(
+    live, bids_in, slots_in, points, send, keep, bids, slots, held, acc, small, arrived,
+    *, blocks, shards, halves, rows, width
+):
+    sub = lax.axis_index("sub")
+    firsts = [
+        pltpu.make_async_copy(bids_in, bids, small.at[0]),
+        pltpu.make_async_copy(slots_in, slots, small.at[1]),
+    ]
+    for copy in firsts:
+        copy.start()
     copies = []
     for block in range(blocks):
         span = pl.ds(block * SLOT, SLOT)
         copies.append(pltpu.make_async_copy(points.at[span], held.at[span], arrived.at[block]))
         copies[-1].start()
     acc[...] = jnp.zeros_like(acc)
+    for copy in firsts:
+        copy.wait()
     for block in range(blocks):
         copies[block].wait()
 
-        @pl.when(block < live)
+        @pl.when(block < live[0])
         def _(block=block):
             hot = slots[block : block + 1, :] == lax.broadcasted_iota(jnp.int32, (SLOT, SLOT), 0)
             part = jnp.dot(
@@ -57,19 +68,19 @@
             acc[pl.ds(first, SLOT), :] += part
 
     for half in range(halves):
+        near = pl.multiple_of((sub ^ (2 * half)) * width, width)
+        far = pl.multiple_of((sub ^ 1 ^ (2 * half)) * width, width)
         for step in range(shards):
-            row = pl.ds(pl.multiple_of((shard ^ step) * rows, rows), rows)
-            near = pl.multiple_of((sub ^ (2 * half)) * width, width)
-            far = pl.multiple_of((sub ^ 1 ^ (2 * half)) * width, width)
+            row = slice(step * rows, (step + 1) * rows)
             keep[half, step] = acc[row, pl.ds(near, width)]
             send[half, step] = acc[row, pl.ds(far, width)]
 
 
 def score_kernel(
-    place, bids, slots, own, points, *refs, blocks, shards, subs, rows, width, rate, group
+    bids, slots, own, points, *refs, blocks, shards, subs, rows, width, rate, group
 ):
     codes, (fresh, margin, cents) = refs[:subs], refs[subs:]
-    sub, shard = place[0], place[1]
+    sub, shard = lax.axis_index("sub"), lax.axis_index("shard")
     def normalise(step, _):
         pieces = [decode(code[step], rate) for code in codes]
         squares = sum(jnp.sum(piece * piece, axis=1, keepdims=True) for piece in pieces)
@@ -79,7 +90,7 @@
             column = pl.ds(pl.multiple_of((sub ^ index) * width, width), width)
             cents[row, column] = (piece * scale).astype(jnp.bfloat16)
 
-        @pl.when(step == 0)
+        @pl.when(step == shard)
         def _():
             fresh[...] = (own[...] * scale).astype(jnp.bfloat16)
 
@@ -96,7 +107,7 @@
         for inner in range(group):
             at = block * group + inner
             part = score[:, inner * SLOT : (inner + 1) * SLOT]
-            row = (bids[at] ^ shard) * SLOT + slots[at : at + 1, :]
+            row = bids[at] * SLOT + slots[at : at + 1, :]
             hit = lax.broadcasted_iota(jnp.int32, part.shape, 0) == row
             mine = jnp.sum(jnp.where(hit, part, 0.0), axis=0, keepdims=True)
             rival = jnp.max(jnp.where(hit, -jnp.inf, part), axis=0, keepdims=True)
@@ -113,7 +124,6 @@
     halves = subs // 2
     top = POINT_LIMIT * (row_count * shards * subs + prior_weight)
     rate = code_rate(math.ceil(math.log2(top)))
-    place = jnp.stack([lax.axis_index("sub"), lax.axis_index("shard"), live_blocks[0]]).astype(jnp.int32)
     slots = slot_ids.reshape(blocks, SLOT)
     smem = pl.BlockSpec(memory_space=pltpu.SMEM)
     vmem = pl.BlockSpec(memory_space=pltpu.VMEM)
@@ -128,16 +138,19 @@
             sums_kernel, blocks=blocks, shards=shards, halves=halves, rows=rows, width=width
         ),
         out_shape=(piece, piece),
-        in_specs=[smem, smem, vmem, hbm],
+        in_specs=[smem, hbm, hbm, hbm],
         out_specs=(vmem, vmem),
         scratch_shapes=[
+            pltpu.SMEM((blocks,), jnp.int32),
+            pltpu.VMEM((blocks, SLOT), jnp.int32),
             pltpu.VMEM((row_count, feat_width), jnp.bfloat16),
             pltpu.VMEM((total, feat_width), jnp.float32),
+            pltpu.SemaphoreType.DMA((2,)),
             pltpu.SemaphoreType.DMA((blocks,)),
         ],
         compiler_params=pltpu.CompilerParams(vmem_limit_bytes=8 * MIB + 8 * total * feat_width),
         name="sums",
-    )(place, block_ids, slots, points)
+    )(live_blocks, *[pltpu.with_memory_space_constraint(x, pltpu.HBM) for x in (block_ids, slots, points)])
 
     mine = keep + swap(send, "sub", subs, 1)
     span = halves
@@ -148,16 +161,12 @@
         mine = split[:, 0] + decode(there, rate)
         span //= 2
         bits *= 2
-    mine = mine[0]
-    combined = mine[0] + prior_weight * old_centroids.astype(jnp.float32)
-    for step in range(1, shards):
-        there = swap(encode(mine[step], rate), "shard", shards, step)
-        combined = combined + decode(there, rate)
-
-    code = encode(combined, rate)
-    gathered = [jnp.stack([code] + [swap(code, "shard", shards, step) for step in range(1, shards)])]
+    there = lax.all_to_all(encode(mine[0], rate), "shard", split_axis=0, concat_axis=0, tiled=True)
+    combined = jnp.sum(decode(there, rate), axis=0) + prior_weight * old_centroids.astype(jnp.float32)
+
+    gathered = lax.all_gather(encode(combined, rate), "shard", axis=0)
     bits = subs // 2
-    held = {0: gathered[0]}
+    held = {0: gathered}
     while bits >= 1:
         for index in list(held):
             held[index ^ bits] = swap(held[index], "sub", subs, bits)
@@ -179,14 +188,14 @@
             jax.ShapeDtypeStruct((rows, width), jnp.bfloat16),
             jax.ShapeDtypeStruct((blocks, SLOT), jnp.float32),
         ),
-        in_specs=[smem, smem, vmem, vmem, vmem] + [vmem] * subs,
+        in_specs=[smem, vmem, vmem, vmem] + [vmem] * subs,
         out_specs=(vmem, vmem),
         scratch_shapes=[
             pltpu.VMEM((total, feat_width), jnp.bfloat16),
         ],
         compiler_params=pltpu.CompilerParams(vmem_limit_bytes=12 * MIB + 6 * total * feat_width),
         name="scores",
-    )(place, block_ids, slots, combined, points, *[held[index] for index in range(subs)])
+    )(block_ids, slots, combined, points, *[held[index] for index in range(subs)])
     return fresh, margin.reshape(row_count)
 
 

time: 54.7 us -> 59.6 us (1.090)
  blocking collectives: 0 us -> 27.7 us
  starting transfers between devices: 15.2 us -> 3.94 us
  waiting for transfers between devices: 25.9 us -> 16.3 us
  local copies, waits for them, and re-layouts: 3.26 us -> 0.02 us
  Pallas kernels: 7.26 us -> 9.08 us
    all_gather x0 -> x1, blocking collectives: none -> 14.4 us  [local(): gathered = lax.all_gather(encode(combined, rate), 'shard', axis=0)]
    all_to_all x0 -> x1, blocking collectives: none -> 13.3 us  [local(): lax.all_to_all(encode(mine[0], rate), 'shard', split_axis=0, concat_axis=...]
    ppermute x11 -> x5, starting transfers between devices: 15.2 us -> 3.94 us  [swap(): return lax.ppermute(value, axis, [(i, i ^ bits) for i in range(count)])]
    ppermute x11 -> x5, waiting for transfers between devices: 25.9 us -> 16.3 us  [swap(): return lax.ppermute(value, axis, [(i, i ^ bits) for i in range(count)])]
    unnamed x14 -> x8, local copies, waits for them, and re-layouts: 3.26 us -> 0.02 us
    pallas_call x1, Pallas kernels: 2.7 us -> 4.49 us  [local(): pl.pallas_call(functools.partial(sums_kernel, blocks=blocks, shards=shard...]
  transfers between devices with their start and end apart: 11 -> 5, of which waited for: 8 -> 4; matrix products, arithmetic and copies ran while one was open for 0% -> 0% of each run, Pallas kernels for 0% -> 0%
where the time goes in v2:
time: 59.6 us; the launch traced here: 59.7 us
  blocking collectives  27.7 us (46%)
  waiting for transfers between devices  16.3 us (27%)
  Pallas kernels  9.08 us (15%)
  starting transfers between devices  3.94 us (7%)
  between operations  1.34 us (2%)
  other arithmetic  1.27 us (2%)
    ppermute x5, waiting for transfers between devices, swap(): return lax.ppermute(value, axis, [(i, i ^ bits) for i in range(count)])  16.3 us
    all_gather x1, blocking collectives, local(): gathered = lax.all_gather(encode(combined, rate), 'shard', axis=0)  14.4 us
    all_to_all x1, blocking collectives, local(): lax.all_to_all(encode(mine[0], rate), 'shard', split_axis=0, concat_axis=...  13.3 us
    pallas_call x1, Pallas kernels, local(): pl.pallas_call(functools.partial(score_kernel, blocks=blocks, shards=shar...  4.59 us
    pallas_call x1, Pallas kernels, local(): pl.pallas_call(functools.partial(sums_kernel, blocks=blocks, shards=shard...  4.49 us
    ppermute x5, starting transfers between devices, swap(): return lax.ppermute(value, axis, [(i, i ^ bits) for i in range(count)])  3.94 us
  transfers between devices with their start and end apart: 5, of which 4 were waited for; matrix products, arithmetic and copies ran while one was open for 0% of the time, Pallas kernels for 0%

profile of v2, /device:TPU:0, one launch (start us, length us, event | category | flops | bytes accessed | tf_op | source)
XLA Modules:
  0.0 59.7 jit_solution(3127696341991497579)
XLA Ops:
  1.3 4.5 %sums.1 = (f32[2,4,128,256]{3,2,1,0:T(8,128)S(1)}, f32[2,4,128,256]{3,2,1,0:T(8,128)S(1)}) custom-call(s32[1]{0:T(128)S(6)} %copy.7.live, s32[12]{0:T(128)} %bids.1, s32[12,128]{1,0:T(8,128)} %bitcast.22, bf16[1536,1024]{1,0:T(8,128)(2,1)} %points.3), custom_call_target="tpu_custom_call" | custom-call | tf_op jit(solution)/shard_map/sums/pallas_call | solution.py:136
  5.8 0.0 copy-start.3
  5.8 0.1 collective-permute-start
  5.9 2.6 %collective-permute-done = f32[2,4,128,256]{3,2,1,0:T(8,128)S(1)} collective-permute-done((f32[2,4,128,256]{3,2,1,0:T(8,128)S(1)}, f32[2,4,128,256]{3,2,1,0:T(8,128)S(1)}, u32[]{:S(2)}, u32[]{:S(2)}) %collective-permute-start) | collective-permute-done | bytes 1048608 | tf_op jit(solution)/shard_map/ppermute | solution.py:133
  8.5 0.0 copy-start
  8.5 0.0 copy-start.1
  8.5 0.0 copy-start.2
  8.5 0.1 add_bitcast_fusion
  8.7 0.3 fusion.1
  8.9 3.0 %collective-permute-start.1 = (s16[1,4,128,256]{3,2,1,0:T(8,128)(2,1)S(1)}, s16[1,4,128,256]{3,2,1,0:T(8,128)(2,1)S(1)}, u32[]{:S(2)}, u32[]{:S(2)}) collective-permute-start(s16[1,4,128,256]{3,2,1,0:T(8,128)(2,1)S(1)} %fusion.1), channel_id=1, source_target_pairs={{0,2},{1,3},{2,0},{3,1},{4,6},{5,7},{6,4},{7,5},{8,10},{9,11},{10,... | collective-permute-start | bytes 786440 | tf_op jit(solution)/shard_map/ppermute | solution.py:133
  11.9 6.6 %collective-permute-done.1 = s16[1,4,128,256]{3,2,1,0:T(8,128)(2,1)S(1)} collective-permute-done((s16[1,4,128,256]{3,2,1,0:T(8,128)(2,1)S(1)}, s16[1,4,128,256]{3,2,1,0:T(8,128)(2,1)S(1)}, u32[]{:S(2)}, u32[]{:S(2)}) %collective-permute-start.1) | collective-permute-done | bytes 262176 | tf_op jit(solution)/shard_map/ppermute | solution.py:133
  18.5 0.5 fusion.5
  19.1 13.3 %all_to_all.5 = s16[4,128,256]{2,1,0:T(8,128)(2,1)S(1)} all-to-all(s16[4,128,256]{2,1,0:T(8,128)(2,1)S(1)} %fusion.5), channel_id=1, replica_groups=mesh['groups'=2,'shard'=4,'sub'=4] {'shard'}, dimensions={0} | all-to-all | bytes 524288 | tf_op jit(solution)/shard_map/all_to_all | solution.py:164
  32.3 0.3 fusion.7
  32.6 0.0 copy-done.3
  32.6 0.1 fusion.9
  32.7 14.4 %all-gather = s16[512,256]{1,0:T(8,128)(2,1)S(1)} all-gather(s16[128,256]{1,0:T(8,128)(2,1)S(1)} %get-tuple-element.10), channel_id=2, replica_groups=mesh['groups'=2,'shard'=4,'sub'=4] {'shard'}, dimensions={0}, use_global_device_ids=true | all-gather | bytes 327680 | tf_op jit(solution)/shard_map/all_gather | solution.py:167
  47.1 0.9 %collective-permute-start.3 = (s16[4,128,256]{2,1,0:T(8,128)(2,1)S(1)}, s16[4,128,256]{2,1,0:T(8,128)(2,1)S(1)}, u32[]{:S(2)}, u32[]{:S(2)}) collective-permute-start(s16[4,128,256]{2,1,0:T(8,128)(2,1)S(1)} %bitcast.19), channel_id=1, source_target_pairs={{0,2},{1,3},{2,0},{3,1},{4,6},{5,7},{6,4},{7,5},{8,10},{9,11},{10,... | collective-permute-start | bytes 786440 | tf_op jit(solution)/shard_map/ppermute | solution.py:133
  48.0 0.0 collective-permute-start.2
  48.0 5.5 %collective-permute-done.3.refs_2_ = s16[4,128,256]{2,1,0:T(8,128)(2,1)S(1)} collective-permute-done((s16[4,128,256]{2,1,0:T(8,128)(2,1)S(1)}, s16[4,128,256]{2,1,0:T(8,128)(2,1)S(1)}, u32[]{:S(2)}, u32[]{:S(2)}) %collective-permute-start.3) | collective-permute-done | bytes 262176 | tf_op jit(solution)/shard_map/ppermute | solution.py:133
  53.5 0.0 collective-permute-start.4
  53.5 0.0 collective-permute-done.2.refs_1_
  53.5 1.5 %collective-permute-done.4.refs_3_ = s16[4,128,256]{2,1,0:T(8,128)(2,1)S(1)} collective-permute-done((s16[4,128,256]{2,1,0:T(8,128)(2,1)S(1)}, s16[4,128,256]{2,1,0:T(8,128)(2,1)S(1)}, u32[]{:S(2)}, u32[]{:S(2)}) %collective-permute-start.4) | collective-permute-done | bytes 262176 | tf_op jit(solution)/shard_map/ppermute | solution.py:133
  55.1 0.0 copy-done
  55.1 0.0 copy-done.1
  55.1 0.0 copy-done.2
  55.1 4.6 %scores.1 = (bf16[128,256]{1,0:T(8,128)(2,1)}, f32[12,128]{1,0:T(8,128)}) custom-call(s32[12]{0:T(128)S(1)} %copy-done.2, s32[12,128]{1,0:T(8,128)S(1)} %bitcast.23, f32[128,256]{1,0:T(8,128)S(1)} %get-tuple-element.11.own, bf16[1536,1024]{1,0:T(8,128)(2,1)S(1)} %copy-done, s16[4,128,256]{2,1,0:T(8,128)(2,1)S(1)} %bitcast.21, ...), custom_call_target="tpu_custom_call" | custom-call | tf_op jit(solution)/shard_map/scores/pallas_call | solution.py:176
Async XLA Ops:
  5.8 26.8 %copy-start.3 = (bf16[128,256]{1,0:T(8,128)(2,1)S(1)}, bf16[128,256]{1,0:T(8,128)(2,1)}, u32[]{:S(2)}) copy-start(bf16[128,256]{1,0:T(8,128)(2,1)} %param.9) | copy-start | bytes 196612
  5.8 2.7 %collective-permute-start = (f32[2,4,128,256]{3,2,1,0:T(8,128)S(1)}, f32[2,4,128,256]{3,2,1,0:T(8,128)S(1)}, u32[]{:S(2)}, u32[]{:S(2)}) collective-permute-start(f32[2,4,128,256]{3,2,1,0:T(8,128)S(1)} %get-tuple-element.7), channel_id=1, source_target_pairs={{0,1},{1,0},{2,3},{3,2},{4,5},{5,4},{6,7},{7,6},{8,9},{9,8},{10,11... | collective-permute-start | bytes 3145736 | tf_op jit(solution)/shard_map/ppermute | solution.py:133
  8.5 46.5 %copy-start = (bf16[1536,1024]{1,0:T(8,128)(2,1)S(1)}, bf16[1536,1024]{1,0:T(8,128)(2,1)}, u32[]{:S(2)}) copy-start(bf16[1536,1024]{1,0:T(8,128)(2,1)} %points.3) | copy-start | bytes 9437188
  8.5 46.5 %copy-start.1 = (s32[1536]{0:T(1024)S(1)}, s32[1536]{0:T(1024)}, u32[]{:S(2)}) copy-start(s32[1536]{0:T(1024)} %param.7) | copy-start | bytes 18436
  8.5 46.5 %copy-start.2 = (s32[12]{0:T(128)S(1)}, s32[12]{0:T(128)}, u32[]{:S(2)}) copy-start(s32[12]{0:T(128)} %bids.1) | copy-start | bytes 148
  8.9 9.6 %collective-permute-start.1 = (s16[1,4,128,256]{3,2,1,0:T(8,128)(2,1)S(1)}, s16[1,4,128,256]{3,2,1,0:T(8,128)(2,1)S(1)}, u32[]{:S(2)}, u32[]{:S(2)}) collective-permute-start(s16[1,4,128,256]{3,2,1,0:T(8,128)(2,1)S(1)} %fusion.1), channel_id=1, source_target_pairs={{0,2},{1,3},{2,0},{3,1},{4,6},{5,7},{6,4},{7,5},{8,10},{9,11},{10,... | collective-permute-start | bytes 786440 | tf_op jit(solution)/shard_map/ppermute | solution.py:133
  47.1 6.4 %collective-permute-start.3 = (s16[4,128,256]{2,1,0:T(8,128)(2,1)S(1)}, s16[4,128,256]{2,1,0:T(8,128)(2,1)S(1)}, u32[]{:S(2)}, u32[]{:S(2)}) collective-permute-start(s16[4,128,256]{2,1,0:T(8,128)(2,1)S(1)} %bitcast.19), channel_id=1, source_target_pairs={{0,2},{1,3},{2,0},{3,1},{4,6},{5,7},{6,4},{7,5},{8,10},{9,11},{10,... | collective-permute-start | bytes 786440 | tf_op jit(solution)/shard_map/ppermute | solution.py:133
  48.0 5.5 %collective-permute-start.2 = (s16[4,128,256]{2,1,0:T(8,128)(2,1)S(1)}, s16[4,128,256]{2,1,0:T(8,128)(2,1)S(1)}, u32[]{:S(2)}, u32[]{:S(2)}) collective-permute-start(s16[4,128,256]{2,1,0:T(8,128)(2,1)S(1)} %bitcast.20), channel_id=1, source_target_pairs={{0,1},{1,0},{2,3},{3,2},{4,5},{5,4},{6,7},{7,6},{8,9},{9,8},{10,11... | collective-permute-start | bytes 786440 | tf_op jit(solution)/shard_map/ppermute | solution.py:133
  53.5 1.5 %collective-permute-start.4 = (s16[4,128,256]{2,1,0:T(8,128)(2,1)S(1)}, s16[4,128,256]{2,1,0:T(8,128)(2,1)S(1)}, u32[]{:S(2)}, u32[]{:S(2)}) collective-permute-start(s16[4,128,256]{2,1,0:T(8,128)(2,1)S(1)} %collective-permute-done.3.refs_2_), channel_id=1, source_target_pairs={{0,1},{1,0},{2,3},{3,2},{4,5},{5,4},{6,7},{7,6},{8,9},{9,8},{10,11... | collective-permute-start | bytes 786440 | tf_op jit(solution)/shard_map/ppermute | solution.py:133

commit v3 on v2

v3 whole, which is shorter than its diff:
```python
import functools
import math

import jax
import jax.numpy as jnp
from jax import lax
from jax.experimental import pallas as pl
from jax.experimental.pallas import tpu as pltpu
from jax.sharding import PartitionSpec as P

SLOT = 128
POINT_LIMIT = 6.0

prior_weight = 4.0
norm_eps = 1e-06

LOW_EXP = -32
MIB = 1 << 20


def code_rate(top_exp):
    return 32767.0 / (top_exp - LOW_EXP)


def encode(value, rate):
    size = jnp.maximum(jnp.abs(value), 2.0**LOW_EXP)
    level = jnp.floor((jnp.log2(size) - LOW_EXP) * rate + 0.5)
    return jnp.where(value < 0.0, -level, level).astype(jnp.int32).astype(jnp.int16)


def decode(code, rate):
    level = code.astype(jnp.int32).astype(jnp.float32)
    size = jnp.exp2(jnp.abs(level) * (1.0 / rate) + LOW_EXP)
    return jnp.where(level == 0.0, 0.0, jnp.where(level < 0.0, -size, size))


def bits_of(count):
    return [1 << bit for bit in range(count.bit_length() - 1)]


def steps_of(subs, shards, half):
    subs_first = [("sub", bit) for bit in bits_of(subs)[1:]]
    shards_all = [("shard", bit) for bit in bits_of(shards)]
    if half == 0:
        return subs_first + shards_all
    return shards_all[:1] + subs_first + shards_all[1:]


def pieces_of(steps):
    pieces = [(0, 0)]
    for axis, bit in reversed(steps):
        far = [(sub ^ bit, shard) if axis == "sub" else (sub, shard ^ bit) for sub, shard in pieces]
        pieces = pieces + far
    return pieces


def sums_kernel(
    live, bids_in, slots_in, points, *refs, blocks, shards, subs, rows, width
):
    outs, (bids, slots, held, acc, small, arrived) = refs[:4], refs[4:]
    sub, shard = lax.axis_index("sub"), lax.axis_index("shard")
    firsts = [
        pltpu.make_async_copy(bids_in, bids, small.at[0]),
        pltpu.make_async_copy(slots_in, slots, small.at[1]),
    ]
    for copy in firsts:
        copy.start()
    copies = []
    for block in range(blocks):
        span = pl.ds(block * SLOT, SLOT)
        copies.append(pltpu.make_async_copy(points.at[span], held.at[span], arrived.at[block]))
        copies[-1].start()
    acc[...] = jnp.zeros_like(acc)
    for copy in firsts:
        copy.wait()
    for block in range(blocks):
        copies[block].wait()

        @pl.when(block < live[0])
        def _(block=block):
            hot = slots[block : block + 1, :] == lax.broadcasted_iota(jnp.int32, (SLOT, SLOT), 0)
            part = jnp.dot(
                hot.astype(jnp.bfloat16),
                held[block * SLOT : (block + 1) * SLOT, :],
                preferred_element_type=jnp.float32,
            )
            first = pl.multiple_of(bids[block] * SLOT, SLOT)
            acc[pl.ds(first, SLOT), :] += part

    half_rows = rows // 2
    for half in range(2):
        send, keep = outs[2 * half : 2 * half + 2]
        for index, (over_sub, over_shard) in enumerate(pieces_of(steps_of(subs, shards, half))):
            row = pl.ds(pl.multiple_of((shard ^ over_shard) * rows + half * half_rows, half_rows), half_rows)
            near = pl.multiple_of((sub ^ over_sub) * width, width)
            far = pl.multiple_of((sub ^ 1 ^ over_sub) * width, width)
            keep[index] = acc[row, pl.ds(near, width)]
            send[index] = acc[row, pl.ds(far, width)]


def score_kernel(
    bids, slots, own, points, near, far, *refs, half, blocks, shards, subs, rows, width, rate, group
):
    if half:
        (mine_in, rival_in, fresh_in), (fresh, margin, cents) = refs[:3], refs[3:]
    else:
        fresh, mine_out, rival_out, cents = refs
    sub, shard = lax.axis_index("sub"), lax.axis_index("shard")
    half_rows = rows // 2
    pieces = pieces_of(steps_of(subs, shards, half))
    for over_shard in range(shards):
        parts = []
        for index, (over_sub, piece_shard) in enumerate(pieces):
            if piece_shard == over_shard:
                parts.append((sub ^ over_sub, decode(near[index], rate)))
                parts.append((sub ^ 1 ^ over_sub, decode(far[index], rate)))
        squares = sum(jnp.sum(part * part, axis=1, keepdims=True) for _, part in parts)
        scale = lax.rsqrt(squares + norm_eps)
        row = pl.ds(pl.multiple_of((shard ^ over_shard) * half_rows, half_rows), half_rows)
        for place, part in parts:
            cents[row, pl.ds(pl.multiple_of(place * width, width), width)] = (part * scale).astype(jnp.bfloat16)
        if over_shard == 0:
            updated = (own[...] * scale).astype(jnp.bfloat16)
            if half:
                fresh[:half_rows] = fresh_in[...]
                fresh[half_rows:] = updated
            else:
                fresh[...] = updated

    for block in range(blocks // group):
        score = lax.dot_general(
            cents[...],
            points[block * group * SLOT : (block + 1) * group * SLOT, :],
            (((1,), (1,)), ((), ())),
            preferred_element_type=jnp.float32,
        )
        for inner in range(group):
            at = block * group + inner
            line = slice(at, at + 1)
            part = score[:, inner * SLOT : (inner + 1) * SLOT]
            slot = slots[line, :] - half * half_rows
            row = jnp.where((slot >= 0) & (slot < half_rows), bids[at] * half_rows + slot, -1)
            hit = lax.broadcasted_iota(jnp.int32, part.shape, 0) == row
            mine = jnp.sum(jnp.where(hit, part, 0.0), axis=0, keepdims=True)
            rival = jnp.max(jnp.where(hit, -jnp.inf, part), axis=0, keepdims=True)
            if half:
                margin[line, :] = (mine_in[line, :] + mine) - jnp.maximum(rival_in[line, :], rival)
            else:
                mine_out[line, :] = mine
                rival_out[line, :] = rival


def local(points, block_ids, slot_ids, live_blocks, old_centroids):
    row_count, feat_width = points.shape
    blocks = row_count // SLOT
    shards = lax.axis_size("shard")
    subs = lax.axis_size("sub")
    counts = {"sub": subs, "shard": shards}
    rows, width = old_centroids.shape
    half_rows = rows // 2
    total = rows * shards
    top = POINT_LIMIT * (row_count * shards * subs + prior_weight)
    rate = code_rate(math.ceil(math.log2(top)))
    slots = slot_ids.reshape(blocks, SLOT)
    smem = pl.BlockSpec(memory_space=pltpu.SMEM)
    vmem = pl.BlockSpec(memory_space=pltpu.VMEM)
    hbm = pl.BlockSpec(memory_space=pltpu.HBM)

    def swap(value, axis, bit):
        return lax.ppermute(value, axis, [(i, i ^ bit) for i in range(counts[axis])])

    piece = jax.ShapeDtypeStruct((shards * subs // 2, half_rows, width), jnp.float32)
    sums = pl.pallas_call(
        functools.partial(sums_kernel, blocks=blocks, shards=shards, subs=subs, rows=rows, width=width),
        out_shape=(piece,) * 4,
        in_specs=[smem, hbm, hbm, hbm],
        out_specs=(vmem,) * 4,
        scratch_shapes=[
            pltpu.SMEM((blocks,), jnp.int32),
            pltpu.VMEM((blocks, SLOT), jnp.int32),
            pltpu.VMEM((row_count, feat_width), jnp.bfloat16),
            pltpu.VMEM((total, feat_width), jnp.float32),
            pltpu.SemaphoreType.DMA((2,)),
            pltpu.SemaphoreType.DMA((blocks,)),
        ],
        compiler_params=pltpu.CompilerParams(vmem_limit_bytes=8 * MIB + 8 * total * feat_width),
        name="sums",
    )(live_blocks, *[pltpu.with_memory_space_constraint(x, pltpu.HBM) for x in (block_ids, slots, points)])

    steps = [steps_of(subs, shards, half) for half in range(2)]
    prior = prior_weight * old_centroids.astype(jnp.float32)
    crossed = [swap(sums[2 * half], "sub", 1) for half in range(2)]
    mine = [sums[2 * half + 1] + crossed[half] for half in range(2)]
    for turn in range(len(steps[0]) - 1):
        for half in range(2):
            axis, bit = steps[half][turn]
            count = mine[half].shape[0] // 2
            there = swap(encode(mine[half][count:], rate), axis, bit)
            mine[half] = mine[half][:count] + decode(there, rate)
    codes = []
    owned = []
    for half in range(2):
        axis, bit = steps[half][-1]
        with_prior = mine[half][0] + prior[half * half_rows : (half + 1) * half_rows]
        pair = jnp.stack([with_prior, mine[half][1]])
        there = decode(swap(encode(pair, rate), axis, bit), rate)
        owned.append(with_prior + there[1])
        codes.append(encode(jnp.stack([owned[half], mine[half][1] + there[0]]), rate))
    for turn in reversed(range(len(steps[0]) - 1)):
        for half in range(2):
            axis, bit = steps[half][turn]
            codes[half] = jnp.concatenate([codes[half], swap(codes[half], axis, bit)])
    others = [swap(codes[half], "sub", 1) for half in range(2)]

    group = 2 if blocks % 2 == 0 else 1

    def scores(half, earlier):
        line = jax.ShapeDtypeStruct((blocks, SLOT), jnp.float32)
        fresh = jax.ShapeDtypeStruct((rows if half else half_rows, width), jnp.bfloat16)
        return pl.pallas_call(
            functools.partial(
                score_kernel,
                half=half,
                blocks=blocks,
                shards=shards,
                subs=subs,
                rows=rows,
                width=width,
                rate=rate,
                group=group,
            ),
            out_shape=(fresh, line) if half else (fresh, line, line),
            in_specs=[smem] + [vmem] * (5 + len(earlier)),
            out_specs=(vmem,) * (2 if half else 3),
            scratch_shapes=[pltpu.VMEM((total // 2, feat_width), jnp.bfloat16)],
            compiler_params=pltpu.CompilerParams(vmem_limit_bytes=12 * MIB + 6 * total * feat_width),
            cost_estimate=pl.CostEstimate(
                flops=row_count * total * feat_width,
                bytes_accessed=2 * row_count * feat_width,
                transcendentals=total * feat_width // 2,
            ),
            name=f"scores{half}",
        )(block_ids, slots, owned[half], points, codes[half], others[half], *earlier)

    fresh, own_score, rival = scores(0, ())
    fresh, margin = scores(1, (own_score, rival, fresh))
    return fresh, margin.reshape(row_count)


def solution(mesh):
    return jax.shard_map(
        local,
        mesh=mesh,
        in_specs=(
            P(("groups", "shard", "sub"), None),
            P(("groups", "shard", "sub")),
            P(("groups", "shard", "sub")),
            P(("groups", "shard", "sub")),
            P(("groups", "shard"), "sub"),
        ),
        out_specs=(P(("groups", "shard"), "sub"), P(("groups", "shard", "sub"))),
        check_vma=False,
    )
```

time: 59.6 us -> 46.8 us (0.79)
  blocking collectives: 27.7 us -> 0 us
  starting transfers between devices: 3.94 us -> 14.1 us
  waiting for transfers between devices: 16.3 us -> 20.1 us
    all_gather x1 -> x0, blocking collectives: 14.4 us -> none  [local(): gathered = lax.all_gather(encode(combined, rate), 'shard', axis=0)]
    all_to_all x1 -> x0, blocking collectives: 13.3 us -> none  [local(): lax.all_to_all(encode(mine[0], rate), 'shard', split_axis=0, concat_axis=...]
    ppermute x5 -> x14, starting transfers between devices: 3.94 us -> 14.1 us  [swap(): lax.ppermute(value, axis, [(i, i ^ bit) for i in range(counts[axis])])]
    ppermute x5 -> x14, waiting for transfers between devices: 16.3 us -> 20.1 us  [swap(): lax.ppermute(value, axis, [(i, i ^ bit) for i in range(counts[axis])])]
    add x0 -> x9, other arithmetic: none -> 0.64 us  [the longest x4 0.44 us: local(): mine[half] = mine[half][:count] + decode(there, rate)]
    pallas_call x1, Pallas kernels: 4.49 us -> 3.86 us  [local(): pl.pallas_call(functools.partial(sums_kernel, blocks=blocks, shards=shard...]
    pallas_call x1 -> x2, Pallas kernels: 4.59 us -> 5.2 us  [scores(): pl.pallas_call(functools.partial(score_kernel, half=half, blocks=blocks,...]
  transfers between devices with their start and end apart: 5 -> 14, of which waited for: 4 -> 11; matrix products, arithmetic and copies ran while one was open for 0% -> 3% of each run, Pallas kernels for 0% -> 5%
where the time goes in v3:
time: 46.8 us; the launch traced here: 46.4 us
  waiting for transfers between devices  20.1 us (43%)
  starting transfers between devices  14.1 us (30%)
  Pallas kernels  9.06 us (19%)
  other arithmetic  1.57 us (3%)
  between operations  1.52 us (3%)
    ppermute x14, waiting for transfers between devices, swap(): lax.ppermute(value, axis, [(i, i ^ bit) for i in range(counts[axis])])  20.1 us
    ppermute x14, starting transfers between devices, swap(): lax.ppermute(value, axis, [(i, i ^ bit) for i in range(counts[axis])])  14.1 us
    pallas_call x2, Pallas kernels, scores(): pl.pallas_call(functools.partial(score_kernel, half=half, blocks=blocks,...  5.2 us
    pallas_call x1, Pallas kernels, local(): pl.pallas_call(functools.partial(sums_kernel, blocks=blocks, shards=shard...  3.86 us
  transfers between devices with their start and end apart: 14, of which 11 were waited for; matrix products, arithmetic and copies ran while one was open for 3% of the time, Pallas kernels for 5%

profile of v3, /device:TPU:0, one launch (start us, length us, event | category | flops | bytes accessed | tf_op | source)
XLA Modules:
  0.0 46.4 jit_solution(14573527053537376608)
XLA Ops:
  0.6 0.0 copy-start.3
  1.3 3.9 %sums.1 = (f32[8,64,256]{2,1,0:T(8,128)S(1)}, f32[8,64,256]{2,1,0:T(8,128)S(1)}, f32[8,64,256]{2,1,0:T(8,128)S(1)}, f32[8,64,256]{2,1,0:T(8,128)S(1)}) custom-call(s32[1]{0:T(128)S(6)} %copy.7.live, s32[12]{0:T(128)} %bids.3, s32[12,128]{1,0:T(8,128)} %bitcast.34, bf16[1536,1024]{1,0:T(8,128)(2,1)} %points.5), custom_call_target="tpu_custom_call" | custom-call | tf_op jit(solution)/shard_map/sums/pallas_call | solution.py:173
  5.2 0.9 %collective-permute-start.7 = (f32[8,64,256]{2,1,0:T(8,128)S(1)}, f32[8,64,256]{2,1,0:T(8,128)S(1)}, u32[]{:S(2)}, u32[]{:S(2)}) collective-permute-start(f32[8,64,256]{2,1,0:T(8,128)S(1)} %get-tuple-element.14), channel_id=1, source_target_pairs={{0,1},{1,0},{2,3},{3,2},{4,5},{5,4},{6,7},{7,6},{8,9},{9,8},{10,11... | collective-permute-start | bytes 1572872 | tf_op jit(solution)/shard_map/ppermute | solution.py:170
  6.1 0.1 collective-permute-start
  6.2 0.0 copy-done.3
  6.2 1.4 %collective-permute-done.7 = f32[8,64,256]{2,1,0:T(8,128)S(1)} collective-permute-done((f32[8,64,256]{2,1,0:T(8,128)S(1)}, f32[8,64,256]{2,1,0:T(8,128)S(1)}, u32[]{:S(2)}, u32[]{:S(2)}) %collective-permute-start.7) | collective-permute-done | bytes 524320 | tf_op jit(solution)/shard_map/ppermute | solution.py:170
  7.7 0.1 add.101
  7.7 0.1 fusion.5
  7.9 3.1 %collective-permute-start.8 = (s16[4,64,256]{2,1,0:T(8,128)(2,1)S(1)}, s16[4,64,256]{2,1,0:T(8,128)(2,1)S(1)}, u32[]{:S(2)}, u32[]{:S(2)}) collective-permute-start(s16[4,64,256]{2,1,0:T(8,128)(2,1)S(1)} %fusion.5), channel_id=1, source_target_pairs={{0,2},{1,3},{2,0},{3,1},{4,6},{5,7},{6,4},{7,5},{8,10},{9,11},{10,... | collective-permute-start | bytes 393224 | tf_op jit(solution)/shard_map/ppermute | solution.py:170
  11.0 0.0 collective-permute-done
  11.0 0.1 add.88
  11.1 0.1 fusion.1
  11.2 1.0 %collective-permute-start.1 = (s16[4,64,256]{2,1,0:T(8,128)(2,1)S(1)}, s16[4,64,256]{2,1,0:T(8,128)(2,1)S(1)}, u32[]{:S(2)}, u32[]{:S(2)}) collective-permute-start(s16[4,64,256]{2,1,0:T(8,128)(2,1)S(1)} %fusion.1), channel_id=1, source_target_pairs={{0,4},{4,0},{8,12},{12,8},{1,5},{5,1},{9,13},{13,9},{2,6},{6,2},{1... | collective-permute-start | bytes 393224 | tf_op jit(solution)/shard_map/ppermute | solution.py:170
  12.2 2.6 %collective-permute-done.8 = s16[4,64,256]{2,1,0:T(8,128)(2,1)S(1)} collective-permute-done((s16[4,64,256]{2,1,0:T(8,128)(2,1)S(1)}, s16[4,64,256]{2,1,0:T(8,128)(2,1)S(1)}, u32[]{:S(2)}, u32[]{:S(2)}) %collective-permute-start.8) | collective-permute-done | bytes 131104 | tf_op jit(solution)/shard_map/ppermute | solution.py:170
  14.8 0.1 fusion.7
  15.0 0.0 copy-start
  15.0 0.0 copy-start.1
  15.0 0.0 copy-start.2
  15.0 0.1 fusion.18
  15.1 1.9 %collective-permute-start.9 = (s16[2,64,256]{2,1,0:T(8,128)(2,1)S(1)}, s16[2,64,256]{2,1,0:T(8,128)(2,1)S(1)}, u32[]{:S(2)}, u32[]{:S(2)}) collective-permute-start(s16[2,64,256]{2,1,0:T(8,128)(2,1)S(1)} %fusion.18), channel_id=1, source_target_pairs={{0,4},{4,0},{8,12},{12,8},{1,5},{5,1},{9,13},{13,9},{2,6},{6,2},{1... | collective-permute-start | bytes 196616 | tf_op jit(solution)/shard_map/ppermute | solution.py:170
  17.0 0.0 collective-permute-done.1
  17.0 0.1 fusion.3
  17.1 0.1 fusion.9
  17.2 0.9 %collective-permute-start.2 = (s16[2,64,256]{2,1,0:T(8,128)(2,1)S(1)}, s16[2,64,256]{2,1,0:T(8,128)(2,1)S(1)}, u32[]{:S(2)}, u32[]{:S(2)}) collective-permute-start(s16[2,64,256]{2,1,0:T(8,128)(2,1)S(1)} %fusion.9), channel_id=1, source_target_pairs={{0,2},{1,3},{2,0},{3,1},{4,6},{5,7},{6,4},{7,5},{8,10},{9,11},{10,... | collective-permute-start | bytes 196616 | tf_op jit(solution)/shard_map/ppermute | solution.py:170
  18.1 1.3 %collective-permute-done.9 = s16[2,64,256]{2,1,0:T(8,128)(2,1)S(1)} collective-permute-done((s16[2,64,256]{2,1,0:T(8,128)(2,1)S(1)}, s16[2,64,256]{2,1,0:T(8,128)(2,1)S(1)}, u32[]{:S(2)}, u32[]{:S(2)}) %collective-permute-start.9) | collective-permute-done | bytes 65568 | tf_op jit(solution)/shard_map/ppermute | solution.py:170
  19.4 0.1 fusion.20
  19.5 2.0 %collective-permute-done.2 = s16[2,64,256]{2,1,0:T(8,128)(2,1)S(1)} collective-permute-done((s16[2,64,256]{2,1,0:T(8,128)(2,1)S(1)}, s16[2,64,256]{2,1,0:T(8,128)(2,1)S(1)}, u32[]{:S(2)}, u32[]{:S(2)}) %collective-permute-start.2) | collective-permute-done | bytes 65568 | tf_op jit(solution)/shard_map/ppermute | solution.py:170
  21.5 0.1 fusion.11
  21.6 0.1 fusion.22
  21.7 2.1 %collective-permute-start.10 = (s16[2,64,256]{2,1,0:T(8,128)(2,1)S(1)}, s16[2,64,256]{2,1,0:T(8,128)(2,1)S(1)}, u32[]{:S(2)}, u32[]{:S(2)}) collective-permute-start(s16[2,64,256]{2,1,0:T(8,128)(2,1)S(1)} %fusion.22), channel_id=1, source_target_pairs={{0,8},{4,12},{8,0},{12,4},{1,9},{5,13},{9,1},{13,5},{2,10},{6,14},... | collective-permute-start | bytes 196616 | tf_op jit(solution)/shard_map/ppermute | solution.py:170
  23.9 0.1 fusion.13
  23.9 0.9 %collective-permute-start.3 = (s16[2,64,256]{2,1,0:T(8,128)(2,1)S(1)}, s16[2,64,256]{2,1,0:T(8,128)(2,1)S(1)}, u32[]{:S(2)}, u32[]{:S(2)}) collective-permute-start(s16[2,64,256]{2,1,0:T(8,128)(2,1)S(1)} %fusion.13), channel_id=1, source_target_pairs={{0,8},{4,12},{8,0},{12,4},{1,9},{5,13},{9,1},{13,5},{2,10},{6,14},... | collective-permute-start | bytes 196616 | tf_op jit(solution)/shard_map/ppermute | solution.py:170
  24.8 3.5 %collective-permute-done.10 = s16[2,64,256]{2,1,0:T(8,128)(2,1)S(1)} collective-permute-done((s16[2,64,256]{2,1,0:T(8,128)(2,1)S(1)}, s16[2,64,256]{2,1,0:T(8,128)(2,1)S(1)}, u32[]{:S(2)}, u32[]{:S(2)}) %collective-permute-start.10) | collective-permute-done | bytes 65568 | tf_op jit(solution)/shard_map/ppermute | solution.py:170
  28.3 0.1 fusion.23
  28.4 1.4 %collective-permute-done.3 = s16[2,64,256]{2,1,0:T(8,128)(2,1)S(1)} collective-permute-done((s16[2,64,256]{2,1,0:T(8,128)(2,1)S(1)}, s16[2,64,256]{2,1,0:T(8,128)(2,1)S(1)}, u32[]{:S(2)}, u32[]{:S(2)}) %collective-permute-start.3) | collective-permute-done | bytes 65568 | tf_op jit(solution)/shard_map/ppermute | solution.py:170
  29.9 0.1 fusion.14
  30.0 0.1 fusion.25
  30.1 0.4 collective-permute-start.11
  30.5 0.1 fusion.16
  30.6 0.8 %collective-permute-start.4 = (s16[2,64,256]{2,1,0:T(8,128)(2,1)S(1)}, s16[2,64,256]{2,1,0:T(8,128)(2,1)S(1)}, u32[]{:S(2)}, u32[]{:S(2)}) collective-permute-start(s16[2,64,256]{2,1,0:T(8,128)(2,1)S(1)} %fusion.16), channel_id=1, source_target_pairs={{0,2},{1,3},{2,0},{3,1},{4,6},{5,7},{6,4},{7,5},{8,10},{9,11},{10,... | collective-permute-start | bytes 196616 | tf_op jit(solution)/shard_map/ppermute | solution.py:170
  31.4 3.1 %collective-permute-done.11 = s16[2,64,256]{2,1,0:T(8,128)(2,1)S(1)} collective-permute-done((s16[2,64,256]{2,1,0:T(8,128)(2,1)S(1)}, s16[2,64,256]{2,1,0:T(8,128)(2,1)S(1)}, u32[]{:S(2)}, u32[]{:S(2)}) %collective-permute-start.11) | collective-permute-done | bytes 65568 | tf_op jit(solution)/shard_map/ppermute | solution.py:170
  34.5 0.7 %collective-permute-start.12 = (s16[4,64,256]{2,1,0:T(8,128)(2,1)S(1)}, s16[4,64,256]{2,1,0:T(8,128)(2,1)S(1)}, u32[]{:S(2)}, u32[]{:S(2)}) collective-permute-start(s16[4,64,256]{2,1,0:T(8,128)(2,1)S(1)} %pad_add_fusion.3), channel_id=1, source_target_pairs={{0,2},{1,3},{2,0},{3,1},{4,6},{5,7},{6,4},{7,5},{8,10},{9,11},{10,... | collective-permute-start | bytes 393224 | tf_op jit(solution)/shard_map/ppermute | solution.py:170
  35.2 0.4 collective-permute-done.4
  35.6 1.0 %collective-permute-start.5 = (s16[4,64,256]{2,1,0:T(8,128)(2,1)S(1)}, s16[4,64,256]{2,1,0:T(8,128)(2,1)S(1)}, u32[]{:S(2)}, u32[]{:S(2)}) collective-permute-start(s16[4,64,256]{2,1,0:T(8,128)(2,1)S(1)} %pad_add_fusion.2), channel_id=1, source_target_pairs={{0,4},{4,0},{8,12},{12,8},{1,5},{5,1},{9,13},{13,9},{2,6},{6,2},{1... | collective-permute-start | bytes 393224 | tf_op jit(solution)/shard_map/ppermute | solution.py:170
  36.6 2.9 %collective-permute-done.12 = s16[4,64,256]{2,1,0:T(8,128)(2,1)S(1)} collective-permute-done((s16[4,64,256]{2,1,0:T(8,128)(2,1)S(1)}, s16[4,64,256]{2,1,0:T(8,128)(2,1)S(1)}, u32[]{:S(2)}, u32[]{:S(2)}) %collective-permute-start.12) | collective-permute-done | bytes 131104 | tf_op jit(solution)/shard_map/ppermute | solution.py:170
  39.6 0.1 collective-permute-start.13
  39.7 1.0 %collective-permute-done.5 = s16[4,64,256]{2,1,0:T(8,128)(2,1)S(1)} collective-permute-done((s16[4,64,256]{2,1,0:T(8,128)(2,1)S(1)}, s16[4,64,256]{2,1,0:T(8,128)(2,1)S(1)}, u32[]{:S(2)}, u32[]{:S(2)}) %collective-permute-start.5) | collective-permute-done | bytes 131104 | tf_op jit(solution)/shard_map/ppermute | solution.py:170
  40.7 0.1 collective-permute-start.6
  40.7 0.5 collective-permute-done.13.far
  41.2 0.0 copy-done
  41.2 0.0 copy-done.1
  41.2 0.0 copy-done.2
  41.2 2.3 %scores0.1 = (bf16[64,256]{1,0:T(8,128)(2,1)S(1)}, f32[12,128]{1,0:T(8,128)S(1)}, f32[12,128]{1,0:T(8,128)S(1)}) custom-call(s32[12]{0:T(128)S(1)} %copy-done.2, s32[12,128]{1,0:T(8,128)S(1)} %bitcast.35, f32[64,256]{1,0:T(8,128)S(1)} %get-tuple-element.20.own, bf16[1536,1024]{1,0:T(8,128)(2,1)S(1)} %copy-done, s16[8,64,256]{2,1,0:T(8,128)(2,1)S(1)} %pad_add_fusion.1.near, ...), custom_call_target="tpu_custom_call" | custom-call | flops 805306368 | bytes 3145728 | tf_op jit(solution)/shard_map/scores0/pallas_call | solution.py:220
  43.5 0.0 collective-permute-done.6.far
  43.5 2.9 %scores1.1 = (bf16[128,256]{1,0:T(8,128)(2,1)}, f32[12,128]{1,0:T(8,128)}) custom-call(s32[12]{0:T(128)S(1)} %copy-done.2, s32[12,128]{1,0:T(8,128)S(1)} %bitcast.36, f32[64,256]{1,0:T(8,128)S(1)} %get-tuple-element.21.own, bf16[1536,1024]{1,0:T(8,128)(2,1)S(1)} %copy-done, s16[8,64,256]{2,1,0:T(8,128)(2,1)S(1)} %pad_add_fusion.near, ...), custom_call_target="tpu_custom_call" | custom-call | flops 805306368 | bytes 3145728 | tf_op jit(solution)/shard_map/scores1/pallas_call | solution.py:220
  (11 shorter events, 0.2 us)
Async XLA Ops:
  0.6 5.6 %copy-start.3 = (bf16[128,256]{1,0:T(8,128)(2,1)S(1)}, bf16[128,256]{1,0:T(8,128)(2,1)}, u32[]{:S(2)}) copy-start(bf16[128,256]{1,0:T(8,128)(2,1)} %param.9) | copy-start | bytes 196612
  5.2 2.5 %collective-permute-start.7 = (f32[8,64,256]{2,1,0:T(8,128)S(1)}, f32[8,64,256]{2,1,0:T(8,128)S(1)}, u32[]{:S(2)}, u32[]{:S(2)}) collective-permute-start(f32[8,64,256]{2,1,0:T(8,128)S(1)} %get-tuple-element.14), channel_id=1, source_target_pairs={{0,1},{1,0},{2,3},{3,2},{4,5},{5,4},{6,7},{7,6},{8,9},{9,8},{10,11... | collective-permute-start | bytes 1572872 | tf_op jit(solution)/shard_map/ppermute | solution.py:170
  6.1 4.9 %collective-permute-start = (f32[8,64,256]{2,1,0:T(8,128)S(1)}, f32[8,64,256]{2,1,0:T(8,128)S(1)}, u32[]{:S(2)}, u32[]{:S(2)}) collective-permute-start(f32[8,64,256]{2,1,0:T(8,128)S(1)} %get-tuple-element.12), channel_id=1, source_target_pairs={{0,1},{1,0},{2,3},{3,2},{4,5},{5,4},{6,7},{7,6},{8,9},{9,8},{10,11... | collective-permute-start | bytes 1572872 | tf_op jit(solution)/shard_map/ppermute | solution.py:170
  7.9 6.9 %collective-permute-start.8 = (s16[4,64,256]{2,1,0:T(8,128)(2,1)S(1)}, s16[4,64,256]{2,1,0:T(8,128)(2,1)S(1)}, u32[]{:S(2)}, u32[]{:S(2)}) collective-permute-start(s16[4,64,256]{2,1,0:T(8,128)(2,1)S(1)} %fusion.5), channel_id=1, source_target_pairs={{0,2},{1,3},{2,0},{3,1},{4,6},{5,7},{6,4},{7,5},{8,10},{9,11},{10,... | collective-permute-start | bytes 393224 | tf_op jit(solution)/shard_map/ppermute | solution.py:170
  11.2 5.7 %collective-permute-start.1 = (s16[4,64,256]{2,1,0:T(8,128)(2,1)S(1)}, s16[4,64,256]{2,1,0:T(8,128)(2,1)S(1)}, u32[]{:S(2)}, u32[]{:S(2)}) collective-permute-start(s16[4,64,256]{2,1,0:T(8,128)(2,1)S(1)} %fusion.1), channel_id=1, source_target_pairs={{0,4},{4,0},{8,12},{12,8},{1,5},{5,1},{9,13},{13,9},{2,6},{6,2},{1... | collective-permute-start | bytes 393224 | tf_op jit(solution)/shard_map/ppermute | solution.py:170
  15.0 26.2 %copy-start = (bf16[1536,1024]{1,0:T(8,128)(2,1)S(1)}, bf16[1536,1024]{1,0:T(8,128)(2,1)}, u32[]{:S(2)}) copy-start(bf16[1536,1024]{1,0:T(8,128)(2,1)} %points.5) | copy-start | bytes 9437188
  15.0 26.2 %copy-start.1 = (s32[1536]{0:T(1024)S(1)}, s32[1536]{0:T(1024)}, u32[]{:S(2)}) copy-start(s32[1536]{0:T(1024)} %param.7) | copy-start | bytes 18436
  15.0 26.2 %copy-start.2 = (s32[12]{0:T(128)S(1)}, s32[12]{0:T(128)}, u32[]{:S(2)}) copy-start(s32[12]{0:T(128)} %bids.3) | copy-start | bytes 148
  15.1 4.3 %collective-permute-start.9 = (s16[2,64,256]{2,1,0:T(8,128)(2,1)S(1)}, s16[2,64,256]{2,1,0:T(8,128)(2,1)S(1)}, u32[]{:S(2)}, u32[]{:S(2)}) collective-permute-start(s16[2,64,256]{2,1,0:T(8,128)(2,1)S(1)} %fusion.18), channel_id=1, source_target_pairs={{0,4},{4,0},{8,12},{12,8},{1,5},{5,1},{9,13},{13,9},{2,6},{6,2},{1... | collective-permute-start | bytes 196616 | tf_op jit(solution)/shard_map/ppermute | solution.py:170
  17.2 4.3 %collective-permute-start.2 = (s16[2,64,256]{2,1,0:T(8,128)(2,1)S(1)}, s16[2,64,256]{2,1,0:T(8,128)(2,1)S(1)}, u32[]{:S(2)}, u32[]{:S(2)}) collective-permute-start(s16[2,64,256]{2,1,0:T(8,128)(2,1)S(1)} %fusion.9), channel_id=1, source_target_pairs={{0,2},{1,3},{2,0},{3,1},{4,6},{5,7},{6,4},{7,5},{8,10},{9,11},{10,... | collective-permute-start | bytes 196616 | tf_op jit(solution)/shard_map/ppermute | solution.py:170
  21.7 6.6 %collective-permute-start.10 = (s16[2,64,256]{2,1,0:T(8,128)(2,1)S(1)}, s16[2,64,256]{2,1,0:T(8,128)(2,1)S(1)}, u32[]{:S(2)}, u32[]{:S(2)}) collective-permute-start(s16[2,64,256]{2,1,0:T(8,128)(2,1)S(1)} %fusion.22), channel_id=1, source_target_pairs={{0,8},{4,12},{8,0},{12,4},{1,9},{5,13},{9,1},{13,5},{2,10},{6,14},... | collective-permute-start | bytes 196616 | tf_op jit(solution)/shard_map/ppermute | solution.py:170
  23.9 5.9 %collective-permute-start.3 = (s16[2,64,256]{2,1,0:T(8,128)(2,1)S(1)}, s16[2,64,256]{2,1,0:T(8,128)(2,1)S(1)}, u32[]{:S(2)}, u32[]{:S(2)}) collective-permute-start(s16[2,64,256]{2,1,0:T(8,128)(2,1)S(1)} %fusion.13), channel_id=1, source_target_pairs={{0,8},{4,12},{8,0},{12,4},{1,9},{5,13},{9,1},{13,5},{2,10},{6,14},... | collective-permute-start | bytes 196616 | tf_op jit(solution)/shard_map/ppermute | solution.py:170
  30.1 4.5 %collective-permute-start.11 = (s16[2,64,256]{2,1,0:T(8,128)(2,1)S(1)}, s16[2,64,256]{2,1,0:T(8,128)(2,1)S(1)}, u32[]{:S(2)}, u32[]{:S(2)}) collective-permute-start(s16[2,64,256]{2,1,0:T(8,128)(2,1)S(1)} %fusion.25), channel_id=1, source_target_pairs={{0,4},{4,0},{8,12},{12,8},{1,5},{5,1},{9,13},{13,9},{2,6},{6,2},{1... | collective-permute-start | bytes 196616 | tf_op jit(solution)/shard_map/ppermute | solution.py:170
  30.6 5.0 %collective-permute-start.4 = (s16[2,64,256]{2,1,0:T(8,128)(2,1)S(1)}, s16[2,64,256]{2,1,0:T(8,128)(2,1)S(1)}, u32[]{:S(2)}, u32[]{:S(2)}) collective-permute-start(s16[2,64,256]{2,1,0:T(8,128)(2,1)S(1)} %fusion.16), channel_id=1, source_target_pairs={{0,2},{1,3},{2,0},{3,1},{4,6},{5,7},{6,4},{7,5},{8,10},{9,11},{10,... | collective-permute-start | bytes 196616 | tf_op jit(solution)/shard_map/ppermute | solution.py:170
  34.5 5.0 %collective-permute-start.12 = (s16[4,64,256]{2,1,0:T(8,128)(2,1)S(1)}, s16[4,64,256]{2,1,0:T(8,128)(2,1)S(1)}, u32[]{:S(2)}, u32[]{:S(2)}) collective-permute-start(s16[4,64,256]{2,1,0:T(8,128)(2,1)S(1)} %pad_add_fusion.3), channel_id=1, source_target_pairs={{0,2},{1,3},{2,0},{3,1},{4,6},{5,7},{6,4},{7,5},{8,10},{9,11},{10,... | collective-permute-start | bytes 393224 | tf_op jit(solution)/shard_map/ppermute | solution.py:170
  35.6 5.0 %collective-permute-start.5 = (s16[4,64,256]{2,1,0:T(8,128)(2,1)S(1)}, s16[4,64,256]{2,1,0:T(8,128)(2,1)S(1)}, u32[]{:S(2)}, u32[]{:S(2)}) collective-permute-start(s16[4,64,256]{2,1,0:T(8,128)(2,1)S(1)} %pad_add_fusion.2), channel_id=1, source_target_pairs={{0,4},{4,0},{8,12},{12,8},{1,5},{5,1},{9,13},{13,9},{2,6},{6,2},{1... | collective-permute-start | bytes 393224 | tf_op jit(solution)/shard_map/ppermute | solution.py:170
  39.6 1.6 %collective-permute-start.13 = (s16[8,64,256]{2,1,0:T(8,128)(2,1)S(1)}, s16[8,64,256]{2,1,0:T(8,128)(2,1)S(1)}, u32[]{:S(2)}, u32[]{:S(2)}) collective-permute-start(s16[8,64,256]{2,1,0:T(8,128)(2,1)S(1)} %pad_add_fusion.1.near), channel_id=1, source_target_pairs={{0,1},{1,0},{2,3},{3,2},{4,5},{5,4},{6,7},{7,6},{8,9},{9,8},{10,11... | collective-permute-start | bytes 786440 | tf_op jit(solution)/shard_map/ppermute | solution.py:170
  40.7 2.8 %collective-permute-start.6 = (s16[8,64,256]{2,1,0:T(8,128)(2,1)S(1)}, s16[8,64,256]{2,1,0:T(8,128)(2,1)S(1)}, u32[]{:S(2)}, u32[]{:S(2)}) collective-permute-start(s16[8,64,256]{2,1,0:T(8,128)(2,1)S(1)} %pad_add_fusion.near), channel_id=1, source_target_pairs={{0,1},{1,0},{2,3},{3,2},{4,5},{5,4},{6,7},{7,6},{8,9},{9,8},{10,11... | collective-permute-start | bytes 786440 | tf_op jit(solution)/shard_map/ppermute | solution.py:170

commit v4 on v2

v4 whole, which is shorter than its diff:
```python
import functools
import math

import jax
import jax.numpy as jnp
from jax import lax
from jax.experimental import pallas as pl
from jax.experimental.pallas import tpu as pltpu
from jax.sharding import PartitionSpec as P

SLOT = 128
POINT_LIMIT = 6.0

prior_weight = 4.0
norm_eps = 1e-06

LOW_EXP = -32
MIB = 1 << 20


def code_rate(top_exp):
    return 32767.0 / (top_exp - LOW_EXP)


def encode(value, rate):
    size = jnp.maximum(jnp.abs(value), 2.0**LOW_EXP)
    level = jnp.floor((jnp.log2(size) - LOW_EXP) * rate + 0.5)
    return jnp.where(value < 0.0, -level, level).astype(jnp.int32).astype(jnp.int16)


def decode(code, rate):
    level = code.astype(jnp.int32).astype(jnp.float32)
    size = jnp.exp2(jnp.abs(level) * (1.0 / rate) + LOW_EXP)
    return jnp.where(level == 0.0, 0.0, jnp.where(level < 0.0, -size, size))


def bits_of(count):
    return [1 << bit for bit in range(count.bit_length() - 1)]


def steps_of(subs, shards, side):
    subs_rest = [("sub", bit) for bit in bits_of(subs)[1:]]
    shards_all = [("shard", bit) for bit in bits_of(shards)]
    if side == 0:
        return subs_rest + shards_all
    return shards_all[:1] + subs_rest + shards_all[1:]


def piece_at(steps, over_sub, over_shard):
    place = 0
    for axis, bit in steps:
        over = over_sub if axis == "sub" else over_shard
        place = place * 2 + (over // bit) % 2
    return place


def sided(side, subs, shards, over_sub, over_shard):
    places = [piece_at(steps_of(subs, shards, s), over_sub, over_shard) for s in range(2)]
    return jnp.where(side == 0, places[0], places[1])


def sums_kernel(
    live_in, bids_in, slots_in, old_in, points, keep, send, live, bids, slots, old, held, small, arrived,
    *, blocks, shards, subs, width
):
    sub, shard = lax.axis_index("sub"), lax.axis_index("shard")
    side = sub % 2
    firsts = [
        pltpu.make_async_copy(here, there, small.at[index])
        for index, (here, there) in enumerate(
            [(live_in, live), (bids_in, bids), (slots_in, slots), (old_in, old)]
        )
    ]
    for copy in firsts:
        copy.start()
    copies = []
    for block in range(blocks):
        span = pl.ds(block * SLOT, SLOT)
        copies.append(pltpu.make_async_copy(points.at[span], held.at[span], arrived.at[block]))
        copies[-1].start()
    keep[...] = jnp.zeros_like(keep)
    send[...] = jnp.zeros_like(send)
    for copy in firsts:
        copy.wait()
    keep[0] = prior_weight * old[...].astype(jnp.float32)
    for block in range(blocks):
        copies[block].wait()

        @pl.when(block < live[0])
        def _(block=block):
            hot = slots[block : block + 1, :] == lax.broadcasted_iota(jnp.int32, (SLOT, SLOT), 0)
            hot = hot.astype(jnp.bfloat16)
            over_shard = bids[block] ^ shard
            for over_sub in range(0, subs, 2):
                for sums, flip in ((keep, 0), (send, 1)):
                    place = sided(side ^ flip, subs, shards, over_sub, over_shard)
                    column = pl.multiple_of((sub ^ over_sub ^ flip) * width, width)
                    sums[place] += jnp.dot(
                        hot,
                        held[block * SLOT : (block + 1) * SLOT, pl.ds(column, width)],
                        preferred_element_type=jnp.float32,
                    )


def pair_kernel(*refs, rate):
    terms, (mine, code) = refs[:-2], refs[-2:]
    total = terms[0][...] + terms[1][...]
    for term in terms[2:]:
        total = total + decode(term[...], rate)
    mine[...] = total
    code[...] = encode(total, rate)


def finish_kernel(mine, there, own, code, *, rate):
    own[...] = mine[0] + decode(there[1], rate)
    code[0] = encode(own[...], rate)
    code[1] = encode(mine[1] + decode(there[0], rate), rate)


def score_kernel(
    bids, slots, own, points, near, far, fresh, margin, cents, *, blocks, shards, subs, rows, width, rate, group
):
    sub, shard = lax.axis_index("sub"), lax.axis_index("shard")
    side = sub % 2
    for over_shard in range(shards):
        parts = []
        for over_sub in range(0, subs, 2):
            parts.append((sub ^ over_sub, decode(near[sided(side, subs, shards, over_sub, over_shard)], rate)))
            parts.append((sub ^ 1 ^ over_sub, decode(far[sided(1 - side, subs, shards, over_sub, over_shard)], rate)))
        squares = sum(jnp.sum(part * part, axis=1, keepdims=True) for _, part in parts)
        scale = lax.rsqrt(squares + norm_eps)
        row = pl.ds(pl.multiple_of((shard ^ over_shard) * rows, rows), rows)
        for place, part in parts:
            cents[row, pl.ds(pl.multiple_of(place * width, width), width)] = (part * scale).astype(jnp.bfloat16)
        if over_shard == 0:
            fresh[...] = (own[...] * scale).astype(jnp.bfloat16)

    for block in range(blocks // group):
        score = lax.dot_general(
            cents[...],
            points[block * group * SLOT : (block + 1) * group * SLOT, :],
            (((1,), (1,)), ((), ())),
            preferred_element_type=jnp.float32,
        )
        for inner in range(group):
            at = block * group + inner
            line = slice(at, at + 1)
            part = score[:, inner * SLOT : (inner + 1) * SLOT]
            hit = lax.broadcasted_iota(jnp.int32, part.shape, 0) == bids[at] * SLOT + slots[line, :]
            mine = jnp.sum(jnp.where(hit, part, 0.0), axis=0, keepdims=True)
            rival = jnp.max(jnp.where(hit, -jnp.inf, part), axis=0, keepdims=True)
            margin[line, :] = mine - rival


def local(points, block_ids, slot_ids, live_blocks, old_centroids):
    row_count, feat_width = points.shape
    blocks = row_count // SLOT
    shards = lax.axis_size("shard")
    subs = lax.axis_size("sub")
    rows, width = old_centroids.shape
    total = rows * shards
    top = POINT_LIMIT * (row_count * shards * subs + prior_weight)
    rate = code_rate(math.ceil(math.log2(top)))
    slots = slot_ids.reshape(blocks, SLOT)
    steps = [steps_of(subs, shards, side) for side in range(2)]
    pieces = 1 << len(steps[0])
    smem = pl.BlockSpec(memory_space=pltpu.SMEM)
    vmem = pl.BlockSpec(memory_space=pltpu.VMEM)
    hbm = pl.BlockSpec(memory_space=pltpu.HBM)

    def swap(value, turn):
        pairs = []
        for shard in range(shards):
            for sub in range(subs):
                axis, bit = steps[sub % 2][turn] if turn >= 0 else ("sub", 1)
                there = (shard ^ bit, sub) if axis == "shard" else (shard, sub ^ bit)
                pairs.append((shard * subs + sub, there[0] * subs + there[1]))
        return lax.ppermute(value, ("shard", "sub"), pairs)

    def in_hbm(value):
        return pltpu.with_memory_space_constraint(value, pltpu.HBM)

    piece = jax.ShapeDtypeStruct((pieces, rows, width), jnp.float32)
    keep, send = pl.pallas_call(
        functools.partial(sums_kernel, blocks=blocks, shards=shards, subs=subs, width=width),
        out_shape=(piece, piece),
        in_specs=[hbm] * 5,
        out_specs=(vmem, vmem),
        scratch_shapes=[
            pltpu.SMEM((1,), jnp.int32),
            pltpu.SMEM((blocks,), jnp.int32),
            pltpu.VMEM((blocks, SLOT), jnp.int32),
            pltpu.VMEM((rows, width), jnp.bfloat16),
            pltpu.VMEM((row_count, feat_width), jnp.bfloat16),
            pltpu.SemaphoreType.DMA((4,)),
            pltpu.SemaphoreType.DMA((blocks,)),
        ],
        compiler_params=pltpu.CompilerParams(vmem_limit_bytes=8 * MIB + 4 * total * feat_width),
        name="sums",
    )(live_blocks, in_hbm(block_ids), in_hbm(slots), in_hbm(old_centroids), in_hbm(points))

    terms = [keep, swap(send, -1)]

    def so_far(first, end):
        value = terms[0][first:end] + terms[1][first:end]
        for term in terms[2:]:
            value = value + decode(term[first:end], rate)
        return value

    count = pieces
    for turn in range(len(steps[0]) - 1):
        count //= 2
        terms.append(swap(encode(so_far(count, 2 * count), rate), turn))

    two = (2, rows, width)
    first_two = pl.BlockSpec(two, lambda step: (0, 0, 0))
    mine, code = pl.pallas_call(
        functools.partial(pair_kernel, rate=rate),
        grid=(1,),
        out_shape=(jax.ShapeDtypeStruct(two, jnp.float32), jax.ShapeDtypeStruct(two, jnp.int16)),
        in_specs=[first_two] * len(terms),
        out_specs=(first_two, first_two),
        name="pair",
    )(*terms)
    own, code = pl.pallas_call(
        functools.partial(finish_kernel, rate=rate),
        out_shape=(jax.ShapeDtypeStruct((rows, width), jnp.float32), jax.ShapeDtypeStruct(two, jnp.int16)),
        name="finish",
    )(mine, swap(code, len(steps[0]) - 1))

    near = code
    for turn in reversed(range(1, len(steps[0]) - 1)):
        near = jnp.concatenate([near, swap(near, turn)])
    last = swap(near, 0)
    far = jnp.concatenate([swap(near, -1), swap(last, -1)])
    near = jnp.concatenate([near, last])

    group = 2 if blocks % 2 == 0 else 1
    fresh, margin = pl.pallas_call(
        functools.partial(
            score_kernel, blocks=blocks, shards=shards, subs=subs, rows=rows, width=width, rate=rate, group=group
        ),
        out_shape=(
            jax.ShapeDtypeStruct((rows, width), jnp.bfloat16),
            jax.ShapeDtypeStruct((blocks, SLOT), jnp.float32),
        ),
        in_specs=[smem] + [vmem] * 5,
        out_specs=(vmem, vmem),
        scratch_shapes=[pltpu.VMEM((total, feat_width), jnp.bfloat16)],
        compiler_params=pltpu.CompilerParams(vmem_limit_bytes=12 * MIB + 6 * total * feat_width),
        name="scores",
    )(block_ids, slots, own, points, near, far)
    return fresh, margin.reshape(row_count)


def solution(mesh):
    return jax.shard_map(
        local,
        mesh=mesh,
        in_specs=(
            P(("groups", "shard", "sub"), None),
            P(("groups", "shard", "sub")),
            P(("groups", "shard", "sub")),
            P(("groups", "shard", "sub")),
            P(("groups", "shard"), "sub"),
        ),
        out_specs=(P(("groups", "shard"), "sub"), P(("groups", "shard", "sub"))),
        check_vma=False,
    )
```

time: 59.6 us -> 54.4 us (0.913)
  blocking collectives: 27.7 us -> 0 us
  waiting for transfers between devices: 16.3 us -> 26.2 us
  starting transfers between devices: 3.94 us -> 8.95 us
  Pallas kernels: 9.08 us -> 12.9 us
  local copies, waits for them, and re-layouts: 0.02 us -> 3.18 us
    all_gather x1 -> x0, blocking collectives: 14.4 us -> none  [local(): gathered = lax.all_gather(encode(combined, rate), 'shard', axis=0)]
    all_to_all x1 -> x0, blocking collectives: 13.3 us -> none  [local(): lax.all_to_all(encode(mine[0], rate), 'shard', split_axis=0, concat_axis=...]
    ppermute x5 -> x8, waiting for transfers between devices: 16.3 us -> 26.2 us  [swap(): return lax.ppermute(value, ('shard', 'sub'), pairs)]
    ppermute x5 -> x8, starting transfers between devices: 3.94 us -> 8.95 us  [swap(): return lax.ppermute(value, ('shard', 'sub'), pairs)]
    pallas_call x0 -> x2, Pallas kernels: none -> 3.97 us  [the longest x1 2.12 us: local(): pl.pallas_call(functools.partial(pair_kernel, rate=rate), grid=(1,), out_...]
    unnamed x8 -> x19, local copies, waits for them, and re-layouts: 0.02 us -> 3.18 us
    concatenate x0 -> x2, other arithmetic: none -> 0.99 us  [the longest x1 0.96 us: local(): near = jnp.concatenate([near, last])]
  transfers between devices with their start and end apart: 5 -> 8, of which waited for: 4 -> 7; matrix products, arithmetic and copies ran while one was open for 0% -> 4% of each run, Pallas kernels for 0% -> 0%
where the time goes in v4:
time: 54.4 us; the launch traced here: 54.1 us
  waiting for transfers between devices  26.2 us (48%)
  Pallas kernels  12.9 us (24%)
  starting transfers between devices  8.95 us (16%)
  local copies, waits for them, and re-layouts  3.18 us (6%)
  other arithmetic  1.54 us (3%)
  between operations  1.4 us (3%)
    ppermute x8, waiting for transfers between devices, swap(): return lax.ppermute(value, ('shard', 'sub'), pairs)  26.2 us
    ppermute x8, starting transfers between devices, swap(): return lax.ppermute(value, ('shard', 'sub'), pairs)  8.95 us
    pallas_call x1, Pallas kernels, local(): pl.pallas_call(functools.partial(sums_kernel, blocks=blocks, shards=shard...  4.55 us
    pallas_call x1, Pallas kernels, local(): pl.pallas_call(functools.partial(score_kernel, blocks=blocks, shards=shar...  4.34 us
    unnamed x19, local copies, waits for them, and re-layouts  3.18 us
    pallas_call x1, Pallas kernels, local(): pl.pallas_call(functools.partial(pair_kernel, rate=rate), grid=(1,), out_...  2.12 us
    pallas_call x1, Pallas kernels, local(): pl.pallas_call(functools.partial(finish_kernel, rate=rate), out_shape=(ja...  1.85 us
  transfers between devices with their start and end apart: 8, of which 7 were waited for; matrix products, arithmetic and copies ran while one was open for 4% of the time, Pallas kernels for 0%

profile of v4, /device:TPU:0, one launch (start us, length us, event | category | flops | bytes accessed | tf_op | source)
XLA Modules:
  0.0 54.1 jit_solution(8356024114542749108)
XLA Ops:
  1.3 4.6 %sums.1 = (f32[8,128,256]{2,1,0:T(8,128)S(1)}, f32[8,128,256]{2,1,0:T(8,128)S(1)}) custom-call(s32[1]{0:T(128)S(6)} %copy.8.live_in, s32[12]{0:T(128)} %bids.1, s32[12,128]{1,0:T(8,128)} %bitcast.2, bf16[128,256]{1,0:T(8,128)(2,1)} %old_in.1, bf16[1536,1024]{1,0:T(8,128)(2,1)} %points.3), custom_call_target="tpu_custom_call" | custom-call | tf_op jit(solution)/shard_map/sums/pallas_call | solution.py:184
  5.8 0.0 copy-start.1
  5.8 0.5 collective-permute-start
  6.4 2.3 %collective-permute-done.refs_1_ = f32[8,128,256]{2,1,0:T(8,128)S(1)} collective-permute-done((f32[8,128,256]{2,1,0:T(8,128)S(1)}, f32[8,128,256]{2,1,0:T(8,128)S(1)}, u32[]{:S(2)}, u32[]{:S(2)}) %collective-permute-start) | collective-permute-done | bytes 1048608 | tf_op jit(solution)/shard_map/ppermute | solution.py:178
  8.6 0.0 copy-start.5
  8.7 0.3 fusion.1
  8.9 0.0 copy-start
  8.9 0.0 copy-start.3
  8.9 0.0 copy-start.4
  9.0 1.6 %collective-permute-start.1 = (s16[4,128,256]{2,1,0:T(8,128)(2,1)S(1)}, s16[4,128,256]{2,1,0:T(8,128)(2,1)S(1)}, u32[]{:S(2)}, u32[]{:S(2)}) collective-permute-start(s16[4,128,256]{2,1,0:T(8,128)(2,1)S(1)} %fusion.1), channel_id=1, source_target_pairs={{0,2},{1,5},{2,0},{3,7},{4,6},{5,1},{6,4},{7,3},{8,10},{9,13},{10,... | collective-permute-start | bytes 786440 | tf_op jit(solution)/shard_map/ppermute | solution.py:178
  10.6 4.8 %collective-permute-done.1.refs_2_ = s16[4,128,256]{2,1,0:T(8,128)(2,1)S(1)} collective-permute-done((s16[4,128,256]{2,1,0:T(8,128)(2,1)S(1)}, s16[4,128,256]{2,1,0:T(8,128)(2,1)S(1)}, u32[]{:S(2)}, u32[]{:S(2)}) %collective-permute-start.1) | collective-permute-done | bytes 262176 | tf_op jit(solution)/shard_map/ppermute | solution.py:178
  15.4 0.0 copy-done.1
  15.4 0.0 copy-start.6
  15.4 0.3 fusion.5
  15.7 0.0 copy-done.5
  15.7 2.5 %collective-permute-start.2 = (s16[2,128,256]{2,1,0:T(8,128)(2,1)S(1)}, s16[2,128,256]{2,1,0:T(8,128)(2,1)S(1)}, u32[]{:S(2)}, u32[]{:S(2)}) collective-permute-start(s16[2,128,256]{2,1,0:T(8,128)(2,1)S(1)} %fusion.5), channel_id=1, source_target_pairs={{0,4},{1,3},{2,6},{3,1},{4,0},{5,7},{6,2},{7,5},{8,12},{9,11},{10,... | collective-permute-start | bytes 393224 | tf_op jit(solution)/shard_map/ppermute | solution.py:178
  18.2 2.9 %collective-permute-done.2.refs_3_ = s16[2,128,256]{2,1,0:T(8,128)(2,1)S(1)} collective-permute-done((s16[2,128,256]{2,1,0:T(8,128)(2,1)S(1)}, s16[2,128,256]{2,1,0:T(8,128)(2,1)S(1)}, u32[]{:S(2)}, u32[]{:S(2)}) %collective-permute-start.2) | collective-permute-done | bytes 131104 | tf_op jit(solution)/shard_map/ppermute | solution.py:178
  21.1 0.0 copy-done.6
  21.1 0.0 copy-start.7
  21.1 0.7 %copy-done.7 = s16[2,128,256]{2,1,0:T(8,128)(2,1)} copy-done((s16[2,128,256]{2,1,0:T(8,128)(2,1)}, s16[2,128,256]{2,1,0:T(8,128)(2,1)S(1)}, u32[]{:S(2)}) %copy-start.7) | copy-done | bytes 131096
  21.8 2.1 %pair.1 = (f32[2,128,256]{2,1,0:T(8,128)}, s16[2,128,256]{2,1,0:T(8,128)(2,1)}) custom-call(f32[8,128,256]{2,1,0:T(8,128)} %copy-done.1, f32[8,128,256]{2,1,0:T(8,128)} %copy-done.5, s16[4,128,256]{2,1,0:T(8,128)(2,1)} %copy-done.6, s16[2,128,256]{2,1,0:T(8,128)(2,1)} %copy-done.7), custom_call_target="tpu_custom_call" | custom-call | tf_op jit(solution)/shard_map/pair/pallas_call | solution.py:217
  23.9 3.3 %collective-permute-start.3 = (s16[2,128,256]{2,1,0:T(8,128)(2,1)}, s16[2,128,256]{2,1,0:T(8,128)(2,1)S(1)}, u32[]{:S(2)}, u32[]{:S(2)}) collective-permute-start(s16[2,128,256]{2,1,0:T(8,128)(2,1)} %get-tuple-element.13), channel_id=1, source_target_pairs={{0,8},{1,9},{2,10},{3,11},{4,12},{5,13},{6,14},{7,15},{8,0},{9,1},... | collective-permute-start | bytes 393224 | tf_op jit(solution)/shard_map/ppermute | solution.py:178
  27.2 4.8 %collective-permute-done.3.there = s16[2,128,256]{2,1,0:T(8,128)(2,1)S(1)} collective-permute-done((s16[2,128,256]{2,1,0:T(8,128)(2,1)}, s16[2,128,256]{2,1,0:T(8,128)(2,1)S(1)}, u32[]{:S(2)}, u32[]{:S(2)}) %collective-permute-start.3) | collective-permute-done | bytes 131104 | tf_op jit(solution)/shard_map/ppermute | solution.py:178
  32.1 0.0 copy-start.8
  32.1 0.6 %copy-done.8 = s16[2,128,256]{2,1,0:T(8,128)(2,1)} copy-done((s16[2,128,256]{2,1,0:T(8,128)(2,1)}, s16[2,128,256]{2,1,0:T(8,128)(2,1)S(1)}, u32[]{:S(2)}) %copy-start.8) | copy-done | bytes 131096
  32.7 1.9 %finish.1 = (f32[128,256]{1,0:T(8,128)}, s16[2,128,256]{2,1,0:T(8,128)(2,1)}) custom-call(f32[2,128,256]{2,1,0:T(8,128)} %get-tuple-element.12.mine, s16[2,128,256]{2,1,0:T(8,128)(2,1)} %copy-done.8), custom_call_target="tpu_custom_call" | custom-call | tf_op jit(solution)/shard_map/finish/pallas_call | solution.py:225
  34.6 0.8 %collective-permute-start.4 = (s16[2,128,256]{2,1,0:T(8,128)(2,1)}, s16[2,128,256]{2,1,0:T(8,128)(2,1)S(1)}, u32[]{:S(2)}, u32[]{:S(2)}) collective-permute-start(s16[2,128,256]{2,1,0:T(8,128)(2,1)} %get-tuple-element.15), channel_id=1, source_target_pairs={{0,4},{1,3},{2,6},{3,1},{4,0},{5,7},{6,2},{7,5},{8,12},{9,11},{10,... | collective-permute-start | bytes 393224 | tf_op jit(solution)/shard_map/ppermute | solution.py:178
  35.4 0.9 %constant_dynamic-update-slice_fusion.1 = s16[4,128,256]{2,1,0:T(8,128)(2,1)S(1)} fusion(s16[2,128,256]{2,1,0:T(8,128)(2,1)} %get-tuple-element.15), kind=kLoop, calls=%fused_computation.16 | loop fusion | bytes 262144
  36.3 4.5 %collective-permute-done.4 = s16[2,128,256]{2,1,0:T(8,128)(2,1)S(1)} collective-permute-done((s16[2,128,256]{2,1,0:T(8,128)(2,1)}, s16[2,128,256]{2,1,0:T(8,128)(2,1)S(1)}, u32[]{:S(2)}, u32[]{:S(2)}) %collective-permute-start.4) | collective-permute-done | bytes 131104 | tf_op jit(solution)/shard_map/ppermute | solution.py:178
  40.8 0.1 collective-permute-start.5
  40.9 0.0 collective-permute-start.6
  41.0 6.3 %collective-permute-done.5 = s16[4,128,256]{2,1,0:T(8,128)(2,1)S(1)} collective-permute-done((s16[4,128,256]{2,1,0:T(8,128)(2,1)S(1)}, s16[4,128,256]{2,1,0:T(8,128)(2,1)S(1)}, u32[]{:S(2)}, u32[]{:S(2)}) %collective-permute-start.5) | collective-permute-done | bytes 262176 | tf_op jit(solution)/shard_map/ppermute | solution.py:178
  47.3 0.0 collective-permute-start.7
  47.3 1.0 %pad_add_fusion.near = s16[8,128,256]{2,1,0:T(8,128)(2,1)S(1)} fusion(s16[4,128,256]{2,1,0:T(8,128)(2,1)S(1)} %collective-permute-done.5, s16[2,128,256]{2,1,0:T(8,128)(2,1)S(1)} %collective-permute-done.4, s16[2,128,256]{2,1,0:T(8,128)(2,1)} %get-tuple-element.15), kind=kLoop, calls=%fused_computation.4 | loop fusion | flops 524288 | bytes 1048576 | tf_op jit(solution)/shard_map/concatenate | solution.py:236
  48.2 0.0 collective-permute-done.6
  48.2 0.6 %collective-permute-done.7 = s16[4,128,256]{2,1,0:T(8,128)(2,1)S(1)} collective-permute-done((s16[4,128,256]{2,1,0:T(8,128)(2,1)S(1)}, s16[4,128,256]{2,1,0:T(8,128)(2,1)S(1)}, u32[]{:S(2)}, u32[]{:S(2)}) %collective-permute-start.7) | collective-permute-done | bytes 262176 | tf_op jit(solution)/shard_map/ppermute | solution.py:178
  48.8 0.0 copy-done
  48.8 0.0 copy-done.3
  48.9 0.0 copy-done.4
  48.9 0.0 copy-start.2
  48.9 0.9 %copy-done.2 = f32[128,256]{1,0:T(8,128)S(1)} copy-done((f32[128,256]{1,0:T(8,128)S(1)}, f32[128,256]{1,0:T(8,128)}, u32[]{:S(2)}) %copy-start.2) | copy-done | bytes 131096
  49.8 4.3 %scores.1 = (bf16[128,256]{1,0:T(8,128)(2,1)}, f32[12,128]{1,0:T(8,128)}) custom-call(s32[12]{0:T(128)S(1)} %copy-done.4, s32[12,128]{1,0:T(8,128)S(1)} %bitcast.3, f32[128,256]{1,0:T(8,128)S(1)} %copy-done.2, bf16[1536,1024]{1,0:T(8,128)(2,1)S(1)} %copy-done, s16[8,128,256]{2,1,0:T(8,128)(2,1)S(1)} %pad_add_fusion.near, ...), custom_call_target="tpu_custom_call" | custom-call | tf_op jit(solution)/shard_map/scores/pallas_call | solution.py:239
  (2 shorter events, 0.0 us)
Async XLA Ops:
  5.8 9.6 %copy-start.1 = (f32[8,128,256]{2,1,0:T(8,128)}, f32[8,128,256]{2,1,0:T(8,128)S(1)}, u32[]{:S(2)}) copy-start(f32[8,128,256]{2,1,0:T(8,128)S(1)} %get-tuple-element.10.refs_0_) | copy-start | bytes 3145732
  5.8 2.8 %collective-permute-start = (f32[8,128,256]{2,1,0:T(8,128)S(1)}, f32[8,128,256]{2,1,0:T(8,128)S(1)}, u32[]{:S(2)}, u32[]{:S(2)}) collective-permute-start(f32[8,128,256]{2,1,0:T(8,128)S(1)} %get-tuple-element.11), channel_id=1, source_target_pairs={{0,1},{1,0},{2,3},{3,2},{4,5},{5,4},{6,7},{7,6},{8,9},{9,8},{10,11... | collective-permute-start | bytes 3145736 | tf_op jit(solution)/shard_map/ppermute | solution.py:178
  8.6 7.0 %copy-start.5 = (f32[8,128,256]{2,1,0:T(8,128)}, f32[8,128,256]{2,1,0:T(8,128)S(1)}, u32[]{:S(2)}) copy-start(f32[8,128,256]{2,1,0:T(8,128)S(1)} %collective-permute-done.refs_1_) | copy-start | bytes 3145732
  8.9 39.9 %copy-start = (bf16[1536,1024]{1,0:T(8,128)(2,1)S(1)}, bf16[1536,1024]{1,0:T(8,128)(2,1)}, u32[]{:S(2)}) copy-start(bf16[1536,1024]{1,0:T(8,128)(2,1)} %points.3) | copy-start | bytes 9437188
  8.9 39.9 %copy-start.3 = (s32[1536]{0:T(1024)S(1)}, s32[1536]{0:T(1024)}, u32[]{:S(2)}) copy-start(s32[1536]{0:T(1024)} %param.7) | copy-start | bytes 18436
  8.9 39.9 %copy-start.4 = (s32[12]{0:T(128)S(1)}, s32[12]{0:T(128)}, u32[]{:S(2)}) copy-start(s32[12]{0:T(128)} %bids.1) | copy-start | bytes 148
  9.0 6.4 %collective-permute-start.1 = (s16[4,128,256]{2,1,0:T(8,128)(2,1)S(1)}, s16[4,128,256]{2,1,0:T(8,128)(2,1)S(1)}, u32[]{:S(2)}, u32[]{:S(2)}) collective-permute-start(s16[4,128,256]{2,1,0:T(8,128)(2,1)S(1)} %fusion.1), channel_id=1, source_target_pairs={{0,2},{1,5},{2,0},{3,7},{4,6},{5,1},{6,4},{7,3},{8,10},{9,13},{10,... | collective-permute-start | bytes 786440 | tf_op jit(solution)/shard_map/ppermute | solution.py:178
  15.4 5.7 %copy-start.6 = (s16[4,128,256]{2,1,0:T(8,128)(2,1)}, s16[4,128,256]{2,1,0:T(8,128)(2,1)S(1)}, u32[]{:S(2)}) copy-start(s16[4,128,256]{2,1,0:T(8,128)(2,1)S(1)} %collective-permute-done.1.refs_2_) | copy-start | bytes 786436
  15.7 5.4 %collective-permute-start.2 = (s16[2,128,256]{2,1,0:T(8,128)(2,1)S(1)}, s16[2,128,256]{2,1,0:T(8,128)(2,1)S(1)}, u32[]{:S(2)}, u32[]{:S(2)}) collective-permute-start(s16[2,128,256]{2,1,0:T(8,128)(2,1)S(1)} %fusion.5), channel_id=1, source_target_pairs={{0,4},{1,3},{2,6},{3,1},{4,0},{5,7},{6,2},{7,5},{8,12},{9,11},{10,... | collective-permute-start | bytes 393224 | tf_op jit(solution)/shard_map/ppermute | solution.py:178
  21.1 0.7 %copy-start.7 = (s16[2,128,256]{2,1,0:T(8,128)(2,1)}, s16[2,128,256]{2,1,0:T(8,128)(2,1)S(1)}, u32[]{:S(2)}) copy-start(s16[2,128,256]{2,1,0:T(8,128)(2,1)S(1)} %collective-permute-done.2.refs_3_) | copy-start | bytes 393220
  23.9 8.2 %collective-permute-start.3 = (s16[2,128,256]{2,1,0:T(8,128)(2,1)}, s16[2,128,256]{2,1,0:T(8,128)(2,1)S(1)}, u32[]{:S(2)}, u32[]{:S(2)}) collective-permute-start(s16[2,128,256]{2,1,0:T(8,128)(2,1)} %get-tuple-element.13), channel_id=1, source_target_pairs={{0,8},{1,9},{2,10},{3,11},{4,12},{5,13},{6,14},{7,15},{8,0},{9,1},... | collective-permute-start | bytes 393224 | tf_op jit(solution)/shard_map/ppermute | solution.py:178
  32.1 0.6 %copy-start.8 = (s16[2,128,256]{2,1,0:T(8,128)(2,1)}, s16[2,128,256]{2,1,0:T(8,128)(2,1)S(1)}, u32[]{:S(2)}) copy-start(s16[2,128,256]{2,1,0:T(8,128)(2,1)S(1)} %collective-permute-done.3.there) | copy-start | bytes 393220
  34.6 6.2 %collective-permute-start.4 = (s16[2,128,256]{2,1,0:T(8,128)(2,1)}, s16[2,128,256]{2,1,0:T(8,128)(2,1)S(1)}, u32[]{:S(2)}, u32[]{:S(2)}) collective-permute-start(s16[2,128,256]{2,1,0:T(8,128)(2,1)} %get-tuple-element.15), channel_id=1, source_target_pairs={{0,4},{1,3},{2,6},{3,1},{4,0},{5,7},{6,2},{7,5},{8,12},{9,11},{10,... | collective-permute-start | bytes 393224 | tf_op jit(solution)/shard_map/ppermute | solution.py:178
  40.8 6.4 %collective-permute-start.5 = (s16[4,128,256]{2,1,0:T(8,128)(2,1)S(1)}, s16[4,128,256]{2,1,0:T(8,128)(2,1)S(1)}, u32[]{:S(2)}, u32[]{:S(2)}) collective-permute-start(s16[4,128,256]{2,1,0:T(8,128)(2,1)S(1)} %constant_dynamic-update-slice_fusion), channel_id=1, source_target_pairs={{0,2},{1,5},{2,0},{3,7},{4,6},{5,1},{6,4},{7,3},{8,10},{9,13},{10,... | collective-permute-start | bytes 786440 | tf_op jit(solution)/shard_map/ppermute | solution.py:178
  40.9 7.3 %collective-permute-start.6 = (s16[4,128,256]{2,1,0:T(8,128)(2,1)S(1)}, s16[4,128,256]{2,1,0:T(8,128)(2,1)S(1)}, u32[]{:S(2)}, u32[]{:S(2)}) collective-permute-start(s16[4,128,256]{2,1,0:T(8,128)(2,1)S(1)} %constant_dynamic-update-slice_fusion), channel_id=1, source_target_pairs={{0,1},{1,0},{2,3},{3,2},{4,5},{5,4},{6,7},{7,6},{8,9},{9,8},{10,11... | collective-permute-start | bytes 786440 | tf_op jit(solution)/shard_map/ppermute | solution.py:178
  47.3 1.5 %collective-permute-start.7 = (s16[4,128,256]{2,1,0:T(8,128)(2,1)S(1)}, s16[4,128,256]{2,1,0:T(8,128)(2,1)S(1)}, u32[]{:S(2)}, u32[]{:S(2)}) collective-permute-start(s16[4,128,256]{2,1,0:T(8,128)(2,1)S(1)} %collective-permute-done.5), channel_id=1, source_target_pairs={{0,1},{1,0},{2,3},{3,2},{4,5},{5,4},{6,7},{7,6},{8,9},{9,8},{10,11... | collective-permute-start | bytes 786440 | tf_op jit(solution)/shard_map/ppermute | solution.py:178
  48.9 0.9 %copy-start.2 = (f32[128,256]{1,0:T(8,128)S(1)}, f32[128,256]{1,0:T(8,128)}, u32[]{:S(2)}) copy-start(f32[128,256]{1,0:T(8,128)} %get-tuple-element.14.own) | copy-start | bytes 393220

commit v5 on v4

v5 whole, which is shorter than its diff:
```python
import functools
import math

import jax
import jax.numpy as jnp
from jax import lax
from jax.experimental import pallas as pl
from jax.experimental.pallas import tpu as pltpu
from jax.sharding import PartitionSpec as P

SLOT = 128
POINT_LIMIT = 6.0

prior_weight = 4.0
norm_eps = 1e-06

LOW_EXP = -32
MIB = 1 << 20


def code_rate(top_exp):
    return 32767.0 / (top_exp - LOW_EXP)


def encode(value, rate):
    size = jnp.maximum(jnp.abs(value), 2.0**LOW_EXP)
    level = jnp.floor((jnp.log2(size) - LOW_EXP) * rate + 0.5)
    return jnp.where(value < 0.0, -level, level).astype(jnp.int32).astype(jnp.int16)


def decode(code, rate):
    level = code.astype(jnp.int32).astype(jnp.float32)
    size = jnp.exp2(jnp.abs(level) * (1.0 / rate) + LOW_EXP)
    return jnp.where(level == 0.0, 0.0, jnp.where(level < 0.0, -size, size))


def bits_of(count):
    return [1 << bit for bit in range(count.bit_length() - 1)]


def near_group(subs, shards):
    group = [(0, 0)]
    for bit in bits_of(subs)[1:]:
        group = group + [(sub ^ bit, shard) for sub, shard in group]
    group = group + [(sub, shard ^ 1) for sub, shard in group]
    return group[:1] + group[:0:-1]


def late_bits(shards):
    return bits_of(shards)[1:]


def late_place(bits, over_shard):
    place = 0
    for bit in bits:
        place = place * 2 + (over_shard // bit) % 2
    return place


def sums_kernel(
    live_in, bids_in, slots_in, points, *refs, blocks, shards, subs, width, flip, owned
):
    if owned:
        old_in, sums, live, bids, slots, held, small, arrived, old = refs
    else:
        sums, live, bids, slots, held, small, arrived = refs
    sub, shard = lax.axis_index("sub"), lax.axis_index("shard")
    width_all = (subs // 2) * width
    firsts = [
        pltpu.make_async_copy(live_in, live, small.at[0]),
        pltpu.make_async_copy(bids_in, bids, small.at[1]),
        pltpu.make_async_copy(slots_in, slots, small.at[2]),
    ]
    if owned:
        firsts.append(pltpu.make_async_copy(old_in, old, small.at[3]))
    for copy in firsts:
        copy.start()
    copies = []
    for block in range(blocks):
        span = pl.ds(block * SLOT, SLOT)
        for index, over_sub in enumerate(range(0, subs, 2)):
            column = pl.multiple_of((sub ^ over_sub ^ flip) * width, width)
            copies.append(
                pltpu.make_async_copy(
                    points.at[span, pl.ds(column, width)],
                    held.at[span, pl.ds(index * width, width)],
                    arrived.at[block * (subs // 2) + index],
                )
            )
            copies[-1].start()
    sums[...] = jnp.zeros_like(sums)
    for copy in firsts:
        copy.wait()
    if owned:
        sums[0, 0] = prior_weight * old[...].astype(jnp.float32)
    group = near_group(subs, shards)
    bits = late_bits(shards)
    for block in range(blocks):
        slot = jnp.where(block < live[0], slots[block : block + 1, :], -1)
        hot = (slot == lax.broadcasted_iota(jnp.int32, (SLOT, SLOT), 0)).astype(jnp.bfloat16)
        over_shard = bids[block] ^ shard
        late = late_place(bits, over_shard)
        for index, over_sub in enumerate(range(0, subs, 2)):
            copies[block * (subs // 2) + index].wait()
            part = jnp.dot(
                hot,
                held[block * SLOT : (block + 1) * SLOT, index * width : (index + 1) * width],
                preferred_element_type=jnp.float32,
            )
            at = jnp.where(over_shard % 2 == 0, group.index((over_sub, 0)), group.index((over_sub, 1)))
            sums[at, late] += part


def mix_kernel(keep, crossed, *refs, rate):
    terms, (mine, code) = refs[:-2], refs[-2:]
    total = keep[0] + crossed[0]
    for term in terms:
        total = total + decode(term[...], rate)
    mine[...] = total
    code[...] = encode(total, rate)


def finish_kernel(mine, there, own, code, *, rate):
    own[...] = mine[0] + decode(there[1], rate)
    code[0] = encode(own[...], rate)
    code[1] = encode(mine[1] + decode(there[0], rate), rate)


def score_kernel(
    bids, slots, own, points, *refs, blocks, shards, subs, rows, width, rate, group
):
    chips = near_group(subs, shards)
    near, far, (fresh, margin, cents) = refs[: len(chips)], refs[len(chips) : 2 * len(chips)], refs[2 * len(chips) :]
    sub, shard = lax.axis_index("sub"), lax.axis_index("shard")
    bits = late_bits(shards)
    for over_shard in range(shards):
        late = late_place(bits, over_shard)
        parts = []
        for over_sub in range(0, subs, 2):
            chip = chips.index((over_sub, over_shard % 2))
            parts.append((sub ^ over_sub, decode(near[chip][late], rate)))
            parts.append((sub ^ 1 ^ over_sub, decode(far[chip][late], rate)))
        squares = sum(jnp.sum(part * part, axis=1, keepdims=True) for _, part in parts)
        scale = lax.rsqrt(squares + norm_eps)
        row = pl.ds(pl.multiple_of((shard ^ over_shard) * rows, rows), rows)
        for place, part in parts:
            cents[row, pl.ds(pl.multiple_of(place * width, width), width)] = (part * scale).astype(jnp.bfloat16)
        if over_shard == 0:
            fresh[...] = (own[...] * scale).astype(jnp.bfloat16)

    for block in range(blocks // group):
        score = lax.dot_general(
            cents[...],
            points[block * group * SLOT : (block + 1) * group * SLOT, :],
            (((1,), (1,)), ((), ())),
            preferred_element_type=jnp.float32,
        )
        for inner in range(group):
            at = block * group + inner
            line = slice(at, at + 1)
            part = score[:, inner * SLOT : (inner + 1) * SLOT]
            hit = lax.broadcasted_iota(jnp.int32, part.shape, 0) == bids[at] * SLOT + slots[line, :]
            mine = jnp.sum(jnp.where(hit, part, 0.0), axis=0, keepdims=True)
            rival = jnp.max(jnp.where(hit, -jnp.inf, part), axis=0, keepdims=True)
            margin[line, :] = mine - rival


def local(points, block_ids, slot_ids, live_blocks, old_centroids):
    row_count, feat_width = points.shape
    blocks = row_count // SLOT
    shards = lax.axis_size("shard")
    subs = lax.axis_size("sub")
    rows, width = old_centroids.shape
    total = rows * shards
    top = POINT_LIMIT * (row_count * shards * subs + prior_weight)
    rate = code_rate(math.ceil(math.log2(top)))
    slots = slot_ids.reshape(blocks, SLOT)
    chips = near_group(subs, shards)
    bits = late_bits(shards)
    late = 1 << len(bits)
    small_limit = 4 * MIB + 8 * total * feat_width
    smem = pl.BlockSpec(memory_space=pltpu.SMEM)
    vmem = pl.BlockSpec(memory_space=pltpu.VMEM)
    hbm = pl.BlockSpec(memory_space=pltpu.HBM)

    def swap(value, over_sub, over_shard):
        pairs = []
        for shard in range(shards):
            for sub in range(subs):
                pairs.append((shard * subs + sub, (shard ^ over_shard) * subs + (sub ^ over_sub)))
        return lax.ppermute(value, ("shard", "sub"), pairs)

    def in_hbm(value):
        return pltpu.with_memory_space_constraint(value, pltpu.HBM)

    def sums(flip, *owned):
        return pl.pallas_call(
            functools.partial(
                sums_kernel, blocks=blocks, shards=shards, subs=subs, width=width, flip=flip, owned=bool(owned)
            ),
            out_shape=jax.ShapeDtypeStruct((len(chips), late, rows, width), jnp.float32),
            in_specs=[hbm] * (4 + len(owned)),
            out_specs=vmem,
            scratch_shapes=[
                pltpu.SMEM((1,), jnp.int32),
                pltpu.SMEM((blocks,), jnp.int32),
                pltpu.VMEM((blocks, SLOT), jnp.int32),
                pltpu.VMEM((row_count, feat_width // 2), jnp.bfloat16),
                pltpu.SemaphoreType.DMA((4,)),
                pltpu.SemaphoreType.DMA((blocks * subs // 2,)),
            ]
            + [pltpu.VMEM((rows, width), jnp.bfloat16)] * len(owned),
            compiler_params=pltpu.CompilerParams(vmem_limit_bytes=8 * MIB + 2 * total * feat_width),
            cost_estimate=pl.CostEstimate(
                flops=row_count * SLOT * feat_width,
                bytes_accessed=row_count * feat_width,
                transcendentals=0,
            ),
            name="sums_keep" if owned else "sums_send",
        )(live_blocks, in_hbm(block_ids), in_hbm(slots), in_hbm(points), *[in_hbm(x) for x in owned])

    crossed = swap(sums(1), 1, 0)
    keep = sums(0, old_centroids)
    terms = []
    for index, (over_sub, over_shard) in list(enumerate(chips))[1:]:
        terms.append(swap(encode(keep[index] + crossed[index], rate), over_sub, over_shard))

    piece = (late, rows, width)
    mine, code = pl.pallas_call(
        functools.partial(mix_kernel, rate=rate),
        out_shape=(jax.ShapeDtypeStruct(piece, jnp.float32), jax.ShapeDtypeStruct(piece, jnp.int16)),
        compiler_params=pltpu.CompilerParams(vmem_limit_bytes=small_limit),
        name="mix",
    )(keep, crossed, *terms)
    for bit in bits[:-1]:
        half = mine.shape[0] // 2
        mine = mine[:half] + decode(swap(encode(mine[half:], rate), 0, bit), rate)
        code = encode(mine, rate)
    two = (2, rows, width)
    own, code = pl.pallas_call(
        functools.partial(finish_kernel, rate=rate),
        out_shape=(jax.ShapeDtypeStruct((rows, width), jnp.float32), jax.ShapeDtypeStruct(two, jnp.int16)),
        compiler_params=pltpu.CompilerParams(vmem_limit_bytes=small_limit),
        name="finish",
    )(mine, swap(code, 0, bits[-1]))
    for bit in reversed(bits[:-1]):
        code = jnp.concatenate([code, swap(code, 0, bit)])
    near = [code] + [swap(code, over_sub, over_shard) for over_sub, over_shard in chips[1:]]
    far = [swap(block, 1, 0) for block in near]

    group = 2 if blocks % 2 == 0 else 1
    fresh, margin = pl.pallas_call(
        functools.partial(
            score_kernel, blocks=blocks, shards=shards, subs=subs, rows=rows, width=width, rate=rate, group=group
        ),
        out_shape=(
            jax.ShapeDtypeStruct((rows, width), jnp.bfloat16),
            jax.ShapeDtypeStruct((blocks, SLOT), jnp.float32),
        ),
        in_specs=[smem] + [vmem] * (3 + 2 * len(chips)),
        out_specs=(vmem, vmem),
        scratch_shapes=[pltpu.VMEM((total, feat_width), jnp.bfloat16)],
        compiler_params=pltpu.CompilerParams(vmem_limit_bytes=12 * MIB + 6 * total * feat_width),
        name="scores",
    )(block_ids, slots, own, points, *near, *far)
    return fresh, margin.reshape(row_count)


def solution(mesh):
    return jax.shard_map(
        local,
        mesh=mesh,
        in_specs=(
            P(("groups", "shard", "sub"), None),
            P(("groups", "shard", "sub")),
            P(("groups", "shard", "sub")),
            P(("groups", "shard", "sub")),
            P(("groups", "shard"), "sub"),
        ),
        out_specs=(P(("groups", "shard"), "sub"), P(("groups", "shard", "sub"))),
        check_vma=False,
    )
```

time: 54.4 us -> 48.9 us (0.90)
  waiting for transfers between devices: 26.2 us -> 19.6 us
  Pallas kernels: 12.9 us -> 16.4 us
  local copies, waits for them, and re-layouts: 3.18 us -> 0.02 us
  starting transfers between devices: 8.95 us -> 11 us
  other arithmetic: 1.54 us -> 0.41 us
    ppermute x8 -> x12, waiting for transfers between devices: 26.2 us -> 19.6 us  [swap(): return lax.ppermute(value, ('shard', 'sub'), pairs)]
    pallas_call x2 -> x3, Pallas kernels: 6.67 us -> 11.8 us  [the longest x2 11.3 us: sums(): pl.pallas_call(functools.partial(sums_kernel, blocks=blocks, shards=shard...]
    unnamed x19 -> x6, local copies, waits for them, and re-layouts: 3.18 us -> 0.02 us
    ppermute x8 -> x12, starting transfers between devices: 8.95 us -> 11 us  [swap(): return lax.ppermute(value, ('shard', 'sub'), pairs)]
    pallas_call x1, Pallas kernels: 1.85 us -> 0.22 us  [local(): pl.pallas_call(functools.partial(finish_kernel, rate=rate), out_shape=(ja...]
    concatenate x2 -> x0, other arithmetic: 0.99 us -> none  [the longest x1 0.96 us: local(): near = jnp.concatenate([near, last])]
  transfers between devices with their start and end apart: 8 -> 12, of which waited for: 7 -> 8; matrix products, arithmetic and copies ran while one was open for 4% -> 0% of each run, Pallas kernels for 0% -> 12%
where the time goes in v5:
time: 48.9 us; the launch traced here: 48.7 us
  waiting for transfers between devices  19.6 us (40%)
  Pallas kernels  16.4 us (34%)
  starting transfers between devices  11 us (22%)
  between operations  1.35 us (3%)
    ppermute x12, waiting for transfers between devices, swap(): return lax.ppermute(value, ('shard', 'sub'), pairs)  19.6 us
    pallas_call x2, Pallas kernels, sums(): pl.pallas_call(functools.partial(sums_kernel, blocks=blocks, shards=shard...  11.3 us
    ppermute x12, starting transfers between devices, swap(): return lax.ppermute(value, ('shard', 'sub'), pairs)  11 us
    pallas_call x1, Pallas kernels, local(): pl.pallas_call(functools.partial(score_kernel, blocks=blocks, shards=shar...  4.38 us
  transfers between devices with their start and end apart: 12, of which 8 were waited for; matrix products, arithmetic and copies ran while one was open for 0% of the time, Pallas kernels for 12%

profile of v5, /device:TPU:0, one launch (start us, length us, event | category | flops | bytes accessed | tf_op | source)
XLA Modules:
  0.0 48.7 jit_solution(6430715318007284472)
XLA Ops:
  1.3 5.6 %sums_send.1 = f32[4,2,128,256]{3,2,1,0:T(8,128)S(1)} custom-call(s32[1]{0:T(128)S(6)} %copy.7.live_in, s32[12]{0:T(128)} %bids.1, s32[12,128]{1,0:T(8,128)} %bitcast.14, bf16[1536,1024]{1,0:T(8,128)(2,1)} %points.5), custom_call_target="tpu_custom_call" | custom-call | flops 201326592 | bytes 1572864 | tf_op jit(solution)/shard_map/sums_send/pallas_call | solution.py:197
  6.9 0.5 %collective-permute-start = (f32[4,2,128,256]{3,2,1,0:T(8,128)S(1)}, f32[4,2,128,256]{3,2,1,0:T(8,128)S(1)}, u32[]{:S(2)}, u32[]{:S(2)}) collective-permute-start(f32[4,2,128,256]{3,2,1,0:T(8,128)S(1)} %sums_send.1), channel_id=1, source_target_pairs={{0,1},{1,0},{2,3},{3,2},{4,5},{5,4},{6,7},{7,6},{8,9},{9,8},{10,11... | collective-permute-start | bytes 3145736 | tf_op jit(solution)/shard_map/ppermute | solution.py:191
  7.4 5.7 %sums_keep.1.keep = f32[4,2,128,256]{3,2,1,0:T(8,128)S(1)} custom-call(s32[1]{0:T(128)S(6)} %copy.7.live_in, s32[12]{0:T(128)} %bids.1, s32[12,128]{1,0:T(8,128)} %bitcast.15, bf16[1536,1024]{1,0:T(8,128)(2,1)} %points.5, bf16[128,256]{1,0:T(8,128)(2,1)} %refs_0_.1), custom_call_target="tpu_custom_call" | custom-call | flops 201326592 | bytes 1572864 | tf_op jit(solution)/shard_map/sums_keep/pallas_call | solution.py:197
  13.1 0.0 copy-start
  13.2 0.0 copy-start.1
  13.2 0.0 copy-start.2
  13.2 0.0 collective-permute-done.crossed
  13.2 0.4 fusion.5
  13.6 3.6 %collective-permute-start.1 = (s16[2,128,256]{2,1,0:T(8,128)(2,1)S(1)}, s16[2,128,256]{2,1,0:T(8,128)(2,1)S(1)}, u32[]{:S(2)}, u32[]{:S(2)}) collective-permute-start(s16[2,128,256]{2,1,0:T(8,128)(2,1)S(1)} %get-tuple-element.16), channel_id=1, source_target_pairs={{0,6},{1,7},{2,4},{3,5},{4,2},{5,3},{6,0},{7,1},{8,14},{9,15},{10,... | collective-permute-start | bytes 393224 | tf_op jit(solution)/shard_map/ppermute | solution.py:191
  17.2 0.4 collective-permute-start.2
  17.6 0.2 collective-permute-start.3
  17.8 3.7 %collective-permute-done.1.refs_0_ = s16[2,128,256]{2,1,0:T(8,128)(2,1)S(1)} collective-permute-done((s16[2,128,256]{2,1,0:T(8,128)(2,1)S(1)}, s16[2,128,256]{2,1,0:T(8,128)(2,1)S(1)}, u32[]{:S(2)}, u32[]{:S(2)}) %collective-permute-start.1) | collective-permute-done | bytes 131104 | tf_op jit(solution)/shard_map/ppermute | solution.py:191
  21.5 2.8 %collective-permute-done.2.refs_1_ = s16[2,128,256]{2,1,0:T(8,128)(2,1)S(1)} collective-permute-done((s16[2,128,256]{2,1,0:T(8,128)(2,1)S(1)}, s16[2,128,256]{2,1,0:T(8,128)(2,1)S(1)}, u32[]{:S(2)}, u32[]{:S(2)}) %collective-permute-start.2) | collective-permute-done | bytes 131104 | tf_op jit(solution)/shard_map/ppermute | solution.py:191
  24.3 0.0 collective-permute-done.3.refs_2_
  24.4 0.4 mix.1
  24.8 2.7 %collective-permute-start.4 = (s16[2,128,256]{2,1,0:T(8,128)(2,1)S(1)}, s16[2,128,256]{2,1,0:T(8,128)(2,1)S(1)}, u32[]{:S(2)}, u32[]{:S(2)}) collective-permute-start(s16[2,128,256]{2,1,0:T(8,128)(2,1)S(1)} %get-tuple-element.9), channel_id=1, source_target_pairs={{0,8},{1,9},{2,10},{3,11},{4,12},{5,13},{6,14},{7,15},{8,0},{9,1},... | collective-permute-start | bytes 393224 | tf_op jit(solution)/shard_map/ppermute | solution.py:191
  27.4 6.4 %collective-permute-done.4.there = s16[2,128,256]{2,1,0:T(8,128)(2,1)S(1)} collective-permute-done((s16[2,128,256]{2,1,0:T(8,128)(2,1)S(1)}, s16[2,128,256]{2,1,0:T(8,128)(2,1)S(1)}, u32[]{:S(2)}, u32[]{:S(2)}) %collective-permute-start.4) | collective-permute-done | bytes 131104 | tf_op jit(solution)/shard_map/ppermute | solution.py:191
  33.8 0.2 finish.1
  34.1 0.8 %collective-permute-start.6 = (s16[2,128,256]{2,1,0:T(8,128)(2,1)S(1)}, s16[2,128,256]{2,1,0:T(8,128)(2,1)S(1)}, u32[]{:S(2)}, u32[]{:S(2)}) collective-permute-start(s16[2,128,256]{2,1,0:T(8,128)(2,1)S(1)} %get-tuple-element.11.refs_0_), channel_id=1, source_target_pairs={{0,4},{1,5},{2,6},{3,7},{4,0},{5,1},{6,2},{7,3},{8,12},{9,13},{10,... | collective-permute-start | bytes 393224 | tf_op jit(solution)/shard_map/ppermute | solution.py:191
  34.9 1.5 %collective-permute-start.7 = (s16[2,128,256]{2,1,0:T(8,128)(2,1)S(1)}, s16[2,128,256]{2,1,0:T(8,128)(2,1)S(1)}, u32[]{:S(2)}, u32[]{:S(2)}) collective-permute-start(s16[2,128,256]{2,1,0:T(8,128)(2,1)S(1)} %get-tuple-element.11.refs_0_), channel_id=1, source_target_pairs={{0,2},{1,3},{2,0},{3,1},{4,6},{5,7},{6,4},{7,5},{8,10},{9,11},{10,... | collective-permute-start | bytes 393224 | tf_op jit(solution)/shard_map/ppermute | solution.py:191
  36.4 1.3 %collective-permute-start.5 = (s16[2,128,256]{2,1,0:T(8,128)(2,1)S(1)}, s16[2,128,256]{2,1,0:T(8,128)(2,1)S(1)}, u32[]{:S(2)}, u32[]{:S(2)}) collective-permute-start(s16[2,128,256]{2,1,0:T(8,128)(2,1)S(1)} %get-tuple-element.11.refs_0_), channel_id=1, source_target_pairs={{0,6},{1,7},{2,4},{3,5},{4,2},{5,3},{6,0},{7,1},{8,14},{9,15},{10,... | collective-permute-start | bytes 393224 | tf_op jit(solution)/shard_map/ppermute | solution.py:191
  37.6 0.0 collective-permute-start.8
  37.6 2.3 %collective-permute-done.6.refs_2_ = s16[2,128,256]{2,1,0:T(8,128)(2,1)S(1)} collective-permute-done((s16[2,128,256]{2,1,0:T(8,128)(2,1)S(1)}, s16[2,128,256]{2,1,0:T(8,128)(2,1)S(1)}, u32[]{:S(2)}, u32[]{:S(2)}) %collective-permute-start.6) | collective-permute-done | bytes 131104 | tf_op jit(solution)/shard_map/ppermute | solution.py:191
  39.9 0.0 collective-permute-start.10
  39.9 1.9 %collective-permute-done.7.refs_3_ = s16[2,128,256]{2,1,0:T(8,128)(2,1)S(1)} collective-permute-done((s16[2,128,256]{2,1,0:T(8,128)(2,1)S(1)}, s16[2,128,256]{2,1,0:T(8,128)(2,1)S(1)}, u32[]{:S(2)}, u32[]{:S(2)}) %collective-permute-start.7) | collective-permute-done | bytes 131104 | tf_op jit(solution)/shard_map/ppermute | solution.py:191
  41.8 0.0 collective-permute-start.11
  41.8 1.1 %collective-permute-done.5.refs_1_ = s16[2,128,256]{2,1,0:T(8,128)(2,1)S(1)} collective-permute-done((s16[2,128,256]{2,1,0:T(8,128)(2,1)S(1)}, s16[2,128,256]{2,1,0:T(8,128)(2,1)S(1)}, u32[]{:S(2)}, u32[]{:S(2)}) %collective-permute-start.5) | collective-permute-done | bytes 131104 | tf_op jit(solution)/shard_map/ppermute | solution.py:191
  42.9 0.0 collective-permute-start.9
  42.9 0.0 collective-permute-done.8.refs_4_
  42.9 0.0 collective-permute-done.10.refs_6_
  42.9 0.2 collective-permute-done.11.refs_7_
  43.2 1.1 %collective-permute-done.9.refs_5_ = s16[2,128,256]{2,1,0:T(8,128)(2,1)S(1)} collective-permute-done((s16[2,128,256]{2,1,0:T(8,128)(2,1)S(1)}, s16[2,128,256]{2,1,0:T(8,128)(2,1)S(1)}, u32[]{:S(2)}, u32[]{:S(2)}) %collective-permute-start.9) | collective-permute-done | bytes 131104 | tf_op jit(solution)/shard_map/ppermute | solution.py:191
  44.3 0.0 copy-done
  44.3 0.0 copy-done.1
  44.3 0.0 copy-done.2
  44.3 4.4 %scores.1 = (bf16[128,256]{1,0:T(8,128)(2,1)}, f32[12,128]{1,0:T(8,128)}) custom-call(s32[12]{0:T(128)S(1)} %copy-done.2, s32[12,128]{1,0:T(8,128)S(1)} %bitcast.16, f32[128,256]{1,0:T(8,128)S(1)} %get-tuple-element.10.own, bf16[1536,1024]{1,0:T(8,128)(2,1)S(1)} %copy-done, s16[2,128,256]{2,1,0:T(8,128)(2,1)S(1)} %get-tuple-element.11.refs_0_, ...), custom_call_target="tpu_custom_call" | custom-call | tf_op jit(solution)/shard_map/scores/pallas_call | solution.py:252
Async XLA Ops:
  6.9 6.3 %collective-permute-start = (f32[4,2,128,256]{3,2,1,0:T(8,128)S(1)}, f32[4,2,128,256]{3,2,1,0:T(8,128)S(1)}, u32[]{:S(2)}, u32[]{:S(2)}) collective-permute-start(f32[4,2,128,256]{3,2,1,0:T(8,128)S(1)} %sums_send.1), channel_id=1, source_target_pairs={{0,1},{1,0},{2,3},{3,2},{4,5},{5,4},{6,7},{7,6},{8,9},{9,8},{10,11... | collective-permute-start | bytes 3145736 | tf_op jit(solution)/shard_map/ppermute | solution.py:191
  13.1 31.1 %copy-start = (bf16[1536,1024]{1,0:T(8,128)(2,1)S(1)}, bf16[1536,1024]{1,0:T(8,128)(2,1)}, u32[]{:S(2)}) copy-start(bf16[1536,1024]{1,0:T(8,128)(2,1)} %points.5) | copy-start | bytes 9437188
  13.2 31.1 %copy-start.1 = (s32[1536]{0:T(1024)S(1)}, s32[1536]{0:T(1024)}, u32[]{:S(2)}) copy-start(s32[1536]{0:T(1024)} %param.7) | copy-start | bytes 18436
  13.2 31.1 %copy-start.2 = (s32[12]{0:T(128)S(1)}, s32[12]{0:T(128)}, u32[]{:S(2)}) copy-start(s32[12]{0:T(128)} %bids.1) | copy-start | bytes 148
  13.6 7.9 %collective-permute-start.1 = (s16[2,128,256]{2,1,0:T(8,128)(2,1)S(1)}, s16[2,128,256]{2,1,0:T(8,128)(2,1)S(1)}, u32[]{:S(2)}, u32[]{:S(2)}) collective-permute-start(s16[2,128,256]{2,1,0:T(8,128)(2,1)S(1)} %get-tuple-element.16), channel_id=1, source_target_pairs={{0,6},{1,7},{2,4},{3,5},{4,2},{5,3},{6,0},{7,1},{8,14},{9,15},{10,... | collective-permute-start | bytes 393224 | tf_op jit(solution)/shard_map/ppermute | solution.py:191
  17.2 7.2 %collective-permute-start.2 = (s16[2,128,256]{2,1,0:T(8,128)(2,1)S(1)}, s16[2,128,256]{2,1,0:T(8,128)(2,1)S(1)}, u32[]{:S(2)}, u32[]{:S(2)}) collective-permute-start(s16[2,128,256]{2,1,0:T(8,128)(2,1)S(1)} %get-tuple-element.15), channel_id=1, source_target_pairs={{0,4},{1,5},{2,6},{3,7},{4,0},{5,1},{6,2},{7,3},{8,12},{9,13},{10,... | collective-permute-start | bytes 393224 | tf_op jit(solution)/shard_map/ppermute | solution.py:191
  17.6 6.7 %collective-permute-start.3 = (s16[2,128,256]{2,1,0:T(8,128)(2,1)S(1)}, s16[2,128,256]{2,1,0:T(8,128)(2,1)S(1)}, u32[]{:S(2)}, u32[]{:S(2)}) collective-permute-start(s16[2,128,256]{2,1,0:T(8,128)(2,1)S(1)} %get-tuple-element.14), channel_id=1, source_target_pairs={{0,2},{1,3},{2,0},{3,1},{4,6},{5,7},{6,4},{7,5},{8,10},{9,11},{10,... | collective-permute-start | bytes 393224 | tf_op jit(solution)/shard_map/ppermute | solution.py:191
  24.8 9.1 %collective-permute-start.4 = (s16[2,128,256]{2,1,0:T(8,128)(2,1)S(1)}, s16[2,128,256]{2,1,0:T(8,128)(2,1)S(1)}, u32[]{:S(2)}, u32[]{:S(2)}) collective-permute-start(s16[2,128,256]{2,1,0:T(8,128)(2,1)S(1)} %get-tuple-element.9), channel_id=1, source_target_pairs={{0,8},{1,9},{2,10},{3,11},{4,12},{5,13},{6,14},{7,15},{8,0},{9,1},... | collective-permute-start | bytes 393224 | tf_op jit(solution)/shard_map/ppermute | solution.py:191
  34.1 5.8 %collective-permute-start.6 = (s16[2,128,256]{2,1,0:T(8,128)(2,1)S(1)}, s16[2,128,256]{2,1,0:T(8,128)(2,1)S(1)}, u32[]{:S(2)}, u32[]{:S(2)}) collective-permute-start(s16[2,128,256]{2,1,0:T(8,128)(2,1)S(1)} %get-tuple-element.11.refs_0_), channel_id=1, source_target_pairs={{0,4},{1,5},{2,6},{3,7},{4,0},{5,1},{6,2},{7,3},{8,12},{9,13},{10,... | collective-permute-start | bytes 393224 | tf_op jit(solution)/shard_map/ppermute | solution.py:191
  34.9 7.0 %collective-permute-start.7 = (s16[2,128,256]{2,1,0:T(8,128)(2,1)S(1)}, s16[2,128,256]{2,1,0:T(8,128)(2,1)S(1)}, u32[]{:S(2)}, u32[]{:S(2)}) collective-permute-start(s16[2,128,256]{2,1,0:T(8,128)(2,1)S(1)} %get-tuple-element.11.refs_0_), channel_id=1, source_target_pairs={{0,2},{1,3},{2,0},{3,1},{4,6},{5,7},{6,4},{7,5},{8,10},{9,11},{10,... | collective-permute-start | bytes 393224 | tf_op jit(solution)/shard_map/ppermute | solution.py:191
  36.4 6.6 %collective-permute-start.5 = (s16[2,128,256]{2,1,0:T(8,128)(2,1)S(1)}, s16[2,128,256]{2,1,0:T(8,128)(2,1)S(1)}, u32[]{:S(2)}, u32[]{:S(2)}) collective-permute-start(s16[2,128,256]{2,1,0:T(8,128)(2,1)S(1)} %get-tuple-element.11.refs_0_), channel_id=1, source_target_pairs={{0,6},{1,7},{2,4},{3,5},{4,2},{5,3},{6,0},{7,1},{8,14},{9,15},{10,... | collective-permute-start | bytes 393224 | tf_op jit(solution)/shard_map/ppermute | solution.py:191
  37.6 5.3 %collective-permute-start.8 = (s16[2,128,256]{2,1,0:T(8,128)(2,1)S(1)}, s16[2,128,256]{2,1,0:T(8,128)(2,1)S(1)}, u32[]{:S(2)}, u32[]{:S(2)}) collective-permute-start(s16[2,128,256]{2,1,0:T(8,128)(2,1)S(1)} %get-tuple-element.11.refs_0_), channel_id=1, source_target_pairs={{0,1},{1,0},{2,3},{3,2},{4,5},{5,4},{6,7},{7,6},{8,9},{9,8},{10,11... | collective-permute-start | bytes 393224 | tf_op jit(solution)/shard_map/ppermute | solution.py:191
  39.9 3.0 %collective-permute-start.10 = (s16[2,128,256]{2,1,0:T(8,128)(2,1)S(1)}, s16[2,128,256]{2,1,0:T(8,128)(2,1)S(1)}, u32[]{:S(2)}, u32[]{:S(2)}) collective-permute-start(s16[2,128,256]{2,1,0:T(8,128)(2,1)S(1)} %collective-permute-done.6.refs_2_), channel_id=1, source_target_pairs={{0,1},{1,0},{2,3},{3,2},{4,5},{5,4},{6,7},{7,6},{8,9},{9,8},{10,11... | collective-permute-start | bytes 393224 | tf_op jit(solution)/shard_map/ppermute | solution.py:191
  41.8 1.3 %collective-permute-start.11 = (s16[2,128,256]{2,1,0:T(8,128)(2,1)S(1)}, s16[2,128,256]{2,1,0:T(8,128)(2,1)S(1)}, u32[]{:S(2)}, u32[]{:S(2)}) collective-permute-start(s16[2,128,256]{2,1,0:T(8,128)(2,1)S(1)} %collective-permute-done.7.refs_3_), channel_id=1, source_target_pairs={{0,1},{1,0},{2,3},{3,2},{4,5},{5,4},{6,7},{7,6},{8,9},{9,8},{10,11... | collective-permute-start | bytes 393224 | tf_op jit(solution)/shard_map/ppermute | solution.py:191
  42.9 1.3 %collective-permute-start.9 = (s16[2,128,256]{2,1,0:T(8,128)(2,1)S(1)}, s16[2,128,256]{2,1,0:T(8,128)(2,1)S(1)}, u32[]{:S(2)}, u32[]{:S(2)}) collective-permute-start(s16[2,128,256]{2,1,0:T(8,128)(2,1)S(1)} %collective-permute-done.5.refs_1_), channel_id=1, source_target_pairs={{0,1},{1,0},{2,3},{3,2},{4,5},{5,4},{6,7},{7,6},{8,9},{9,8},{10,11... | collective-permute-start | bytes 393224 | tf_op jit(solution)/shard_map/ppermute | solution.py:191

commit v6 on v5

--- a/solution.py
+++ b/solution.py
@@ -57,58 +57,80 @@
     return place
 
 
-def sums_kernel(
-    live_in, bids_in, slots_in, points, *refs, blocks, shards, subs, width, flip, owned
+def add_block(sums, hot, rows_of, over_shard, *, sub, subs, shards, width, flip):
+    group = near_group(subs, shards)
+    late = late_place(late_bits(shards), over_shard)
+    for over_sub in range(0, subs, 2):
+        column = pl.multiple_of((sub ^ over_sub ^ flip) * width, width)
+        part = jnp.dot(hot, rows_of(pl.ds(column, width)), preferred_element_type=jnp.float32)
+        at = jnp.where(over_shard % 2 == 0, group.index((over_sub, 0)), group.index((over_sub, 1)))
+        sums[at, late] += part
+
+
+def hot_rows(slots, block, live):
+    slot = jnp.where(block < live, slots[block : block + 1, :], -1)
+    return (slot == lax.broadcasted_iota(jnp.int32, (SLOT, SLOT), 0)).astype(jnp.bfloat16)
+
+
+def send_kernel(
+    live_in, bids_in, slots_in, points, sums, held, live, bids, slots, small, arrived, *, blocks, group, shards, subs, width
 ):
-    if owned:
-        old_in, sums, live, bids, slots, held, small, arrived, old = refs
-    else:
-        sums, live, bids, slots, held, small, arrived = refs
     sub, shard = lax.axis_index("sub"), lax.axis_index("shard")
-    width_all = (subs // 2) * width
     firsts = [
         pltpu.make_async_copy(live_in, live, small.at[0]),
         pltpu.make_async_copy(bids_in, bids, small.at[1]),
         pltpu.make_async_copy(slots_in, slots, small.at[2]),
     ]
-    if owned:
-        firsts.append(pltpu.make_async_copy(old_in, old, small.at[3]))
     for copy in firsts:
         copy.start()
     copies = []
-    for block in range(blocks):
-        span = pl.ds(block * SLOT, SLOT)
-        for index, over_sub in enumerate(range(0, subs, 2)):
-            column = pl.multiple_of((sub ^ over_sub ^ flip) * width, width)
-            copies.append(
-                pltpu.make_async_copy(
-                    points.at[span, pl.ds(column, width)],
-                    held.at[span, pl.ds(index * width, width)],
-                    arrived.at[block * (subs // 2) + index],
-                )
-            )
-            copies[-1].start()
+    for first in range(0, blocks, group):
+        span = pl.ds(first * SLOT, group * SLOT)
+        copies.append(pltpu.make_async_copy(points.at[span], held.at[span], arrived.at[first // group]))
+        copies[-1].start()
     sums[...] = jnp.zeros_like(sums)
     for copy in firsts:
         copy.wait()
-    if owned:
-        sums[0, 0] = prior_weight * old[...].astype(jnp.float32)
-    group = near_group(subs, shards)
-    bits = late_bits(shards)
     for block in range(blocks):
-        slot = jnp.where(block < live[0], slots[block : block + 1, :], -1)
-        hot = (slot == lax.broadcasted_iota(jnp.int32, (SLOT, SLOT), 0)).astype(jnp.bfloat16)
-        over_shard = bids[block] ^ shard
-        late = late_place(bits, over_shard)
-        for index, over_sub in enumerate(range(0, subs, 2)):
-            copies[block * (subs // 2) + index].wait()
-            part = jnp.dot(
-                hot,
-                held[block * SLOT : (block + 1) * SLOT, index * width : (index + 1) * width],
-                preferred_element_type=jnp.float32,
-            )
-            at = jnp.where(over_shard % 2 == 0, group.index((over_sub, 0)), group.index((over_sub, 1)))
-            sums[at, late] += part
+        if block % group == 0:
+            copies[block // group].wait()
+        span = slice(block * SLOT, (block + 1) * SLOT)
+        add_block(
+            sums,
+            hot_rows(slots, block, live[0]),
+            lambda column, span=span: held[span, column],
+            bids[block] ^ shard,
+            sub=sub,
+            subs=subs,
+            shards=shards,
+            width=width,
+            flip=1,
+        )
+
+
+def keep_kernel(live, bids, slots, old, points, sums, *, blocks, shards, subs, width):
+    sub, shard = lax.axis_index("sub"), lax.axis_index("shard")
+    sums[...] = jnp.zeros_like(sums)
+    sums[0, 0] = prior_weight * old[...].astype(jnp.float32)
+    for block in range(blocks):
+        span = slice(block * SLOT, (block + 1) * SLOT)
+        add_block(
+            sums,
+            hot_rows(slots, block, live[0]),
+            lambda column, span=span: points[span, column],
+            bids[block] ^ shard,
+            sub=sub,
+            subs=subs,
+            shards=shards,
+            width=width,
+            flip=0,
+        )
+
+
+def turn_kernel(points, turned):
+    count = points.shape[0] // 2
+    for first in range(0, points.shape[0], count):
+        turned[:, first : first + count] = points[first : first + count, :].T
 
 
 def mix_kernel(keep, crossed, *refs, rate):
@@ -127,7 +149,7 @@
 
 
 def score_kernel(
-    bids, slots, own, points, *refs, blocks, shards, subs, rows, width, rate, group
+    bids, slots, own, turned, *refs, blocks, shards, subs, rows, width, rate, group
 ):
     chips = near_group(subs, shards)
     near, far, (fresh, margin, cents) = refs[: len(chips)], refs[len(chips) : 2 * len(chips)], refs[2 * len(chips) :]
@@ -149,10 +171,9 @@
             fresh[...] = (own[...] * scale).astype(jnp.bfloat16)
 
     for block in range(blocks // group):
-        score = lax.dot_general(
+        score = jnp.dot(
             cents[...],
-            points[block * group * SLOT : (block + 1) * group * SLOT, :],
-            (((1,), (1,)), ((), ())),
+            turned[:, block * group * SLOT : (block + 1) * group * SLOT],
             preferred_element_type=jnp.float32,
         )
         for inner in range(group):
@@ -193,34 +214,36 @@
     def in_hbm(value):
         return pltpu.with_memory_space_constraint(value, pltpu.HBM)
 
-    def sums(flip, *owned):
-        return pl.pallas_call(
-            functools.partial(
-                sums_kernel, blocks=blocks, shards=shards, subs=subs, width=width, flip=flip, owned=bool(owned)
-            ),
-            out_shape=jax.ShapeDtypeStruct((len(chips), late, rows, width), jnp.float32),
-            in_specs=[hbm] * (4 + len(owned)),
-            out_specs=vmem,
-            scratch_shapes=[
-                pltpu.SMEM((1,), jnp.int32),
-                pltpu.SMEM((blocks,), jnp.int32),
-                pltpu.VMEM((blocks, SLOT), jnp.int32),
-                pltpu.VMEM((row_count, feat_width // 2), jnp.bfloat16),
-                pltpu.SemaphoreType.DMA((4,)),
-                pltpu.SemaphoreType.DMA((blocks * subs // 2,)),
-            ]
-            + [pltpu.VMEM((rows, width), jnp.bfloat16)] * len(owned),
-            compiler_params=pltpu.CompilerParams(vmem_limit_bytes=8 * MIB + 2 * total * feat_width),
-            cost_estimate=pl.CostEstimate(
-                flops=row_count * SLOT * feat_width,
-                bytes_accessed=row_count * feat_width,
-                transcendentals=0,
-            ),
-            name="sums_keep" if owned else "sums_send",
-        )(live_blocks, in_hbm(block_ids), in_hbm(slots), in_hbm(points), *[in_hbm(x) for x in owned])
-
-    crossed = swap(sums(1), 1, 0)
-    keep = sums(0, old_centroids)
+    group = 2 if blocks % 2 == 0 else 1
+    shape = jax.ShapeDtypeStruct((len(chips), late, rows, width), jnp.float32)
+    cost = pl.CostEstimate(flops=row_count * SLOT * feat_width, bytes_accessed=row_count * feat_width, transcendentals=0)
+    sizes = dict(blocks=blocks, shards=shards, subs=subs, width=width)
+    send, held = pl.pallas_call(
+        functools.partial(send_kernel, group=group, **sizes),
+        out_shape=(shape, jax.ShapeDtypeStruct(points.shape, points.dtype)),
+        in_specs=[hbm] * 4,
+        out_specs=(vmem, vmem),
+        scratch_shapes=[
+            pltpu.SMEM((1,), jnp.int32),
+            pltpu.SMEM((blocks,), jnp.int32),
+            pltpu.VMEM((blocks, SLOT), jnp.int32),
+            pltpu.SemaphoreType.DMA((3,)),
+            pltpu.SemaphoreType.DMA((blocks // group,)),
+        ],
+        compiler_params=pltpu.CompilerParams(vmem_limit_bytes=8 * MIB + 4 * total * feat_width),
+        cost_estimate=cost,
+        name="sums_send",
+    )(live_blocks, in_hbm(block_ids), in_hbm(slots), in_hbm(points))
+    crossed = swap(send, 1, 0)
+    keep = pl.pallas_call(
+        functools.partial(keep_kernel, **sizes),
+        out_shape=shape,
+        in_specs=[smem, smem, vmem, vmem, vmem],
+        out_specs=vmem,
+        compiler_params=pltpu.CompilerParams(vmem_limit_bytes=8 * MIB + 4 * total * feat_width),
+        cost_estimate=cost,
+        name="sums_keep",
+    )(live_blocks, block_ids, slots, old_centroids, held)
     terms = []
     for index, (over_sub, over_shard) in list(enumerate(chips))[1:]:
         terms.append(swap(encode(keep[index] + crossed[index], rate), over_sub, over_shard))
@@ -232,6 +255,16 @@
         compiler_params=pltpu.CompilerParams(vmem_limit_bytes=small_limit),
         name="mix",
     )(keep, crossed, *terms)
+    held, code = lax.optimization_barrier((held, code))
+    turned = pl.pallas_call(
+        turn_kernel,
+        out_shape=jax.ShapeDtypeStruct((feat_width, row_count), points.dtype),
+        in_specs=[vmem],
+        out_specs=vmem,
+        compiler_params=pltpu.CompilerParams(vmem_limit_bytes=8 * MIB + 4 * total * feat_width),
+        cost_estimate=cost,
+        name="turn",
+    )(held)
     for bit in bits[:-1]:
         half = mine.shape[0] // 2
         mine = mine[:half] + decode(swap(encode(mine[half:], rate), 0, bit), rate)
@@ -248,7 +281,6 @@
     near = [code] + [swap(code, over_sub, over_shard) for over_sub, over_shard in chips[1:]]
     far = [swap(block, 1, 0) for block in near]
 
-    group = 2 if blocks % 2 == 0 else 1
     fresh, margin = pl.pallas_call(
         functools.partial(
             score_kernel, blocks=blocks, shards=shards, subs=subs, rows=rows, width=width, rate=rate, group=group
@@ -262,7 +294,7 @@
         scratch_shapes=[pltpu.VMEM((total, feat_width), jnp.bfloat16)],
         compiler_params=pltpu.CompilerParams(vmem_limit_bytes=12 * MIB + 6 * total * feat_width),
         name="scores",
-    )(block_ids, slots, own, points, *near, *far)
+    )(block_ids, slots, own, turned, *near, *far)
     return fresh, margin.reshape(row_count)
 
 

time: 48.9 us -> 42.6 us (0.87)
  Pallas kernels: 16.4 us -> 10.1 us
  waiting for transfers between devices: 19.6 us -> 18.7 us
  starting transfers between devices: 11 us -> 11.8 us
    pallas_call x2 -> x3, Pallas kernels: 11.3 us -> 5.2 us  [the longest x1 3.14 us: local(): pl.pallas_call(functools.partial(send_kernel, group=group, **sizes), out_...]
    ppermute x12, waiting for transfers between devices: 19.6 us -> 18.7 us  [swap(): return lax.ppermute(value, ('shard', 'sub'), pairs)]
    ppermute x12, starting transfers between devices: 11 us -> 11.8 us  [swap(): return lax.ppermute(value, ('shard', 'sub'), pairs)]
  transfers between devices with their start and end apart: 12 -> 12, of which waited for: 8 -> 7; matrix products, arithmetic and copies ran while one was open for 0% -> 0% of each run, Pallas kernels for 12% -> 5%
where the time goes in v6:
time: 42.6 us; the launch traced here: 42.4 us
  waiting for transfers between devices  18.7 us (44%)
  starting transfers between devices  11.8 us (28%)
  Pallas kernels  10.1 us (24%)
  between operations  1.4 us (3%)
    ppermute x12, waiting for transfers between devices, swap(): return lax.ppermute(value, ('shard', 'sub'), pairs)  18.7 us
    ppermute x12, starting transfers between devices, swap(): return lax.ppermute(value, ('shard', 'sub'), pairs)  11.8 us
    pallas_call x1, Pallas kernels, local(): pl.pallas_call(functools.partial(score_kernel, blocks=blocks, shards=shar...  4.3 us
    pallas_call x1, Pallas kernels, local(): pl.pallas_call(functools.partial(send_kernel, group=group, **sizes), out_...  3.14 us
    pallas_call x1, Pallas kernels, local(): pl.pallas_call(functools.partial(keep_kernel, **sizes), out_shape=shape,...  1.2 us
    pallas_call x1, Pallas kernels, local(): pl.pallas_call(turn_kernel, out_shape=jax.ShapeDtypeStruct((feat_width, r...  0.86 us
  transfers between devices with their start and end apart: 12, of which 7 were waited for; matrix products, arithmetic and copies ran while one was open for 0% of the time, Pallas kernels for 5%

profile of v6, /device:TPU:0, one launch (start us, length us, event | category | flops | bytes accessed | tf_op | source)
XLA Modules:
  0.0 42.4 jit_solution(8644599878927711191)
XLA Ops:
  0.6 0.0 copy-start.2
  0.6 0.0 copy-start
  0.7 0.0 copy-start.1
  1.3 3.1 %sums_send.1 = (f32[4,2,128,256]{3,2,1,0:T(8,128)S(1)}, bf16[1536,1024]{1,0:T(8,128)(2,1)S(1)}) custom-call(s32[1]{0:T(128)S(6)} %copy.7.live_in.live, s32[12]{0:T(128)} %bids.3, s32[12,128]{1,0:T(8,128)} %bitcast.14, bf16[1536,1024]{1,0:T(8,128)(2,1)} %points.1), custom_call_target="tpu_custom_call" | custom-call | flops 201326592 | bytes 1572864 | tf_op jit(solution)/shard_map/sums_send/pallas_call | solution.py:221
  4.5 0.5 %collective-permute-start = (f32[4,2,128,256]{3,2,1,0:T(8,128)S(1)}, f32[4,2,128,256]{3,2,1,0:T(8,128)S(1)}, u32[]{:S(2)}, u32[]{:S(2)}) collective-permute-start(f32[4,2,128,256]{3,2,1,0:T(8,128)S(1)} %get-tuple-element.13), channel_id=1, source_target_pairs={{0,1},{1,0},{2,3},{3,2},{4,5},{5,4},{6,7},{7,6},{8,9},{9,8},{10,11... | collective-permute-start | bytes 3145736 | tf_op jit(solution)/shard_map/ppermute | solution.py:212
  5.0 0.0 copy-done.2
  5.0 0.0 copy-done
  5.0 0.0 copy-done.1
  5.0 1.2 %sums_keep.1.keep = f32[4,2,128,256]{3,2,1,0:T(8,128)S(1)} custom-call(s32[1]{0:T(128)S(6)} %copy.7.live_in.live, s32[12]{0:T(128)S(1)} %copy-done.2, s32[12,128]{1,0:T(8,128)S(1)} %bitcast.15, bf16[128,256]{1,0:T(8,128)(2,1)S(1)} %copy-done.1, bf16[1536,1024]{1,0:T(8,128)(2,1)S(1)} %get-tuple-element.18.points), custom_call_target="tpu_custom_call" | custom-call | flops 201326592 | bytes 1572864 | tf_op jit(solution)/shard_map/sums_keep/pallas_call | solution.py:238
  6.2 1.1 %collective-permute-done.crossed = f32[4,2,128,256]{3,2,1,0:T(8,128)S(1)} collective-permute-done((f32[4,2,128,256]{3,2,1,0:T(8,128)S(1)}, f32[4,2,128,256]{3,2,1,0:T(8,128)S(1)}, u32[]{:S(2)}, u32[]{:S(2)}) %collective-permute-start) | collective-permute-done | bytes 1048608 | tf_op jit(solution)/shard_map/ppermute | solution.py:212
  7.3 0.4 fusion.5
  7.7 4.0 %collective-permute-start.1 = (s16[2,128,256]{2,1,0:T(8,128)(2,1)S(1)}, s16[2,128,256]{2,1,0:T(8,128)(2,1)S(1)}, u32[]{:S(2)}, u32[]{:S(2)}) collective-permute-start(s16[2,128,256]{2,1,0:T(8,128)(2,1)S(1)} %get-tuple-element.24), channel_id=1, source_target_pairs={{0,6},{1,7},{2,4},{3,5},{4,2},{5,3},{6,0},{7,1},{8,14},{9,15},{10,... | collective-permute-start | bytes 393224 | tf_op jit(solution)/shard_map/ppermute | solution.py:212
  11.6 0.4 %collective-permute-start.2 = (s16[2,128,256]{2,1,0:T(8,128)(2,1)S(1)}, s16[2,128,256]{2,1,0:T(8,128)(2,1)S(1)}, u32[]{:S(2)}, u32[]{:S(2)}) collective-permute-start(s16[2,128,256]{2,1,0:T(8,128)(2,1)S(1)} %get-tuple-element.23), channel_id=1, source_target_pairs={{0,4},{1,5},{2,6},{3,7},{4,0},{5,1},{6,2},{7,3},{8,12},{9,13},{10,... | collective-permute-start | bytes 393224 | tf_op jit(solution)/shard_map/ppermute | solution.py:212
  12.1 0.2 collective-permute-start.3
  12.3 3.6 %collective-permute-done.1.refs_0_ = s16[2,128,256]{2,1,0:T(8,128)(2,1)S(1)} collective-permute-done((s16[2,128,256]{2,1,0:T(8,128)(2,1)S(1)}, s16[2,128,256]{2,1,0:T(8,128)(2,1)S(1)}, u32[]{:S(2)}, u32[]{:S(2)}) %collective-permute-start.1) | collective-permute-done | bytes 131104 | tf_op jit(solution)/shard_map/ppermute | solution.py:212
  15.9 2.5 %collective-permute-done.2.refs_1_ = s16[2,128,256]{2,1,0:T(8,128)(2,1)S(1)} collective-permute-done((s16[2,128,256]{2,1,0:T(8,128)(2,1)S(1)}, s16[2,128,256]{2,1,0:T(8,128)(2,1)S(1)}, u32[]{:S(2)}, u32[]{:S(2)}) %collective-permute-start.2) | collective-permute-done | bytes 131104 | tf_op jit(solution)/shard_map/ppermute | solution.py:212
  18.4 0.0 collective-permute-done.3.refs_2_
  18.4 0.4 mix.1
  18.8 2.7 %collective-permute-start.4 = (s16[2,128,256]{2,1,0:T(8,128)(2,1)S(1)}, s16[2,128,256]{2,1,0:T(8,128)(2,1)S(1)}, u32[]{:S(2)}, u32[]{:S(2)}) collective-permute-start(s16[2,128,256]{2,1,0:T(8,128)(2,1)S(1)} %get-tuple-element.16), channel_id=1, source_target_pairs={{0,8},{1,9},{2,10},{3,11},{4,12},{5,13},{6,14},{7,15},{8,0},{9,1},... | collective-permute-start | bytes 393224 | tf_op jit(solution)/shard_map/ppermute | solution.py:212
  21.5 6.1 %collective-permute-done.4.there = s16[2,128,256]{2,1,0:T(8,128)(2,1)S(1)} collective-permute-done((s16[2,128,256]{2,1,0:T(8,128)(2,1)S(1)}, s16[2,128,256]{2,1,0:T(8,128)(2,1)S(1)}, u32[]{:S(2)}, u32[]{:S(2)}) %collective-permute-start.4) | collective-permute-done | bytes 131104 | tf_op jit(solution)/shard_map/ppermute | solution.py:212
  27.6 0.2 finish.1
  27.8 2.1 %collective-permute-start.5 = (s16[2,128,256]{2,1,0:T(8,128)(2,1)S(1)}, s16[2,128,256]{2,1,0:T(8,128)(2,1)S(1)}, u32[]{:S(2)}, u32[]{:S(2)}) collective-permute-start(s16[2,128,256]{2,1,0:T(8,128)(2,1)S(1)} %get-tuple-element.19.refs_0_), channel_id=1, source_target_pairs={{0,6},{1,7},{2,4},{3,5},{4,2},{5,3},{6,0},{7,1},{8,14},{9,15},{10,... | collective-permute-start | bytes 393224 | tf_op jit(solution)/shard_map/ppermute | solution.py:212
  29.9 1.3 %collective-permute-start.6 = (s16[2,128,256]{2,1,0:T(8,128)(2,1)S(1)}, s16[2,128,256]{2,1,0:T(8,128)(2,1)S(1)}, u32[]{:S(2)}, u32[]{:S(2)}) collective-permute-start(s16[2,128,256]{2,1,0:T(8,128)(2,1)S(1)} %get-tuple-element.19.refs_0_), channel_id=1, source_target_pairs={{0,4},{1,5},{2,6},{3,7},{4,0},{5,1},{6,2},{7,3},{8,12},{9,13},{10,... | collective-permute-start | bytes 393224 | tf_op jit(solution)/shard_map/ppermute | solution.py:212
  31.2 0.1 collective-permute-start.7
  31.3 0.0 collective-permute-start.8
  31.3 3.8 %collective-permute-done.5.refs_1_ = s16[2,128,256]{2,1,0:T(8,128)(2,1)S(1)} collective-permute-done((s16[2,128,256]{2,1,0:T(8,128)(2,1)S(1)}, s16[2,128,256]{2,1,0:T(8,128)(2,1)S(1)}, u32[]{:S(2)}, u32[]{:S(2)}) %collective-permute-start.5) | collective-permute-done | bytes 131104 | tf_op jit(solution)/shard_map/ppermute | solution.py:212
  35.1 0.0 collective-permute-start.9
  35.1 1.5 %collective-permute-done.6.refs_2_ = s16[2,128,256]{2,1,0:T(8,128)(2,1)S(1)} collective-permute-done((s16[2,128,256]{2,1,0:T(8,128)(2,1)S(1)}, s16[2,128,256]{2,1,0:T(8,128)(2,1)S(1)}, u32[]{:S(2)}, u32[]{:S(2)}) %collective-permute-start.6) | collective-permute-done | bytes 131104 | tf_op jit(solution)/shard_map/ppermute | solution.py:212
  36.6 0.0 collective-permute-start.10
  36.6 0.0 collective-permute-done.7.refs_3_
  36.6 0.5 %collective-permute-start.11 = (s16[2,128,256]{2,1,0:T(8,128)(2,1)S(1)}, s16[2,128,256]{2,1,0:T(8,128)(2,1)S(1)}, u32[]{:S(2)}, u32[]{:S(2)}) collective-permute-start(s16[2,128,256]{2,1,0:T(8,128)(2,1)S(1)} %collective-permute-done.7.refs_3_), channel_id=1, source_target_pairs={{0,1},{1,0},{2,3},{3,2},{4,5},{5,4},{6,7},{7,6},{8,9},{9,8},{10,11... | collective-permute-start | bytes 393224 | tf_op jit(solution)/shard_map/ppermute | solution.py:212
  37.1 0.9 %turn.1.turned = bf16[1024,1536]{1,0:T(8,128)(2,1)S(1)} custom-call(bf16[1536,1024]{1,0:T(8,128)(2,1)S(1)} %get-tuple-element.18.points), custom_call_target="tpu_custom_call" | custom-call | flops 201326592 | bytes 1572864 | tf_op jit(solution)/shard_map/turn/pallas_call | solution.py:259
  38.0 0.0 collective-permute-done.8.refs_4_
  38.0 0.0 collective-permute-done.9.refs_5_
  38.0 0.0 collective-permute-done.10.refs_6_
  38.0 0.1 collective-permute-done.11.refs_7_
  38.1 4.3 %scores.1 = (bf16[128,256]{1,0:T(8,128)(2,1)}, f32[12,128]{1,0:T(8,128)}) custom-call(s32[12]{0:T(128)S(1)} %copy-done.2, s32[12,128]{1,0:T(8,128)S(1)} %bitcast.16, f32[128,256]{1,0:T(8,128)S(1)} %get-tuple-element.17.own, bf16[1024,1536]{1,0:T(8,128)(2,1)S(1)} %turn.1.turned, s16[2,128,256]{2,1,0:T(8,128)(2,1)S(1)} %get-tuple-element.19.refs_0_, ...), custom_call_target="tpu_custom_call" | custom-call | tf_op jit(solution)/shard_map/scores/pallas_call | solution.py:284
Async XLA Ops:
  0.6 4.4 %copy-start.2 = (s32[12]{0:T(128)S(1)}, s32[12]{0:T(128)}, u32[]{:S(2)}) copy-start(s32[12]{0:T(128)} %bids.3) | copy-start | bytes 148
  0.6 4.4 %copy-start = (s32[1536]{0:T(1024)S(1)}, s32[1536]{0:T(1024)}, u32[]{:S(2)}) copy-start(s32[1536]{0:T(1024)} %param.7) | copy-start | bytes 18436
  0.7 4.3 %copy-start.1 = (bf16[128,256]{1,0:T(8,128)(2,1)S(1)}, bf16[128,256]{1,0:T(8,128)(2,1)}, u32[]{:S(2)}) copy-start(bf16[128,256]{1,0:T(8,128)(2,1)} %old.1) | copy-start | bytes 196612
  4.5 2.8 %collective-permute-start = (f32[4,2,128,256]{3,2,1,0:T(8,128)S(1)}, f32[4,2,128,256]{3,2,1,0:T(8,128)S(1)}, u32[]{:S(2)}, u32[]{:S(2)}) collective-permute-start(f32[4,2,128,256]{3,2,1,0:T(8,128)S(1)} %get-tuple-element.13), channel_id=1, source_target_pairs={{0,1},{1,0},{2,3},{3,2},{4,5},{5,4},{6,7},{7,6},{8,9},{9,8},{10,11... | collective-permute-start | bytes 3145736 | tf_op jit(solution)/shard_map/ppermute | solution.py:212
  7.7 8.2 %collective-permute-start.1 = (s16[2,128,256]{2,1,0:T(8,128)(2,1)S(1)}, s16[2,128,256]{2,1,0:T(8,128)(2,1)S(1)}, u32[]{:S(2)}, u32[]{:S(2)}) collective-permute-start(s16[2,128,256]{2,1,0:T(8,128)(2,1)S(1)} %get-tuple-element.24), channel_id=1, source_target_pairs={{0,6},{1,7},{2,4},{3,5},{4,2},{5,3},{6,0},{7,1},{8,14},{9,15},{10,... | collective-permute-start | bytes 393224 | tf_op jit(solution)/shard_map/ppermute | solution.py:212
  11.6 6.8 %collective-permute-start.2 = (s16[2,128,256]{2,1,0:T(8,128)(2,1)S(1)}, s16[2,128,256]{2,1,0:T(8,128)(2,1)S(1)}, u32[]{:S(2)}, u32[]{:S(2)}) collective-permute-start(s16[2,128,256]{2,1,0:T(8,128)(2,1)S(1)} %get-tuple-element.23), channel_id=1, source_target_pairs={{0,4},{1,5},{2,6},{3,7},{4,0},{5,1},{6,2},{7,3},{8,12},{9,13},{10,... | collective-permute-start | bytes 393224 | tf_op jit(solution)/shard_map/ppermute | solution.py:212
  12.1 6.3 %collective-permute-start.3 = (s16[2,128,256]{2,1,0:T(8,128)(2,1)S(1)}, s16[2,128,256]{2,1,0:T(8,128)(2,1)S(1)}, u32[]{:S(2)}, u32[]{:S(2)}) collective-permute-start(s16[2,128,256]{2,1,0:T(8,128)(2,1)S(1)} %get-tuple-element.22), channel_id=1, source_target_pairs={{0,2},{1,3},{2,0},{3,1},{4,6},{5,7},{6,4},{7,5},{8,10},{9,11},{10,... | collective-permute-start | bytes 393224 | tf_op jit(solution)/shard_map/ppermute | solution.py:212
  18.8 8.7 %collective-permute-start.4 = (s16[2,128,256]{2,1,0:T(8,128)(2,1)S(1)}, s16[2,128,256]{2,1,0:T(8,128)(2,1)S(1)}, u32[]{:S(2)}, u32[]{:S(2)}) collective-permute-start(s16[2,128,256]{2,1,0:T(8,128)(2,1)S(1)} %get-tuple-element.16), channel_id=1, source_target_pairs={{0,8},{1,9},{2,10},{3,11},{4,12},{5,13},{6,14},{7,15},{8,0},{9,1},... | collective-permute-start | bytes 393224 | tf_op jit(solution)/shard_map/ppermute | solution.py:212
  27.8 7.3 %collective-permute-start.5 = (s16[2,128,256]{2,1,0:T(8,128)(2,1)S(1)}, s16[2,128,256]{2,1,0:T(8,128)(2,1)S(1)}, u32[]{:S(2)}, u32[]{:S(2)}) collective-permute-start(s16[2,128,256]{2,1,0:T(8,128)(2,1)S(1)} %get-tuple-element.19.refs_0_), channel_id=1, source_target_pairs={{0,6},{1,7},{2,4},{3,5},{4,2},{5,3},{6,0},{7,1},{8,14},{9,15},{10,... | collective-permute-start | bytes 393224 | tf_op jit(solution)/shard_map/ppermute | solution.py:212
  29.9 6.7 %collective-permute-start.6 = (s16[2,128,256]{2,1,0:T(8,128)(2,1)S(1)}, s16[2,128,256]{2,1,0:T(8,128)(2,1)S(1)}, u32[]{:S(2)}, u32[]{:S(2)}) collective-permute-start(s16[2,128,256]{2,1,0:T(8,128)(2,1)S(1)} %get-tuple-element.19.refs_0_), channel_id=1, source_target_pairs={{0,4},{1,5},{2,6},{3,7},{4,0},{5,1},{6,2},{7,3},{8,12},{9,13},{10,... | collective-permute-start | bytes 393224 | tf_op jit(solution)/shard_map/ppermute | solution.py:212
  31.2 5.4 %collective-permute-start.7 = (s16[2,128,256]{2,1,0:T(8,128)(2,1)S(1)}, s16[2,128,256]{2,1,0:T(8,128)(2,1)S(1)}, u32[]{:S(2)}, u32[]{:S(2)}) collective-permute-start(s16[2,128,256]{2,1,0:T(8,128)(2,1)S(1)} %get-tuple-element.19.refs_0_), channel_id=1, source_target_pairs={{0,2},{1,3},{2,0},{3,1},{4,6},{5,7},{6,4},{7,5},{8,10},{9,11},{10,... | collective-permute-start | bytes 393224 | tf_op jit(solution)/shard_map/ppermute | solution.py:212
  31.3 6.6 %collective-permute-start.8 = (s16[2,128,256]{2,1,0:T(8,128)(2,1)S(1)}, s16[2,128,256]{2,1,0:T(8,128)(2,1)S(1)}, u32[]{:S(2)}, u32[]{:S(2)}) collective-permute-start(s16[2,128,256]{2,1,0:T(8,128)(2,1)S(1)} %get-tuple-element.19.refs_0_), channel_id=1, source_target_pairs={{0,1},{1,0},{2,3},{3,2},{4,5},{5,4},{6,7},{7,6},{8,9},{9,8},{10,11... | collective-permute-start | bytes 393224 | tf_op jit(solution)/shard_map/ppermute | solution.py:212
  35.1 2.9 %collective-permute-start.9 = (s16[2,128,256]{2,1,0:T(8,128)(2,1)S(1)}, s16[2,128,256]{2,1,0:T(8,128)(2,1)S(1)}, u32[]{:S(2)}, u32[]{:S(2)}) collective-permute-start(s16[2,128,256]{2,1,0:T(8,128)(2,1)S(1)} %collective-permute-done.5.refs_1_), channel_id=1, source_target_pairs={{0,1},{1,0},{2,3},{3,2},{4,5},{5,4},{6,7},{7,6},{8,9},{9,8},{10,11... | collective-permute-start | bytes 393224 | tf_op jit(solution)/shard_map/ppermute | solution.py:212
  36.6 1.4 %collective-permute-start.10 = (s16[2,128,256]{2,1,0:T(8,128)(2,1)S(1)}, s16[2,128,256]{2,1,0:T(8,128)(2,1)S(1)}, u32[]{:S(2)}, u32[]{:S(2)}) collective-permute-start(s16[2,128,256]{2,1,0:T(8,128)(2,1)S(1)} %collective-permute-done.6.refs_2_), channel_id=1, source_target_pairs={{0,1},{1,0},{2,3},{3,2},{4,5},{5,4},{6,7},{7,6},{8,9},{9,8},{10,11... | collective-permute-start | bytes 393224 | tf_op jit(solution)/shard_map/ppermute | solution.py:212
  36.6 1.5 %collective-permute-start.11 = (s16[2,128,256]{2,1,0:T(8,128)(2,1)S(1)}, s16[2,128,256]{2,1,0:T(8,128)(2,1)S(1)}, u32[]{:S(2)}, u32[]{:S(2)}) collective-permute-start(s16[2,128,256]{2,1,0:T(8,128)(2,1)S(1)} %collective-permute-done.7.refs_3_), channel_id=1, source_target_pairs={{0,1},{1,0},{2,3},{3,2},{4,5},{5,4},{6,7},{7,6},{8,9},{9,8},{10,11... | collective-permute-start | bytes 393224 | tf_op jit(solution)/shard_map/ppermute | solution.py:212

commit v7 on v6

v7 whole, which is shorter than its diff:
```python
import functools
import math

import jax
import jax.numpy as jnp
from jax import lax
from jax.experimental import pallas as pl
from jax.experimental.pallas import tpu as pltpu
from jax.sharding import PartitionSpec as P

SLOT = 128
POINT_LIMIT = 6.0

prior_weight = 4.0
norm_eps = 1e-06

LOW_EXP = -32
MIB = 1 << 20


def code_rate(top_exp):
    return 32767.0 / (top_exp - LOW_EXP)


def encode(value, rate):
    size = jnp.maximum(jnp.abs(value), 2.0**LOW_EXP)
    level = jnp.floor((jnp.log2(size) - LOW_EXP) * rate + 0.5)
    return jnp.where(value < 0.0, -level, level).astype(jnp.int32).astype(jnp.int16)


def decode(code, rate):
    level = code.astype(jnp.int32).astype(jnp.float32)
    size = jnp.exp2(jnp.abs(level) * (1.0 / rate) + LOW_EXP)
    return jnp.where(level < 0.0, -size, size)


def bits_of(count):
    return [1 << bit for bit in range(count.bit_length() - 1)]


def near_group(subs, shards):
    group = [(0, 0)]
    for bit in bits_of(subs)[1:]:
        group = group + [(sub ^ bit, shard) for sub, shard in group]
    group = group + [(sub, shard ^ 1) for sub, shard in group]
    return group[:1] + group[:0:-1]


def late_bits(shards):
    return bits_of(shards)[1:]


def late_place(bits, over_shard):
    place = 0
    for bit in bits:
        place = place * 2 + (over_shard // bit) % 2
    return place


def add_block(halves, hot, rows_of, over_shard, *, sub, subs, shards, width, flip):
    group = near_group(subs, shards)
    late = late_place(late_bits(shards), over_shard)
    for over_sub in range(0, subs, 2):
        column = pl.multiple_of((sub ^ over_sub ^ flip) * width, width)
        part = jnp.dot(hot, rows_of(pl.ds(column, width)), preferred_element_type=jnp.float32)
        at = jnp.where(over_shard % 2 == 0, group.index((over_sub, 0)), group.index((over_sub, 1)))
        half_rows = part.shape[0] // 2
        halves[0][at, late] += part[:half_rows]
        halves[1][at, late] += part[half_rows:]


def hot_rows(slots, block, live):
    slot = jnp.where(block < live, slots[block : block + 1, :], -1)
    return (slot == lax.broadcasted_iota(jnp.int32, (SLOT, SLOT), 0)).astype(jnp.bfloat16)


def send_kernel(
    live_in, bids_in, slots_in, points, first_half, second_half, held, live, bids, slots, small, arrived, *, blocks, group, shards, subs, width
):
    sub, shard = lax.axis_index("sub"), lax.axis_index("shard")
    firsts = [
        pltpu.make_async_copy(live_in, live, small.at[0]),
        pltpu.make_async_copy(bids_in, bids, small.at[1]),
        pltpu.make_async_copy(slots_in, slots, small.at[2]),
    ]
    for copy in firsts:
        copy.start()
    copies = []
    for first in range(0, blocks, group):
        span = pl.ds(first * SLOT, group * SLOT)
        copies.append(pltpu.make_async_copy(points.at[span], held.at[span], arrived.at[first // group]))
        copies[-1].start()
    for sums in (first_half, second_half):
        sums[...] = jnp.zeros_like(sums)
    for copy in firsts:
        copy.wait()
    for block in range(blocks):
        if block % group == 0:
            copies[block // group].wait()
        span = slice(block * SLOT, (block + 1) * SLOT)
        add_block(
            (first_half, second_half),
            hot_rows(slots, block, live[0]),
            lambda column, span=span: held[span, column],
            bids[block] ^ shard,
            sub=sub,
            subs=subs,
            shards=shards,
            width=width,
            flip=1,
        )


def keep_kernel(live, bids, slots, old, points, first_half, second_half, *, blocks, shards, subs, width):
    sub, shard = lax.axis_index("sub"), lax.axis_index("shard")
    prior = prior_weight * old[...].astype(jnp.float32)
    half_rows = prior.shape[0] // 2
    for half, sums in enumerate((first_half, second_half)):
        sums[...] = jnp.zeros_like(sums)
        sums[0, 0] = prior[half * half_rows : (half + 1) * half_rows]
    for block in range(blocks):
        span = slice(block * SLOT, (block + 1) * SLOT)
        add_block(
            (first_half, second_half),
            hot_rows(slots, block, live[0]),
            lambda column, span=span: points[span, column],
            bids[block] ^ shard,
            sub=sub,
            subs=subs,
            shards=shards,
            width=width,
            flip=0,
        )


def mix_kernel(keep, crossed, *refs, rate):
    terms, (mine, code) = refs[:-2], refs[-2:]
    total = keep[0] + crossed[0]
    for term in terms:
        total = total + decode(term[...], rate)
    mine[...] = total
    code[...] = encode(total, rate)


def finish_kernel(mine, there, own, code, *, rate):
    own[...] = mine[0] + decode(there[1], rate)
    code[0] = encode(own[...], rate)
    code[1] = encode(mine[1] + decode(there[0], rate), rate)


def score_kernel(
    bids, slots, own, points, near, far, *refs, half, blocks, shards, subs, rows, width, rate, group
):
    if half:
        (mine_in, rival_in, fresh_in), (fresh, margin, cents) = refs[:3], refs[3:]
    else:
        fresh, mine_out, rival_out, cents = refs
    chips = near_group(subs, shards)
    sub, shard = lax.axis_index("sub"), lax.axis_index("shard")
    bits = late_bits(shards)
    late_count = 1 << len(bits)
    half_rows = rows // 2
    for over_shard in range(shards):
        parts = []
        for over_sub in range(0, subs, 2):
            piece = chips.index((over_sub, over_shard % 2)) * late_count + late_place(bits, over_shard)
            parts.append((sub ^ over_sub, decode(near[piece], rate)))
            parts.append((sub ^ 1 ^ over_sub, decode(far[piece], rate)))
        squares = sum(jnp.sum(part * part, axis=1, keepdims=True) for _, part in parts)
        scale = lax.rsqrt(squares + norm_eps)
        row = pl.ds(pl.multiple_of((shard ^ over_shard) * half_rows, half_rows), half_rows)
        for place, part in parts:
            cents[row, pl.ds(pl.multiple_of(place * width, width), width)] = (part * scale).astype(jnp.bfloat16)
        if over_shard == 0:
            updated = (own[...] * scale).astype(jnp.bfloat16)
            if half:
                fresh[:half_rows] = fresh_in[...]
                fresh[half_rows:] = updated
            else:
                fresh[...] = updated

    lanes = 8
    row_of = lax.broadcasted_iota(jnp.int32, (half_rows, SLOT), 0)
    for block in range(blocks // group):
        score = lax.dot_general(
            cents[...],
            points[block * group * SLOT : (block + 1) * group * SLOT, :],
            (((1,), (1,)), ((), ())),
            preferred_element_type=jnp.float32,
        )
        for inner in range(group):
            at = block * group + inner
            line = slice(at, at + 1)
            part = score[:, inner * SLOT : (inner + 1) * SLOT].reshape(shards, half_rows, SLOT)
            own_part = part[0]
            for segment in range(1, shards):
                own_part = jnp.where(bids[at] == segment, part[segment], own_part)
            hit = row_of == slots[line, :] - half * half_rows
            mine = jnp.sum(jnp.where(hit, own_part, 0.0), axis=0, keepdims=True)
            rivals = jnp.where(hit, -jnp.inf, own_part).reshape(half_rows // lanes, lanes, SLOT).max(axis=0)
            for segment in range(shards):
                best = part[segment].reshape(half_rows // lanes, lanes, SLOT).max(axis=0)
                rivals = jnp.maximum(rivals, jnp.where(bids[at] == segment, -jnp.inf, best))
            rival = jnp.max(rivals, axis=0, keepdims=True)
            if half:
                margin[line, :] = (mine_in[line, :] + mine) - jnp.maximum(rival_in[line, :], rival)
            else:
                mine_out[line, :] = mine
                rival_out[line, :] = rival


def local(points, block_ids, slot_ids, live_blocks, old_centroids):
    row_count, feat_width = points.shape
    blocks = row_count // SLOT
    shards = lax.axis_size("shard")
    subs = lax.axis_size("sub")
    rows, width = old_centroids.shape
    half_rows = rows // 2
    total = rows * shards
    top = POINT_LIMIT * (row_count * shards * subs + prior_weight)
    rate = code_rate(math.ceil(math.log2(top)))
    slots = slot_ids.reshape(blocks, SLOT)
    chips = near_group(subs, shards)
    bits = late_bits(shards)
    late = 1 << len(bits)
    group = 2 if blocks % 2 == 0 else 1
    limit = pltpu.CompilerParams(vmem_limit_bytes=8 * MIB + 4 * total * feat_width)
    smem = pl.BlockSpec(memory_space=pltpu.SMEM)
    vmem = pl.BlockSpec(memory_space=pltpu.VMEM)
    hbm = pl.BlockSpec(memory_space=pltpu.HBM)

    def swap(value, over_sub, over_shard):
        pairs = []
        for shard in range(shards):
            for sub in range(subs):
                pairs.append((shard * subs + sub, (shard ^ over_shard) * subs + (sub ^ over_sub)))
        return lax.ppermute(value, ("shard", "sub"), pairs)

    def in_hbm(value):
        return pltpu.with_memory_space_constraint(value, pltpu.HBM)

    shape = jax.ShapeDtypeStruct((len(chips), late, half_rows, width), jnp.float32)
    cost = pl.CostEstimate(flops=row_count * SLOT * feat_width, bytes_accessed=row_count * feat_width, transcendentals=0)
    sizes = dict(blocks=blocks, shards=shards, subs=subs, width=width)
    *send, held = pl.pallas_call(
        functools.partial(send_kernel, group=group, **sizes),
        out_shape=(shape, shape, jax.ShapeDtypeStruct(points.shape, points.dtype)),
        in_specs=[hbm] * 4,
        out_specs=(vmem, vmem, vmem),
        scratch_shapes=[
            pltpu.SMEM((1,), jnp.int32),
            pltpu.SMEM((blocks,), jnp.int32),
            pltpu.VMEM((blocks, SLOT), jnp.int32),
            pltpu.SemaphoreType.DMA((3,)),
            pltpu.SemaphoreType.DMA((blocks // group,)),
        ],
        compiler_params=limit,
        cost_estimate=cost,
        name="sums_send",
    )(live_blocks, in_hbm(block_ids), in_hbm(slots), in_hbm(points))
    crossed = [swap(sums, 1, 0) for sums in send]
    keep = pl.pallas_call(
        functools.partial(keep_kernel, **sizes),
        out_shape=(shape, shape),
        in_specs=[smem, smem, vmem, vmem, vmem],
        out_specs=(vmem, vmem),
        compiler_params=limit,
        cost_estimate=cost,
        name="sums_keep",
    )(live_blocks, block_ids, slots, old_centroids, held)

    piece = (late, half_rows, width)
    two = (2, half_rows, width)

    def reduce_near(half):
        terms = []
        for index, (over_sub, over_shard) in list(enumerate(chips))[1:]:
            terms.append(swap(encode(keep[half][index] + crossed[half][index], rate), over_sub, over_shard))
        return terms

    def reduce_late(half, terms):
        mine, code = pl.pallas_call(
            functools.partial(mix_kernel, rate=rate),
            out_shape=(jax.ShapeDtypeStruct(piece, jnp.float32), jax.ShapeDtypeStruct(piece, jnp.int16)),
            compiler_params=limit,
            name=f"mix{half}",
        )(keep[half], crossed[half], *terms)
        for bit in bits[:-1]:
            count = mine.shape[0] // 2
            mine = mine[:count] + decode(swap(encode(mine[count:], rate), 0, bit), rate)
            code = encode(mine, rate)
        return mine, swap(code, 0, bits[-1])

    def gather(half, mine, there):
        own, code = pl.pallas_call(
            functools.partial(finish_kernel, rate=rate),
            out_shape=(
                jax.ShapeDtypeStruct((half_rows, width), jnp.float32),
                jax.ShapeDtypeStruct(two, jnp.int16),
            ),
            compiler_params=limit,
            name=f"finish{half}",
        )(mine, there)
        for bit in reversed(bits[:-1]):
            code = jnp.concatenate([code, swap(code, 0, bit)])
        near = jnp.concatenate([code] + [swap(code, over_sub, over_shard) for over_sub, over_shard in chips[1:]])
        return own, near

    def scores(half, own, near, far, *earlier):
        line = jax.ShapeDtypeStruct((blocks, SLOT), jnp.float32)
        fresh = jax.ShapeDtypeStruct((rows if half else half_rows, width), jnp.bfloat16)
        return pl.pallas_call(
            functools.partial(
                score_kernel,
                half=half,
                blocks=blocks,
                shards=shards,
                subs=subs,
                rows=rows,
                width=width,
                rate=rate,
                group=group,
            ),
            out_shape=(fresh, line) if half else (fresh, line, line),
            in_specs=[smem] + [vmem] * (5 + len(earlier)),
            out_specs=(vmem,) * (2 if half else 3),
            scratch_shapes=[pltpu.VMEM((total // 2, feat_width), jnp.bfloat16)],
            compiler_params=pltpu.CompilerParams(vmem_limit_bytes=12 * MIB + 6 * total * feat_width),
            cost_estimate=pl.CostEstimate(
                flops=row_count * total * feat_width,
                bytes_accessed=2 * row_count * feat_width,
                transcendentals=total * feat_width // 2,
            ),
            name=f"scores{half}",
        )(block_ids, slots, own, held, near, far, *earlier)

    terms = [reduce_near(half) for half in range(2)]
    pairs = [reduce_late(half, terms[half]) for half in range(2)]
    gathered = [gather(half, *pairs[half]) for half in range(2)]
    far = [swap(near, 1, 0) for _, near in gathered]
    fresh, mine, rival = scores(0, *gathered[0], far[0])
    fresh, margin = scores(1, *gathered[1], far[1], mine, rival, fresh)
    return fresh, margin.reshape(row_count)


def solution(mesh):
    return jax.shard_map(
        local,
        mesh=mesh,
        in_specs=(
            P(("groups", "shard", "sub"), None),
            P(("groups", "shard", "sub")),
            P(("groups", "shard", "sub")),
            P(("groups", "shard", "sub")),
            P(("groups", "shard"), "sub"),
        ),
        out_specs=(P(("groups", "shard"), "sub"), P(("groups", "shard", "sub"))),
        check_vma=False,
    )
```

time: 42.6 us -> 44.7 us (1.049)
  starting transfers between devices: 11.8 us -> 20 us
  waiting for transfers between devices: 18.7 us -> 12.7 us
    ppermute x12 -> x18, starting transfers between devices: 11.8 us -> 20 us  [swap(): return lax.ppermute(value, ('shard', 'sub'), pairs)]
    ppermute x12 -> x18, waiting for transfers between devices: 18.7 us -> 12.7 us  [swap(): return lax.ppermute(value, ('shard', 'sub'), pairs)]
    pallas_call x5 -> x7, Pallas kernels: 7 us -> 6.8 us  [the longest x2 4.94 us: scores(): pl.pallas_call(functools.partial(score_kernel, half=half, blocks=blocks,...]
  transfers between devices with their start and end apart: 12 -> 18, of which waited for: 7 -> 7; matrix products, arithmetic and copies ran while one was open for 0% -> 1% of each run, Pallas kernels for 5% -> 9%
where the time goes in v7:
time: 44.7 us; the launch traced here: 44.6 us
  starting transfers between devices  20 us (45%)
  waiting for transfers between devices  12.7 us (28%)
  Pallas kernels  9.92 us (22%)
  between operations  1.47 us (3%)
    ppermute x18, starting transfers between devices, swap(): return lax.ppermute(value, ('shard', 'sub'), pairs)  20 us
    ppermute x18, waiting for transfers between devices, swap(): return lax.ppermute(value, ('shard', 'sub'), pairs)  12.7 us
    pallas_call x2, Pallas kernels, scores(): pl.pallas_call(functools.partial(score_kernel, half=half, blocks=blocks,...  4.94 us
    pallas_call x1, Pallas kernels, local(): pl.pallas_call(functools.partial(send_kernel, group=group, **sizes), out_...  3.12 us
    pallas_call x1, Pallas kernels, local(): pl.pallas_call(functools.partial(keep_kernel, **sizes), out_shape=(shape,...  1.28 us
  transfers between devices with their start and end apart: 18, of which 7 were waited for; matrix products, arithmetic and copies ran while one was open for 1% of the time, Pallas kernels for 9%

profile of v7, /device:TPU:0, one launch (start us, length us, event | category | flops | bytes accessed | tf_op | source)
XLA Modules:
  0.0 44.6 jit_solution(18384695619484048014)
XLA Ops:
  0.6 0.0 copy-start.2
  0.6 0.0 copy-start
  0.7 0.0 copy-start.1
  1.3 3.1 %sums_send.1 = (f32[4,2,64,256]{3,2,1,0:T(8,128)S(1)}, f32[4,2,64,256]{3,2,1,0:T(8,128)S(1)}, bf16[1536,1024]{1,0:T(8,128)(2,1)S(1)}) custom-call(s32[1]{0:T(128)S(6)} %copy.13.live_in.live, s32[12]{0:T(128)} %bids.5, s32[12,128]{1,0:T(8,128)} %bitcast.26, bf16[1536,1024]{1,0:T(8,128)(2,1)} %points.1), custom_call_target="tpu_custom_call" | custom-call | flops 201326592 | bytes 1572864 | tf_op jit(solution)/shard_map/sums_send/pallas_call | solution.py:245
  4.5 0.5 %collective-permute-start = (f32[4,2,64,256]{3,2,1,0:T(8,128)S(1)}, f32[4,2,64,256]{3,2,1,0:T(8,128)S(1)}, u32[]{:S(2)}, u32[]{:S(2)}) collective-permute-start(f32[4,2,64,256]{3,2,1,0:T(8,128)S(1)} %get-tuple-element.22), channel_id=1, source_target_pairs={{0,1},{1,0},{2,3},{3,2},{4,5},{5,4},{6,7},{7,6},{8,9},{9,8},{10,11... | collective-permute-start | bytes 1572872 | tf_op jit(solution)/shard_map/ppermute | solution.py:237
  5.0 0.1 collective-permute-start.9
  5.1 0.0 copy-done.2
  5.1 0.0 copy-done
  5.1 0.0 copy-done.1
  5.1 1.3 %sums_keep.1 = (f32[4,2,64,256]{3,2,1,0:T(8,128)S(1)}, f32[4,2,64,256]{3,2,1,0:T(8,128)S(1)}) custom-call(s32[1]{0:T(128)S(6)} %copy.13.live_in.live, s32[12]{0:T(128)S(1)} %copy-done.2, s32[12,128]{1,0:T(8,128)S(1)} %bitcast.27, bf16[128,256]{1,0:T(8,128)(2,1)S(1)} %copy-done.1, bf16[1536,1024]{1,0:T(8,128)(2,1)S(1)} %get-tuple-element.20.points), custom_call_target="tpu_custom_call" | custom-call | flops 201326592 | bytes 1572864 | tf_op jit(solution)/shard_map/sums_keep/pallas_call | solution.py:262
  6.3 0.2 collective-permute-done.crossed
  6.5 0.2 fusion.5
  6.7 2.9 %collective-permute-start.3 = (s16[2,64,256]{2,1,0:T(8,128)(2,1)S(1)}, s16[2,64,256]{2,1,0:T(8,128)(2,1)S(1)}, u32[]{:S(2)}, u32[]{:S(2)}) collective-permute-start(s16[2,64,256]{2,1,0:T(8,128)(2,1)S(1)} %get-tuple-element.41), channel_id=1, source_target_pairs={{0,2},{1,3},{2,0},{3,1},{4,6},{5,7},{6,4},{7,5},{8,10},{9,11},{10,... | collective-permute-start | bytes 196616 | tf_op jit(solution)/shard_map/ppermute | solution.py:237
  9.6 1.6 %collective-permute-start.2 = (s16[2,64,256]{2,1,0:T(8,128)(2,1)S(1)}, s16[2,64,256]{2,1,0:T(8,128)(2,1)S(1)}, u32[]{:S(2)}, u32[]{:S(2)}) collective-permute-start(s16[2,64,256]{2,1,0:T(8,128)(2,1)S(1)} %get-tuple-element.42), channel_id=1, source_target_pairs={{0,4},{1,5},{2,6},{3,7},{4,0},{5,1},{6,2},{7,3},{8,12},{9,13},{10,... | collective-permute-start | bytes 196616 | tf_op jit(solution)/shard_map/ppermute | solution.py:237
  11.2 0.0 collective-permute-start.1
  11.2 0.0 collective-permute-done.9.crossed
  11.2 0.2 fusion.11
  11.4 2.0 %collective-permute-start.12 = (s16[2,64,256]{2,1,0:T(8,128)(2,1)S(1)}, s16[2,64,256]{2,1,0:T(8,128)(2,1)S(1)}, u32[]{:S(2)}, u32[]{:S(2)}) collective-permute-start(s16[2,64,256]{2,1,0:T(8,128)(2,1)S(1)} %get-tuple-element.38), channel_id=1, source_target_pairs={{0,2},{1,3},{2,0},{3,1},{4,6},{5,7},{6,4},{7,5},{8,10},{9,11},{10,... | collective-permute-start | bytes 196616 | tf_op jit(solution)/shard_map/ppermute | solution.py:237
  13.4 1.6 %collective-permute-start.11 = (s16[2,64,256]{2,1,0:T(8,128)(2,1)S(1)}, s16[2,64,256]{2,1,0:T(8,128)(2,1)S(1)}, u32[]{:S(2)}, u32[]{:S(2)}) collective-permute-start(s16[2,64,256]{2,1,0:T(8,128)(2,1)S(1)} %get-tuple-element.39), channel_id=1, source_target_pairs={{0,4},{1,5},{2,6},{3,7},{4,0},{5,1},{6,2},{7,3},{8,12},{9,13},{10,... | collective-permute-start | bytes 196616 | tf_op jit(solution)/shard_map/ppermute | solution.py:237
  15.0 0.0 collective-permute-done.3.refs_2_
  15.0 0.0 collective-permute-start.10
  15.0 0.0 collective-permute-done.2.refs_1_
  15.0 1.5 %collective-permute-done.1.refs_0_ = s16[2,64,256]{2,1,0:T(8,128)(2,1)S(1)} collective-permute-done((s16[2,64,256]{2,1,0:T(8,128)(2,1)S(1)}, s16[2,64,256]{2,1,0:T(8,128)(2,1)S(1)}, u32[]{:S(2)}, u32[]{:S(2)}) %collective-permute-start.1) | collective-permute-done | bytes 65568 | tf_op jit(solution)/shard_map/ppermute | solution.py:237
  16.5 0.2 mix1.1
  16.7 2.7 %collective-permute-start.4 = (s16[2,64,256]{2,1,0:T(8,128)(2,1)S(1)}, s16[2,64,256]{2,1,0:T(8,128)(2,1)S(1)}, u32[]{:S(2)}, u32[]{:S(2)}) collective-permute-start(s16[2,64,256]{2,1,0:T(8,128)(2,1)S(1)} %get-tuple-element.24), channel_id=1, source_target_pairs={{0,8},{1,9},{2,10},{3,11},{4,12},{5,13},{6,14},{7,15},{8,0},{9,1},... | collective-permute-start | bytes 196616 | tf_op jit(solution)/shard_map/ppermute | solution.py:237
  19.4 0.0 collective-permute-done.12.refs_2_
  19.4 0.0 collective-permute-done.11.refs_1_
  19.4 1.2 %collective-permute-done.10.refs_0_ = s16[2,64,256]{2,1,0:T(8,128)(2,1)S(1)} collective-permute-done((s16[2,64,256]{2,1,0:T(8,128)(2,1)S(1)}, s16[2,64,256]{2,1,0:T(8,128)(2,1)S(1)}, u32[]{:S(2)}, u32[]{:S(2)}) %collective-permute-start.10) | collective-permute-done | bytes 65568 | tf_op jit(solution)/shard_map/ppermute | solution.py:237
  20.6 0.2 mix0.1
  20.8 2.3 %collective-permute-start.13 = (s16[2,64,256]{2,1,0:T(8,128)(2,1)S(1)}, s16[2,64,256]{2,1,0:T(8,128)(2,1)S(1)}, u32[]{:S(2)}, u32[]{:S(2)}) collective-permute-start(s16[2,64,256]{2,1,0:T(8,128)(2,1)S(1)} %get-tuple-element.30), channel_id=1, source_target_pairs={{0,8},{1,9},{2,10},{3,11},{4,12},{5,13},{6,14},{7,15},{8,0},{9,1},... | collective-permute-start | bytes 196616 | tf_op jit(solution)/shard_map/ppermute | solution.py:237
  23.1 0.8 %collective-permute-done.4.there = s16[2,64,256]{2,1,0:T(8,128)(2,1)S(1)} collective-permute-done((s16[2,64,256]{2,1,0:T(8,128)(2,1)S(1)}, s16[2,64,256]{2,1,0:T(8,128)(2,1)S(1)}, u32[]{:S(2)}, u32[]{:S(2)}) %collective-permute-start.4) | collective-permute-done | bytes 65568 | tf_op jit(solution)/shard_map/ppermute | solution.py:237
  23.9 0.1 finish1.1
  24.0 0.8 %collective-permute-start.7 = (s16[2,64,256]{2,1,0:T(8,128)(2,1)S(1)}, s16[2,64,256]{2,1,0:T(8,128)(2,1)S(1)}, u32[]{:S(2)}, u32[]{:S(2)}) collective-permute-start(s16[2,64,256]{2,1,0:T(8,128)(2,1)S(1)} %get-tuple-element.26), channel_id=1, source_target_pairs={{0,2},{1,3},{2,0},{3,1},{4,6},{5,7},{6,4},{7,5},{8,10},{9,11},{10,... | collective-permute-start | bytes 196616 | tf_op jit(solution)/shard_map/ppermute | solution.py:237
  24.8 0.6 %collective-permute-start.6 = (s16[2,64,256]{2,1,0:T(8,128)(2,1)S(1)}, s16[2,64,256]{2,1,0:T(8,128)(2,1)S(1)}, u32[]{:S(2)}, u32[]{:S(2)}) collective-permute-start(s16[2,64,256]{2,1,0:T(8,128)(2,1)S(1)} %get-tuple-element.26), channel_id=1, source_target_pairs={{0,4},{1,5},{2,6},{3,7},{4,0},{5,1},{6,2},{7,3},{8,12},{9,13},{10,... | collective-permute-start | bytes 196616 | tf_op jit(solution)/shard_map/ppermute | solution.py:237
  25.3 2.2 %collective-permute-start.5 = (s16[2,64,256]{2,1,0:T(8,128)(2,1)S(1)}, s16[2,64,256]{2,1,0:T(8,128)(2,1)S(1)}, u32[]{:S(2)}, u32[]{:S(2)}) collective-permute-start(s16[2,64,256]{2,1,0:T(8,128)(2,1)S(1)} %get-tuple-element.26), channel_id=1, source_target_pairs={{0,6},{1,7},{2,4},{3,5},{4,2},{5,3},{6,0},{7,1},{8,14},{9,15},{10,... | collective-permute-start | bytes 196616 | tf_op jit(solution)/shard_map/ppermute | solution.py:237
  27.6 0.0 collective-permute-done.13.there
  27.6 0.1 finish0.1
  27.7 0.8 %collective-permute-start.16 = (s16[2,64,256]{2,1,0:T(8,128)(2,1)S(1)}, s16[2,64,256]{2,1,0:T(8,128)(2,1)S(1)}, u32[]{:S(2)}, u32[]{:S(2)}) collective-permute-start(s16[2,64,256]{2,1,0:T(8,128)(2,1)S(1)} %get-tuple-element.32), channel_id=1, source_target_pairs={{0,2},{1,3},{2,0},{3,1},{4,6},{5,7},{6,4},{7,5},{8,10},{9,11},{10,... | collective-permute-start | bytes 196616 | tf_op jit(solution)/shard_map/ppermute | solution.py:237
  28.5 0.9 %collective-permute-start.14 = (s16[2,64,256]{2,1,0:T(8,128)(2,1)S(1)}, s16[2,64,256]{2,1,0:T(8,128)(2,1)S(1)}, u32[]{:S(2)}, u32[]{:S(2)}) collective-permute-start(s16[2,64,256]{2,1,0:T(8,128)(2,1)S(1)} %get-tuple-element.32), channel_id=1, source_target_pairs={{0,6},{1,7},{2,4},{3,5},{4,2},{5,3},{6,0},{7,1},{8,14},{9,15},{10,... | collective-permute-start | bytes 196616 | tf_op jit(solution)/shard_map/ppermute | solution.py:237
  29.4 4.3 %collective-permute-done.14 = s16[2,64,256]{2,1,0:T(8,128)(2,1)S(1)} collective-permute-done((s16[2,64,256]{2,1,0:T(8,128)(2,1)S(1)}, s16[2,64,256]{2,1,0:T(8,128)(2,1)S(1)}, u32[]{:S(2)}, u32[]{:S(2)}) %collective-permute-start.14) | collective-permute-done | bytes 65568 | tf_op jit(solution)/shard_map/ppermute | solution.py:237
  33.7 0.5 %collective-permute-start.15 = (s16[2,64,256]{2,1,0:T(8,128)(2,1)S(1)}, s16[2,64,256]{2,1,0:T(8,128)(2,1)S(1)}, u32[]{:S(2)}, u32[]{:S(2)}) collective-permute-start(s16[2,64,256]{2,1,0:T(8,128)(2,1)S(1)} %get-tuple-element.32), channel_id=1, source_target_pairs={{0,4},{1,5},{2,6},{3,7},{4,0},{5,1},{6,2},{7,3},{8,12},{9,13},{10,... | collective-permute-start | bytes 196616 | tf_op jit(solution)/shard_map/ppermute | solution.py:237
  34.2 3.8 %collective-permute-done.15 = s16[2,64,256]{2,1,0:T(8,128)(2,1)S(1)} collective-permute-done((s16[2,64,256]{2,1,0:T(8,128)(2,1)S(1)}, s16[2,64,256]{2,1,0:T(8,128)(2,1)S(1)}, u32[]{:S(2)}, u32[]{:S(2)}) %collective-permute-start.15) | collective-permute-done | bytes 65568 | tf_op jit(solution)/shard_map/ppermute | solution.py:237
  38.0 0.0 collective-permute-done.16
  38.0 0.1 collective-permute-start.17
  38.1 0.0 collective-permute-done.5
  38.1 0.0 collective-permute-done.6
  38.1 0.0 collective-permute-done.7
  38.1 0.5 %collective-permute-start.8 = (s16[8,64,256]{2,1,0:T(8,128)(2,1)S(1)}, s16[8,64,256]{2,1,0:T(8,128)(2,1)S(1)}, u32[]{:S(2)}, u32[]{:S(2)}) collective-permute-start(s16[8,64,256]{2,1,0:T(8,128)(2,1)S(1)} %constant_dynamic-update-slice_fusion.near), channel_id=1, source_target_pairs={{0,1},{1,0},{2,3},{3,2},{4,5},{5,4},{6,7},{7,6},{8,9},{9,8},{10,11... | collective-permute-start | bytes 786440 | tf_op jit(solution)/shard_map/ppermute | solution.py:237
  38.7 0.9 %collective-permute-done.17.far = s16[8,64,256]{2,1,0:T(8,128)(2,1)S(1)} collective-permute-done((s16[8,64,256]{2,1,0:T(8,128)(2,1)S(1)}, s16[8,64,256]{2,1,0:T(8,128)(2,1)S(1)}, u32[]{:S(2)}, u32[]{:S(2)}) %collective-permute-start.17) | collective-permute-done | bytes 262176 | tf_op jit(solution)/shard_map/ppermute | solution.py:237
  39.6 2.2 %scores0.1 = (bf16[64,256]{1,0:T(8,128)(2,1)S(1)}, f32[12,128]{1,0:T(8,128)S(1)}, f32[12,128]{1,0:T(8,128)S(1)}) custom-call(s32[12]{0:T(128)S(1)} %copy-done.2, s32[12,128]{1,0:T(8,128)S(1)} %bitcast.28, f32[64,256]{1,0:T(8,128)S(1)} %get-tuple-element.31.own, bf16[1536,1024]{1,0:T(8,128)(2,1)S(1)} %get-tuple-element.20.points, ...), custom_call_target="tpu_custom_call" | custom-call | flops 805306368 | bytes 3145728 | tf_op jit(solution)/shard_map/scores0/pallas_call | solution.py:312
  41.8 0.0 collective-permute-done.8.far
  41.8 2.8 %scores1.1 = (bf16[128,256]{1,0:T(8,128)(2,1)}, f32[12,128]{1,0:T(8,128)}) custom-call(s32[12]{0:T(128)S(1)} %copy-done.2, s32[12,128]{1,0:T(8,128)S(1)} %bitcast.29, f32[64,256]{1,0:T(8,128)S(1)} %get-tuple-element.25.own, bf16[1536,1024]{1,0:T(8,128)(2,1)S(1)} %get-tuple-element.20.points, s16[8,64,256]{2,1,0:T(8,128)(2,1)S(1)} %constant_dynamic-update-slice_fusion.near, ...), custom_call_target="tpu_custom_call" | custom-call | flops 805306368 | bytes 3145728 | tf_op jit(solution)/shard_map/scores1/pallas_call | solution.py:312
  (8 shorter events, 0.0 us)
Async XLA Ops:
  0.6 4.4 %copy-start.2 = (s32[12]{0:T(128)S(1)}, s32[12]{0:T(128)}, u32[]{:S(2)}) copy-start(s32[12]{0:T(128)} %bids.5) | copy-start | bytes 148
  0.6 4.4 %copy-start = (s32[1536]{0:T(1024)S(1)}, s32[1536]{0:T(1024)}, u32[]{:S(2)}) copy-start(s32[1536]{0:T(1024)} %param.7) | copy-start | bytes 18436
  0.7 4.4 %copy-start.1 = (bf16[128,256]{1,0:T(8,128)(2,1)S(1)}, bf16[128,256]{1,0:T(8,128)(2,1)}, u32[]{:S(2)}) copy-start(bf16[128,256]{1,0:T(8,128)(2,1)} %old.1) | copy-start | bytes 196612
  4.5 2.1 %collective-permute-start = (f32[4,2,64,256]{3,2,1,0:T(8,128)S(1)}, f32[4,2,64,256]{3,2,1,0:T(8,128)S(1)}, u32[]{:S(2)}, u32[]{:S(2)}) collective-permute-start(f32[4,2,64,256]{3,2,1,0:T(8,128)S(1)} %get-tuple-element.22), channel_id=1, source_target_pairs={{0,1},{1,0},{2,3},{3,2},{4,5},{5,4},{6,7},{7,6},{8,9},{9,8},{10,11... | collective-permute-start | bytes 1572872 | tf_op jit(solution)/shard_map/ppermute | solution.py:237
  5.0 6.3 %collective-permute-start.9 = (f32[4,2,64,256]{3,2,1,0:T(8,128)S(1)}, f32[4,2,64,256]{3,2,1,0:T(8,128)S(1)}, u32[]{:S(2)}, u32[]{:S(2)}) collective-permute-start(f32[4,2,64,256]{3,2,1,0:T(8,128)S(1)} %get-tuple-element.28), channel_id=1, source_target_pairs={{0,1},{1,0},{2,3},{3,2},{4,5},{5,4},{6,7},{7,6},{8,9},{9,8},{10,11... | collective-permute-start | bytes 1572872 | tf_op jit(solution)/shard_map/ppermute | solution.py:237
  6.7 8.3 %collective-permute-start.3 = (s16[2,64,256]{2,1,0:T(8,128)(2,1)S(1)}, s16[2,64,256]{2,1,0:T(8,128)(2,1)S(1)}, u32[]{:S(2)}, u32[]{:S(2)}) collective-permute-start(s16[2,64,256]{2,1,0:T(8,128)(2,1)S(1)} %get-tuple-element.41), channel_id=1, source_target_pairs={{0,2},{1,3},{2,0},{3,1},{4,6},{5,7},{6,4},{7,5},{8,10},{9,11},{10,... | collective-permute-start | bytes 196616 | tf_op jit(solution)/shard_map/ppermute | solution.py:237
  9.6 5.4 %collective-permute-start.2 = (s16[2,64,256]{2,1,0:T(8,128)(2,1)S(1)}, s16[2,64,256]{2,1,0:T(8,128)(2,1)S(1)}, u32[]{:S(2)}, u32[]{:S(2)}) collective-permute-start(s16[2,64,256]{2,1,0:T(8,128)(2,1)S(1)} %get-tuple-element.42), channel_id=1, source_target_pairs={{0,4},{1,5},{2,6},{3,7},{4,0},{5,1},{6,2},{7,3},{8,12},{9,13},{10,... | collective-permute-start | bytes 196616 | tf_op jit(solution)/shard_map/ppermute | solution.py:237
  11.2 5.3 %collective-permute-start.1 = (s16[2,64,256]{2,1,0:T(8,128)(2,1)S(1)}, s16[2,64,256]{2,1,0:T(8,128)(2,1)S(1)}, u32[]{:S(2)}, u32[]{:S(2)}) collective-permute-start(s16[2,64,256]{2,1,0:T(8,128)(2,1)S(1)} %get-tuple-element.43), channel_id=1, source_target_pairs={{0,6},{1,7},{2,4},{3,5},{4,2},{5,3},{6,0},{7,1},{8,14},{9,15},{10,... | collective-permute-start | bytes 196616 | tf_op jit(solution)/shard_map/ppermute | solution.py:237
  11.4 7.9 %collective-permute-start.12 = (s16[2,64,256]{2,1,0:T(8,128)(2,1)S(1)}, s16[2,64,256]{2,1,0:T(8,128)(2,1)S(1)}, u32[]{:S(2)}, u32[]{:S(2)}) collective-permute-start(s16[2,64,256]{2,1,0:T(8,128)(2,1)S(1)} %get-tuple-element.38), channel_id=1, source_target_pairs={{0,2},{1,3},{2,0},{3,1},{4,6},{5,7},{6,4},{7,5},{8,10},{9,11},{10,... | collective-permute-start | bytes 196616 | tf_op jit(solution)/shard_map/ppermute | solution.py:237
  13.4 5.9 %collective-permute-start.11 = (s16[2,64,256]{2,1,0:T(8,128)(2,1)S(1)}, s16[2,64,256]{2,1,0:T(8,128)(2,1)S(1)}, u32[]{:S(2)}, u32[]{:S(2)}) collective-permute-start(s16[2,64,256]{2,1,0:T(8,128)(2,1)S(1)} %get-tuple-element.39), channel_id=1, source_target_pairs={{0,4},{1,5},{2,6},{3,7},{4,0},{5,1},{6,2},{7,3},{8,12},{9,13},{10,... | collective-permute-start | bytes 196616 | tf_op jit(solution)/shard_map/ppermute | solution.py:237
  15.0 5.6 %collective-permute-start.10 = (s16[2,64,256]{2,1,0:T(8,128)(2,1)S(1)}, s16[2,64,256]{2,1,0:T(8,128)(2,1)S(1)}, u32[]{:S(2)}, u32[]{:S(2)}) collective-permute-start(s16[2,64,256]{2,1,0:T(8,128)(2,1)S(1)} %get-tuple-element.40), channel_id=1, source_target_pairs={{0,6},{1,7},{2,4},{3,5},{4,2},{5,3},{6,0},{7,1},{8,14},{9,15},{10,... | collective-permute-start | bytes 196616 | tf_op jit(solution)/shard_map/ppermute | solution.py:237
  16.7 7.2 %collective-permute-start.4 = (s16[2,64,256]{2,1,0:T(8,128)(2,1)S(1)}, s16[2,64,256]{2,1,0:T(8,128)(2,1)S(1)}, u32[]{:S(2)}, u32[]{:S(2)}) collective-permute-start(s16[2,64,256]{2,1,0:T(8,128)(2,1)S(1)} %get-tuple-element.24), channel_id=1, source_target_pairs={{0,8},{1,9},{2,10},{3,11},{4,12},{5,13},{6,14},{7,15},{8,0},{9,1},... | collective-permute-start | bytes 196616 | tf_op jit(solution)/shard_map/ppermute | solution.py:237
  20.8 6.8 %collective-permute-start.13 = (s16[2,64,256]{2,1,0:T(8,128)(2,1)S(1)}, s16[2,64,256]{2,1,0:T(8,128)(2,1)S(1)}, u32[]{:S(2)}, u32[]{:S(2)}) collective-permute-start(s16[2,64,256]{2,1,0:T(8,128)(2,1)S(1)} %get-tuple-element.30), channel_id=1, source_target_pairs={{0,8},{1,9},{2,10},{3,11},{4,12},{5,13},{6,14},{7,15},{8,0},{9,1},... | collective-permute-start | bytes 196616 | tf_op jit(solution)/shard_map/ppermute | solution.py:237
  24.0 14.1 %collective-permute-start.7 = (s16[2,64,256]{2,1,0:T(8,128)(2,1)S(1)}, s16[2,64,256]{2,1,0:T(8,128)(2,1)S(1)}, u32[]{:S(2)}, u32[]{:S(2)}) collective-permute-start(s16[2,64,256]{2,1,0:T(8,128)(2,1)S(1)} %get-tuple-element.26), channel_id=1, source_target_pairs={{0,2},{1,3},{2,0},{3,1},{4,6},{5,7},{6,4},{7,5},{8,10},{9,11},{10,... | collective-permute-start | bytes 196616 | tf_op jit(solution)/shard_map/ppermute | solution.py:237
  24.8 13.3 %collective-permute-start.6 = (s16[2,64,256]{2,1,0:T(8,128)(2,1)S(1)}, s16[2,64,256]{2,1,0:T(8,128)(2,1)S(1)}, u32[]{:S(2)}, u32[]{:S(2)}) collective-permute-start(s16[2,64,256]{2,1,0:T(8,128)(2,1)S(1)} %get-tuple-element.26), channel_id=1, source_target_pairs={{0,4},{1,5},{2,6},{3,7},{4,0},{5,1},{6,2},{7,3},{8,12},{9,13},{10,... | collective-permute-start | bytes 196616 | tf_op jit(solution)/shard_map/ppermute | solution.py:237
  25.3 12.7 %collective-permute-start.5 = (s16[2,64,256]{2,1,0:T(8,128)(2,1)S(1)}, s16[2,64,256]{2,1,0:T(8,128)(2,1)S(1)}, u32[]{:S(2)}, u32[]{:S(2)}) collective-permute-start(s16[2,64,256]{2,1,0:T(8,128)(2,1)S(1)} %get-tuple-element.26), channel_id=1, source_target_pairs={{0,6},{1,7},{2,4},{3,5},{4,2},{5,3},{6,0},{7,1},{8,14},{9,15},{10,... | collective-permute-start | bytes 196616 | tf_op jit(solution)/shard_map/ppermute | solution.py:237
  27.7 10.3 %collective-permute-start.16 = (s16[2,64,256]{2,1,0:T(8,128)(2,1)S(1)}, s16[2,64,256]{2,1,0:T(8,128)(2,1)S(1)}, u32[]{:S(2)}, u32[]{:S(2)}) collective-permute-start(s16[2,64,256]{2,1,0:T(8,128)(2,1)S(1)} %get-tuple-element.32), channel_id=1, source_target_pairs={{0,2},{1,3},{2,0},{3,1},{4,6},{5,7},{6,4},{7,5},{8,10},{9,11},{10,... | collective-permute-start | bytes 196616 | tf_op jit(solution)/shard_map/ppermute | solution.py:237
  28.5 5.2 %collective-permute-start.14 = (s16[2,64,256]{2,1,0:T(8,128)(2,1)S(1)}, s16[2,64,256]{2,1,0:T(8,128)(2,1)S(1)}, u32[]{:S(2)}, u32[]{:S(2)}) collective-permute-start(s16[2,64,256]{2,1,0:T(8,128)(2,1)S(1)} %get-tuple-element.32), channel_id=1, source_target_pairs={{0,6},{1,7},{2,4},{3,5},{4,2},{5,3},{6,0},{7,1},{8,14},{9,15},{10,... | collective-permute-start | bytes 196616 | tf_op jit(solution)/shard_map/ppermute | solution.py:237
  33.7 4.3 %collective-permute-start.15 = (s16[2,64,256]{2,1,0:T(8,128)(2,1)S(1)}, s16[2,64,256]{2,1,0:T(8,128)(2,1)S(1)}, u32[]{:S(2)}, u32[]{:S(2)}) collective-permute-start(s16[2,64,256]{2,1,0:T(8,128)(2,1)S(1)} %get-tuple-element.32), channel_id=1, source_target_pairs={{0,4},{1,5},{2,6},{3,7},{4,0},{5,1},{6,2},{7,3},{8,12},{9,13},{10,... | collective-permute-start | bytes 196616 | tf_op jit(solution)/shard_map/ppermute | solution.py:237
  38.0 1.6 %collective-permute-start.17 = (s16[8,64,256]{2,1,0:T(8,128)(2,1)S(1)}, s16[8,64,256]{2,1,0:T(8,128)(2,1)S(1)}, u32[]{:S(2)}, u32[]{:S(2)}) collective-permute-start(s16[8,64,256]{2,1,0:T(8,128)(2,1)S(1)} %constant_dynamic-update-slice_fusion.4.near), channel_id=1, source_target_pairs={{0,1},{1,0},{2,3},{3,2},{4,5},{5,4},{6,7},{7,6},{8,9},{9,8},{10,11... | collective-permute-start | bytes 786440 | tf_op jit(solution)/shard_map/ppermute | solution.py:237
  38.1 3.6 %collective-permute-start.8 = (s16[8,64,256]{2,1,0:T(8,128)(2,1)S(1)}, s16[8,64,256]{2,1,0:T(8,128)(2,1)S(1)}, u32[]{:S(2)}, u32[]{:S(2)}) collective-permute-start(s16[8,64,256]{2,1,0:T(8,128)(2,1)S(1)} %constant_dynamic-update-slice_fusion.near), channel_id=1, source_target_pairs={{0,1},{1,0},{2,3},{3,2},{4,5},{5,4},{6,7},{7,6},{8,9},{9,8},{10,11... | collective-permute-start | bytes 786440 | tf_op jit(solution)/shard_map/ppermute | solution.py:237

commit v8 on v7

--- a/solution.py
+++ b/solution.py
@@ -272,26 +272,28 @@
     piece = (late, half_rows, width)
     two = (2, half_rows, width)
 
-    def reduce_near(half):
-        terms = []
-        for index, (over_sub, over_shard) in list(enumerate(chips))[1:]:
-            terms.append(swap(encode(keep[half][index] + crossed[half][index], rate), over_sub, over_shard))
-        return terms
-
-    def reduce_late(half, terms):
+    def after(value, *others):
+        return lax.optimization_barrier((value, *others))[0] if others else value
+
+    def reduce_near(half, *earlier):
+        there = after(crossed[half], *earlier)
+        codes = [encode(keep[half][index] + there[index], rate) for index in range(1, len(chips))]
+        return codes, [swap(code, *chip) for code, chip in zip(codes, chips[1:])]
+
+    def reduce_late(half, terms, *earlier):
         mine, code = pl.pallas_call(
             functools.partial(mix_kernel, rate=rate),
             out_shape=(jax.ShapeDtypeStruct(piece, jnp.float32), jax.ShapeDtypeStruct(piece, jnp.int16)),
             compiler_params=limit,
             name=f"mix{half}",
-        )(keep[half], crossed[half], *terms)
+        )(after(keep[half], *earlier), crossed[half], *terms)
         for bit in bits[:-1]:
             count = mine.shape[0] // 2
             mine = mine[:count] + decode(swap(encode(mine[count:], rate), 0, bit), rate)
             code = encode(mine, rate)
         return mine, swap(code, 0, bits[-1])
 
-    def gather(half, mine, there):
+    def finish(half, mine, there, *earlier):
         own, code = pl.pallas_call(
             functools.partial(finish_kernel, rate=rate),
             out_shape=(
@@ -300,11 +302,20 @@
             ),
             compiler_params=limit,
             name=f"finish{half}",
-        )(mine, there)
+        )(after(mine, *earlier), there)
         for bit in reversed(bits[:-1]):
             code = jnp.concatenate([code, swap(code, 0, bit)])
-        near = jnp.concatenate([code] + [swap(code, over_sub, over_shard) for over_sub, over_shard in chips[1:]])
-        return own, near
+        return own, code
+
+    def gather_near(codes):
+        near = [[code] for code in codes]
+        for half in range(2):
+            for index, chip in enumerate(chips[1:]):
+                code = codes[half]
+                if half and index == len(chips) - 2:
+                    code = after(code, near[0][1])
+                near[half].append(swap(code, *chip))
+        return [jnp.concatenate(blocks) for blocks in near]
 
     def scores(half, own, near, far, *earlier):
         line = jax.ShapeDtypeStruct((blocks, SLOT), jnp.float32)
@@ -334,12 +345,17 @@
             name=f"scores{half}",
         )(block_ids, slots, own, held, near, far, *earlier)
 
-    terms = [reduce_near(half) for half in range(2)]
-    pairs = [reduce_late(half, terms[half]) for half in range(2)]
-    gathered = [gather(half, *pairs[half]) for half in range(2)]
-    far = [swap(near, 1, 0) for _, near in gathered]
-    fresh, mine, rival = scores(0, *gathered[0], far[0])
-    fresh, margin = scores(1, *gathered[1], far[1], mine, rival, fresh)
+    first_codes, first_terms = reduce_near(0)
+    _, second_terms = reduce_near(1, *first_codes)
+    first = reduce_late(0, first_terms)
+    second = reduce_late(1, second_terms, first[0])
+    first_own, first_code = finish(0, *first)
+    second_own, second_code = finish(1, *second, first_code)
+    own, codes = (first_own, second_own), (first_code, second_code)
+    near = gather_near(codes)
+    fresh, mine, rival = scores(0, own[0], near[0], swap(near[0], 1, 0))
+    far = swap(near[1], 1, 0)
+    fresh, margin = scores(1, own[1], near[1], far, mine, rival, fresh)
     return fresh, margin.reshape(row_count)
 
 

time: 44.7 us -> 40.1 us (0.90)
  waiting for transfers between devices: 12.7 us -> 7.67 us
    ppermute x18, waiting for transfers between devices: 12.7 us -> 7.67 us  [swap(): return lax.ppermute(value, ('shard', 'sub'), pairs)]
  transfers between devices with their start and end apart: 18 -> 18, of which waited for: 7 -> 7; matrix products, arithmetic and copies ran while one was open for 1% -> 1% of each run, Pallas kernels for 9% -> 10%
where the time goes in v8:
time: 40.1 us; the launch traced here: 39.9 us
  starting transfers between devices  20.3 us (51%)
  Pallas kernels  9.93 us (25%)
  waiting for transfers between devices  7.67 us (19%)
  between operations  1.46 us (4%)
  other arithmetic  0.41 us (1%)
    ppermute x18, starting transfers between devices, swap(): return lax.ppermute(value, ('shard', 'sub'), pairs)  20.3 us
    ppermute x18, waiting for transfers between devices, swap(): return lax.ppermute(value, ('shard', 'sub'), pairs)  7.67 us
    pallas_call x2, Pallas kernels, scores(): pl.pallas_call(functools.partial(score_kernel, half=half, blocks=blocks,...  4.95 us
    pallas_call x1, Pallas kernels, local(): pl.pallas_call(functools.partial(send_kernel, group=group, **sizes), out_...  3.12 us
    pallas_call x1, Pallas kernels, local(): pl.pallas_call(functools.partial(keep_kernel, **sizes), out_shape=(shape,...  1.29 us
  transfers between devices with their start and end apart: 18, of which 7 were waited for; matrix products, arithmetic and copies ran while one was open for 1% of the time, Pallas kernels for 10%

profile of v8, /device:TPU:0, one launch (start us, length us, event | category | flops | bytes accessed | tf_op | source)
XLA Modules:
  0.0 39.9 jit_solution(6902729165722034877)
XLA Ops:
  0.6 0.0 copy-start.2
  0.6 0.0 copy-start
  0.7 0.0 copy-start.1
  1.3 3.1 %sums_send.1 = (f32[4,2,64,256]{3,2,1,0:T(8,128)S(1)}, f32[4,2,64,256]{3,2,1,0:T(8,128)S(1)}, bf16[1536,1024]{1,0:T(8,128)(2,1)S(1)}) custom-call(s32[1]{0:T(128)S(6)} %copy.13.live_in.live, s32[12]{0:T(128)} %bids.5, s32[12,128]{1,0:T(8,128)} %bitcast.26, bf16[1536,1024]{1,0:T(8,128)(2,1)} %points.1), custom_call_target="tpu_custom_call" | custom-call | flops 201326592 | bytes 1572864 | tf_op jit(solution)/shard_map/sums_send/pallas_call | solution.py:245
  4.5 0.5 %collective-permute-start = (f32[4,2,64,256]{3,2,1,0:T(8,128)S(1)}, f32[4,2,64,256]{3,2,1,0:T(8,128)S(1)}, u32[]{:S(2)}, u32[]{:S(2)}) collective-permute-start(f32[4,2,64,256]{3,2,1,0:T(8,128)S(1)} %get-tuple-element.27), channel_id=1, source_target_pairs={{0,1},{1,0},{2,3},{3,2},{4,5},{5,4},{6,7},{7,6},{8,9},{9,8},{10,11... | collective-permute-start | bytes 1572872 | tf_op jit(solution)/shard_map/ppermute | solution.py:237
  5.0 0.1 collective-permute-start.4
  5.1 0.0 copy-done.2
  5.1 0.0 copy-done
  5.1 0.0 copy-done.1
  5.1 1.3 %sums_keep.1 = (f32[4,2,64,256]{3,2,1,0:T(8,128)S(1)}, f32[4,2,64,256]{3,2,1,0:T(8,128)S(1)}) custom-call(s32[1]{0:T(128)S(6)} %copy.13.live_in.live, s32[12]{0:T(128)S(1)} %copy-done.2, s32[12,128]{1,0:T(8,128)S(1)} %bitcast.27, bf16[128,256]{1,0:T(8,128)(2,1)S(1)} %copy-done.1, bf16[1536,1024]{1,0:T(8,128)(2,1)S(1)} %get-tuple-element.24.points), custom_call_target="tpu_custom_call" | custom-call | flops 201326592 | bytes 1572864 | tf_op jit(solution)/shard_map/sums_keep/pallas_call | solution.py:262
  6.4 0.2 collective-permute-done.crossed
  6.5 0.2 fusion.5
  6.7 2.9 %collective-permute-start.3 = (s16[2,64,256]{2,1,0:T(8,128)(2,1)S(1)}, s16[2,64,256]{2,1,0:T(8,128)(2,1)S(1)}, u32[]{:S(2)}, u32[]{:S(2)}) collective-permute-start(s16[2,64,256]{2,1,0:T(8,128)(2,1)S(1)} %get-tuple-element.49), channel_id=1, source_target_pairs={{0,2},{1,3},{2,0},{3,1},{4,6},{5,7},{6,4},{7,5},{8,10},{9,11},{10,... | collective-permute-start | bytes 196616 | tf_op jit(solution)/shard_map/ppermute | solution.py:237
  9.6 1.6 %collective-permute-start.2 = (s16[2,64,256]{2,1,0:T(8,128)(2,1)S(1)}, s16[2,64,256]{2,1,0:T(8,128)(2,1)S(1)}, u32[]{:S(2)}, u32[]{:S(2)}) collective-permute-start(s16[2,64,256]{2,1,0:T(8,128)(2,1)S(1)} %get-tuple-element.50), channel_id=1, source_target_pairs={{0,4},{1,5},{2,6},{3,7},{4,0},{5,1},{6,2},{7,3},{8,12},{9,13},{10,... | collective-permute-start | bytes 196616 | tf_op jit(solution)/shard_map/ppermute | solution.py:237
  11.2 0.0 collective-permute-start.1
  11.2 0.0 collective-permute-done.4.crossed
  11.2 0.2 fusion.11
  11.4 2.0 %collective-permute-start.7 = (s16[2,64,256]{2,1,0:T(8,128)(2,1)S(1)}, s16[2,64,256]{2,1,0:T(8,128)(2,1)S(1)}, u32[]{:S(2)}, u32[]{:S(2)}) collective-permute-start(s16[2,64,256]{2,1,0:T(8,128)(2,1)S(1)} %get-tuple-element.46), channel_id=1, source_target_pairs={{0,2},{1,3},{2,0},{3,1},{4,6},{5,7},{6,4},{7,5},{8,10},{9,11},{10,... | collective-permute-start | bytes 196616 | tf_op jit(solution)/shard_map/ppermute | solution.py:237
  13.4 1.6 %collective-permute-start.6 = (s16[2,64,256]{2,1,0:T(8,128)(2,1)S(1)}, s16[2,64,256]{2,1,0:T(8,128)(2,1)S(1)}, u32[]{:S(2)}, u32[]{:S(2)}) collective-permute-start(s16[2,64,256]{2,1,0:T(8,128)(2,1)S(1)} %get-tuple-element.47), channel_id=1, source_target_pairs={{0,4},{1,5},{2,6},{3,7},{4,0},{5,1},{6,2},{7,3},{8,12},{9,13},{10,... | collective-permute-start | bytes 196616 | tf_op jit(solution)/shard_map/ppermute | solution.py:237
  15.0 0.0 collective-permute-done.3.refs_2_
  15.0 0.0 collective-permute-start.5
  15.0 0.0 collective-permute-done.2.refs_1_
  15.0 1.5 %collective-permute-done.1.refs_0_ = s16[2,64,256]{2,1,0:T(8,128)(2,1)S(1)} collective-permute-done((s16[2,64,256]{2,1,0:T(8,128)(2,1)S(1)}, s16[2,64,256]{2,1,0:T(8,128)(2,1)S(1)}, u32[]{:S(2)}, u32[]{:S(2)}) %collective-permute-start.1) | collective-permute-done | bytes 65568 | tf_op jit(solution)/shard_map/ppermute | solution.py:237
  16.5 0.2 mix0.1
  16.7 2.7 %collective-permute-start.8 = (s16[2,64,256]{2,1,0:T(8,128)(2,1)S(1)}, s16[2,64,256]{2,1,0:T(8,128)(2,1)S(1)}, u32[]{:S(2)}, u32[]{:S(2)}) collective-permute-start(s16[2,64,256]{2,1,0:T(8,128)(2,1)S(1)} %get-tuple-element.33), channel_id=1, source_target_pairs={{0,8},{1,9},{2,10},{3,11},{4,12},{5,13},{6,14},{7,15},{8,0},{9,1},... | collective-permute-start | bytes 196616 | tf_op jit(solution)/shard_map/ppermute | solution.py:237
  19.4 0.0 collective-permute-done.7.refs_2_
  19.4 0.0 collective-permute-done.6.refs_1_
  19.4 1.2 %collective-permute-done.5.refs_0_ = s16[2,64,256]{2,1,0:T(8,128)(2,1)S(1)} collective-permute-done((s16[2,64,256]{2,1,0:T(8,128)(2,1)S(1)}, s16[2,64,256]{2,1,0:T(8,128)(2,1)S(1)}, u32[]{:S(2)}, u32[]{:S(2)}) %collective-permute-start.5) | collective-permute-done | bytes 65568 | tf_op jit(solution)/shard_map/ppermute | solution.py:237
  20.6 0.2 mix1.1
  20.8 2.3 %collective-permute-start.9 = (s16[2,64,256]{2,1,0:T(8,128)(2,1)S(1)}, s16[2,64,256]{2,1,0:T(8,128)(2,1)S(1)}, u32[]{:S(2)}, u32[]{:S(2)}) collective-permute-start(s16[2,64,256]{2,1,0:T(8,128)(2,1)S(1)} %get-tuple-element.36), channel_id=1, source_target_pairs={{0,8},{1,9},{2,10},{3,11},{4,12},{5,13},{6,14},{7,15},{8,0},{9,1},... | collective-permute-start | bytes 196616 | tf_op jit(solution)/shard_map/ppermute | solution.py:237
  23.1 0.8 %collective-permute-done.8.there = s16[2,64,256]{2,1,0:T(8,128)(2,1)S(1)} collective-permute-done((s16[2,64,256]{2,1,0:T(8,128)(2,1)S(1)}, s16[2,64,256]{2,1,0:T(8,128)(2,1)S(1)}, u32[]{:S(2)}, u32[]{:S(2)}) %collective-permute-start.8) | collective-permute-done | bytes 65568 | tf_op jit(solution)/shard_map/ppermute | solution.py:237
  23.9 0.1 finish0.1
  24.0 0.8 %collective-permute-start.16 = (s16[2,64,256]{2,1,0:T(8,128)(2,1)S(1)}, s16[2,64,256]{2,1,0:T(8,128)(2,1)S(1)}, u32[]{:S(2)}, u32[]{:S(2)}) collective-permute-start(s16[2,64,256]{2,1,0:T(8,128)(2,1)S(1)} %get-tuple-element.34), channel_id=1, source_target_pairs={{0,2},{1,3},{2,0},{3,1},{4,6},{5,7},{6,4},{7,5},{8,10},{9,11},{10,... | collective-permute-start | bytes 196616 | tf_op jit(solution)/shard_map/ppermute | solution.py:237
  24.8 0.6 %collective-permute-start.15 = (s16[2,64,256]{2,1,0:T(8,128)(2,1)S(1)}, s16[2,64,256]{2,1,0:T(8,128)(2,1)S(1)}, u32[]{:S(2)}, u32[]{:S(2)}) collective-permute-start(s16[2,64,256]{2,1,0:T(8,128)(2,1)S(1)} %get-tuple-element.34), channel_id=1, source_target_pairs={{0,4},{1,5},{2,6},{3,7},{4,0},{5,1},{6,2},{7,3},{8,12},{9,13},{10,... | collective-permute-start | bytes 196616 | tf_op jit(solution)/shard_map/ppermute | solution.py:237
  25.4 2.2 %collective-permute-start.12 = (s16[2,64,256]{2,1,0:T(8,128)(2,1)S(1)}, s16[2,64,256]{2,1,0:T(8,128)(2,1)S(1)}, u32[]{:S(2)}, u32[]{:S(2)}) collective-permute-start(s16[2,64,256]{2,1,0:T(8,128)(2,1)S(1)} %get-tuple-element.34), channel_id=1, source_target_pairs={{0,6},{1,7},{2,4},{3,5},{4,2},{5,3},{6,0},{7,1},{8,14},{9,15},{10,... | collective-permute-start | bytes 196616 | tf_op jit(solution)/shard_map/ppermute | solution.py:237
  27.6 0.0 collective-permute-done.9.there
  27.6 0.1 finish1.1
  27.7 0.3 collective-permute-start.11
  27.9 2.0 %collective-permute-start.10 = (s16[2,64,256]{2,1,0:T(8,128)(2,1)S(1)}, s16[2,64,256]{2,1,0:T(8,128)(2,1)S(1)}, u32[]{:S(2)}, u32[]{:S(2)}) collective-permute-start(s16[2,64,256]{2,1,0:T(8,128)(2,1)S(1)} %get-tuple-element.39), channel_id=1, source_target_pairs={{0,6},{1,7},{2,4},{3,5},{4,2},{5,3},{6,0},{7,1},{8,14},{9,15},{10,... | collective-permute-start | bytes 196616 | tf_op jit(solution)/shard_map/ppermute | solution.py:237
  29.9 0.7 %collective-permute-done.12 = s16[2,64,256]{2,1,0:T(8,128)(2,1)S(1)} collective-permute-done((s16[2,64,256]{2,1,0:T(8,128)(2,1)S(1)}, s16[2,64,256]{2,1,0:T(8,128)(2,1)S(1)}, u32[]{:S(2)}, u32[]{:S(2)}) %collective-permute-start.12) | collective-permute-done | bytes 65568 | tf_op jit(solution)/shard_map/ppermute | solution.py:237
  30.6 0.8 %collective-permute-start.13 = (s16[2,64,256]{2,1,0:T(8,128)(2,1)S(1)}, s16[2,64,256]{2,1,0:T(8,128)(2,1)S(1)}, u32[]{:S(2)}, u32[]{:S(2)}) collective-permute-start(s16[2,64,256]{2,1,0:T(8,128)(2,1)S(1)} %get-tuple-element.39), channel_id=1, source_target_pairs={{0,2},{1,3},{2,0},{3,1},{4,6},{5,7},{6,4},{7,5},{8,10},{9,11},{10,... | collective-permute-start | bytes 196616 | tf_op jit(solution)/shard_map/ppermute | solution.py:237
  31.5 0.0 collective-permute-done.15
  31.5 0.0 collective-permute-done.16
  31.5 0.1 collective-permute-start.17
  31.6 1.5 %collective-permute-done.10 = s16[2,64,256]{2,1,0:T(8,128)(2,1)S(1)} collective-permute-done((s16[2,64,256]{2,1,0:T(8,128)(2,1)S(1)}, s16[2,64,256]{2,1,0:T(8,128)(2,1)S(1)}, u32[]{:S(2)}, u32[]{:S(2)}) %collective-permute-start.10) | collective-permute-done | bytes 65568 | tf_op jit(solution)/shard_map/ppermute | solution.py:237
  33.1 0.0 collective-permute-done.11
  33.1 1.8 %collective-permute-done.13 = s16[2,64,256]{2,1,0:T(8,128)(2,1)S(1)} collective-permute-done((s16[2,64,256]{2,1,0:T(8,128)(2,1)S(1)}, s16[2,64,256]{2,1,0:T(8,128)(2,1)S(1)}, u32[]{:S(2)}, u32[]{:S(2)}) %collective-permute-start.13) | collective-permute-done | bytes 65568 | tf_op jit(solution)/shard_map/ppermute | solution.py:237
  34.9 0.0 collective-permute-start.14
  34.9 0.0 collective-permute-done.17.far
  34.9 2.2 %scores0.1 = (bf16[64,256]{1,0:T(8,128)(2,1)S(1)}, f32[12,128]{1,0:T(8,128)S(1)}, f32[12,128]{1,0:T(8,128)S(1)}) custom-call(s32[12]{0:T(128)S(1)} %copy-done.2, s32[12,128]{1,0:T(8,128)S(1)} %bitcast.28, f32[64,256]{1,0:T(8,128)S(1)} %get-tuple-element.40.own, bf16[1536,1024]{1,0:T(8,128)(2,1)S(1)} %get-tuple-element.24.points, ...), custom_call_target="tpu_custom_call" | custom-call | flops 805306368 | bytes 3145728 | tf_op jit(solution)/shard_map/scores0/pallas_call | solution.py:323
  37.1 0.0 collective-permute-done.14.far
  37.1 2.8 %scores1.1 = (bf16[128,256]{1,0:T(8,128)(2,1)}, f32[12,128]{1,0:T(8,128)}) custom-call(s32[12]{0:T(128)S(1)} %copy-done.2, s32[12,128]{1,0:T(8,128)S(1)} %bitcast.29, f32[64,256]{1,0:T(8,128)S(1)} %get-tuple-element.37.own, bf16[1536,1024]{1,0:T(8,128)(2,1)S(1)} %get-tuple-element.24.points, s16[8,64,256]{2,1,0:T(8,128)(2,1)S(1)} %constant_dynamic-update-slice_fusion.near, ...), custom_call_target="tpu_custom_call" | custom-call | flops 805306368 | bytes 3145728 | tf_op jit(solution)/shard_map/scores1/pallas_call | solution.py:323
  (8 shorter events, 0.0 us)
Async XLA Ops:
  0.6 4.4 %copy-start.2 = (s32[12]{0:T(128)S(1)}, s32[12]{0:T(128)}, u32[]{:S(2)}) copy-start(s32[12]{0:T(128)} %bids.5) | copy-start | bytes 148
  0.6 4.4 %copy-start = (s32[1536]{0:T(1024)S(1)}, s32[1536]{0:T(1024)}, u32[]{:S(2)}) copy-start(s32[1536]{0:T(1024)} %param.7) | copy-start | bytes 18436
  0.7 4.4 %copy-start.1 = (bf16[128,256]{1,0:T(8,128)(2,1)S(1)}, bf16[128,256]{1,0:T(8,128)(2,1)}, u32[]{:S(2)}) copy-start(bf16[128,256]{1,0:T(8,128)(2,1)} %old.1) | copy-start | bytes 196612
  4.5 2.0 %collective-permute-start = (f32[4,2,64,256]{3,2,1,0:T(8,128)S(1)}, f32[4,2,64,256]{3,2,1,0:T(8,128)S(1)}, u32[]{:S(2)}, u32[]{:S(2)}) collective-permute-start(f32[4,2,64,256]{3,2,1,0:T(8,128)S(1)} %get-tuple-element.27), channel_id=1, source_target_pairs={{0,1},{1,0},{2,3},{3,2},{4,5},{5,4},{6,7},{7,6},{8,9},{9,8},{10,11... | collective-permute-start | bytes 1572872 | tf_op jit(solution)/shard_map/ppermute | solution.py:237
  5.0 6.3 %collective-permute-start.4 = (f32[4,2,64,256]{3,2,1,0:T(8,128)S(1)}, f32[4,2,64,256]{3,2,1,0:T(8,128)S(1)}, u32[]{:S(2)}, u32[]{:S(2)}) collective-permute-start(f32[4,2,64,256]{3,2,1,0:T(8,128)S(1)} %get-tuple-element.30), channel_id=1, source_target_pairs={{0,1},{1,0},{2,3},{3,2},{4,5},{5,4},{6,7},{7,6},{8,9},{9,8},{10,11... | collective-permute-start | bytes 1572872 | tf_op jit(solution)/shard_map/ppermute | solution.py:237
  6.7 8.3 %collective-permute-start.3 = (s16[2,64,256]{2,1,0:T(8,128)(2,1)S(1)}, s16[2,64,256]{2,1,0:T(8,128)(2,1)S(1)}, u32[]{:S(2)}, u32[]{:S(2)}) collective-permute-start(s16[2,64,256]{2,1,0:T(8,128)(2,1)S(1)} %get-tuple-element.49), channel_id=1, source_target_pairs={{0,2},{1,3},{2,0},{3,1},{4,6},{5,7},{6,4},{7,5},{8,10},{9,11},{10,... | collective-permute-start | bytes 196616 | tf_op jit(solution)/shard_map/ppermute | solution.py:237
  9.6 5.4 %collective-permute-start.2 = (s16[2,64,256]{2,1,0:T(8,128)(2,1)S(1)}, s16[2,64,256]{2,1,0:T(8,128)(2,1)S(1)}, u32[]{:S(2)}, u32[]{:S(2)}) collective-permute-start(s16[2,64,256]{2,1,0:T(8,128)(2,1)S(1)} %get-tuple-element.50), channel_id=1, source_target_pairs={{0,4},{1,5},{2,6},{3,7},{4,0},{5,1},{6,2},{7,3},{8,12},{9,13},{10,... | collective-permute-start | bytes 196616 | tf_op jit(solution)/shard_map/ppermute | solution.py:237
  11.2 5.3 %collective-permute-start.1 = (s16[2,64,256]{2,1,0:T(8,128)(2,1)S(1)}, s16[2,64,256]{2,1,0:T(8,128)(2,1)S(1)}, u32[]{:S(2)}, u32[]{:S(2)}) collective-permute-start(s16[2,64,256]{2,1,0:T(8,128)(2,1)S(1)} %get-tuple-element.51), channel_id=1, source_target_pairs={{0,6},{1,7},{2,4},{3,5},{4,2},{5,3},{6,0},{7,1},{8,14},{9,15},{10,... | collective-permute-start | bytes 196616 | tf_op jit(solution)/shard_map/ppermute | solution.py:237
  11.4 7.9 %collective-permute-start.7 = (s16[2,64,256]{2,1,0:T(8,128)(2,1)S(1)}, s16[2,64,256]{2,1,0:T(8,128)(2,1)S(1)}, u32[]{:S(2)}, u32[]{:S(2)}) collective-permute-start(s16[2,64,256]{2,1,0:T(8,128)(2,1)S(1)} %get-tuple-element.46), channel_id=1, source_target_pairs={{0,2},{1,3},{2,0},{3,1},{4,6},{5,7},{6,4},{7,5},{8,10},{9,11},{10,... | collective-permute-start | bytes 196616 | tf_op jit(solution)/shard_map/ppermute | solution.py:237
  13.4 5.9 %collective-permute-start.6 = (s16[2,64,256]{2,1,0:T(8,128)(2,1)S(1)}, s16[2,64,256]{2,1,0:T(8,128)(2,1)S(1)}, u32[]{:S(2)}, u32[]{:S(2)}) collective-permute-start(s16[2,64,256]{2,1,0:T(8,128)(2,1)S(1)} %get-tuple-element.47), channel_id=1, source_target_pairs={{0,4},{1,5},{2,6},{3,7},{4,0},{5,1},{6,2},{7,3},{8,12},{9,13},{10,... | collective-permute-start | bytes 196616 | tf_op jit(solution)/shard_map/ppermute | solution.py:237
  15.0 5.6 %collective-permute-start.5 = (s16[2,64,256]{2,1,0:T(8,128)(2,1)S(1)}, s16[2,64,256]{2,1,0:T(8,128)(2,1)S(1)}, u32[]{:S(2)}, u32[]{:S(2)}) collective-permute-start(s16[2,64,256]{2,1,0:T(8,128)(2,1)S(1)} %get-tuple-element.48), channel_id=1, source_target_pairs={{0,6},{1,7},{2,4},{3,5},{4,2},{5,3},{6,0},{7,1},{8,14},{9,15},{10,... | collective-permute-start | bytes 196616 | tf_op jit(solution)/shard_map/ppermute | solution.py:237
  16.7 7.2 %collective-permute-start.8 = (s16[2,64,256]{2,1,0:T(8,128)(2,1)S(1)}, s16[2,64,256]{2,1,0:T(8,128)(2,1)S(1)}, u32[]{:S(2)}, u32[]{:S(2)}) collective-permute-start(s16[2,64,256]{2,1,0:T(8,128)(2,1)S(1)} %get-tuple-element.33), channel_id=1, source_target_pairs={{0,8},{1,9},{2,10},{3,11},{4,12},{5,13},{6,14},{7,15},{8,0},{9,1},... | collective-permute-start | bytes 196616 | tf_op jit(solution)/shard_map/ppermute | solution.py:237
  20.8 6.8 %collective-permute-start.9 = (s16[2,64,256]{2,1,0:T(8,128)(2,1)S(1)}, s16[2,64,256]{2,1,0:T(8,128)(2,1)S(1)}, u32[]{:S(2)}, u32[]{:S(2)}) collective-permute-start(s16[2,64,256]{2,1,0:T(8,128)(2,1)S(1)} %get-tuple-element.36), channel_id=1, source_target_pairs={{0,8},{1,9},{2,10},{3,11},{4,12},{5,13},{6,14},{7,15},{8,0},{9,1},... | collective-permute-start | bytes 196616 | tf_op jit(solution)/shard_map/ppermute | solution.py:237
  24.0 7.5 %collective-permute-start.16 = (s16[2,64,256]{2,1,0:T(8,128)(2,1)S(1)}, s16[2,64,256]{2,1,0:T(8,128)(2,1)S(1)}, u32[]{:S(2)}, u32[]{:S(2)}) collective-permute-start(s16[2,64,256]{2,1,0:T(8,128)(2,1)S(1)} %get-tuple-element.34), channel_id=1, source_target_pairs={{0,2},{1,3},{2,0},{3,1},{4,6},{5,7},{6,4},{7,5},{8,10},{9,11},{10,... | collective-permute-start | bytes 196616 | tf_op jit(solution)/shard_map/ppermute | solution.py:237
  24.8 6.7 %collective-permute-start.15 = (s16[2,64,256]{2,1,0:T(8,128)(2,1)S(1)}, s16[2,64,256]{2,1,0:T(8,128)(2,1)S(1)}, u32[]{:S(2)}, u32[]{:S(2)}) collective-permute-start(s16[2,64,256]{2,1,0:T(8,128)(2,1)S(1)} %get-tuple-element.34), channel_id=1, source_target_pairs={{0,4},{1,5},{2,6},{3,7},{4,0},{5,1},{6,2},{7,3},{8,12},{9,13},{10,... | collective-permute-start | bytes 196616 | tf_op jit(solution)/shard_map/ppermute | solution.py:237
  25.4 5.3 %collective-permute-start.12 = (s16[2,64,256]{2,1,0:T(8,128)(2,1)S(1)}, s16[2,64,256]{2,1,0:T(8,128)(2,1)S(1)}, u32[]{:S(2)}, u32[]{:S(2)}) collective-permute-start(s16[2,64,256]{2,1,0:T(8,128)(2,1)S(1)} %get-tuple-element.34), channel_id=1, source_target_pairs={{0,6},{1,7},{2,4},{3,5},{4,2},{5,3},{6,0},{7,1},{8,14},{9,15},{10,... | collective-permute-start | bytes 196616 | tf_op jit(solution)/shard_map/ppermute | solution.py:237
  27.7 5.4 %collective-permute-start.11 = (s16[2,64,256]{2,1,0:T(8,128)(2,1)S(1)}, s16[2,64,256]{2,1,0:T(8,128)(2,1)S(1)}, u32[]{:S(2)}, u32[]{:S(2)}) collective-permute-start(s16[2,64,256]{2,1,0:T(8,128)(2,1)S(1)} %get-tuple-element.39), channel_id=1, source_target_pairs={{0,4},{1,5},{2,6},{3,7},{4,0},{5,1},{6,2},{7,3},{8,12},{9,13},{10,... | collective-permute-start | bytes 196616 | tf_op jit(solution)/shard_map/ppermute | solution.py:237
  27.9 5.2 %collective-permute-start.10 = (s16[2,64,256]{2,1,0:T(8,128)(2,1)S(1)}, s16[2,64,256]{2,1,0:T(8,128)(2,1)S(1)}, u32[]{:S(2)}, u32[]{:S(2)}) collective-permute-start(s16[2,64,256]{2,1,0:T(8,128)(2,1)S(1)} %get-tuple-element.39), channel_id=1, source_target_pairs={{0,6},{1,7},{2,4},{3,5},{4,2},{5,3},{6,0},{7,1},{8,14},{9,15},{10,... | collective-permute-start | bytes 196616 | tf_op jit(solution)/shard_map/ppermute | solution.py:237
  30.6 4.3 %collective-permute-start.13 = (s16[2,64,256]{2,1,0:T(8,128)(2,1)S(1)}, s16[2,64,256]{2,1,0:T(8,128)(2,1)S(1)}, u32[]{:S(2)}, u32[]{:S(2)}) collective-permute-start(s16[2,64,256]{2,1,0:T(8,128)(2,1)S(1)} %get-tuple-element.39), channel_id=1, source_target_pairs={{0,2},{1,3},{2,0},{3,1},{4,6},{5,7},{6,4},{7,5},{8,10},{9,11},{10,... | collective-permute-start | bytes 196616 | tf_op jit(solution)/shard_map/ppermute | solution.py:237
  31.5 3.4 %collective-permute-start.17 = (s16[8,64,256]{2,1,0:T(8,128)(2,1)S(1)}, s16[8,64,256]{2,1,0:T(8,128)(2,1)S(1)}, u32[]{:S(2)}, u32[]{:S(2)}) collective-permute-start(s16[8,64,256]{2,1,0:T(8,128)(2,1)S(1)} %constant_dynamic-update-slice_fusion.4.near), channel_id=1, source_target_pairs={{0,1},{1,0},{2,3},{3,2},{4,5},{5,4},{6,7},{7,6},{8,9},{9,8},{10,11... | collective-permute-start | bytes 786440 | tf_op jit(solution)/shard_map/ppermute | solution.py:237
  34.9 2.2 %collective-permute-start.14 = (s16[8,64,256]{2,1,0:T(8,128)(2,1)S(1)}, s16[8,64,256]{2,1,0:T(8,128)(2,1)S(1)}, u32[]{:S(2)}, u32[]{:S(2)}) collective-permute-start(s16[8,64,256]{2,1,0:T(8,128)(2,1)S(1)} %constant_dynamic-update-slice_fusion.near), channel_id=1, source_target_pairs={{0,1},{1,0},{2,3},{3,2},{4,5},{5,4},{6,7},{7,6},{8,9},{9,8},{10,11... | collective-permute-start | bytes 786440 | tf_op jit(solution)/shard_map/ppermute | solution.py:237

commit v9 on v8

--- a/solution.py
+++ b/solution.py
@@ -43,7 +43,7 @@
     for bit in bits_of(subs)[1:]:
         group = group + [(sub ^ bit, shard) for sub, shard in group]
     group = group + [(sub, shard ^ 1) for sub, shard in group]
-    return group[:1] + group[:0:-1]
+    return group
 
 
 def late_bits(shards):
@@ -89,7 +89,7 @@
     for first in range(0, blocks, group):
         span = pl.ds(first * SLOT, group * SLOT)
         copies.append(pltpu.make_async_copy(points.at[span], held.at[span], arrived.at[first // group]))
-        copies[-1].start()
+        copies[-1].start(priority=(first // group) % 2)
     for sums in (first_half, second_half):
         sums[...] = jnp.zeros_like(sums)
     for copy in firsts:
@@ -148,13 +148,7 @@
     code[1] = encode(mine[1] + decode(there[0], rate), rate)
 
 
-def score_kernel(
-    bids, slots, own, points, near, far, *refs, half, blocks, shards, subs, rows, width, rate, group
-):
-    if half:
-        (mine_in, rival_in, fresh_in), (fresh, margin, cents) = refs[:3], refs[3:]
-    else:
-        fresh, mine_out, rival_out, cents = refs
+def rows_kernel(own, near, far, fresh, cents, *, half, shards, subs, rows, width, rate):
     chips = near_group(subs, shards)
     sub, shard = lax.axis_index("sub"), lax.axis_index("shard")
     bits = late_bits(shards)
@@ -172,13 +166,17 @@
         for place, part in parts:
             cents[row, pl.ds(pl.multiple_of(place * width, width), width)] = (part * scale).astype(jnp.bfloat16)
         if over_shard == 0:
-            updated = (own[...] * scale).astype(jnp.bfloat16)
-            if half:
-                fresh[:half_rows] = fresh_in[...]
-                fresh[half_rows:] = updated
-            else:
-                fresh[...] = updated
-
+            fresh[...] = (own[...] * scale).astype(jnp.bfloat16)
+
+
+def score_kernel(bids, slots, points, cents, *refs, half, blocks, shards, rows, group):
+    if half:
+        mine_in, rival_in, fresh_first, fresh_second, fresh, margin = refs
+        fresh[: rows // 2] = fresh_first[...]
+        fresh[rows // 2 :] = fresh_second[...]
+    else:
+        mine_out, rival_out = refs
+    half_rows = rows // 2
     lanes = 8
     row_of = lax.broadcasted_iota(jnp.int32, (half_rows, SLOT), 0)
     for block in range(blocks // group):
@@ -308,42 +306,41 @@
         return own, code
 
     def gather_near(codes):
-        near = [[code] for code in codes]
-        for half in range(2):
-            for index, chip in enumerate(chips[1:]):
-                code = codes[half]
-                if half and index == len(chips) - 2:
-                    code = after(code, near[0][1])
-                near[half].append(swap(code, *chip))
-        return [jnp.concatenate(blocks) for blocks in near]
-
-    def scores(half, own, near, far, *earlier):
-        line = jax.ShapeDtypeStruct((blocks, SLOT), jnp.float32)
-        fresh = jax.ShapeDtypeStruct((rows if half else half_rows, width), jnp.bfloat16)
+        first = jnp.concatenate([codes[0]] + [swap(codes[0], *chip) for chip in chips[1:]])
+        ready = [after(codes[1], first)] + [codes[1]] * (len(chips) - 2)
+        return first, jnp.concatenate([codes[1]] + [swap(code, *chip) for code, chip in zip(ready, chips[1:])])
+
+    def rows_of(half, own, near, far):
         return pl.pallas_call(
             functools.partial(
-                score_kernel,
-                half=half,
-                blocks=blocks,
-                shards=shards,
-                subs=subs,
-                rows=rows,
-                width=width,
-                rate=rate,
-                group=group,
-            ),
-            out_shape=(fresh, line) if half else (fresh, line, line),
-            in_specs=[smem] + [vmem] * (5 + len(earlier)),
-            out_specs=(vmem,) * (2 if half else 3),
-            scratch_shapes=[pltpu.VMEM((total // 2, feat_width), jnp.bfloat16)],
-            compiler_params=pltpu.CompilerParams(vmem_limit_bytes=12 * MIB + 6 * total * feat_width),
+                rows_kernel, half=half, shards=shards, subs=subs, rows=rows, width=width, rate=rate
+            ),
+            out_shape=(
+                jax.ShapeDtypeStruct((half_rows, width), jnp.bfloat16),
+                jax.ShapeDtypeStruct((total // 2, feat_width), jnp.bfloat16),
+            ),
+            compiler_params=limit,
+            name=f"rows{half}",
+        )(own, near, far)
+
+    def scores(half, cents, *earlier):
+        line = jax.ShapeDtypeStruct((blocks, SLOT), jnp.float32)
+        fresh = jax.ShapeDtypeStruct((rows, width), jnp.bfloat16)
+        return pl.pallas_call(
+            functools.partial(
+                score_kernel, half=half, blocks=blocks, shards=shards, rows=rows, group=group
+            ),
+            out_shape=(fresh, line) if half else (line, line),
+            in_specs=[smem] + [vmem] * (3 + len(earlier)),
+            out_specs=(vmem, vmem),
+            compiler_params=limit,
             cost_estimate=pl.CostEstimate(
                 flops=row_count * total * feat_width,
                 bytes_accessed=2 * row_count * feat_width,
-                transcendentals=total * feat_width // 2,
+                transcendentals=0,
             ),
             name=f"scores{half}",
-        )(block_ids, slots, own, held, near, far, *earlier)
+        )(block_ids, slots, held, cents, *earlier)
 
     first_codes, first_terms = reduce_near(0)
     _, second_terms = reduce_near(1, *first_codes)
@@ -353,9 +350,11 @@
     second_own, second_code = finish(1, *second, first_code)
     own, codes = (first_own, second_own), (first_code, second_code)
     near = gather_near(codes)
-    fresh, mine, rival = scores(0, own[0], near[0], swap(near[0], 1, 0))
-    far = swap(near[1], 1, 0)
-    fresh, margin = scores(1, own[1], near[1], far, mine, rival, fresh)
+    far = [swap(block, 1, 0) for block in near]
+    first_fresh, first_rows = rows_of(0, own[0], near[0], far[0])
+    mine, rival = scores(0, first_rows)
+    second_fresh, second_rows = rows_of(1, own[1], near[1], far[1])
+    fresh, margin = scores(1, second_rows, mine, rival, first_fresh, second_fresh)
     return fresh, margin.reshape(row_count)
 
 

time: 40.1 us -> 38.7 us (0.965)
  waiting for transfers between devices: 7.67 us -> 5.1 us
  starting transfers between devices: 20.3 us -> 21.7 us
  Pallas kernels: 9.93 us -> 9.51 us
    ppermute x18, waiting for transfers between devices: 7.67 us -> 5.1 us  [swap(): return lax.ppermute(value, ('shard', 'sub'), pairs)]
    ppermute x18, starting transfers between devices: 20.3 us -> 21.7 us  [swap(): return lax.ppermute(value, ('shard', 'sub'), pairs)]
    pallas_call x2, Pallas kernels: 4.95 us -> 3.94 us  [scores(): pl.pallas_call(functools.partial(score_kernel, half=half, blocks=blocks,...]
    pallas_call x0 -> x2, Pallas kernels: none -> 0.95 us  [rows_of(): pl.pallas_call(functools.partial(rows_kernel, half=half, shards=shards, s...]
where the time goes in v9:
time: 38.7 us; the launch traced here: 38.3 us
  starting transfers between devices  21.7 us (56%)
  Pallas kernels  9.51 us (25%)
  waiting for transfers between devices  5.1 us (13%)
  between operations  1.49 us (4%)
  other arithmetic  0.41 us (1%)
    ppermute x18, starting transfers between devices, swap(): return lax.ppermute(value, ('shard', 'sub'), pairs)  21.7 us
    ppermute x18, waiting for transfers between devices, swap(): return lax.ppermute(value, ('shard', 'sub'), pairs)  5.1 us
    pallas_call x2, Pallas kernels, scores(): pl.pallas_call(functools.partial(score_kernel, half=half, blocks=blocks,...  3.94 us
    pallas_call x1, Pallas kernels, local(): pl.pallas_call(functools.partial(send_kernel, group=group, **sizes), out_...  2.75 us
    pallas_call x1, Pallas kernels, local(): pl.pallas_call(functools.partial(keep_kernel, **sizes), out_shape=(shape,...  1.29 us
    pallas_call x2, Pallas kernels, rows_of(): pl.pallas_call(functools.partial(rows_kernel, half=half, shards=shards, s...  0.95 us
  transfers between devices with their start and end apart: 18, of which 7 were waited for; matrix products, arithmetic and copies ran while one was open for 1% of the time, Pallas kernels for 10%

profile of v9, /device:TPU:0, one launch (start us, length us, event | category | flops | bytes accessed | tf_op | source)
XLA Modules:
  0.0 38.3 jit_solution(6643381857413512064)
XLA Ops:
  0.6 0.0 copy-start.2
  0.6 0.0 copy-start
  0.7 0.0 copy-start.1
  1.3 2.7 %sums_send.1 = (f32[4,2,64,256]{3,2,1,0:T(8,128)S(1)}, f32[4,2,64,256]{3,2,1,0:T(8,128)S(1)}, bf16[1536,1024]{1,0:T(8,128)(2,1)S(1)}) custom-call(s32[1]{0:T(128)S(6)} %copy.13.live_in.live, s32[12]{0:T(128)} %bids.5, s32[12,128]{1,0:T(8,128)} %bitcast.26, bf16[1536,1024]{1,0:T(8,128)(2,1)} %points.1), custom_call_target="tpu_custom_call" | custom-call | flops 201326592 | bytes 1572864 | tf_op jit(solution)/shard_map/sums_send/pallas_call | solution.py:243
  4.1 0.5 %collective-permute-start = (f32[4,2,64,256]{3,2,1,0:T(8,128)S(1)}, f32[4,2,64,256]{3,2,1,0:T(8,128)S(1)}, u32[]{:S(2)}, u32[]{:S(2)}) collective-permute-start(f32[4,2,64,256]{3,2,1,0:T(8,128)S(1)} %get-tuple-element.30), channel_id=1, source_target_pairs={{0,1},{1,0},{2,3},{3,2},{4,5},{5,4},{6,7},{7,6},{8,9},{9,8},{10,11... | collective-permute-start | bytes 1572872 | tf_op jit(solution)/shard_map/ppermute | solution.py:235
  4.6 0.1 collective-permute-start.4
  4.7 0.0 copy-done.2
  4.7 0.0 copy-done
  4.7 0.0 copy-done.1
  4.7 1.3 %sums_keep.1 = (f32[4,2,64,256]{3,2,1,0:T(8,128)S(1)}, f32[4,2,64,256]{3,2,1,0:T(8,128)S(1)}) custom-call(s32[1]{0:T(128)S(6)} %copy.13.live_in.live, s32[12]{0:T(128)S(1)} %copy-done.2, s32[12,128]{1,0:T(8,128)S(1)} %bitcast.27, bf16[128,256]{1,0:T(8,128)(2,1)S(1)} %copy-done.1, bf16[1536,1024]{1,0:T(8,128)(2,1)S(1)} %get-tuple-element.27.points), custom_call_target="tpu_custom_call" | custom-call | flops 201326592 | bytes 1572864 | tf_op jit(solution)/shard_map/sums_keep/pallas_call | solution.py:260
  6.0 0.2 collective-permute-done.crossed
  6.1 0.2 fusion.5
  6.3 3.9 %collective-permute-start.3 = (s16[2,64,256]{2,1,0:T(8,128)(2,1)S(1)}, s16[2,64,256]{2,1,0:T(8,128)(2,1)S(1)}, u32[]{:S(2)}, u32[]{:S(2)}) collective-permute-start(s16[2,64,256]{2,1,0:T(8,128)(2,1)S(1)} %get-tuple-element.55), channel_id=1, source_target_pairs={{0,6},{1,7},{2,4},{3,5},{4,2},{5,3},{6,0},{7,1},{8,14},{9,15},{10,... | collective-permute-start | bytes 196616 | tf_op jit(solution)/shard_map/ppermute | solution.py:235
  10.3 0.4 %collective-permute-start.2 = (s16[2,64,256]{2,1,0:T(8,128)(2,1)S(1)}, s16[2,64,256]{2,1,0:T(8,128)(2,1)S(1)}, u32[]{:S(2)}, u32[]{:S(2)}) collective-permute-start(s16[2,64,256]{2,1,0:T(8,128)(2,1)S(1)} %get-tuple-element.56), channel_id=1, source_target_pairs={{0,4},{1,5},{2,6},{3,7},{4,0},{5,1},{6,2},{7,3},{8,12},{9,13},{10,... | collective-permute-start | bytes 196616 | tf_op jit(solution)/shard_map/ppermute | solution.py:235
  10.7 0.2 collective-permute-start.1
  10.9 0.0 collective-permute-done.4.crossed
  10.9 0.2 fusion.11
  11.1 2.9 %collective-permute-start.7 = (s16[2,64,256]{2,1,0:T(8,128)(2,1)S(1)}, s16[2,64,256]{2,1,0:T(8,128)(2,1)S(1)}, u32[]{:S(2)}, u32[]{:S(2)}) collective-permute-start(s16[2,64,256]{2,1,0:T(8,128)(2,1)S(1)} %get-tuple-element.52), channel_id=1, source_target_pairs={{0,6},{1,7},{2,4},{3,5},{4,2},{5,3},{6,0},{7,1},{8,14},{9,15},{10,... | collective-permute-start | bytes 196616 | tf_op jit(solution)/shard_map/ppermute | solution.py:235
  14.1 0.4 %collective-permute-start.6 = (s16[2,64,256]{2,1,0:T(8,128)(2,1)S(1)}, s16[2,64,256]{2,1,0:T(8,128)(2,1)S(1)}, u32[]{:S(2)}, u32[]{:S(2)}) collective-permute-start(s16[2,64,256]{2,1,0:T(8,128)(2,1)S(1)} %get-tuple-element.53), channel_id=1, source_target_pairs={{0,4},{1,5},{2,6},{3,7},{4,0},{5,1},{6,2},{7,3},{8,12},{9,13},{10,... | collective-permute-start | bytes 196616 | tf_op jit(solution)/shard_map/ppermute | solution.py:235
  14.5 0.0 collective-permute-done.3.refs_2_
  14.5 0.2 collective-permute-start.5
  14.8 0.1 collective-permute-done.2.refs_1_
  14.8 0.9 %collective-permute-done.1.refs_0_ = s16[2,64,256]{2,1,0:T(8,128)(2,1)S(1)} collective-permute-done((s16[2,64,256]{2,1,0:T(8,128)(2,1)S(1)}, s16[2,64,256]{2,1,0:T(8,128)(2,1)S(1)}, u32[]{:S(2)}, u32[]{:S(2)}) %collective-permute-start.1) | collective-permute-done | bytes 65568 | tf_op jit(solution)/shard_map/ppermute | solution.py:235
  15.7 0.2 mix0.1
  15.9 2.7 %collective-permute-start.8 = (s16[2,64,256]{2,1,0:T(8,128)(2,1)S(1)}, s16[2,64,256]{2,1,0:T(8,128)(2,1)S(1)}, u32[]{:S(2)}, u32[]{:S(2)}) collective-permute-start(s16[2,64,256]{2,1,0:T(8,128)(2,1)S(1)} %get-tuple-element.36), channel_id=1, source_target_pairs={{0,8},{1,9},{2,10},{3,11},{4,12},{5,13},{6,14},{7,15},{8,0},{9,1},... | collective-permute-start | bytes 196616 | tf_op jit(solution)/shard_map/ppermute | solution.py:235
  18.6 0.0 collective-permute-done.7.refs_2_
  18.6 0.2 collective-permute-done.6.refs_1_
  18.7 0.1 collective-permute-done.5.refs_0_
  18.8 0.2 mix1.1
  19.0 2.7 %collective-permute-start.9 = (s16[2,64,256]{2,1,0:T(8,128)(2,1)S(1)}, s16[2,64,256]{2,1,0:T(8,128)(2,1)S(1)}, u32[]{:S(2)}, u32[]{:S(2)}) collective-permute-start(s16[2,64,256]{2,1,0:T(8,128)(2,1)S(1)} %get-tuple-element.39), channel_id=1, source_target_pairs={{0,8},{1,9},{2,10},{3,11},{4,12},{5,13},{6,14},{7,15},{8,0},{9,1},... | collective-permute-start | bytes 196616 | tf_op jit(solution)/shard_map/ppermute | solution.py:235
  21.6 0.0 collective-permute-done.8.there
  21.6 0.1 finish0.1
  21.7 2.3 %collective-permute-start.12 = (s16[2,64,256]{2,1,0:T(8,128)(2,1)S(1)}, s16[2,64,256]{2,1,0:T(8,128)(2,1)S(1)}, u32[]{:S(2)}, u32[]{:S(2)}) collective-permute-start(s16[2,64,256]{2,1,0:T(8,128)(2,1)S(1)} %get-tuple-element.37), channel_id=1, source_target_pairs={{0,6},{1,7},{2,4},{3,5},{4,2},{5,3},{6,0},{7,1},{8,14},{9,15},{10,... | collective-permute-start | bytes 196616 | tf_op jit(solution)/shard_map/ppermute | solution.py:235
  24.0 0.1 collective-permute-start.11
  24.1 1.4 %collective-permute-start.10 = (s16[2,64,256]{2,1,0:T(8,128)(2,1)S(1)}, s16[2,64,256]{2,1,0:T(8,128)(2,1)S(1)}, u32[]{:S(2)}, u32[]{:S(2)}) collective-permute-start(s16[2,64,256]{2,1,0:T(8,128)(2,1)S(1)} %get-tuple-element.37), channel_id=1, source_target_pairs={{0,2},{1,3},{2,0},{3,1},{4,6},{5,7},{6,4},{7,5},{8,10},{9,11},{10,... | collective-permute-start | bytes 196616 | tf_op jit(solution)/shard_map/ppermute | solution.py:235
  25.5 0.0 collective-permute-done.9.there
  25.5 0.1 finish1.1
  25.6 2.1 %collective-permute-start.15 = (s16[2,64,256]{2,1,0:T(8,128)(2,1)S(1)}, s16[2,64,256]{2,1,0:T(8,128)(2,1)S(1)}, u32[]{:S(2)}, u32[]{:S(2)}) collective-permute-start(s16[2,64,256]{2,1,0:T(8,128)(2,1)S(1)} %get-tuple-element.42), channel_id=1, source_target_pairs={{0,6},{1,7},{2,4},{3,5},{4,2},{5,3},{6,0},{7,1},{8,14},{9,15},{10,... | collective-permute-start | bytes 196616 | tf_op jit(solution)/shard_map/ppermute | solution.py:235
  27.7 0.1 collective-permute-start.14
  27.8 1.1 %collective-permute-done.10 = s16[2,64,256]{2,1,0:T(8,128)(2,1)S(1)} collective-permute-done((s16[2,64,256]{2,1,0:T(8,128)(2,1)S(1)}, s16[2,64,256]{2,1,0:T(8,128)(2,1)S(1)}, u32[]{:S(2)}, u32[]{:S(2)}) %collective-permute-start.10) | collective-permute-done | bytes 65568 | tf_op jit(solution)/shard_map/ppermute | solution.py:235
  28.8 0.0 collective-permute-done.11
  28.9 0.0 collective-permute-done.12
  28.9 1.6 %collective-permute-start.13 = (s16[2,64,256]{2,1,0:T(8,128)(2,1)S(1)}, s16[2,64,256]{2,1,0:T(8,128)(2,1)S(1)}, u32[]{:S(2)}, u32[]{:S(2)}) collective-permute-start(s16[2,64,256]{2,1,0:T(8,128)(2,1)S(1)} %get-tuple-element.42), channel_id=1, source_target_pairs={{0,2},{1,3},{2,0},{3,1},{4,6},{5,7},{6,4},{7,5},{8,10},{9,11},{10,... | collective-permute-start | bytes 196616 | tf_op jit(solution)/shard_map/ppermute | solution.py:235
  30.5 0.0 collective-permute-start.17
  30.5 2.7 %collective-permute-done.13 = s16[2,64,256]{2,1,0:T(8,128)(2,1)S(1)} collective-permute-done((s16[2,64,256]{2,1,0:T(8,128)(2,1)S(1)}, s16[2,64,256]{2,1,0:T(8,128)(2,1)S(1)}, u32[]{:S(2)}, u32[]{:S(2)}) %collective-permute-start.13) | collective-permute-done | bytes 65568 | tf_op jit(solution)/shard_map/ppermute | solution.py:235
  33.2 0.0 collective-permute-done.14
  33.2 0.0 collective-permute-done.15
  33.3 0.1 collective-permute-start.16
  33.3 0.0 collective-permute-done.17.far
  33.4 0.5 %rows0.1 = (bf16[64,256]{1,0:T(8,128)(2,1)S(1)}, bf16[256,1024]{1,0:T(8,128)(2,1)S(1)}) custom-call(f32[64,256]{1,0:T(8,128)S(1)} %get-tuple-element.44.own, s16[8,64,256]{2,1,0:T(8,128)(2,1)S(1)} %constant_dynamic-update-slice_fusion.near, s16[8,64,256]{2,1,0:T(8,128)(2,1)S(1)} %collective-permute-done.17.far), custom_call_target="tpu_custom_call" | custom-call | tf_op jit(solution)/shard_map/rows0/pallas_call | solution.py:314
  33.8 1.7 %scores0.1 = (f32[12,128]{1,0:T(8,128)S(1)}, f32[12,128]{1,0:T(8,128)S(1)}) custom-call(s32[12]{0:T(128)S(1)} %copy-done.2, s32[12,128]{1,0:T(8,128)S(1)} %bitcast.28, bf16[1536,1024]{1,0:T(8,128)(2,1)S(1)} %get-tuple-element.27.points, bf16[256,1024]{1,0:T(8,128)(2,1)S(1)} %get-tuple-element.45.cents), custom_call_target="tpu_custom_call" | custom-call | flops 805306368 | bytes 3145728 | tf_op jit(solution)/shard_map/scores0/pallas_call | solution.py:329
  35.5 0.0 collective-permute-done.16.far
  35.5 0.5 %rows1.1 = (bf16[64,256]{1,0:T(8,128)(2,1)S(1)}, bf16[256,1024]{1,0:T(8,128)(2,1)S(1)}) custom-call(f32[64,256]{1,0:T(8,128)S(1)} %get-tuple-element.40.own, s16[8,64,256]{2,1,0:T(8,128)(2,1)S(1)} %constant_dynamic-update-slice_fusion.4.near, s16[8,64,256]{2,1,0:T(8,128)(2,1)S(1)} %collective-permute-done.16.far), custom_call_target="tpu_custom_call" | custom-call | tf_op jit(solution)/shard_map/rows1/pallas_call | solution.py:314
  36.0 2.3 %scores1.1 = (bf16[128,256]{1,0:T(8,128)(2,1)}, f32[12,128]{1,0:T(8,128)}) custom-call(s32[12]{0:T(128)S(1)} %copy-done.2, s32[12,128]{1,0:T(8,128)S(1)} %bitcast.29, bf16[1536,1024]{1,0:T(8,128)(2,1)S(1)} %get-tuple-element.27.points, bf16[256,1024]{1,0:T(8,128)(2,1)S(1)} %get-tuple-element.43.cents, f32[12,128]{1,0:T(8,128)S(1)} %get-tuple-element.46.refs_0_, ...), custom_call_target="tpu_custom_call" | custom-call | flops 805306368 | bytes 3145728 | tf_op jit(solution)/shard_map/scores1/pallas_call | solution.py:329
  (8 shorter events, 0.0 us)
Async XLA Ops:
  0.6 4.1 %copy-start.2 = (s32[12]{0:T(128)S(1)}, s32[12]{0:T(128)}, u32[]{:S(2)}) copy-start(s32[12]{0:T(128)} %bids.5) | copy-start | bytes 148
  0.6 4.0 %copy-start = (s32[1536]{0:T(1024)S(1)}, s32[1536]{0:T(1024)}, u32[]{:S(2)}) copy-start(s32[1536]{0:T(1024)} %param.7) | copy-start | bytes 18436
  0.7 4.0 %copy-start.1 = (bf16[128,256]{1,0:T(8,128)(2,1)S(1)}, bf16[128,256]{1,0:T(8,128)(2,1)}, u32[]{:S(2)}) copy-start(bf16[128,256]{1,0:T(8,128)(2,1)} %old.1) | copy-start | bytes 196612
  4.1 2.0 %collective-permute-start = (f32[4,2,64,256]{3,2,1,0:T(8,128)S(1)}, f32[4,2,64,256]{3,2,1,0:T(8,128)S(1)}, u32[]{:S(2)}, u32[]{:S(2)}) collective-permute-start(f32[4,2,64,256]{3,2,1,0:T(8,128)S(1)} %get-tuple-element.30), channel_id=1, source_target_pairs={{0,1},{1,0},{2,3},{3,2},{4,5},{5,4},{6,7},{7,6},{8,9},{9,8},{10,11... | collective-permute-start | bytes 1572872 | tf_op jit(solution)/shard_map/ppermute | solution.py:235
  4.6 6.3 %collective-permute-start.4 = (f32[4,2,64,256]{3,2,1,0:T(8,128)S(1)}, f32[4,2,64,256]{3,2,1,0:T(8,128)S(1)}, u32[]{:S(2)}, u32[]{:S(2)}) collective-permute-start(f32[4,2,64,256]{3,2,1,0:T(8,128)S(1)} %get-tuple-element.33), channel_id=1, source_target_pairs={{0,1},{1,0},{2,3},{3,2},{4,5},{5,4},{6,7},{7,6},{8,9},{9,8},{10,11... | collective-permute-start | bytes 1572872 | tf_op jit(solution)/shard_map/ppermute | solution.py:235
  6.3 8.2 %collective-permute-start.3 = (s16[2,64,256]{2,1,0:T(8,128)(2,1)S(1)}, s16[2,64,256]{2,1,0:T(8,128)(2,1)S(1)}, u32[]{:S(2)}, u32[]{:S(2)}) collective-permute-start(s16[2,64,256]{2,1,0:T(8,128)(2,1)S(1)} %get-tuple-element.55), channel_id=1, source_target_pairs={{0,6},{1,7},{2,4},{3,5},{4,2},{5,3},{6,0},{7,1},{8,14},{9,15},{10,... | collective-permute-start | bytes 196616 | tf_op jit(solution)/shard_map/ppermute | solution.py:235
  10.3 4.5 %collective-permute-start.2 = (s16[2,64,256]{2,1,0:T(8,128)(2,1)S(1)}, s16[2,64,256]{2,1,0:T(8,128)(2,1)S(1)}, u32[]{:S(2)}, u32[]{:S(2)}) collective-permute-start(s16[2,64,256]{2,1,0:T(8,128)(2,1)S(1)} %get-tuple-element.56), channel_id=1, source_target_pairs={{0,4},{1,5},{2,6},{3,7},{4,0},{5,1},{6,2},{7,3},{8,12},{9,13},{10,... | collective-permute-start | bytes 196616 | tf_op jit(solution)/shard_map/ppermute | solution.py:235
  10.7 5.0 %collective-permute-start.1 = (s16[2,64,256]{2,1,0:T(8,128)(2,1)S(1)}, s16[2,64,256]{2,1,0:T(8,128)(2,1)S(1)}, u32[]{:S(2)}, u32[]{:S(2)}) collective-permute-start(s16[2,64,256]{2,1,0:T(8,128)(2,1)S(1)} %get-tuple-element.57), channel_id=1, source_target_pairs={{0,2},{1,3},{2,0},{3,1},{4,6},{5,7},{6,4},{7,5},{8,10},{9,11},{10,... | collective-permute-start | bytes 196616 | tf_op jit(solution)/shard_map/ppermute | solution.py:235
  11.1 7.4 %collective-permute-start.7 = (s16[2,64,256]{2,1,0:T(8,128)(2,1)S(1)}, s16[2,64,256]{2,1,0:T(8,128)(2,1)S(1)}, u32[]{:S(2)}, u32[]{:S(2)}) collective-permute-start(s16[2,64,256]{2,1,0:T(8,128)(2,1)S(1)} %get-tuple-element.52), channel_id=1, source_target_pairs={{0,6},{1,7},{2,4},{3,5},{4,2},{5,3},{6,0},{7,1},{8,14},{9,15},{10,... | collective-permute-start | bytes 196616 | tf_op jit(solution)/shard_map/ppermute | solution.py:235
  14.1 4.7 %collective-permute-start.6 = (s16[2,64,256]{2,1,0:T(8,128)(2,1)S(1)}, s16[2,64,256]{2,1,0:T(8,128)(2,1)S(1)}, u32[]{:S(2)}, u32[]{:S(2)}) collective-permute-start(s16[2,64,256]{2,1,0:T(8,128)(2,1)S(1)} %get-tuple-element.53), channel_id=1, source_target_pairs={{0,4},{1,5},{2,6},{3,7},{4,0},{5,1},{6,2},{7,3},{8,12},{9,13},{10,... | collective-permute-start | bytes 196616 | tf_op jit(solution)/shard_map/ppermute | solution.py:235
  14.5 4.3 %collective-permute-start.5 = (s16[2,64,256]{2,1,0:T(8,128)(2,1)S(1)}, s16[2,64,256]{2,1,0:T(8,128)(2,1)S(1)}, u32[]{:S(2)}, u32[]{:S(2)}) collective-permute-start(s16[2,64,256]{2,1,0:T(8,128)(2,1)S(1)} %get-tuple-element.54), channel_id=1, source_target_pairs={{0,2},{1,3},{2,0},{3,1},{4,6},{5,7},{6,4},{7,5},{8,10},{9,11},{10,... | collective-permute-start | bytes 196616 | tf_op jit(solution)/shard_map/ppermute | solution.py:235
  15.9 5.7 %collective-permute-start.8 = (s16[2,64,256]{2,1,0:T(8,128)(2,1)S(1)}, s16[2,64,256]{2,1,0:T(8,128)(2,1)S(1)}, u32[]{:S(2)}, u32[]{:S(2)}) collective-permute-start(s16[2,64,256]{2,1,0:T(8,128)(2,1)S(1)} %get-tuple-element.36), channel_id=1, source_target_pairs={{0,8},{1,9},{2,10},{3,11},{4,12},{5,13},{6,14},{7,15},{8,0},{9,1},... | collective-permute-start | bytes 196616 | tf_op jit(solution)/shard_map/ppermute | solution.py:235
  19.0 6.5 %collective-permute-start.9 = (s16[2,64,256]{2,1,0:T(8,128)(2,1)S(1)}, s16[2,64,256]{2,1,0:T(8,128)(2,1)S(1)}, u32[]{:S(2)}, u32[]{:S(2)}) collective-permute-start(s16[2,64,256]{2,1,0:T(8,128)(2,1)S(1)} %get-tuple-element.39), channel_id=1, source_target_pairs={{0,8},{1,9},{2,10},{3,11},{4,12},{5,13},{6,14},{7,15},{8,0},{9,1},... | collective-permute-start | bytes 196616 | tf_op jit(solution)/shard_map/ppermute | solution.py:235
  21.7 7.1 %collective-permute-start.12 = (s16[2,64,256]{2,1,0:T(8,128)(2,1)S(1)}, s16[2,64,256]{2,1,0:T(8,128)(2,1)S(1)}, u32[]{:S(2)}, u32[]{:S(2)}) collective-permute-start(s16[2,64,256]{2,1,0:T(8,128)(2,1)S(1)} %get-tuple-element.37), channel_id=1, source_target_pairs={{0,6},{1,7},{2,4},{3,5},{4,2},{5,3},{6,0},{7,1},{8,14},{9,15},{10,... | collective-permute-start | bytes 196616 | tf_op jit(solution)/shard_map/ppermute | solution.py:235
  24.0 4.8 %collective-permute-start.11 = (s16[2,64,256]{2,1,0:T(8,128)(2,1)S(1)}, s16[2,64,256]{2,1,0:T(8,128)(2,1)S(1)}, u32[]{:S(2)}, u32[]{:S(2)}) collective-permute-start(s16[2,64,256]{2,1,0:T(8,128)(2,1)S(1)} %get-tuple-element.37), channel_id=1, source_target_pairs={{0,4},{1,5},{2,6},{3,7},{4,0},{5,1},{6,2},{7,3},{8,12},{9,13},{10,... | collective-permute-start | bytes 196616 | tf_op jit(solution)/shard_map/ppermute | solution.py:235
  24.1 4.7 %collective-permute-start.10 = (s16[2,64,256]{2,1,0:T(8,128)(2,1)S(1)}, s16[2,64,256]{2,1,0:T(8,128)(2,1)S(1)}, u32[]{:S(2)}, u32[]{:S(2)}) collective-permute-start(s16[2,64,256]{2,1,0:T(8,128)(2,1)S(1)} %get-tuple-element.37), channel_id=1, source_target_pairs={{0,2},{1,3},{2,0},{3,1},{4,6},{5,7},{6,4},{7,5},{8,10},{9,11},{10,... | collective-permute-start | bytes 196616 | tf_op jit(solution)/shard_map/ppermute | solution.py:235
  25.6 7.7 %collective-permute-start.15 = (s16[2,64,256]{2,1,0:T(8,128)(2,1)S(1)}, s16[2,64,256]{2,1,0:T(8,128)(2,1)S(1)}, u32[]{:S(2)}, u32[]{:S(2)}) collective-permute-start(s16[2,64,256]{2,1,0:T(8,128)(2,1)S(1)} %get-tuple-element.42), channel_id=1, source_target_pairs={{0,6},{1,7},{2,4},{3,5},{4,2},{5,3},{6,0},{7,1},{8,14},{9,15},{10,... | collective-permute-start | bytes 196616 | tf_op jit(solution)/shard_map/ppermute | solution.py:235
  27.7 5.5 %collective-permute-start.14 = (s16[2,64,256]{2,1,0:T(8,128)(2,1)S(1)}, s16[2,64,256]{2,1,0:T(8,128)(2,1)S(1)}, u32[]{:S(2)}, u32[]{:S(2)}) collective-permute-start(s16[2,64,256]{2,1,0:T(8,128)(2,1)S(1)} %get-tuple-element.42), channel_id=1, source_target_pairs={{0,4},{1,5},{2,6},{3,7},{4,0},{5,1},{6,2},{7,3},{8,12},{9,13},{10,... | collective-permute-start | bytes 196616 | tf_op jit(solution)/shard_map/ppermute | solution.py:235
  28.9 4.3 %collective-permute-start.13 = (s16[2,64,256]{2,1,0:T(8,128)(2,1)S(1)}, s16[2,64,256]{2,1,0:T(8,128)(2,1)S(1)}, u32[]{:S(2)}, u32[]{:S(2)}) collective-permute-start(s16[2,64,256]{2,1,0:T(8,128)(2,1)S(1)} %get-tuple-element.42), channel_id=1, source_target_pairs={{0,2},{1,3},{2,0},{3,1},{4,6},{5,7},{6,4},{7,5},{8,10},{9,11},{10,... | collective-permute-start | bytes 196616 | tf_op jit(solution)/shard_map/ppermute | solution.py:235
  30.5 2.8 %collective-permute-start.17 = (s16[8,64,256]{2,1,0:T(8,128)(2,1)S(1)}, s16[8,64,256]{2,1,0:T(8,128)(2,1)S(1)}, u32[]{:S(2)}, u32[]{:S(2)}) collective-permute-start(s16[8,64,256]{2,1,0:T(8,128)(2,1)S(1)} %constant_dynamic-update-slice_fusion.near), channel_id=1, source_target_pairs={{0,1},{1,0},{2,3},{3,2},{4,5},{5,4},{6,7},{7,6},{8,9},{9,8},{10,11... | collective-permute-start | bytes 786440 | tf_op jit(solution)/shard_map/ppermute | solution.py:235
  33.3 2.2 %collective-permute-start.16 = (s16[8,64,256]{2,1,0:T(8,128)(2,1)S(1)}, s16[8,64,256]{2,1,0:T(8,128)(2,1)S(1)}, u32[]{:S(2)}, u32[]{:S(2)}) collective-permute-start(s16[8,64,256]{2,1,0:T(8,128)(2,1)S(1)} %constant_dynamic-update-slice_fusion.4.near), channel_id=1, source_target_pairs={{0,1},{1,0},{2,3},{3,2},{4,5},{5,4},{6,7},{7,6},{8,9},{9,8},{10,11... | collective-permute-start | bytes 786440 | tf_op jit(solution)/shard_map/ppermute | solution.py:235

commit v10 on v9

v10 whole, which is shorter than its diff:
```python
import functools
import math

import jax
import jax.numpy as jnp
from jax import lax
from jax.experimental import pallas as pl
from jax.experimental.pallas import tpu as pltpu
from jax.sharding import PartitionSpec as P

SLOT = 128
POINT_LIMIT = 6.0

prior_weight = 4.0
norm_eps = 1e-06

LOW_EXP = -32
MIB = 1 << 20


def code_rate(top_exp):
    return 32767.0 / (top_exp - LOW_EXP)


def encode(value, rate):
    size = jnp.maximum(jnp.abs(value), 2.0**LOW_EXP)
    level = jnp.floor((jnp.log2(size) - LOW_EXP) * rate + 0.5)
    return jnp.where(value < 0.0, -level, level).astype(jnp.int32).astype(jnp.int16)


def decode(code, rate):
    level = code.astype(jnp.int32).astype(jnp.float32)
    size = jnp.exp2(jnp.abs(level) * (1.0 / rate) + LOW_EXP)
    return jnp.where(level < 0.0, -size, size)


def bits_of(count):
    return [1 << bit for bit in range(count.bit_length() - 1)]


def late_bits(shards):
    return bits_of(shards)[1:]


def late_place(bits, over_shard):
    place = 0
    for bit in bits:
        place = place * 2 + (over_shard // bit) % 2
    return place


def add_block(sums, hot, rows_of, over_shard, *, sub, shards, width, flip):
    bits = late_bits(shards)
    late = late_place(bits, over_shard)
    count = 1 << len(bits)
    for over_sub in (0, 2):
        column = pl.multiple_of((sub ^ over_sub ^ flip) * width, width)
        part = jnp.dot(hot, rows_of(pl.ds(column, width)), preferred_element_type=jnp.float32)
        half_rows = part.shape[0] // 2
        first = (over_shard % 2 if over_sub == 0 else 1 - over_shard % 2) * 2 * count
        for half in range(2):
            rows = part[half * half_rows : (half + 1) * half_rows]
            sums[over_sub // 2][first + half * count + late] += rows


def hot_rows(slots, block, live):
    slot = jnp.where(block < live, slots[block : block + 1, :], -1)
    return (slot == lax.broadcasted_iota(jnp.int32, (SLOT, SLOT), 0)).astype(jnp.bfloat16)


def send_kernel(
    live_in, bids_in, slots_in, points, here, there, held, live, bids, slots, small, arrived, *, blocks, group, shards, width
):
    sub, shard = lax.axis_index("sub"), lax.axis_index("shard")
    firsts = [
        pltpu.make_async_copy(live_in, live, small.at[0]),
        pltpu.make_async_copy(bids_in, bids, small.at[1]),
        pltpu.make_async_copy(slots_in, slots, small.at[2]),
    ]
    for copy in firsts:
        copy.start()
    copies = []
    for first in range(0, blocks, group):
        span = pl.ds(first * SLOT, group * SLOT)
        copies.append(pltpu.make_async_copy(points.at[span], held.at[span], arrived.at[first // group]))
        copies[-1].start(priority=(first // group) % 2)
    for sums in (here, there):
        sums[...] = jnp.zeros_like(sums)
    for copy in firsts:
        copy.wait()
    for block in range(blocks):
        if block % group == 0:
            copies[block // group].wait()
        span = slice(block * SLOT, (block + 1) * SLOT)
        add_block(
            (here, there),
            hot_rows(slots, block, live[0]),
            lambda column, span=span: held[span, column],
            bids[block] ^ shard,
            sub=sub,
            shards=shards,
            width=width,
            flip=1,
        )


def keep_kernel(live, bids, slots, old, points, here, there, *, blocks, shards, width):
    sub, shard = lax.axis_index("sub"), lax.axis_index("shard")
    prior = prior_weight * old[...].astype(jnp.float32)
    half_rows = prior.shape[0] // 2
    for sums in (here, there):
        sums[...] = jnp.zeros_like(sums)
    for half in range(2):
        here[half << len(late_bits(shards))] = prior[half * half_rows : (half + 1) * half_rows]
    for block in range(blocks):
        span = slice(block * SLOT, (block + 1) * SLOT)
        add_block(
            (here, there),
            hot_rows(slots, block, live[0]),
            lambda column, span=span: points[span, column],
            bids[block] ^ shard,
            sub=sub,
            shards=shards,
            width=width,
            flip=0,
        )


def mix_kernel(keep, crossed, by_z, by_x, both, mine, code, *, half, rate):
    count = mine.shape[0]
    span = slice(half * count, (half + 1) * count)
    total = keep[span] + crossed[span]
    for term in (both[span], by_x[...], by_z[...]):
        total = total + decode(term, rate)
    mine[...] = total
    code[...] = encode(total, rate)


def finish_kernel(mine, there, own, code, *, rate):
    own[...] = mine[0] + decode(there[1], rate)
    code[0] = encode(own[...], rate)
    code[1] = encode(mine[1] + decode(there[0], rate), rate)


def rows_kernel(own, near, far, fresh, cents, *, shards, rows, width, rate):
    sub, shard = lax.axis_index("sub"), lax.axis_index("shard")
    bits = late_bits(shards)
    half_rows = rows // 2
    for over_shard in range(shards):
        parts = []
        for over_sub in (0, 2):
            chip = over_sub // 2 + 2 * (over_shard % 2)
            piece = (chip << len(bits)) + late_place(bits, over_shard)
            parts.append((sub ^ over_sub, decode(near[piece], rate)))
            parts.append((sub ^ 1 ^ over_sub, decode(far[piece], rate)))
        squares = sum(jnp.sum(part * part, axis=1, keepdims=True) for _, part in parts)
        scale = lax.rsqrt(squares + norm_eps)
        row = pl.ds(pl.multiple_of((shard ^ over_shard) * half_rows, half_rows), half_rows)
        for place, part in parts:
            cents[row, pl.ds(pl.multiple_of(place * width, width), width)] = (part * scale).astype(jnp.bfloat16)
        if over_shard == 0:
            fresh[...] = (own[...] * scale).astype(jnp.bfloat16)


def score_kernel(bids, slots, points, cents, *refs, half, blocks, rows, group):
    half_rows = rows // 2
    tile = min(256, cents.shape[0])
    lane = lax.broadcasted_iota(jnp.int32, (SLOT, SLOT), 1)
    filler = jnp.zeros((SLOT - blocks, SLOT), jnp.int32)
    turned = jnp.concatenate([slots[...], filler]).T - half * half_rows
    inside = (turned >= 0) & (turned < half_rows)
    mine_of = jnp.full((SLOT, SLOT), -jnp.inf, jnp.float32)
    rival_of = mine_of
    for block in range(0, blocks, group):
        mine = [None] * group
        rival = [None] * group
        for first in range(0, cents.shape[0], tile):
            score = lax.dot_general(
                points[block * SLOT : (block + group) * SLOT, :],
                cents[first : first + tile, :],
                (((1,), (1,)), ((), ())),
                preferred_element_type=jnp.float32,
            )
            for inner in range(group):
                at = block + inner
                row = jnp.where(inside, turned + bids[at] * half_rows, -1)[:, at : at + 1]
                for left in range(0, tile, SLOT):
                    part = score[inner * SLOT : (inner + 1) * SLOT, left : left + SLOT]
                    hit = lane + (first + left) == row
                    for best, here in ((mine, hit), (rival, ~hit)):
                        seen = jnp.where(here, part, -jnp.inf)
                        best[inner] = seen if best[inner] is None else jnp.maximum(best[inner], seen)
        for inner in range(group):
            mine_of = jnp.where(lane == block + inner, jnp.max(mine[inner], axis=1, keepdims=True), mine_of)
            rival_of = jnp.where(lane == block + inner, jnp.max(rival[inner], axis=1, keepdims=True), rival_of)
    if half:
        mine_in, rival_in, fresh_first, fresh_second, fresh, margin = refs
        fresh[:half_rows] = fresh_first[...]
        fresh[half_rows:] = fresh_second[...]
        joined = jnp.maximum(mine_in[...], mine_of) - jnp.maximum(rival_in[...], rival_of)
        margin[...] = joined.T[:blocks]
    else:
        mine_out, rival_out = refs
        mine_out[...] = mine_of
        rival_out[...] = rival_of


def local(points, block_ids, slot_ids, live_blocks, old_centroids):
    row_count, feat_width = points.shape
    blocks = row_count // SLOT
    shards = lax.axis_size("shard")
    subs = lax.axis_size("sub")
    rows, width = old_centroids.shape
    half_rows = rows // 2
    total = rows * shards
    top = POINT_LIMIT * (row_count * shards * subs + prior_weight)
    rate = code_rate(math.ceil(math.log2(top)))
    slots = slot_ids.reshape(blocks, SLOT)
    bits = late_bits(shards)
    late = 1 << len(bits)
    group = 2 if blocks % 2 == 0 else 1
    limit = pltpu.CompilerParams(vmem_limit_bytes=8 * MIB + 4 * total * feat_width)
    smem = pl.BlockSpec(memory_space=pltpu.SMEM)
    vmem = pl.BlockSpec(memory_space=pltpu.VMEM)
    hbm = pl.BlockSpec(memory_space=pltpu.HBM)

    def swap(value, over_sub, over_shard):
        pairs = []
        for shard in range(shards):
            for sub in range(subs):
                pairs.append((shard * subs + sub, (shard ^ over_shard) * subs + (sub ^ over_sub)))
        return lax.ppermute(value, ("shard", "sub"), pairs)

    def in_hbm(value):
        return pltpu.with_memory_space_constraint(value, pltpu.HBM)

    shape = jax.ShapeDtypeStruct((4 * late, half_rows, width), jnp.float32)
    cost = pl.CostEstimate(flops=row_count * SLOT * feat_width, bytes_accessed=row_count * feat_width, transcendentals=0)
    sizes = dict(blocks=blocks, shards=shards, width=width)
    *send, held = pl.pallas_call(
        functools.partial(send_kernel, group=group, **sizes),
        out_shape=(shape, shape, jax.ShapeDtypeStruct(points.shape, points.dtype)),
        in_specs=[hbm] * 4,
        out_specs=(vmem, vmem, vmem),
        scratch_shapes=[
            pltpu.SMEM((1,), jnp.int32),
            pltpu.SMEM((blocks,), jnp.int32),
            pltpu.VMEM((blocks, SLOT), jnp.int32),
            pltpu.SemaphoreType.DMA((3,)),
            pltpu.SemaphoreType.DMA((blocks // group,)),
        ],
        compiler_params=limit,
        cost_estimate=cost,
        name="sums_send",
    )(live_blocks, in_hbm(block_ids), in_hbm(slots), in_hbm(points))
    crossed = [swap(sums, 1, 0) for sums in send]
    keep = pl.pallas_call(
        functools.partial(keep_kernel, **sizes),
        out_shape=(shape, shape),
        in_specs=[smem, smem, vmem, vmem, vmem],
        out_specs=(vmem, vmem),
        compiler_params=limit,
        cost_estimate=cost,
        name="sums_keep",
    )(live_blocks, block_ids, slots, old_centroids, held)

    piece = (late, half_rows, width)
    two = (2, half_rows, width)

    def after(value, *others):
        return lax.optimization_barrier((value, *others))[0] if others else value

    def near_code(side, first, end, *earlier):
        return encode(keep[side][first:end] + after(crossed[side], *earlier)[first:end], rate)

    def reduce_late(half, by_x, by_z, *earlier):
        mine, code = pl.pallas_call(
            functools.partial(mix_kernel, half=half, rate=rate),
            out_shape=(jax.ShapeDtypeStruct(piece, jnp.float32), jax.ShapeDtypeStruct(piece, jnp.int16)),
            compiler_params=limit,
            name=f"mix{half}",
        )(after(keep[0], *earlier), crossed[0], by_z, by_x, both)
        for bit in bits[:-1]:
            count = mine.shape[0] // 2
            mine = mine[:count] + decode(swap(encode(mine[count:], rate), 0, bit), rate)
            code = encode(mine, rate)
        return mine, swap(code, 0, bits[-1])

    def finish(half, mine, there, *earlier):
        own, code = pl.pallas_call(
            functools.partial(finish_kernel, rate=rate),
            out_shape=(
                jax.ShapeDtypeStruct((half_rows, width), jnp.float32),
                jax.ShapeDtypeStruct(two, jnp.int16),
            ),
            compiler_params=limit,
            name=f"finish{half}",
        )(after(mine, *earlier), there)
        for bit in reversed(bits[:-1]):
            code = jnp.concatenate([code, swap(code, 0, bit)])
        return own, code

    def rows_of(half, own, near, far):
        return pl.pallas_call(
            functools.partial(
                rows_kernel, shards=shards, rows=rows, width=width, rate=rate
            ),
            out_shape=(
                jax.ShapeDtypeStruct((half_rows, width), jnp.bfloat16),
                jax.ShapeDtypeStruct((total // 2, feat_width), jnp.bfloat16),
            ),
            compiler_params=limit,
            name=f"rows{half}",
        )(own, near, far)

    def scores(half, cents, *earlier):
        line = jax.ShapeDtypeStruct((blocks if half else SLOT, SLOT), jnp.float32)
        fresh = jax.ShapeDtypeStruct((rows, width), jnp.bfloat16)
        return pl.pallas_call(
            functools.partial(
                score_kernel, half=half, blocks=blocks, rows=rows, group=math.gcd(blocks, 4)
            ),
            out_shape=(fresh, line) if half else (line, line),
            in_specs=[smem] + [vmem] * (3 + len(earlier)),
            out_specs=(vmem, vmem),
            compiler_params=limit,
            cost_estimate=pl.CostEstimate(
                flops=row_count * total * feat_width,
                bytes_accessed=2 * row_count * feat_width,
                transcendentals=0,
            ),
            name=f"scores{half}",
        )(block_ids, slots, held, cents, *earlier)

    both = swap(near_code(1, 0, 2 * late), 2, 1)
    first_codes = near_code(1, 2 * late, 3 * late), near_code(0, 2 * late, 3 * late)
    first_terms = swap(first_codes[0], 2, 0), swap(first_codes[1], 0, 1)
    second_terms = (
        swap(near_code(1, 3 * late, 4 * late, *first_codes), 2, 0),
        swap(near_code(0, 3 * late, 4 * late, *first_codes), 0, 1),
    )
    first = reduce_late(0, *first_terms)
    second = reduce_late(1, *second_terms, first[0])
    first_own, first_code = finish(0, *first)
    second_own, second_code = finish(1, *second, first_code)
    chips = [(2, 0), (0, 1), (2, 1)]
    near = [jnp.concatenate([first_code] + [swap(first_code, *chip) for chip in chips])]
    ready = [after(second_code, near[0]), after(second_code, near[0]), second_code]
    near.append(jnp.concatenate([second_code] + [swap(code, *chip) for code, chip in zip(ready, chips)]))
    far = [swap(block, 1, 0) for block in near]
    first_fresh, first_rows = rows_of(0, first_own, near[0], far[0])
    mine, rival = scores(0, first_rows)
    second_fresh, second_rows = rows_of(1, second_own, near[1], far[1])
    fresh, margin = scores(1, second_rows, mine, rival, first_fresh, second_fresh)
    return fresh, margin.reshape(row_count)


def solution(mesh):
    return jax.shard_map(
        local,
        mesh=mesh,
        in_specs=(
            P(("groups", "shard", "sub"), None),
            P(("groups", "shard", "sub")),
            P(("groups", "shard", "sub")),
            P(("groups", "shard", "sub")),
            P(("groups", "shard"), "sub"),
        ),
        out_specs=(P(("groups", "shard"), "sub"), P(("groups", "shard", "sub"))),
        check_vma=False,
    )
```

time: 38.7 us -> 42.8 us (1.11)
  waiting for transfers between devices: 5.1 us -> 12.5 us
  starting transfers between devices: 21.7 us -> 18.2 us
    ppermute x18 -> x17, waiting for transfers between devices: 5.1 us -> 12.5 us  [swap(): return lax.ppermute(value, ('shard', 'sub'), pairs)]
    ppermute x18 -> x17, starting transfers between devices: 21.7 us -> 18.2 us  [swap(): return lax.ppermute(value, ('shard', 'sub'), pairs)]
    pallas_call x2, Pallas kernels: 3.94 us -> 4.41 us  [scores(): pl.pallas_call(functools.partial(score_kernel, half=half, blocks=blocks,...]
  transfers between devices with their start and end apart: 18 -> 17, of which waited for: 7 -> 7; matrix products, arithmetic and copies ran while one was open for 1% -> 1% of each run, Pallas kernels for 10% -> 10%
where the time goes in v10:
time: 42.8 us; the launch traced here: 42.6 us
  starting transfers between devices  18.2 us (43%)
  waiting for transfers between devices  12.5 us (29%)
  Pallas kernels  9.91 us (23%)
  between operations  1.48 us (3%)
  other arithmetic  0.44 us (1%)
    ppermute x17, starting transfers between devices, swap(): return lax.ppermute(value, ('shard', 'sub'), pairs)  18.2 us
    ppermute x17, waiting for transfers between devices, swap(): return lax.ppermute(value, ('shard', 'sub'), pairs)  12.5 us
    pallas_call x2, Pallas kernels, scores(): pl.pallas_call(functools.partial(score_kernel, half=half, blocks=blocks,...  4.41 us
    pallas_call x1, Pallas kernels, local(): pl.pallas_call(functools.partial(send_kernel, group=group, **sizes), out_...  2.72 us
    pallas_call x1, Pallas kernels, local(): pl.pallas_call(functools.partial(keep_kernel, **sizes), out_shape=(shape,...  1.25 us
    pallas_call x2, Pallas kernels, rows_of(): pl.pallas_call(functools.partial(rows_kernel, shards=shards, rows=rows, w...  0.95 us
  transfers between devices with their start and end apart: 17, of which 7 were waited for; matrix products, arithmetic and copies ran while one was open for 1% of the time, Pallas kernels for 10%

profile of v10, /device:TPU:0, one launch (start us, length us, event | category | flops | bytes accessed | tf_op | source)
XLA Modules:
  0.0 42.6 jit_solution(1769810684376957913)
XLA Ops:
  0.6 0.0 copy-start.2
  0.6 0.0 copy-start
  0.7 0.0 copy-start.1
  1.3 2.7 %sums_send.1 = (f32[8,64,256]{2,1,0:T(8,128)S(1)}, f32[8,64,256]{2,1,0:T(8,128)S(1)}, bf16[1536,1024]{1,0:T(8,128)(2,1)S(1)}) custom-call(s32[1]{0:T(128)S(6)} %copy.13.live_in.live, s32[12]{0:T(128)} %bids.5, s32[12,128]{1,0:T(8,128)} %bitcast.2, bf16[1536,1024]{1,0:T(8,128)(2,1)} %points.1), custom_call_target="tpu_custom_call" | custom-call | flops 201326592 | bytes 1572864 | tf_op jit(solution)/shard_map/sums_send/pallas_call | solution.py:240
  4.1 0.5 %collective-permute-start = (f32[8,64,256]{2,1,0:T(8,128)S(1)}, f32[8,64,256]{2,1,0:T(8,128)S(1)}, u32[]{:S(2)}, u32[]{:S(2)}) collective-permute-start(f32[8,64,256]{2,1,0:T(8,128)S(1)} %get-tuple-element.30), channel_id=1, source_target_pairs={{0,1},{1,0},{2,3},{3,2},{4,5},{5,4},{6,7},{7,6},{8,9},{9,8},{10,11... | collective-permute-start | bytes 1572872 | tf_op jit(solution)/shard_map/ppermute | solution.py:232
  4.6 0.1 collective-permute-start.2
  4.7 0.0 copy-done.2
  4.7 0.0 copy-done
  4.7 0.0 copy-done.1
  4.7 1.2 %sums_keep.1 = (f32[8,64,256]{2,1,0:T(8,128)S(1)}, f32[8,64,256]{2,1,0:T(8,128)S(1)}) custom-call(s32[1]{0:T(128)S(6)} %copy.13.live_in.live, s32[12]{0:T(128)S(1)} %copy-done.2, s32[12,128]{1,0:T(8,128)S(1)} %bitcast.3, bf16[128,256]{1,0:T(8,128)(2,1)S(1)} %copy-done.1, bf16[1536,1024]{1,0:T(8,128)(2,1)S(1)} %get-tuple-element.28.points), custom_call_target="tpu_custom_call" | custom-call | flops 201326592 | bytes 1572864 | tf_op jit(solution)/shard_map/sums_keep/pallas_call | solution.py:257
  5.9 0.2 collective-permute-done.crossed
  6.1 0.1 fusion.3
  6.2 3.0 %collective-permute-start.1 = (s16[2,64,256]{2,1,0:T(8,128)(2,1)S(1)}, s16[2,64,256]{2,1,0:T(8,128)(2,1)S(1)}, u32[]{:S(2)}, u32[]{:S(2)}) collective-permute-start(s16[2,64,256]{2,1,0:T(8,128)(2,1)S(1)} %fusion.3), channel_id=1, source_target_pairs={{0,4},{1,5},{2,6},{3,7},{4,0},{5,1},{6,2},{7,3},{8,12},{9,13},{10,... | collective-permute-start | bytes 196616 | tf_op jit(solution)/shard_map/ppermute | solution.py:232
  9.2 0.0 collective-permute-done.2
  9.2 0.1 fusion.5
  9.3 1.6 %collective-permute-start.3 = (s16[2,64,256]{2,1,0:T(8,128)(2,1)S(1)}, s16[2,64,256]{2,1,0:T(8,128)(2,1)S(1)}, u32[]{:S(2)}, u32[]{:S(2)}) collective-permute-start(s16[2,64,256]{2,1,0:T(8,128)(2,1)S(1)} %fusion.5), channel_id=1, source_target_pairs={{0,2},{1,3},{2,0},{3,1},{4,6},{5,7},{6,4},{7,5},{8,10},{9,11},{10,... | collective-permute-start | bytes 196616 | tf_op jit(solution)/shard_map/ppermute | solution.py:232
  10.8 0.1 fusion.7
  10.9 0.1 fusion.1
  11.1 0.6 %collective-permute-start.4 = (s16[4,64,256]{2,1,0:T(8,128)(2,1)S(1)}, s16[4,64,256]{2,1,0:T(8,128)(2,1)S(1)}, u32[]{:S(2)}, u32[]{:S(2)}) collective-permute-start(s16[4,64,256]{2,1,0:T(8,128)(2,1)S(1)} %fusion.1), channel_id=1, source_target_pairs={{0,6},{1,7},{2,4},{3,5},{4,2},{5,3},{6,0},{7,1},{8,14},{9,15},{10,... | collective-permute-start | bytes 393224 | tf_op jit(solution)/shard_map/ppermute | solution.py:232
  11.7 0.1 fusion.9
  11.8 1.6 %collective-permute-start.6 = (s16[2,64,256]{2,1,0:T(8,128)(2,1)S(1)}, s16[2,64,256]{2,1,0:T(8,128)(2,1)S(1)}, u32[]{:S(2)}, u32[]{:S(2)}) collective-permute-start(s16[2,64,256]{2,1,0:T(8,128)(2,1)S(1)} %fusion.9), channel_id=1, source_target_pairs={{0,2},{1,3},{2,0},{3,1},{4,6},{5,7},{6,4},{7,5},{8,10},{9,11},{10,... | collective-permute-start | bytes 196616 | tf_op jit(solution)/shard_map/ppermute | solution.py:232
  13.3 1.4 %collective-permute-start.5 = (s16[2,64,256]{2,1,0:T(8,128)(2,1)S(1)}, s16[2,64,256]{2,1,0:T(8,128)(2,1)S(1)}, u32[]{:S(2)}, u32[]{:S(2)}) collective-permute-start(s16[2,64,256]{2,1,0:T(8,128)(2,1)S(1)} %fusion.7), channel_id=1, source_target_pairs={{0,4},{1,5},{2,6},{3,7},{4,0},{5,1},{6,2},{7,3},{8,12},{9,13},{10,... | collective-permute-start | bytes 196616 | tf_op jit(solution)/shard_map/ppermute | solution.py:232
  14.8 0.0 collective-permute-done.1.by_z
  14.8 0.1 collective-permute-done.3.by_x
  14.8 3.0 %collective-permute-done.4.both = s16[4,64,256]{2,1,0:T(8,128)(2,1)S(1)} collective-permute-done((s16[4,64,256]{2,1,0:T(8,128)(2,1)S(1)}, s16[4,64,256]{2,1,0:T(8,128)(2,1)S(1)}, u32[]{:S(2)}, u32[]{:S(2)}) %collective-permute-start.4) | collective-permute-done | bytes 131104 | tf_op jit(solution)/shard_map/ppermute | solution.py:232
  17.8 0.2 mix0.1
  18.0 2.6 %collective-permute-start.7 = (s16[2,64,256]{2,1,0:T(8,128)(2,1)S(1)}, s16[2,64,256]{2,1,0:T(8,128)(2,1)S(1)}, u32[]{:S(2)}, u32[]{:S(2)}) collective-permute-start(s16[2,64,256]{2,1,0:T(8,128)(2,1)S(1)} %get-tuple-element.38), channel_id=1, source_target_pairs={{0,8},{1,9},{2,10},{3,11},{4,12},{5,13},{6,14},{7,15},{8,0},{9,1},... | collective-permute-start | bytes 196616 | tf_op jit(solution)/shard_map/ppermute | solution.py:232
  20.7 0.0 collective-permute-done.6.by_x
  20.7 0.0 collective-permute-done.5.by_z
  20.7 0.2 mix1.1
  20.9 0.4 collective-permute-start.8
  21.3 3.5 %collective-permute-done.7.there = s16[2,64,256]{2,1,0:T(8,128)(2,1)S(1)} collective-permute-done((s16[2,64,256]{2,1,0:T(8,128)(2,1)S(1)}, s16[2,64,256]{2,1,0:T(8,128)(2,1)S(1)}, u32[]{:S(2)}, u32[]{:S(2)}) %collective-permute-start.7) | collective-permute-done | bytes 65568 | tf_op jit(solution)/shard_map/ppermute | solution.py:232
  24.8 0.1 finish0.1
  24.9 0.9 %collective-permute-start.11 = (s16[2,64,256]{2,1,0:T(8,128)(2,1)S(1)}, s16[2,64,256]{2,1,0:T(8,128)(2,1)S(1)}, u32[]{:S(2)}, u32[]{:S(2)}) collective-permute-start(s16[2,64,256]{2,1,0:T(8,128)(2,1)S(1)} %get-tuple-element.39), channel_id=1, source_target_pairs={{0,6},{1,7},{2,4},{3,5},{4,2},{5,3},{6,0},{7,1},{8,14},{9,15},{10,... | collective-permute-start | bytes 196616 | tf_op jit(solution)/shard_map/ppermute | solution.py:232
  25.7 1.7 %collective-permute-start.10 = (s16[2,64,256]{2,1,0:T(8,128)(2,1)S(1)}, s16[2,64,256]{2,1,0:T(8,128)(2,1)S(1)}, u32[]{:S(2)}, u32[]{:S(2)}) collective-permute-start(s16[2,64,256]{2,1,0:T(8,128)(2,1)S(1)} %get-tuple-element.39), channel_id=1, source_target_pairs={{0,4},{1,5},{2,6},{3,7},{4,0},{5,1},{6,2},{7,3},{8,12},{9,13},{10,... | collective-permute-start | bytes 196616 | tf_op jit(solution)/shard_map/ppermute | solution.py:232
  27.5 1.0 %collective-permute-start.9 = (s16[2,64,256]{2,1,0:T(8,128)(2,1)S(1)}, s16[2,64,256]{2,1,0:T(8,128)(2,1)S(1)}, u32[]{:S(2)}, u32[]{:S(2)}) collective-permute-start(s16[2,64,256]{2,1,0:T(8,128)(2,1)S(1)} %get-tuple-element.39), channel_id=1, source_target_pairs={{0,2},{1,3},{2,0},{3,1},{4,6},{5,7},{6,4},{7,5},{8,10},{9,11},{10,... | collective-permute-start | bytes 196616 | tf_op jit(solution)/shard_map/ppermute | solution.py:232
  28.4 0.0 collective-permute-done.8.there
  28.4 0.1 finish1.1
  28.5 0.9 %collective-permute-start.14 = (s16[2,64,256]{2,1,0:T(8,128)(2,1)S(1)}, s16[2,64,256]{2,1,0:T(8,128)(2,1)S(1)}, u32[]{:S(2)}, u32[]{:S(2)}) collective-permute-start(s16[2,64,256]{2,1,0:T(8,128)(2,1)S(1)} %get-tuple-element.44), channel_id=1, source_target_pairs={{0,6},{1,7},{2,4},{3,5},{4,2},{5,3},{6,0},{7,1},{8,14},{9,15},{10,... | collective-permute-start | bytes 196616 | tf_op jit(solution)/shard_map/ppermute | solution.py:232
  29.4 2.3 %collective-permute-done.9 = s16[2,64,256]{2,1,0:T(8,128)(2,1)S(1)} collective-permute-done((s16[2,64,256]{2,1,0:T(8,128)(2,1)S(1)}, s16[2,64,256]{2,1,0:T(8,128)(2,1)S(1)}, u32[]{:S(2)}, u32[]{:S(2)}) %collective-permute-start.9) | collective-permute-done | bytes 65568 | tf_op jit(solution)/shard_map/ppermute | solution.py:232
  31.7 0.0 collective-permute-done.10
  31.8 0.0 collective-permute-done.11
  31.8 1.0 %collective-permute-start.12 = (s16[2,64,256]{2,1,0:T(8,128)(2,1)S(1)}, s16[2,64,256]{2,1,0:T(8,128)(2,1)S(1)}, u32[]{:S(2)}, u32[]{:S(2)}) collective-permute-start(s16[2,64,256]{2,1,0:T(8,128)(2,1)S(1)} %get-tuple-element.44), channel_id=1, source_target_pairs={{0,2},{1,3},{2,0},{3,1},{4,6},{5,7},{6,4},{7,5},{8,10},{9,11},{10,... | collective-permute-start | bytes 196616 | tf_op jit(solution)/shard_map/ppermute | solution.py:232
  32.8 0.9 %collective-permute-start.13 = (s16[2,64,256]{2,1,0:T(8,128)(2,1)S(1)}, s16[2,64,256]{2,1,0:T(8,128)(2,1)S(1)}, u32[]{:S(2)}, u32[]{:S(2)}) collective-permute-start(s16[2,64,256]{2,1,0:T(8,128)(2,1)S(1)} %get-tuple-element.44), channel_id=1, source_target_pairs={{0,4},{1,5},{2,6},{3,7},{4,0},{5,1},{6,2},{7,3},{8,12},{9,13},{10,... | collective-permute-start | bytes 196616 | tf_op jit(solution)/shard_map/ppermute | solution.py:232
  33.7 0.0 collective-permute-start.16
  33.7 2.4 %collective-permute-done.12 = s16[2,64,256]{2,1,0:T(8,128)(2,1)S(1)} collective-permute-done((s16[2,64,256]{2,1,0:T(8,128)(2,1)S(1)}, s16[2,64,256]{2,1,0:T(8,128)(2,1)S(1)}, u32[]{:S(2)}, u32[]{:S(2)}) %collective-permute-start.12) | collective-permute-done | bytes 65568 | tf_op jit(solution)/shard_map/ppermute | solution.py:232
  36.1 1.0 %collective-permute-done.13 = s16[2,64,256]{2,1,0:T(8,128)(2,1)S(1)} collective-permute-done((s16[2,64,256]{2,1,0:T(8,128)(2,1)S(1)}, s16[2,64,256]{2,1,0:T(8,128)(2,1)S(1)}, u32[]{:S(2)}, u32[]{:S(2)}) %collective-permute-start.13) | collective-permute-done | bytes 65568 | tf_op jit(solution)/shard_map/ppermute | solution.py:232
  37.1 0.0 collective-permute-done.14
  37.1 0.1 collective-permute-start.15
  37.2 0.0 collective-permute-done.16.far
  37.2 0.5 %rows0.1 = (bf16[64,256]{1,0:T(8,128)(2,1)S(1)}, bf16[256,1024]{1,0:T(8,128)(2,1)S(1)}) custom-call(f32[64,256]{1,0:T(8,128)S(1)} %get-tuple-element.46.own, s16[8,64,256]{2,1,0:T(8,128)(2,1)S(1)} %constant_dynamic-update-slice_fusion.near, s16[8,64,256]{2,1,0:T(8,128)(2,1)S(1)} %collective-permute-done.16.far), custom_call_target="tpu_custom_call" | custom-call | tf_op jit(solution)/shard_map/rows0/pallas_call | solution.py:304
  37.7 1.9 %scores0.1 = (f32[128,128]{1,0:T(8,128)S(1)}, f32[128,128]{1,0:T(8,128)S(1)}) custom-call(s32[12]{0:T(128)S(1)} %copy-done.2, s32[12,128]{1,0:T(8,128)S(1)} %bitcast.4, bf16[1536,1024]{1,0:T(8,128)(2,1)S(1)} %get-tuple-element.28.points, bf16[256,1024]{1,0:T(8,128)(2,1)S(1)} %get-tuple-element.47.cents), custom_call_target="tpu_custom_call" | custom-call | flops 805306368 | bytes 3145728 | tf_op jit(solution)/shard_map/scores0/pallas_call | solution.py:319
  39.6 0.0 collective-permute-done.15.far
  39.6 0.5 %rows1.1 = (bf16[64,256]{1,0:T(8,128)(2,1)S(1)}, bf16[256,1024]{1,0:T(8,128)(2,1)S(1)}) custom-call(f32[64,256]{1,0:T(8,128)S(1)} %get-tuple-element.42.own, s16[8,64,256]{2,1,0:T(8,128)(2,1)S(1)} %constant_dynamic-update-slice_fusion.4.near, s16[8,64,256]{2,1,0:T(8,128)(2,1)S(1)} %collective-permute-done.15.far), custom_call_target="tpu_custom_call" | custom-call | tf_op jit(solution)/shard_map/rows1/pallas_call | solution.py:304
  40.1 2.5 %scores1.1 = (bf16[128,256]{1,0:T(8,128)(2,1)}, f32[12,128]{1,0:T(8,128)}) custom-call(s32[12]{0:T(128)S(1)} %copy-done.2, s32[12,128]{1,0:T(8,128)S(1)} %bitcast.5, bf16[1536,1024]{1,0:T(8,128)(2,1)S(1)} %get-tuple-element.28.points, bf16[256,1024]{1,0:T(8,128)(2,1)S(1)} %get-tuple-element.45.cents, f32[128,128]{1,0:T(8,128)S(1)} %get-tuple-element.48.refs_0_, ...), custom_call_target="tpu_custom_call" | custom-call | flops 805306368 | bytes 3145728 | tf_op jit(solution)/shard_map/scores1/pallas_call | solution.py:319
  (8 shorter events, 0.0 us)
Async XLA Ops:
  0.6 4.0 %copy-start.2 = (s32[12]{0:T(128)S(1)}, s32[12]{0:T(128)}, u32[]{:S(2)}) copy-start(s32[12]{0:T(128)} %bids.5) | copy-start | bytes 148
  0.6 4.0 %copy-start = (s32[1536]{0:T(1024)S(1)}, s32[1536]{0:T(1024)}, u32[]{:S(2)}) copy-start(s32[1536]{0:T(1024)} %param.7) | copy-start | bytes 18436
  0.7 4.0 %copy-start.1 = (bf16[128,256]{1,0:T(8,128)(2,1)S(1)}, bf16[128,256]{1,0:T(8,128)(2,1)}, u32[]{:S(2)}) copy-start(bf16[128,256]{1,0:T(8,128)(2,1)} %old.1) | copy-start | bytes 196612
  4.1 2.1 %collective-permute-start = (f32[8,64,256]{2,1,0:T(8,128)S(1)}, f32[8,64,256]{2,1,0:T(8,128)S(1)}, u32[]{:S(2)}, u32[]{:S(2)}) collective-permute-start(f32[8,64,256]{2,1,0:T(8,128)S(1)} %get-tuple-element.30), channel_id=1, source_target_pairs={{0,1},{1,0},{2,3},{3,2},{4,5},{5,4},{6,7},{7,6},{8,9},{9,8},{10,11... | collective-permute-start | bytes 1572872 | tf_op jit(solution)/shard_map/ppermute | solution.py:232
  4.6 4.6 %collective-permute-start.2 = (f32[8,64,256]{2,1,0:T(8,128)S(1)}, f32[8,64,256]{2,1,0:T(8,128)S(1)}, u32[]{:S(2)}, u32[]{:S(2)}) collective-permute-start(f32[8,64,256]{2,1,0:T(8,128)S(1)} %get-tuple-element.32), channel_id=1, source_target_pairs={{0,1},{1,0},{2,3},{3,2},{4,5},{5,4},{6,7},{7,6},{8,9},{9,8},{10,11... | collective-permute-start | bytes 1572872 | tf_op jit(solution)/shard_map/ppermute | solution.py:232
  6.2 8.6 %collective-permute-start.1 = (s16[2,64,256]{2,1,0:T(8,128)(2,1)S(1)}, s16[2,64,256]{2,1,0:T(8,128)(2,1)S(1)}, u32[]{:S(2)}, u32[]{:S(2)}) collective-permute-start(s16[2,64,256]{2,1,0:T(8,128)(2,1)S(1)} %fusion.3), channel_id=1, source_target_pairs={{0,4},{1,5},{2,6},{3,7},{4,0},{5,1},{6,2},{7,3},{8,12},{9,13},{10,... | collective-permute-start | bytes 196616 | tf_op jit(solution)/shard_map/ppermute | solution.py:232
  9.3 5.6 %collective-permute-start.3 = (s16[2,64,256]{2,1,0:T(8,128)(2,1)S(1)}, s16[2,64,256]{2,1,0:T(8,128)(2,1)S(1)}, u32[]{:S(2)}, u32[]{:S(2)}) collective-permute-start(s16[2,64,256]{2,1,0:T(8,128)(2,1)S(1)} %fusion.5), channel_id=1, source_target_pairs={{0,2},{1,3},{2,0},{3,1},{4,6},{5,7},{6,4},{7,5},{8,10},{9,11},{10,... | collective-permute-start | bytes 196616 | tf_op jit(solution)/shard_map/ppermute | solution.py:232
  11.1 6.7 %collective-permute-start.4 = (s16[4,64,256]{2,1,0:T(8,128)(2,1)S(1)}, s16[4,64,256]{2,1,0:T(8,128)(2,1)S(1)}, u32[]{:S(2)}, u32[]{:S(2)}) collective-permute-start(s16[4,64,256]{2,1,0:T(8,128)(2,1)S(1)} %fusion.1), channel_id=1, source_target_pairs={{0,6},{1,7},{2,4},{3,5},{4,2},{5,3},{6,0},{7,1},{8,14},{9,15},{10,... | collective-permute-start | bytes 393224 | tf_op jit(solution)/shard_map/ppermute | solution.py:232
  11.8 8.9 %collective-permute-start.6 = (s16[2,64,256]{2,1,0:T(8,128)(2,1)S(1)}, s16[2,64,256]{2,1,0:T(8,128)(2,1)S(1)}, u32[]{:S(2)}, u32[]{:S(2)}) collective-permute-start(s16[2,64,256]{2,1,0:T(8,128)(2,1)S(1)} %fusion.9), channel_id=1, source_target_pairs={{0,2},{1,3},{2,0},{3,1},{4,6},{5,7},{6,4},{7,5},{8,10},{9,11},{10,... | collective-permute-start | bytes 196616 | tf_op jit(solution)/shard_map/ppermute | solution.py:232
  13.3 7.3 %collective-permute-start.5 = (s16[2,64,256]{2,1,0:T(8,128)(2,1)S(1)}, s16[2,64,256]{2,1,0:T(8,128)(2,1)S(1)}, u32[]{:S(2)}, u32[]{:S(2)}) collective-permute-start(s16[2,64,256]{2,1,0:T(8,128)(2,1)S(1)} %fusion.7), channel_id=1, source_target_pairs={{0,4},{1,5},{2,6},{3,7},{4,0},{5,1},{6,2},{7,3},{8,12},{9,13},{10,... | collective-permute-start | bytes 196616 | tf_op jit(solution)/shard_map/ppermute | solution.py:232
  18.0 6.8 %collective-permute-start.7 = (s16[2,64,256]{2,1,0:T(8,128)(2,1)S(1)}, s16[2,64,256]{2,1,0:T(8,128)(2,1)S(1)}, u32[]{:S(2)}, u32[]{:S(2)}) collective-permute-start(s16[2,64,256]{2,1,0:T(8,128)(2,1)S(1)} %get-tuple-element.38), channel_id=1, source_target_pairs={{0,8},{1,9},{2,10},{3,11},{4,12},{5,13},{6,14},{7,15},{8,0},{9,1},... | collective-permute-start | bytes 196616 | tf_op jit(solution)/shard_map/ppermute | solution.py:232
  20.9 7.6 %collective-permute-start.8 = (s16[2,64,256]{2,1,0:T(8,128)(2,1)S(1)}, s16[2,64,256]{2,1,0:T(8,128)(2,1)S(1)}, u32[]{:S(2)}, u32[]{:S(2)}) collective-permute-start(s16[2,64,256]{2,1,0:T(8,128)(2,1)S(1)} %get-tuple-element.41), channel_id=1, source_target_pairs={{0,8},{1,9},{2,10},{3,11},{4,12},{5,13},{6,14},{7,15},{8,0},{9,1},... | collective-permute-start | bytes 196616 | tf_op jit(solution)/shard_map/ppermute | solution.py:232
  24.9 6.9 %collective-permute-start.11 = (s16[2,64,256]{2,1,0:T(8,128)(2,1)S(1)}, s16[2,64,256]{2,1,0:T(8,128)(2,1)S(1)}, u32[]{:S(2)}, u32[]{:S(2)}) collective-permute-start(s16[2,64,256]{2,1,0:T(8,128)(2,1)S(1)} %get-tuple-element.39), channel_id=1, source_target_pairs={{0,6},{1,7},{2,4},{3,5},{4,2},{5,3},{6,0},{7,1},{8,14},{9,15},{10,... | collective-permute-start | bytes 196616 | tf_op jit(solution)/shard_map/ppermute | solution.py:232
  25.7 6.0 %collective-permute-start.10 = (s16[2,64,256]{2,1,0:T(8,128)(2,1)S(1)}, s16[2,64,256]{2,1,0:T(8,128)(2,1)S(1)}, u32[]{:S(2)}, u32[]{:S(2)}) collective-permute-start(s16[2,64,256]{2,1,0:T(8,128)(2,1)S(1)} %get-tuple-element.39), channel_id=1, source_target_pairs={{0,4},{1,5},{2,6},{3,7},{4,0},{5,1},{6,2},{7,3},{8,12},{9,13},{10,... | collective-permute-start | bytes 196616 | tf_op jit(solution)/shard_map/ppermute | solution.py:232
  27.5 4.3 %collective-permute-start.9 = (s16[2,64,256]{2,1,0:T(8,128)(2,1)S(1)}, s16[2,64,256]{2,1,0:T(8,128)(2,1)S(1)}, u32[]{:S(2)}, u32[]{:S(2)}) collective-permute-start(s16[2,64,256]{2,1,0:T(8,128)(2,1)S(1)} %get-tuple-element.39), channel_id=1, source_target_pairs={{0,2},{1,3},{2,0},{3,1},{4,6},{5,7},{6,4},{7,5},{8,10},{9,11},{10,... | collective-permute-start | bytes 196616 | tf_op jit(solution)/shard_map/ppermute | solution.py:232
  28.5 8.6 %collective-permute-start.14 = (s16[2,64,256]{2,1,0:T(8,128)(2,1)S(1)}, s16[2,64,256]{2,1,0:T(8,128)(2,1)S(1)}, u32[]{:S(2)}, u32[]{:S(2)}) collective-permute-start(s16[2,64,256]{2,1,0:T(8,128)(2,1)S(1)} %get-tuple-element.44), channel_id=1, source_target_pairs={{0,6},{1,7},{2,4},{3,5},{4,2},{5,3},{6,0},{7,1},{8,14},{9,15},{10,... | collective-permute-start | bytes 196616 | tf_op jit(solution)/shard_map/ppermute | solution.py:232
  31.8 4.3 %collective-permute-start.12 = (s16[2,64,256]{2,1,0:T(8,128)(2,1)S(1)}, s16[2,64,256]{2,1,0:T(8,128)(2,1)S(1)}, u32[]{:S(2)}, u32[]{:S(2)}) collective-permute-start(s16[2,64,256]{2,1,0:T(8,128)(2,1)S(1)} %get-tuple-element.44), channel_id=1, source_target_pairs={{0,2},{1,3},{2,0},{3,1},{4,6},{5,7},{6,4},{7,5},{8,10},{9,11},{10,... | collective-permute-start | bytes 196616 | tf_op jit(solution)/shard_map/ppermute | solution.py:232
  32.8 4.3 %collective-permute-start.13 = (s16[2,64,256]{2,1,0:T(8,128)(2,1)S(1)}, s16[2,64,256]{2,1,0:T(8,128)(2,1)S(1)}, u32[]{:S(2)}, u32[]{:S(2)}) collective-permute-start(s16[2,64,256]{2,1,0:T(8,128)(2,1)S(1)} %get-tuple-element.44), channel_id=1, source_target_pairs={{0,4},{1,5},{2,6},{3,7},{4,0},{5,1},{6,2},{7,3},{8,12},{9,13},{10,... | collective-permute-start | bytes 196616 | tf_op jit(solution)/shard_map/ppermute | solution.py:232
  33.7 3.5 %collective-permute-start.16 = (s16[8,64,256]{2,1,0:T(8,128)(2,1)S(1)}, s16[8,64,256]{2,1,0:T(8,128)(2,1)S(1)}, u32[]{:S(2)}, u32[]{:S(2)}) collective-permute-start(s16[8,64,256]{2,1,0:T(8,128)(2,1)S(1)} %constant_dynamic-update-slice_fusion.near), channel_id=1, source_target_pairs={{0,1},{1,0},{2,3},{3,2},{4,5},{5,4},{6,7},{7,6},{8,9},{9,8},{10,11... | collective-permute-start | bytes 786440 | tf_op jit(solution)/shard_map/ppermute | solution.py:232
  37.1 2.5 %collective-permute-start.15 = (s16[8,64,256]{2,1,0:T(8,128)(2,1)S(1)}, s16[8,64,256]{2,1,0:T(8,128)(2,1)S(1)}, u32[]{:S(2)}, u32[]{:S(2)}) collective-permute-start(s16[8,64,256]{2,1,0:T(8,128)(2,1)S(1)} %constant_dynamic-update-slice_fusion.4.near), channel_id=1, source_target_pairs={{0,1},{1,0},{2,3},{3,2},{4,5},{5,4},{6,7},{7,6},{8,9},{9,8},{10,11... | collective-permute-start | bytes 786440 | tf_op jit(solution)/shard_map/ppermute | solution.py:232

commit v11 on v9

--- a/solution.py
+++ b/solution.py
@@ -169,8 +169,8 @@
             fresh[...] = (own[...] * scale).astype(jnp.bfloat16)
 
 
-def score_kernel(bids, slots, points, cents, *refs, half, blocks, shards, rows, group):
-    if half:
+def score_kernel(bids, slots, points, cents, *refs, half, last, blocks, shards, rows, group):
+    if last:
         mine_in, rival_in, fresh_first, fresh_second, fresh, margin = refs
         fresh[: rows // 2] = fresh_first[...]
         fresh[rows // 2 :] = fresh_second[...]
@@ -200,7 +200,7 @@
                 best = part[segment].reshape(half_rows // lanes, lanes, SLOT).max(axis=0)
                 rivals = jnp.maximum(rivals, jnp.where(bids[at] == segment, -jnp.inf, best))
             rival = jnp.max(rivals, axis=0, keepdims=True)
-            if half:
+            if last:
                 margin[line, :] = (mine_in[line, :] + mine) - jnp.maximum(rival_in[line, :], rival)
             else:
                 mine_out[line, :] = mine
@@ -305,11 +305,6 @@
             code = jnp.concatenate([code, swap(code, 0, bit)])
         return own, code
 
-    def gather_near(codes):
-        first = jnp.concatenate([codes[0]] + [swap(codes[0], *chip) for chip in chips[1:]])
-        ready = [after(codes[1], first)] + [codes[1]] * (len(chips) - 2)
-        return first, jnp.concatenate([codes[1]] + [swap(code, *chip) for code, chip in zip(ready, chips[1:])])
-
     def rows_of(half, own, near, far):
         return pl.pallas_call(
             functools.partial(
@@ -323,14 +318,14 @@
             name=f"rows{half}",
         )(own, near, far)
 
-    def scores(half, cents, *earlier):
+    def scores(half, last, cents, *earlier):
         line = jax.ShapeDtypeStruct((blocks, SLOT), jnp.float32)
         fresh = jax.ShapeDtypeStruct((rows, width), jnp.bfloat16)
         return pl.pallas_call(
             functools.partial(
-                score_kernel, half=half, blocks=blocks, shards=shards, rows=rows, group=group
-            ),
-            out_shape=(fresh, line) if half else (line, line),
+                score_kernel, half=half, last=last, blocks=blocks, shards=shards, rows=rows, group=group
+            ),
+            out_shape=(fresh, line) if last else (line, line),
             in_specs=[smem] + [vmem] * (3 + len(earlier)),
             out_specs=(vmem, vmem),
             compiler_params=limit,
@@ -349,12 +344,14 @@
     first_own, first_code = finish(0, *first)
     second_own, second_code = finish(1, *second, first_code)
     own, codes = (first_own, second_own), (first_code, second_code)
-    near = gather_near(codes)
+    near = jnp.concatenate([codes[0], swap(codes[0], 2, 0)])
+    near = [jnp.concatenate([near, swap(near, 0, 1)])]
+    near.append(jnp.concatenate([codes[1]] + [swap(codes[1], *chip) for chip in chips[1:]]))
     far = [swap(block, 1, 0) for block in near]
+    second_fresh, second_rows = rows_of(1, own[1], near[1], far[1])
+    mine, rival = scores(1, False, second_rows)
     first_fresh, first_rows = rows_of(0, own[0], near[0], far[0])
-    mine, rival = scores(0, first_rows)
-    second_fresh, second_rows = rows_of(1, own[1], near[1], far[1])
-    fresh, margin = scores(1, second_rows, mine, rival, first_fresh, second_fresh)
+    fresh, margin = scores(0, True, first_rows, mine, rival, first_fresh, second_fresh)
     return fresh, margin.reshape(row_count)
 
 

time: 38.7 us -> 38.2 us (0.987)
  starting transfers between devices: 21.7 us -> 20.2 us
  waiting for transfers between devices: 5.1 us -> 6.25 us
    ppermute x18 -> x17, starting transfers between devices: 21.7 us -> 20.2 us  [swap(): return lax.ppermute(value, ('shard', 'sub'), pairs)]
    ppermute x18 -> x17, waiting for transfers between devices: 5.1 us -> 6.25 us  [swap(): return lax.ppermute(value, ('shard', 'sub'), pairs)]
  transfers between devices with their start and end apart: 18 -> 17, of which waited for: 7 -> 8; matrix products, arithmetic and copies ran while one was open for 1% -> 1% of each run, Pallas kernels for 10% -> 11%
where the time goes in v11:
time: 38.2 us; the launch traced here: 38 us
  starting transfers between devices  20.2 us (53%)
  Pallas kernels  9.5 us (25%)
  waiting for transfers between devices  6.25 us (16%)
  between operations  1.49 us (4%)
  other arithmetic  0.42 us (1%)
    ppermute x17, starting transfers between devices, swap(): return lax.ppermute(value, ('shard', 'sub'), pairs)  20.2 us
    ppermute x17, waiting for transfers between devices, swap(): return lax.ppermute(value, ('shard', 'sub'), pairs)  6.25 us
    pallas_call x2, Pallas kernels, scores(): pl.pallas_call(functools.partial(score_kernel, half=half, last=last, bloc...  3.94 us
    pallas_call x1, Pallas kernels, local(): pl.pallas_call(functools.partial(send_kernel, group=group, **sizes), out_...  2.75 us
    pallas_call x1, Pallas kernels, local(): pl.pallas_call(functools.partial(keep_kernel, **sizes), out_shape=(shape,...  1.29 us
    pallas_call x2, Pallas kernels, rows_of(): pl.pallas_call(functools.partial(rows_kernel, half=half, shards=shards, s...  0.95 us
  transfers between devices with their start and end apart: 17, of which 8 were waited for; matrix products, arithmetic and copies ran while one was open for 1% of the time, Pallas kernels for 11%

profile of v11, /device:TPU:0, one launch (start us, length us, event | category | flops | bytes accessed | tf_op | source)
XLA Modules:
  0.0 38.0 jit_solution(18092084852703969542)
XLA Ops:
  0.6 0.0 copy-start.2
  0.6 0.0 copy-start
  0.7 0.0 copy-start.1
  1.3 2.7 %sums_send.1 = (f32[4,2,64,256]{3,2,1,0:T(8,128)S(1)}, f32[4,2,64,256]{3,2,1,0:T(8,128)S(1)}, bf16[1536,1024]{1,0:T(8,128)(2,1)S(1)}) custom-call(s32[1]{0:T(128)S(6)} %copy.12.live_in.live, s32[12]{0:T(128)} %bids.5, s32[12,128]{1,0:T(8,128)} %bitcast.26, bf16[1536,1024]{1,0:T(8,128)(2,1)} %points.1), custom_call_target="tpu_custom_call" | custom-call | flops 201326592 | bytes 1572864 | tf_op jit(solution)/shard_map/sums_send/pallas_call | solution.py:243
  4.1 0.5 %collective-permute-start = (f32[4,2,64,256]{3,2,1,0:T(8,128)S(1)}, f32[4,2,64,256]{3,2,1,0:T(8,128)S(1)}, u32[]{:S(2)}, u32[]{:S(2)}) collective-permute-start(f32[4,2,64,256]{3,2,1,0:T(8,128)S(1)} %get-tuple-element.28), channel_id=1, source_target_pairs={{0,1},{1,0},{2,3},{3,2},{4,5},{5,4},{6,7},{7,6},{8,9},{9,8},{10,11... | collective-permute-start | bytes 1572872 | tf_op jit(solution)/shard_map/ppermute | solution.py:235
  4.6 0.1 collective-permute-start.8
  4.7 0.0 copy-done.2
  4.7 0.0 copy-done
  4.7 0.0 copy-done.1
  4.7 1.3 %sums_keep.1 = (f32[4,2,64,256]{3,2,1,0:T(8,128)S(1)}, f32[4,2,64,256]{3,2,1,0:T(8,128)S(1)}) custom-call(s32[1]{0:T(128)S(6)} %copy.12.live_in.live, s32[12]{0:T(128)S(1)} %copy-done.2, s32[12,128]{1,0:T(8,128)S(1)} %bitcast.27, bf16[128,256]{1,0:T(8,128)(2,1)S(1)} %copy-done.1, bf16[1536,1024]{1,0:T(8,128)(2,1)S(1)} %get-tuple-element.26.points), custom_call_target="tpu_custom_call" | custom-call | flops 201326592 | bytes 1572864 | tf_op jit(solution)/shard_map/sums_keep/pallas_call | solution.py:260
  6.0 0.2 collective-permute-done.crossed
  6.1 0.2 fusion.5
  6.3 3.9 %collective-permute-start.3 = (s16[2,64,256]{2,1,0:T(8,128)(2,1)S(1)}, s16[2,64,256]{2,1,0:T(8,128)(2,1)S(1)}, u32[]{:S(2)}, u32[]{:S(2)}) collective-permute-start(s16[2,64,256]{2,1,0:T(8,128)(2,1)S(1)} %get-tuple-element.53), channel_id=1, source_target_pairs={{0,6},{1,7},{2,4},{3,5},{4,2},{5,3},{6,0},{7,1},{8,14},{9,15},{10,... | collective-permute-start | bytes 196616 | tf_op jit(solution)/shard_map/ppermute | solution.py:235
  10.3 0.4 %collective-permute-start.2 = (s16[2,64,256]{2,1,0:T(8,128)(2,1)S(1)}, s16[2,64,256]{2,1,0:T(8,128)(2,1)S(1)}, u32[]{:S(2)}, u32[]{:S(2)}) collective-permute-start(s16[2,64,256]{2,1,0:T(8,128)(2,1)S(1)} %get-tuple-element.54), channel_id=1, source_target_pairs={{0,4},{1,5},{2,6},{3,7},{4,0},{5,1},{6,2},{7,3},{8,12},{9,13},{10,... | collective-permute-start | bytes 196616 | tf_op jit(solution)/shard_map/ppermute | solution.py:235
  10.7 0.2 collective-permute-start.1
  10.9 0.0 collective-permute-done.8.crossed
  10.9 0.2 fusion.11
  11.1 2.9 %collective-permute-start.11 = (s16[2,64,256]{2,1,0:T(8,128)(2,1)S(1)}, s16[2,64,256]{2,1,0:T(8,128)(2,1)S(1)}, u32[]{:S(2)}, u32[]{:S(2)}) collective-permute-start(s16[2,64,256]{2,1,0:T(8,128)(2,1)S(1)} %get-tuple-element.50), channel_id=1, source_target_pairs={{0,6},{1,7},{2,4},{3,5},{4,2},{5,3},{6,0},{7,1},{8,14},{9,15},{10,... | collective-permute-start | bytes 196616 | tf_op jit(solution)/shard_map/ppermute | solution.py:235
  14.1 0.4 %collective-permute-start.10 = (s16[2,64,256]{2,1,0:T(8,128)(2,1)S(1)}, s16[2,64,256]{2,1,0:T(8,128)(2,1)S(1)}, u32[]{:S(2)}, u32[]{:S(2)}) collective-permute-start(s16[2,64,256]{2,1,0:T(8,128)(2,1)S(1)} %get-tuple-element.51), channel_id=1, source_target_pairs={{0,4},{1,5},{2,6},{3,7},{4,0},{5,1},{6,2},{7,3},{8,12},{9,13},{10,... | collective-permute-start | bytes 196616 | tf_op jit(solution)/shard_map/ppermute | solution.py:235
  14.5 0.0 collective-permute-done.3.refs_2_
  14.5 0.2 collective-permute-start.9
  14.8 0.1 collective-permute-done.2.refs_1_
  14.8 0.9 %collective-permute-done.1.refs_0_ = s16[2,64,256]{2,1,0:T(8,128)(2,1)S(1)} collective-permute-done((s16[2,64,256]{2,1,0:T(8,128)(2,1)S(1)}, s16[2,64,256]{2,1,0:T(8,128)(2,1)S(1)}, u32[]{:S(2)}, u32[]{:S(2)}) %collective-permute-start.1) | collective-permute-done | bytes 65568 | tf_op jit(solution)/shard_map/ppermute | solution.py:235
  15.7 0.2 mix0.1
  15.9 2.7 %collective-permute-start.4 = (s16[2,64,256]{2,1,0:T(8,128)(2,1)S(1)}, s16[2,64,256]{2,1,0:T(8,128)(2,1)S(1)}, u32[]{:S(2)}, u32[]{:S(2)}) collective-permute-start(s16[2,64,256]{2,1,0:T(8,128)(2,1)S(1)} %get-tuple-element.30), channel_id=1, source_target_pairs={{0,8},{1,9},{2,10},{3,11},{4,12},{5,13},{6,14},{7,15},{8,0},{9,1},... | collective-permute-start | bytes 196616 | tf_op jit(solution)/shard_map/ppermute | solution.py:235
  18.6 0.0 collective-permute-done.11.refs_2_
  18.6 0.2 collective-permute-done.10.refs_1_
  18.7 0.1 collective-permute-done.9.refs_0_
  18.8 0.2 mix1.1
  19.0 2.7 %collective-permute-start.12 = (s16[2,64,256]{2,1,0:T(8,128)(2,1)S(1)}, s16[2,64,256]{2,1,0:T(8,128)(2,1)S(1)}, u32[]{:S(2)}, u32[]{:S(2)}) collective-permute-start(s16[2,64,256]{2,1,0:T(8,128)(2,1)S(1)} %get-tuple-element.40), channel_id=1, source_target_pairs={{0,8},{1,9},{2,10},{3,11},{4,12},{5,13},{6,14},{7,15},{8,0},{9,1},... | collective-permute-start | bytes 196616 | tf_op jit(solution)/shard_map/ppermute | solution.py:235
  21.6 0.0 collective-permute-done.4.there
  21.6 0.1 finish0.1
  21.7 0.8 %collective-permute-start.5 = (s16[2,64,256]{2,1,0:T(8,128)(2,1)S(1)}, s16[2,64,256]{2,1,0:T(8,128)(2,1)S(1)}, u32[]{:S(2)}, u32[]{:S(2)}) collective-permute-start(s16[2,64,256]{2,1,0:T(8,128)(2,1)S(1)} %get-tuple-element.32), channel_id=1, source_target_pairs={{0,2},{1,3},{2,0},{3,1},{4,6},{5,7},{6,4},{7,5},{8,10},{9,11},{10,... | collective-permute-start | bytes 196616 | tf_op jit(solution)/shard_map/ppermute | solution.py:235
  22.5 1.7 %collective-permute-done.12.there = s16[2,64,256]{2,1,0:T(8,128)(2,1)S(1)} collective-permute-done((s16[2,64,256]{2,1,0:T(8,128)(2,1)S(1)}, s16[2,64,256]{2,1,0:T(8,128)(2,1)S(1)}, u32[]{:S(2)}, u32[]{:S(2)}) %collective-permute-start.12) | collective-permute-done | bytes 65568 | tf_op jit(solution)/shard_map/ppermute | solution.py:235
  24.2 0.1 finish1.1
  24.3 1.7 %collective-permute-start.15 = (s16[2,64,256]{2,1,0:T(8,128)(2,1)S(1)}, s16[2,64,256]{2,1,0:T(8,128)(2,1)S(1)}, u32[]{:S(2)}, u32[]{:S(2)}) collective-permute-start(s16[2,64,256]{2,1,0:T(8,128)(2,1)S(1)} %get-tuple-element.42), channel_id=1, source_target_pairs={{0,6},{1,7},{2,4},{3,5},{4,2},{5,3},{6,0},{7,1},{8,14},{9,15},{10,... | collective-permute-start | bytes 196616 | tf_op jit(solution)/shard_map/ppermute | solution.py:235
  26.0 0.4 %collective-permute-start.14 = (s16[2,64,256]{2,1,0:T(8,128)(2,1)S(1)}, s16[2,64,256]{2,1,0:T(8,128)(2,1)S(1)}, u32[]{:S(2)}, u32[]{:S(2)}) collective-permute-start(s16[2,64,256]{2,1,0:T(8,128)(2,1)S(1)} %get-tuple-element.42), channel_id=1, source_target_pairs={{0,4},{1,5},{2,6},{3,7},{4,0},{5,1},{6,2},{7,3},{8,12},{9,13},{10,... | collective-permute-start | bytes 196616 | tf_op jit(solution)/shard_map/ppermute | solution.py:235
  26.5 1.4 %collective-permute-start.13 = (s16[2,64,256]{2,1,0:T(8,128)(2,1)S(1)}, s16[2,64,256]{2,1,0:T(8,128)(2,1)S(1)}, u32[]{:S(2)}, u32[]{:S(2)}) collective-permute-start(s16[2,64,256]{2,1,0:T(8,128)(2,1)S(1)} %get-tuple-element.42), channel_id=1, source_target_pairs={{0,2},{1,3},{2,0},{3,1},{4,6},{5,7},{6,4},{7,5},{8,10},{9,11},{10,... | collective-permute-start | bytes 196616 | tf_op jit(solution)/shard_map/ppermute | solution.py:235
  27.9 0.0 collective-permute-done.5
  27.9 1.6 %collective-permute-start.6 = (s16[4,64,256]{2,1,0:T(8,128)(2,1)S(1)}, s16[4,64,256]{2,1,0:T(8,128)(2,1)S(1)}, u32[]{:S(2)}, u32[]{:S(2)}) collective-permute-start(s16[4,64,256]{2,1,0:T(8,128)(2,1)S(1)} %pad_add_fusion), channel_id=1, source_target_pairs={{0,4},{1,5},{2,6},{3,7},{4,0},{5,1},{6,2},{7,3},{8,12},{9,13},{10,... | collective-permute-start | bytes 393224 | tf_op jit(solution)/shard_map/ppermute | solution.py:235
  29.5 1.3 %collective-permute-done.13 = s16[2,64,256]{2,1,0:T(8,128)(2,1)S(1)} collective-permute-done((s16[2,64,256]{2,1,0:T(8,128)(2,1)S(1)}, s16[2,64,256]{2,1,0:T(8,128)(2,1)S(1)}, u32[]{:S(2)}, u32[]{:S(2)}) %collective-permute-start.13) | collective-permute-done | bytes 65568 | tf_op jit(solution)/shard_map/ppermute | solution.py:235
  30.8 0.0 collective-permute-done.14
  30.9 0.0 collective-permute-done.15
  30.9 0.1 collective-permute-start.16
  31.0 2.0 %collective-permute-done.6 = s16[4,64,256]{2,1,0:T(8,128)(2,1)S(1)} collective-permute-done((s16[4,64,256]{2,1,0:T(8,128)(2,1)S(1)}, s16[4,64,256]{2,1,0:T(8,128)(2,1)S(1)}, u32[]{:S(2)}, u32[]{:S(2)}) %collective-permute-start.6) | collective-permute-done | bytes 131104 | tf_op jit(solution)/shard_map/ppermute | solution.py:235
  33.0 0.1 collective-permute-start.7
  33.0 0.0 collective-permute-done.16.far
  33.0 0.5 %rows1.1 = (bf16[64,256]{1,0:T(8,128)(2,1)S(1)}, bf16[256,1024]{1,0:T(8,128)(2,1)S(1)}) custom-call(f32[64,256]{1,0:T(8,128)S(1)} %get-tuple-element.41.own, s16[8,64,256]{2,1,0:T(8,128)(2,1)S(1)} %constant_dynamic-update-slice_fusion.3.near, s16[8,64,256]{2,1,0:T(8,128)(2,1)S(1)} %collective-permute-done.16.far), custom_call_target="tpu_custom_call" | custom-call | tf_op jit(solution)/shard_map/rows1/pallas_call | solution.py:309
  33.5 1.7 %scores1.1 = (f32[12,128]{1,0:T(8,128)S(1)}, f32[12,128]{1,0:T(8,128)S(1)}) custom-call(s32[12]{0:T(128)S(1)} %copy-done.2, s32[12,128]{1,0:T(8,128)S(1)} %bitcast.28, bf16[1536,1024]{1,0:T(8,128)(2,1)S(1)} %get-tuple-element.26.points, bf16[256,1024]{1,0:T(8,128)(2,1)S(1)} %get-tuple-element.43.cents), custom_call_target="tpu_custom_call" | custom-call | flops 805306368 | bytes 3145728 | tf_op jit(solution)/shard_map/scores1/pallas_call | solution.py:324
  35.2 0.0 collective-permute-done.7.far
  35.2 0.5 %rows0.1 = (bf16[64,256]{1,0:T(8,128)(2,1)S(1)}, bf16[256,1024]{1,0:T(8,128)(2,1)S(1)}) custom-call(f32[64,256]{1,0:T(8,128)S(1)} %get-tuple-element.31.own, s16[8,64,256]{2,1,0:T(8,128)(2,1)S(1)} %constant_dynamic-update-slice_fusion.near, s16[8,64,256]{2,1,0:T(8,128)(2,1)S(1)} %collective-permute-done.7.far), custom_call_target="tpu_custom_call" | custom-call | tf_op jit(solution)/shard_map/rows0/pallas_call | solution.py:309
  35.7 2.3 %scores0.1 = (bf16[128,256]{1,0:T(8,128)(2,1)}, f32[12,128]{1,0:T(8,128)}) custom-call(s32[12]{0:T(128)S(1)} %copy-done.2, s32[12,128]{1,0:T(8,128)S(1)} %bitcast.29, bf16[1536,1024]{1,0:T(8,128)(2,1)S(1)} %get-tuple-element.26.points, bf16[256,1024]{1,0:T(8,128)(2,1)S(1)} %get-tuple-element.33.cents, f32[12,128]{1,0:T(8,128)S(1)} %get-tuple-element.44.refs_0_, ...), custom_call_target="tpu_custom_call" | custom-call | flops 805306368 | bytes 3145728 | tf_op jit(solution)/shard_map/scores0/pallas_call | solution.py:324
  (8 shorter events, 0.1 us)
Async XLA Ops:
  0.6 4.1 %copy-start.2 = (s32[12]{0:T(128)S(1)}, s32[12]{0:T(128)}, u32[]{:S(2)}) copy-start(s32[12]{0:T(128)} %bids.5) | copy-start | bytes 148
  0.6 4.0 %copy-start = (s32[1536]{0:T(1024)S(1)}, s32[1536]{0:T(1024)}, u32[]{:S(2)}) copy-start(s32[1536]{0:T(1024)} %param.7) | copy-start | bytes 18436
  0.7 4.0 %copy-start.1 = (bf16[128,256]{1,0:T(8,128)(2,1)S(1)}, bf16[128,256]{1,0:T(8,128)(2,1)}, u32[]{:S(2)}) copy-start(bf16[128,256]{1,0:T(8,128)(2,1)} %old.1) | copy-start | bytes 196612
  4.1 2.0 %collective-permute-start = (f32[4,2,64,256]{3,2,1,0:T(8,128)S(1)}, f32[4,2,64,256]{3,2,1,0:T(8,128)S(1)}, u32[]{:S(2)}, u32[]{:S(2)}) collective-permute-start(f32[4,2,64,256]{3,2,1,0:T(8,128)S(1)} %get-tuple-element.28), channel_id=1, source_target_pairs={{0,1},{1,0},{2,3},{3,2},{4,5},{5,4},{6,7},{7,6},{8,9},{9,8},{10,11... | collective-permute-start | bytes 1572872 | tf_op jit(solution)/shard_map/ppermute | solution.py:235
  4.6 6.3 %collective-permute-start.8 = (f32[4,2,64,256]{3,2,1,0:T(8,128)S(1)}, f32[4,2,64,256]{3,2,1,0:T(8,128)S(1)}, u32[]{:S(2)}, u32[]{:S(2)}) collective-permute-start(f32[4,2,64,256]{3,2,1,0:T(8,128)S(1)} %get-tuple-element.36), channel_id=1, source_target_pairs={{0,1},{1,0},{2,3},{3,2},{4,5},{5,4},{6,7},{7,6},{8,9},{9,8},{10,11... | collective-permute-start | bytes 1572872 | tf_op jit(solution)/shard_map/ppermute | solution.py:235
  6.3 8.2 %collective-permute-start.3 = (s16[2,64,256]{2,1,0:T(8,128)(2,1)S(1)}, s16[2,64,256]{2,1,0:T(8,128)(2,1)S(1)}, u32[]{:S(2)}, u32[]{:S(2)}) collective-permute-start(s16[2,64,256]{2,1,0:T(8,128)(2,1)S(1)} %get-tuple-element.53), channel_id=1, source_target_pairs={{0,6},{1,7},{2,4},{3,5},{4,2},{5,3},{6,0},{7,1},{8,14},{9,15},{10,... | collective-permute-start | bytes 196616 | tf_op jit(solution)/shard_map/ppermute | solution.py:235
  10.3 4.5 %collective-permute-start.2 = (s16[2,64,256]{2,1,0:T(8,128)(2,1)S(1)}, s16[2,64,256]{2,1,0:T(8,128)(2,1)S(1)}, u32[]{:S(2)}, u32[]{:S(2)}) collective-permute-start(s16[2,64,256]{2,1,0:T(8,128)(2,1)S(1)} %get-tuple-element.54), channel_id=1, source_target_pairs={{0,4},{1,5},{2,6},{3,7},{4,0},{5,1},{6,2},{7,3},{8,12},{9,13},{10,... | collective-permute-start | bytes 196616 | tf_op jit(solution)/shard_map/ppermute | solution.py:235
  10.7 5.0 %collective-permute-start.1 = (s16[2,64,256]{2,1,0:T(8,128)(2,1)S(1)}, s16[2,64,256]{2,1,0:T(8,128)(2,1)S(1)}, u32[]{:S(2)}, u32[]{:S(2)}) collective-permute-start(s16[2,64,256]{2,1,0:T(8,128)(2,1)S(1)} %get-tuple-element.55), channel_id=1, source_target_pairs={{0,2},{1,3},{2,0},{3,1},{4,6},{5,7},{6,4},{7,5},{8,10},{9,11},{10,... | collective-permute-start | bytes 196616 | tf_op jit(solution)/shard_map/ppermute | solution.py:235
  11.1 7.4 %collective-permute-start.11 = (s16[2,64,256]{2,1,0:T(8,128)(2,1)S(1)}, s16[2,64,256]{2,1,0:T(8,128)(2,1)S(1)}, u32[]{:S(2)}, u32[]{:S(2)}) collective-permute-start(s16[2,64,256]{2,1,0:T(8,128)(2,1)S(1)} %get-tuple-element.50), channel_id=1, source_target_pairs={{0,6},{1,7},{2,4},{3,5},{4,2},{5,3},{6,0},{7,1},{8,14},{9,15},{10,... | collective-permute-start | bytes 196616 | tf_op jit(solution)/shard_map/ppermute | solution.py:235
  14.1 4.7 %collective-permute-start.10 = (s16[2,64,256]{2,1,0:T(8,128)(2,1)S(1)}, s16[2,64,256]{2,1,0:T(8,128)(2,1)S(1)}, u32[]{:S(2)}, u32[]{:S(2)}) collective-permute-start(s16[2,64,256]{2,1,0:T(8,128)(2,1)S(1)} %get-tuple-element.51), channel_id=1, source_target_pairs={{0,4},{1,5},{2,6},{3,7},{4,0},{5,1},{6,2},{7,3},{8,12},{9,13},{10,... | collective-permute-start | bytes 196616 | tf_op jit(solution)/shard_map/ppermute | solution.py:235
  14.5 4.3 %collective-permute-start.9 = (s16[2,64,256]{2,1,0:T(8,128)(2,1)S(1)}, s16[2,64,256]{2,1,0:T(8,128)(2,1)S(1)}, u32[]{:S(2)}, u32[]{:S(2)}) collective-permute-start(s16[2,64,256]{2,1,0:T(8,128)(2,1)S(1)} %get-tuple-element.52), channel_id=1, source_target_pairs={{0,2},{1,3},{2,0},{3,1},{4,6},{5,7},{6,4},{7,5},{8,10},{9,11},{10,... | collective-permute-start | bytes 196616 | tf_op jit(solution)/shard_map/ppermute | solution.py:235
  15.9 5.7 %collective-permute-start.4 = (s16[2,64,256]{2,1,0:T(8,128)(2,1)S(1)}, s16[2,64,256]{2,1,0:T(8,128)(2,1)S(1)}, u32[]{:S(2)}, u32[]{:S(2)}) collective-permute-start(s16[2,64,256]{2,1,0:T(8,128)(2,1)S(1)} %get-tuple-element.30), channel_id=1, source_target_pairs={{0,8},{1,9},{2,10},{3,11},{4,12},{5,13},{6,14},{7,15},{8,0},{9,1},... | collective-permute-start | bytes 196616 | tf_op jit(solution)/shard_map/ppermute | solution.py:235
  19.0 5.2 %collective-permute-start.12 = (s16[2,64,256]{2,1,0:T(8,128)(2,1)S(1)}, s16[2,64,256]{2,1,0:T(8,128)(2,1)S(1)}, u32[]{:S(2)}, u32[]{:S(2)}) collective-permute-start(s16[2,64,256]{2,1,0:T(8,128)(2,1)S(1)} %get-tuple-element.40), channel_id=1, source_target_pairs={{0,8},{1,9},{2,10},{3,11},{4,12},{5,13},{6,14},{7,15},{8,0},{9,1},... | collective-permute-start | bytes 196616 | tf_op jit(solution)/shard_map/ppermute | solution.py:235
  21.7 6.1 %collective-permute-start.5 = (s16[2,64,256]{2,1,0:T(8,128)(2,1)S(1)}, s16[2,64,256]{2,1,0:T(8,128)(2,1)S(1)}, u32[]{:S(2)}, u32[]{:S(2)}) collective-permute-start(s16[2,64,256]{2,1,0:T(8,128)(2,1)S(1)} %get-tuple-element.32), channel_id=1, source_target_pairs={{0,2},{1,3},{2,0},{3,1},{4,6},{5,7},{6,4},{7,5},{8,10},{9,11},{10,... | collective-permute-start | bytes 196616 | tf_op jit(solution)/shard_map/ppermute | solution.py:235
  24.3 6.6 %collective-permute-start.15 = (s16[2,64,256]{2,1,0:T(8,128)(2,1)S(1)}, s16[2,64,256]{2,1,0:T(8,128)(2,1)S(1)}, u32[]{:S(2)}, u32[]{:S(2)}) collective-permute-start(s16[2,64,256]{2,1,0:T(8,128)(2,1)S(1)} %get-tuple-element.42), channel_id=1, source_target_pairs={{0,6},{1,7},{2,4},{3,5},{4,2},{5,3},{6,0},{7,1},{8,14},{9,15},{10,... | collective-permute-start | bytes 196616 | tf_op jit(solution)/shard_map/ppermute | solution.py:235
  26.0 4.8 %collective-permute-start.14 = (s16[2,64,256]{2,1,0:T(8,128)(2,1)S(1)}, s16[2,64,256]{2,1,0:T(8,128)(2,1)S(1)}, u32[]{:S(2)}, u32[]{:S(2)}) collective-permute-start(s16[2,64,256]{2,1,0:T(8,128)(2,1)S(1)} %get-tuple-element.42), channel_id=1, source_target_pairs={{0,4},{1,5},{2,6},{3,7},{4,0},{5,1},{6,2},{7,3},{8,12},{9,13},{10,... | collective-permute-start | bytes 196616 | tf_op jit(solution)/shard_map/ppermute | solution.py:235
  26.5 4.4 %collective-permute-start.13 = (s16[2,64,256]{2,1,0:T(8,128)(2,1)S(1)}, s16[2,64,256]{2,1,0:T(8,128)(2,1)S(1)}, u32[]{:S(2)}, u32[]{:S(2)}) collective-permute-start(s16[2,64,256]{2,1,0:T(8,128)(2,1)S(1)} %get-tuple-element.42), channel_id=1, source_target_pairs={{0,2},{1,3},{2,0},{3,1},{4,6},{5,7},{6,4},{7,5},{8,10},{9,11},{10,... | collective-permute-start | bytes 196616 | tf_op jit(solution)/shard_map/ppermute | solution.py:235
  27.9 5.0 %collective-permute-start.6 = (s16[4,64,256]{2,1,0:T(8,128)(2,1)S(1)}, s16[4,64,256]{2,1,0:T(8,128)(2,1)S(1)}, u32[]{:S(2)}, u32[]{:S(2)}) collective-permute-start(s16[4,64,256]{2,1,0:T(8,128)(2,1)S(1)} %pad_add_fusion), channel_id=1, source_target_pairs={{0,4},{1,5},{2,6},{3,7},{4,0},{5,1},{6,2},{7,3},{8,12},{9,13},{10,... | collective-permute-start | bytes 393224 | tf_op jit(solution)/shard_map/ppermute | solution.py:235
  30.9 2.2 %collective-permute-start.16 = (s16[8,64,256]{2,1,0:T(8,128)(2,1)S(1)}, s16[8,64,256]{2,1,0:T(8,128)(2,1)S(1)}, u32[]{:S(2)}, u32[]{:S(2)}) collective-permute-start(s16[8,64,256]{2,1,0:T(8,128)(2,1)S(1)} %constant_dynamic-update-slice_fusion.3.near), channel_id=1, source_target_pairs={{0,1},{1,0},{2,3},{3,2},{4,5},{5,4},{6,7},{7,6},{8,9},{9,8},{10,11... | collective-permute-start | bytes 786440 | tf_op jit(solution)/shard_map/ppermute | solution.py:235
  33.0 2.2 %collective-permute-start.7 = (s16[8,64,256]{2,1,0:T(8,128)(2,1)S(1)}, s16[8,64,256]{2,1,0:T(8,128)(2,1)S(1)}, u32[]{:S(2)}, u32[]{:S(2)}) collective-permute-start(s16[8,64,256]{2,1,0:T(8,128)(2,1)S(1)} %constant_dynamic-update-slice_fusion.near), channel_id=1, source_target_pairs={{0,1},{1,0},{2,3},{3,2},{4,5},{5,4},{6,7},{7,6},{8,9},{9,8},{10,11... | collective-permute-start | bytes 786440 | tf_op jit(solution)/shard_map/ppermute | solution.py:235

commit v12 on v11

--- a/solution.py
+++ b/solution.py
@@ -57,16 +57,18 @@
     return place
 
 
-def add_block(halves, hot, rows_of, over_shard, *, sub, subs, shards, width, flip):
-    group = near_group(subs, shards)
-    late = late_place(late_bits(shards), over_shard)
-    for over_sub in range(0, subs, 2):
+def add_block(sums, hot, rows_of, over_shard, *, sub, shards, width, flip):
+    bits = late_bits(shards)
+    late = late_place(bits, over_shard)
+    count = 1 << len(bits)
+    for over_sub in (0, 2):
         column = pl.multiple_of((sub ^ over_sub ^ flip) * width, width)
         part = jnp.dot(hot, rows_of(pl.ds(column, width)), preferred_element_type=jnp.float32)
-        at = jnp.where(over_shard % 2 == 0, group.index((over_sub, 0)), group.index((over_sub, 1)))
         half_rows = part.shape[0] // 2
-        halves[0][at, late] += part[:half_rows]
-        halves[1][at, late] += part[half_rows:]
+        first = (over_shard % 2 if over_sub == 0 else 1 - over_shard % 2) * 2 * count
+        for half in range(2):
+            rows = part[half * half_rows : (half + 1) * half_rows]
+            sums[over_sub // 2][first + half * count + late] += rows
 
 
 def hot_rows(slots, block, live):
@@ -75,7 +77,7 @@
 
 
 def send_kernel(
-    live_in, bids_in, slots_in, points, first_half, second_half, held, live, bids, slots, small, arrived, *, blocks, group, shards, subs, width
+    live_in, bids_in, slots_in, points, here, there, held, live, bids, slots, small, arrived, *, blocks, group, shards, width
 ):
     sub, shard = lax.axis_index("sub"), lax.axis_index("shard")
     firsts = [
@@ -90,7 +92,7 @@
         span = pl.ds(first * SLOT, group * SLOT)
         copies.append(pltpu.make_async_copy(points.at[span], held.at[span], arrived.at[first // group]))
         copies[-1].start(priority=(first // group) % 2)
-    for sums in (first_half, second_half):
+    for sums in (here, there):
         sums[...] = jnp.zeros_like(sums)
     for copy in firsts:
         copy.wait()
@@ -99,45 +101,45 @@
             copies[block // group].wait()
         span = slice(block * SLOT, (block + 1) * SLOT)
         add_block(
-            (first_half, second_half),
+            (here, there),
             hot_rows(slots, block, live[0]),
             lambda column, span=span: held[span, column],
             bids[block] ^ shard,
             sub=sub,
-            subs=subs,
             shards=shards,
             width=width,
             flip=1,
         )
 
 
-def keep_kernel(live, bids, slots, old, points, first_half, second_half, *, blocks, shards, subs, width):
+def keep_kernel(live, bids, slots, old, points, here, there, *, blocks, shards, width):
     sub, shard = lax.axis_index("sub"), lax.axis_index("shard")
     prior = prior_weight * old[...].astype(jnp.float32)
     half_rows = prior.shape[0] // 2
-    for half, sums in enumerate((first_half, second_half)):
+    for sums in (here, there):
         sums[...] = jnp.zeros_like(sums)
-        sums[0, 0] = prior[half * half_rows : (half + 1) * half_rows]
+    for half in range(2):
+        here[half << len(late_bits(shards))] = prior[half * half_rows : (half + 1) * half_rows]
     for block in range(blocks):
         span = slice(block * SLOT, (block + 1) * SLOT)
         add_block(
-            (first_half, second_half),
+            (here, there),
             hot_rows(slots, block, live[0]),
             lambda column, span=span: points[span, column],
             bids[block] ^ shard,
             sub=sub,
-            subs=subs,
             shards=shards,
             width=width,
             flip=0,
         )
 
 
-def mix_kernel(keep, crossed, *refs, rate):
-    terms, (mine, code) = refs[:-2], refs[-2:]
-    total = keep[0] + crossed[0]
-    for term in terms:
-        total = total + decode(term[...], rate)
+def mix_kernel(keep, crossed, by_z, by_x, both, mine, code, *, half, rate):
+    count = mine.shape[0]
+    span = slice(half * count, (half + 1) * count)
+    total = keep[span] + crossed[span]
+    for term in (both[span], by_x[...], by_z[...]):
+        total = total + decode(term, rate)
     mine[...] = total
     code[...] = encode(total, rate)
 
@@ -234,12 +236,15 @@
                 pairs.append((shard * subs + sub, (shard ^ over_shard) * subs + (sub ^ over_sub)))
         return lax.ppermute(value, ("shard", "sub"), pairs)
 
+    def after(value, *others):
+        return lax.optimization_barrier((value, *others))[0] if others else value
+
     def in_hbm(value):
         return pltpu.with_memory_space_constraint(value, pltpu.HBM)
 
-    shape = jax.ShapeDtypeStruct((len(chips), late, half_rows, width), jnp.float32)
+    shape = jax.ShapeDtypeStruct((4 * late, half_rows, width), jnp.float32)
     cost = pl.CostEstimate(flops=row_count * SLOT * feat_width, bytes_accessed=row_count * feat_width, transcendentals=0)
-    sizes = dict(blocks=blocks, shards=shards, subs=subs, width=width)
+    sizes = dict(blocks=blocks, shards=shards, width=width)
     *send, held = pl.pallas_call(
         functools.partial(send_kernel, group=group, **sizes),
         out_shape=(shape, shape, jax.ShapeDtypeStruct(points.shape, points.dtype)),
@@ -270,21 +275,16 @@
     piece = (late, half_rows, width)
     two = (2, half_rows, width)
 
-    def after(value, *others):
-        return lax.optimization_barrier((value, *others))[0] if others else value
-
-    def reduce_near(half, *earlier):
-        there = after(crossed[half], *earlier)
-        codes = [encode(keep[half][index] + there[index], rate) for index in range(1, len(chips))]
-        return codes, [swap(code, *chip) for code, chip in zip(codes, chips[1:])]
-
-    def reduce_late(half, terms, *earlier):
+    def near_code(side, first, end, *earlier):
+        return encode(keep[side][first:end] + after(crossed[side], *earlier)[first:end], rate)
+
+    def reduce_late(half, by_x, by_z, *earlier):
         mine, code = pl.pallas_call(
-            functools.partial(mix_kernel, rate=rate),
+            functools.partial(mix_kernel, half=half, rate=rate),
             out_shape=(jax.ShapeDtypeStruct(piece, jnp.float32), jax.ShapeDtypeStruct(piece, jnp.int16)),
             compiler_params=limit,
             name=f"mix{half}",
-        )(after(keep[half], *earlier), crossed[half], *terms)
+        )(after(keep[0], *earlier), crossed[0], by_z, by_x, both)
         for bit in bits[:-1]:
             count = mine.shape[0] // 2
             mine = mine[:count] + decode(swap(encode(mine[count:], rate), 0, bit), rate)
@@ -337,16 +337,24 @@
             name=f"scores{half}",
         )(block_ids, slots, held, cents, *earlier)
 
-    first_codes, first_terms = reduce_near(0)
-    _, second_terms = reduce_near(1, *first_codes)
-    first = reduce_late(0, first_terms)
-    second = reduce_late(1, second_terms, first[0])
+    diagonal = near_code(1, 0, 2 * late)
+    both = swap(diagonal, 2, 1)
+    by_x = near_code(1, 2 * late, 3 * late, diagonal)
+    by_z = near_code(0, 2 * late, 3 * late, diagonal)
+    first_terms = swap(by_x, 2, 0), swap(by_z, 0, 1)
+    second_terms = (
+        swap(near_code(1, 3 * late, 4 * late, by_x, by_z), 2, 0),
+        swap(near_code(0, 3 * late, 4 * late, by_x, by_z), 0, 1),
+    )
+    first = reduce_late(0, *first_terms)
+    second = reduce_late(1, *second_terms, first[0])
     first_own, first_code = finish(0, *first)
     second_own, second_code = finish(1, *second, first_code)
     own, codes = (first_own, second_own), (first_code, second_code)
     near = jnp.concatenate([codes[0], swap(codes[0], 2, 0)])
+    ready = [after(codes[1], near), after(codes[1], near), codes[1]]
     near = [jnp.concatenate([near, swap(near, 0, 1)])]
-    near.append(jnp.concatenate([codes[1]] + [swap(codes[1], *chip) for chip in chips[1:]]))
+    near.append(jnp.concatenate([codes[1]] + [swap(code, *chip) for code, chip in zip(ready, chips[1:])]))
     far = [swap(block, 1, 0) for block in near]
     second_fresh, second_rows = rows_of(1, own[1], near[1], far[1])
     mine, rival = scores(1, False, second_rows)

time: 38.2 us -> 41.4 us (1.084)
  the two profiles are of different devices: /device:TPU:0 before, /device:TPU:17 now
where the time goes in v12:
time: 41.4 us; the launch traced here: 41.2 us
  starting transfers between devices  23.9 us (58%)
  Pallas kernels  9.42 us (23%)
  waiting for transfers between devices  5.88 us (14%)
  between operations  1.47 us (4%)
  other arithmetic  0.44 us (1%)
    ppermute x16, starting transfers between devices, swap(): return lax.ppermute(value, ('shard', 'sub'), pairs)  23.9 us
    ppermute x16, waiting for transfers between devices, swap(): return lax.ppermute(value, ('shard', 'sub'), pairs)  5.88 us
    pallas_call x2, Pallas kernels, scores(): pl.pallas_call(functools.partial(score_kernel, half=half, last=last, bloc...  3.93 us
    pallas_call x1, Pallas kernels, local(): pl.pallas_call(functools.partial(send_kernel, group=group, **sizes), out_...  2.72 us
    pallas_call x1, Pallas kernels, local(): pl.pallas_call(functools.partial(keep_kernel, **sizes), out_shape=(shape,...  1.25 us
    pallas_call x2, Pallas kernels, rows_of(): pl.pallas_call(functools.partial(rows_kernel, half=half, shards=shards, s...  0.95 us
  transfers between devices with their start and end apart: 16, of which 7 were waited for; matrix products, arithmetic and copies ran while one was open for 1% of the time, Pallas kernels for 10%

profile of v12, /device:TPU:17, one launch (start us, length us, event | category | flops | bytes accessed | tf_op | source)
XLA Modules:
  0.0 41.2 jit_solution(5431806052041557512)
XLA Ops:
  0.6 0.0 copy-start.2
  0.6 0.0 copy-start
  0.7 0.0 copy-start.1
  1.3 2.7 %sums_send.1 = (f32[8,64,256]{2,1,0:T(8,128)S(1)}, f32[8,64,256]{2,1,0:T(8,128)S(1)}, bf16[1536,1024]{1,0:T(8,128)(2,1)S(1)}) custom-call(s32[1]{0:T(128)S(6)} %copy.13.live_in.live, s32[12]{0:T(128)} %bids.5, s32[12,128]{1,0:T(8,128)} %bitcast.2, bf16[1536,1024]{1,0:T(8,128)(2,1)} %points.1), custom_call_target="tpu_custom_call" | custom-call | flops 201326592 | bytes 1572864 | tf_op jit(solution)/shard_map/sums_send/pallas_call | solution.py:248
  4.1 0.7 %collective-permute-start.1 = (f32[8,64,256]{2,1,0:T(8,128)S(1)}, f32[8,64,256]{2,1,0:T(8,128)S(1)}, u32[]{:S(2)}, u32[]{:S(2)}) collective-permute-start(f32[8,64,256]{2,1,0:T(8,128)S(1)} %get-tuple-element.34), channel_id=1, source_target_pairs={{0,1},{1,0},{2,3},{3,2},{4,5},{5,4},{6,7},{7,6},{8,9},{9,8},{10,11... | collective-permute-start | bytes 1572872 | tf_op jit(solution)/shard_map/ppermute | solution.py:237
  4.8 0.1 collective-permute-start
  4.9 0.0 copy-done.2
  4.9 0.0 copy-done
  4.9 0.0 copy-done.1
  4.9 1.2 %sums_keep.1 = (f32[8,64,256]{2,1,0:T(8,128)S(1)}, f32[8,64,256]{2,1,0:T(8,128)S(1)}) custom-call(s32[1]{0:T(128)S(6)} %copy.13.live_in.live, s32[12]{0:T(128)S(1)} %copy-done.2, s32[12,128]{1,0:T(8,128)S(1)} %bitcast.3, bf16[128,256]{1,0:T(8,128)(2,1)S(1)} %copy-done.1, bf16[1536,1024]{1,0:T(8,128)(2,1)S(1)} %get-tuple-element.30.points), custom_call_target="tpu_custom_call" | custom-call | flops 201326592 | bytes 1572864 | tf_op jit(solution)/shard_map/sums_keep/pallas_call | solution.py:265
  6.1 0.2 collective-permute-done.1
  6.3 0.1 fusion.1
  6.5 2.3 %collective-permute-start.4 = (s16[4,64,256]{2,1,0:T(8,128)(2,1)S(1)}, s16[4,64,256]{2,1,0:T(8,128)(2,1)S(1)}, u32[]{:S(2)}, u32[]{:S(2)}) collective-permute-start(s16[4,64,256]{2,1,0:T(8,128)(2,1)S(1)} %fusion.1), channel_id=1, source_target_pairs={{0,6},{1,7},{2,4},{3,5},{4,2},{5,3},{6,0},{7,1},{8,14},{9,15},{10,... | collective-permute-start | bytes 393224 | tf_op jit(solution)/shard_map/ppermute | solution.py:237
  8.8 0.0 collective-permute-done.crossed
  8.8 0.1 fusion.5
  8.8 0.3 collective-permute-start.3
  9.2 0.1 fusion.3
  9.2 0.6 %collective-permute-start.2 = (s16[2,64,256]{2,1,0:T(8,128)(2,1)S(1)}, s16[2,64,256]{2,1,0:T(8,128)(2,1)S(1)}, u32[]{:S(2)}, u32[]{:S(2)}) collective-permute-start(s16[2,64,256]{2,1,0:T(8,128)(2,1)S(1)} %fusion.3), channel_id=1, source_target_pairs={{0,4},{1,5},{2,6},{3,7},{4,0},{5,1},{6,2},{7,3},{8,12},{9,13},{10,... | collective-permute-start | bytes 196616 | tf_op jit(solution)/shard_map/ppermute | solution.py:237
  9.9 0.1 fusion.9
  10.0 0.1 fusion.7
  10.0 1.0 %collective-permute-start.9 = (s16[2,64,256]{2,1,0:T(8,128)(2,1)S(1)}, s16[2,64,256]{2,1,0:T(8,128)(2,1)S(1)}, u32[]{:S(2)}, u32[]{:S(2)}) collective-permute-start(s16[2,64,256]{2,1,0:T(8,128)(2,1)S(1)} %fusion.7), channel_id=1, source_target_pairs={{0,4},{1,5},{2,6},{3,7},{4,0},{5,1},{6,2},{7,3},{8,12},{9,13},{10,... | collective-permute-start | bytes 196616 | tf_op jit(solution)/shard_map/ppermute | solution.py:237
  11.0 1.2 %collective-permute-start.10 = (s16[2,64,256]{2,1,0:T(8,128)(2,1)S(1)}, s16[2,64,256]{2,1,0:T(8,128)(2,1)S(1)}, u32[]{:S(2)}, u32[]{:S(2)}) collective-permute-start(s16[2,64,256]{2,1,0:T(8,128)(2,1)S(1)} %fusion.9), channel_id=1, source_target_pairs={{0,2},{1,3},{2,0},{3,1},{4,6},{5,7},{6,4},{7,5},{8,10},{9,11},{10,... | collective-permute-start | bytes 196616 | tf_op jit(solution)/shard_map/ppermute | solution.py:237
  12.2 2.1 %collective-permute-done.3.by_x = s16[2,64,256]{2,1,0:T(8,128)(2,1)S(1)} collective-permute-done((s16[2,64,256]{2,1,0:T(8,128)(2,1)S(1)}, s16[2,64,256]{2,1,0:T(8,128)(2,1)S(1)}, u32[]{:S(2)}, u32[]{:S(2)}) %collective-permute-start.3) | collective-permute-done | bytes 65568 | tf_op jit(solution)/shard_map/ppermute | solution.py:237
  14.3 0.0 collective-permute-done.2.by_z
  14.3 0.0 collective-permute-done.4.both
  14.3 0.2 mix0.1
  14.5 0.1 collective-permute-start.5
  14.5 0.4 %collective-permute-done.9.by_z = s16[2,64,256]{2,1,0:T(8,128)(2,1)S(1)} collective-permute-done((s16[2,64,256]{2,1,0:T(8,128)(2,1)S(1)}, s16[2,64,256]{2,1,0:T(8,128)(2,1)S(1)}, u32[]{:S(2)}, u32[]{:S(2)}) %collective-permute-start.9) | collective-permute-done | bytes 65568 | tf_op jit(solution)/shard_map/ppermute | solution.py:237
  15.0 0.1 collective-permute-done.10.by_x
  15.1 0.2 mix1.1
  15.3 1.9 %collective-permute-start.11 = (s16[2,64,256]{2,1,0:T(8,128)(2,1)S(1)}, s16[2,64,256]{2,1,0:T(8,128)(2,1)S(1)}, u32[]{:S(2)}, u32[]{:S(2)}) collective-permute-start(s16[2,64,256]{2,1,0:T(8,128)(2,1)S(1)} %get-tuple-element.47), channel_id=1, source_target_pairs={{0,8},{1,9},{2,10},{3,11},{4,12},{5,13},{6,14},{7,15},{8,0},{9,1},... | collective-permute-start | bytes 196616 | tf_op jit(solution)/shard_map/ppermute | solution.py:237
  17.2 1.4 %collective-permute-done.5.there = s16[2,64,256]{2,1,0:T(8,128)(2,1)S(1)} collective-permute-done((s16[2,64,256]{2,1,0:T(8,128)(2,1)S(1)}, s16[2,64,256]{2,1,0:T(8,128)(2,1)S(1)}, u32[]{:S(2)}, u32[]{:S(2)}) %collective-permute-start.5) | collective-permute-done | bytes 65568 | tf_op jit(solution)/shard_map/ppermute | solution.py:237
  18.6 0.1 finish0.1
  18.7 1.3 %collective-permute-start.6 = (s16[2,64,256]{2,1,0:T(8,128)(2,1)S(1)}, s16[2,64,256]{2,1,0:T(8,128)(2,1)S(1)}, u32[]{:S(2)}, u32[]{:S(2)}) collective-permute-start(s16[2,64,256]{2,1,0:T(8,128)(2,1)S(1)} %get-tuple-element.40), channel_id=1, source_target_pairs={{0,2},{1,3},{2,0},{3,1},{4,6},{5,7},{6,4},{7,5},{8,10},{9,11},{10,... | collective-permute-start | bytes 196616 | tf_op jit(solution)/shard_map/ppermute | solution.py:237
  20.0 0.0 collective-permute-done.11.there
  20.0 0.1 finish1.1
  20.1 5.1 %collective-permute-start.14 = (s16[2,64,256]{2,1,0:T(8,128)(2,1)S(1)}, s16[2,64,256]{2,1,0:T(8,128)(2,1)S(1)}, u32[]{:S(2)}, u32[]{:S(2)}) collective-permute-start(s16[2,64,256]{2,1,0:T(8,128)(2,1)S(1)} %get-tuple-element.50), channel_id=1, source_target_pairs={{0,6},{1,7},{2,4},{3,5},{4,2},{5,3},{6,0},{7,1},{8,14},{9,15},{10,... | collective-permute-start | bytes 196616 | tf_op jit(solution)/shard_map/ppermute | solution.py:237
  25.3 0.0 collective-permute-done.6
  25.3 0.8 %collective-permute-start.12 = (s16[2,64,256]{2,1,0:T(8,128)(2,1)S(1)}, s16[2,64,256]{2,1,0:T(8,128)(2,1)S(1)}, u32[]{:S(2)}, u32[]{:S(2)}) collective-permute-start(s16[2,64,256]{2,1,0:T(8,128)(2,1)S(1)} %get-tuple-element.50), channel_id=1, source_target_pairs={{0,2},{1,3},{2,0},{3,1},{4,6},{5,7},{6,4},{7,5},{8,10},{9,11},{10,... | collective-permute-start | bytes 196616 | tf_op jit(solution)/shard_map/ppermute | solution.py:237
  26.1 0.6 %collective-permute-start.13 = (s16[2,64,256]{2,1,0:T(8,128)(2,1)S(1)}, s16[2,64,256]{2,1,0:T(8,128)(2,1)S(1)}, u32[]{:S(2)}, u32[]{:S(2)}) collective-permute-start(s16[2,64,256]{2,1,0:T(8,128)(2,1)S(1)} %get-tuple-element.50), channel_id=1, source_target_pairs={{0,4},{1,5},{2,6},{3,7},{4,0},{5,1},{6,2},{7,3},{8,12},{9,13},{10,... | collective-permute-start | bytes 196616 | tf_op jit(solution)/shard_map/ppermute | solution.py:237
  26.7 0.9 %collective-permute-start.7 = (s16[4,64,256]{2,1,0:T(8,128)(2,1)S(1)}, s16[4,64,256]{2,1,0:T(8,128)(2,1)S(1)}, u32[]{:S(2)}, u32[]{:S(2)}) collective-permute-start(s16[4,64,256]{2,1,0:T(8,128)(2,1)S(1)} %get-tuple-element.58), channel_id=1, source_target_pairs={{0,4},{1,5},{2,6},{3,7},{4,0},{5,1},{6,2},{7,3},{8,12},{9,13},{10,... | collective-permute-start | bytes 393224 | tf_op jit(solution)/shard_map/ppermute | solution.py:237
  27.6 1.1 %collective-permute-done.12 = s16[2,64,256]{2,1,0:T(8,128)(2,1)S(1)} collective-permute-done((s16[2,64,256]{2,1,0:T(8,128)(2,1)S(1)}, s16[2,64,256]{2,1,0:T(8,128)(2,1)S(1)}, u32[]{:S(2)}, u32[]{:S(2)}) %collective-permute-start.12) | collective-permute-done | bytes 65568 | tf_op jit(solution)/shard_map/ppermute | solution.py:237
  28.7 0.6 %collective-permute-done.13 = s16[2,64,256]{2,1,0:T(8,128)(2,1)S(1)} collective-permute-done((s16[2,64,256]{2,1,0:T(8,128)(2,1)S(1)}, s16[2,64,256]{2,1,0:T(8,128)(2,1)S(1)}, u32[]{:S(2)}, u32[]{:S(2)}) %collective-permute-start.13) | collective-permute-done | bytes 65568 | tf_op jit(solution)/shard_map/ppermute | solution.py:237
  29.3 0.0 collective-permute-done.14
  29.3 4.3 %collective-permute-start.15 = (s16[8,64,256]{2,1,0:T(8,128)(2,1)S(1)}, s16[8,64,256]{2,1,0:T(8,128)(2,1)S(1)}, u32[]{:S(2)}, u32[]{:S(2)}) collective-permute-start(s16[8,64,256]{2,1,0:T(8,128)(2,1)S(1)} %constant_dynamic-update-slice_fusion.5.near), channel_id=1, source_target_pairs={{0,1},{1,0},{2,3},{3,2},{4,5},{5,4},{6,7},{7,6},{8,9},{9,8},{10,11... | collective-permute-start | bytes 786440 | tf_op jit(solution)/shard_map/ppermute | solution.py:237
  33.6 0.0 collective-permute-done.7
  33.6 2.7 %collective-permute-start.8 = (s16[8,64,256]{2,1,0:T(8,128)(2,1)S(1)}, s16[8,64,256]{2,1,0:T(8,128)(2,1)S(1)}, u32[]{:S(2)}, u32[]{:S(2)}) collective-permute-start(s16[8,64,256]{2,1,0:T(8,128)(2,1)S(1)} %constant_dynamic-update-slice_fusion.2.near), channel_id=1, source_target_pairs={{0,1},{1,0},{2,3},{3,2},{4,5},{5,4},{6,7},{7,6},{8,9},{9,8},{10,11... | collective-permute-start | bytes 786440 | tf_op jit(solution)/shard_map/ppermute | solution.py:237
  36.3 0.0 collective-permute-done.15.far
  36.3 0.5 %rows1.1 = (bf16[64,256]{1,0:T(8,128)(2,1)S(1)}, bf16[256,1024]{1,0:T(8,128)(2,1)S(1)}) custom-call(f32[64,256]{1,0:T(8,128)S(1)} %get-tuple-element.48.own, s16[8,64,256]{2,1,0:T(8,128)(2,1)S(1)} %constant_dynamic-update-slice_fusion.5.near, s16[8,64,256]{2,1,0:T(8,128)(2,1)S(1)} %collective-permute-done.15.far), custom_call_target="tpu_custom_call" | custom-call | tf_op jit(solution)/shard_map/rows1/pallas_call | solution.py:309
  36.8 1.7 %scores1.1 = (f32[12,128]{1,0:T(8,128)S(1)}, f32[12,128]{1,0:T(8,128)S(1)}) custom-call(s32[12]{0:T(128)S(1)} %copy-done.2, s32[12,128]{1,0:T(8,128)S(1)} %bitcast.4, bf16[1536,1024]{1,0:T(8,128)(2,1)S(1)} %get-tuple-element.30.points, bf16[256,1024]{1,0:T(8,128)(2,1)S(1)} %get-tuple-element.51.cents), custom_call_target="tpu_custom_call" | custom-call | flops 805306368 | bytes 3145728 | tf_op jit(solution)/shard_map/scores1/pallas_call | solution.py:324
  38.4 0.0 collective-permute-done.8.far
  38.5 0.5 %rows0.1 = (bf16[64,256]{1,0:T(8,128)(2,1)S(1)}, bf16[256,1024]{1,0:T(8,128)(2,1)S(1)}) custom-call(f32[64,256]{1,0:T(8,128)S(1)} %get-tuple-element.39.own, s16[8,64,256]{2,1,0:T(8,128)(2,1)S(1)} %constant_dynamic-update-slice_fusion.2.near, s16[8,64,256]{2,1,0:T(8,128)(2,1)S(1)} %collective-permute-done.8.far), custom_call_target="tpu_custom_call" | custom-call | tf_op jit(solution)/shard_map/rows0/pallas_call | solution.py:309
  38.9 2.3 %scores0.1 = (bf16[128,256]{1,0:T(8,128)(2,1)}, f32[12,128]{1,0:T(8,128)}) custom-call(s32[12]{0:T(128)S(1)} %copy-done.2, s32[12,128]{1,0:T(8,128)S(1)} %bitcast.5, bf16[1536,1024]{1,0:T(8,128)(2,1)S(1)} %get-tuple-element.30.points, bf16[256,1024]{1,0:T(8,128)(2,1)S(1)} %get-tuple-element.41.cents, f32[12,128]{1,0:T(8,128)S(1)} %get-tuple-element.52.refs_0_, ...), custom_call_target="tpu_custom_call" | custom-call | flops 805306368 | bytes 3145728 | tf_op jit(solution)/shard_map/scores0/pallas_call | solution.py:324
  (7 shorter events, 0.1 us)
Async XLA Ops:
  0.6 4.3 %copy-start.2 = (s32[12]{0:T(128)S(1)}, s32[12]{0:T(128)}, u32[]{:S(2)}) copy-start(s32[12]{0:T(128)} %bids.5) | copy-start | bytes 148
  0.6 4.2 %copy-start = (s32[1536]{0:T(1024)S(1)}, s32[1536]{0:T(1024)}, u32[]{:S(2)}) copy-start(s32[1536]{0:T(1024)} %param.7) | copy-start | bytes 18436
  0.7 4.2 %copy-start.1 = (bf16[128,256]{1,0:T(8,128)(2,1)S(1)}, bf16[128,256]{1,0:T(8,128)(2,1)}, u32[]{:S(2)}) copy-start(bf16[128,256]{1,0:T(8,128)(2,1)} %old.1) | copy-start | bytes 196612
  4.1 2.3 %collective-permute-start.1 = (f32[8,64,256]{2,1,0:T(8,128)S(1)}, f32[8,64,256]{2,1,0:T(8,128)S(1)}, u32[]{:S(2)}, u32[]{:S(2)}) collective-permute-start(f32[8,64,256]{2,1,0:T(8,128)S(1)} %get-tuple-element.34), channel_id=1, source_target_pairs={{0,1},{1,0},{2,3},{3,2},{4,5},{5,4},{6,7},{7,6},{8,9},{9,8},{10,11... | collective-permute-start | bytes 1572872 | tf_op jit(solution)/shard_map/ppermute | solution.py:237
  4.8 4.0 %collective-permute-start = (f32[8,64,256]{2,1,0:T(8,128)S(1)}, f32[8,64,256]{2,1,0:T(8,128)S(1)}, u32[]{:S(2)}, u32[]{:S(2)}) collective-permute-start(f32[8,64,256]{2,1,0:T(8,128)S(1)} %get-tuple-element.32), channel_id=1, source_target_pairs={{0,1},{1,0},{2,3},{3,2},{4,5},{5,4},{6,7},{7,6},{8,9},{9,8},{10,11... | collective-permute-start | bytes 1572872 | tf_op jit(solution)/shard_map/ppermute | solution.py:237
  6.5 7.8 %collective-permute-start.4 = (s16[4,64,256]{2,1,0:T(8,128)(2,1)S(1)}, s16[4,64,256]{2,1,0:T(8,128)(2,1)S(1)}, u32[]{:S(2)}, u32[]{:S(2)}) collective-permute-start(s16[4,64,256]{2,1,0:T(8,128)(2,1)S(1)} %fusion.1), channel_id=1, source_target_pairs={{0,6},{1,7},{2,4},{3,5},{4,2},{5,3},{6,0},{7,1},{8,14},{9,15},{10,... | collective-permute-start | bytes 393224 | tf_op jit(solution)/shard_map/ppermute | solution.py:237
  8.8 5.4 %collective-permute-start.3 = (s16[2,64,256]{2,1,0:T(8,128)(2,1)S(1)}, s16[2,64,256]{2,1,0:T(8,128)(2,1)S(1)}, u32[]{:S(2)}, u32[]{:S(2)}) collective-permute-start(s16[2,64,256]{2,1,0:T(8,128)(2,1)S(1)} %fusion.5), channel_id=1, source_target_pairs={{0,2},{1,3},{2,0},{3,1},{4,6},{5,7},{6,4},{7,5},{8,10},{9,11},{10,... | collective-permute-start | bytes 196616 | tf_op jit(solution)/shard_map/ppermute | solution.py:237
  9.2 5.0 %collective-permute-start.2 = (s16[2,64,256]{2,1,0:T(8,128)(2,1)S(1)}, s16[2,64,256]{2,1,0:T(8,128)(2,1)S(1)}, u32[]{:S(2)}, u32[]{:S(2)}) collective-permute-start(s16[2,64,256]{2,1,0:T(8,128)(2,1)S(1)} %fusion.3), channel_id=1, source_target_pairs={{0,4},{1,5},{2,6},{3,7},{4,0},{5,1},{6,2},{7,3},{8,12},{9,13},{10,... | collective-permute-start | bytes 196616 | tf_op jit(solution)/shard_map/ppermute | solution.py:237
  10.0 5.0 %collective-permute-start.9 = (s16[2,64,256]{2,1,0:T(8,128)(2,1)S(1)}, s16[2,64,256]{2,1,0:T(8,128)(2,1)S(1)}, u32[]{:S(2)}, u32[]{:S(2)}) collective-permute-start(s16[2,64,256]{2,1,0:T(8,128)(2,1)S(1)} %fusion.7), channel_id=1, source_target_pairs={{0,4},{1,5},{2,6},{3,7},{4,0},{5,1},{6,2},{7,3},{8,12},{9,13},{10,... | collective-permute-start | bytes 196616 | tf_op jit(solution)/shard_map/ppermute | solution.py:237
  11.0 4.1 %collective-permute-start.10 = (s16[2,64,256]{2,1,0:T(8,128)(2,1)S(1)}, s16[2,64,256]{2,1,0:T(8,128)(2,1)S(1)}, u32[]{:S(2)}, u32[]{:S(2)}) collective-permute-start(s16[2,64,256]{2,1,0:T(8,128)(2,1)S(1)} %fusion.9), channel_id=1, source_target_pairs={{0,2},{1,3},{2,0},{3,1},{4,6},{5,7},{6,4},{7,5},{8,10},{9,11},{10,... | collective-permute-start | bytes 196616 | tf_op jit(solution)/shard_map/ppermute | solution.py:237
  14.5 4.1 %collective-permute-start.5 = (s16[2,64,256]{2,1,0:T(8,128)(2,1)S(1)}, s16[2,64,256]{2,1,0:T(8,128)(2,1)S(1)}, u32[]{:S(2)}, u32[]{:S(2)}) collective-permute-start(s16[2,64,256]{2,1,0:T(8,128)(2,1)S(1)} %get-tuple-element.38), channel_id=1, source_target_pairs={{0,8},{1,9},{2,10},{3,11},{4,12},{5,13},{6,14},{7,15},{8,0},{9,1},... | collective-permute-start | bytes 196616 | tf_op jit(solution)/shard_map/ppermute | solution.py:237
  15.3 4.8 %collective-permute-start.11 = (s16[2,64,256]{2,1,0:T(8,128)(2,1)S(1)}, s16[2,64,256]{2,1,0:T(8,128)(2,1)S(1)}, u32[]{:S(2)}, u32[]{:S(2)}) collective-permute-start(s16[2,64,256]{2,1,0:T(8,128)(2,1)S(1)} %get-tuple-element.47), channel_id=1, source_target_pairs={{0,8},{1,9},{2,10},{3,11},{4,12},{5,13},{6,14},{7,15},{8,0},{9,1},... | collective-permute-start | bytes 196616 | tf_op jit(solution)/shard_map/ppermute | solution.py:237
  18.7 6.5 %collective-permute-start.6 = (s16[2,64,256]{2,1,0:T(8,128)(2,1)S(1)}, s16[2,64,256]{2,1,0:T(8,128)(2,1)S(1)}, u32[]{:S(2)}, u32[]{:S(2)}) collective-permute-start(s16[2,64,256]{2,1,0:T(8,128)(2,1)S(1)} %get-tuple-element.40), channel_id=1, source_target_pairs={{0,2},{1,3},{2,0},{3,1},{4,6},{5,7},{6,4},{7,5},{8,10},{9,11},{10,... | collective-permute-start | bytes 196616 | tf_op jit(solution)/shard_map/ppermute | solution.py:237
  20.1 9.1 %collective-permute-start.14 = (s16[2,64,256]{2,1,0:T(8,128)(2,1)S(1)}, s16[2,64,256]{2,1,0:T(8,128)(2,1)S(1)}, u32[]{:S(2)}, u32[]{:S(2)}) collective-permute-start(s16[2,64,256]{2,1,0:T(8,128)(2,1)S(1)} %get-tuple-element.50), channel_id=1, source_target_pairs={{0,6},{1,7},{2,4},{3,5},{4,2},{5,3},{6,0},{7,1},{8,14},{9,15},{10,... | collective-permute-start | bytes 196616 | tf_op jit(solution)/shard_map/ppermute | solution.py:237
  25.3 3.4 %collective-permute-start.12 = (s16[2,64,256]{2,1,0:T(8,128)(2,1)S(1)}, s16[2,64,256]{2,1,0:T(8,128)(2,1)S(1)}, u32[]{:S(2)}, u32[]{:S(2)}) collective-permute-start(s16[2,64,256]{2,1,0:T(8,128)(2,1)S(1)} %get-tuple-element.50), channel_id=1, source_target_pairs={{0,2},{1,3},{2,0},{3,1},{4,6},{5,7},{6,4},{7,5},{8,10},{9,11},{10,... | collective-permute-start | bytes 196616 | tf_op jit(solution)/shard_map/ppermute | solution.py:237
  26.1 3.1 %collective-permute-start.13 = (s16[2,64,256]{2,1,0:T(8,128)(2,1)S(1)}, s16[2,64,256]{2,1,0:T(8,128)(2,1)S(1)}, u32[]{:S(2)}, u32[]{:S(2)}) collective-permute-start(s16[2,64,256]{2,1,0:T(8,128)(2,1)S(1)} %get-tuple-element.50), channel_id=1, source_target_pairs={{0,4},{1,5},{2,6},{3,7},{4,0},{5,1},{6,2},{7,3},{8,12},{9,13},{10,... | collective-permute-start | bytes 196616 | tf_op jit(solution)/shard_map/ppermute | solution.py:237
  26.7 6.9 %collective-permute-start.7 = (s16[4,64,256]{2,1,0:T(8,128)(2,1)S(1)}, s16[4,64,256]{2,1,0:T(8,128)(2,1)S(1)}, u32[]{:S(2)}, u32[]{:S(2)}) collective-permute-start(s16[4,64,256]{2,1,0:T(8,128)(2,1)S(1)} %get-tuple-element.58), channel_id=1, source_target_pairs={{0,4},{1,5},{2,6},{3,7},{4,0},{5,1},{6,2},{7,3},{8,12},{9,13},{10,... | collective-permute-start | bytes 393224 | tf_op jit(solution)/shard_map/ppermute | solution.py:237
  29.3 7.0 %collective-permute-start.15 = (s16[8,64,256]{2,1,0:T(8,128)(2,1)S(1)}, s16[8,64,256]{2,1,0:T(8,128)(2,1)S(1)}, u32[]{:S(2)}, u32[]{:S(2)}) collective-permute-start(s16[8,64,256]{2,1,0:T(8,128)(2,1)S(1)} %constant_dynamic-update-slice_fusion.5.near), channel_id=1, source_target_pairs={{0,1},{1,0},{2,3},{3,2},{4,5},{5,4},{6,7},{7,6},{8,9},{9,8},{10,11... | collective-permute-start | bytes 786440 | tf_op jit(solution)/shard_map/ppermute | solution.py:237
  33.6 4.8 %collective-permute-start.8 = (s16[8,64,256]{2,1,0:T(8,128)(2,1)S(1)}, s16[8,64,256]{2,1,0:T(8,128)(2,1)S(1)}, u32[]{:S(2)}, u32[]{:S(2)}) collective-permute-start(s16[8,64,256]{2,1,0:T(8,128)(2,1)S(1)} %constant_dynamic-update-slice_fusion.2.near), channel_id=1, source_target_pairs={{0,1},{1,0},{2,3},{3,2},{4,5},{5,4},{6,7},{7,6},{8,9},{9,8},{10,11... | collective-permute-start | bytes 786440 | tf_op jit(solution)/shard_map/ppermute | solution.py:237

commit v13 on v11

--- a/solution.py
+++ b/solution.py
@@ -221,7 +221,6 @@
     chips = near_group(subs, shards)
     bits = late_bits(shards)
     late = 1 << len(bits)
-    group = 2 if blocks % 2 == 0 else 1
     limit = pltpu.CompilerParams(vmem_limit_bytes=8 * MIB + 4 * total * feat_width)
     smem = pl.BlockSpec(memory_space=pltpu.SMEM)
     vmem = pl.BlockSpec(memory_space=pltpu.VMEM)
@@ -241,7 +240,7 @@
     cost = pl.CostEstimate(flops=row_count * SLOT * feat_width, bytes_accessed=row_count * feat_width, transcendentals=0)
     sizes = dict(blocks=blocks, shards=shards, subs=subs, width=width)
     *send, held = pl.pallas_call(
-        functools.partial(send_kernel, group=group, **sizes),
+        functools.partial(send_kernel, group=1, **sizes),
         out_shape=(shape, shape, jax.ShapeDtypeStruct(points.shape, points.dtype)),
         in_specs=[hbm] * 4,
         out_specs=(vmem, vmem, vmem),
@@ -250,7 +249,7 @@
             pltpu.SMEM((blocks,), jnp.int32),
             pltpu.VMEM((blocks, SLOT), jnp.int32),
             pltpu.SemaphoreType.DMA((3,)),
-            pltpu.SemaphoreType.DMA((blocks // group,)),
+            pltpu.SemaphoreType.DMA((blocks,)),
         ],
         compiler_params=limit,
         cost_estimate=cost,
@@ -323,7 +322,7 @@
         fresh = jax.ShapeDtypeStruct((rows, width), jnp.bfloat16)
         return pl.pallas_call(
             functools.partial(
-                score_kernel, half=half, last=last, blocks=blocks, shards=shards, rows=rows, group=group
+                score_kernel, half=half, last=last, blocks=blocks, shards=shards, rows=rows, group=math.gcd(blocks, 4)
             ),
             out_shape=(fresh, line) if last else (line, line),
             in_specs=[smem] + [vmem] * (3 + len(earlier)),

time: 38.2 us -> 39 us (1.021)
  Pallas kernels: 9.5 us -> 10.3 us
    pallas_call x1, Pallas kernels: 2.75 us -> 3.59 us  [local(): pl.pallas_call(functools.partial(send_kernel, group=1, **sizes), out_shap...]
  transfers between devices with their start and end apart: 17 -> 17, of which waited for: 8 -> 8; matrix products, arithmetic and copies ran while one was open for 1% -> 1% of each run, Pallas kernels for 11% -> 10%
where the time goes in v13:
time: 39 us; the launch traced here: 38.8 us
  starting transfers between devices  20.2 us (52%)
  Pallas kernels  10.3 us (26%)
  waiting for transfers between devices  6.25 us (16%)
  between operations  1.49 us (4%)
  other arithmetic  0.42 us (1%)
    ppermute x17, starting transfers between devices, swap(): return lax.ppermute(value, ('shard', 'sub'), pairs)  20.2 us
    ppermute x17, waiting for transfers between devices, swap(): return lax.ppermute(value, ('shard', 'sub'), pairs)  6.25 us
    pallas_call x2, Pallas kernels, scores(): pl.pallas_call(functools.partial(score_kernel, half=half, last=last, bloc...  3.93 us
    pallas_call x1, Pallas kernels, local(): pl.pallas_call(functools.partial(send_kernel, group=1, **sizes), out_shap...  3.59 us
    pallas_call x1, Pallas kernels, local(): pl.pallas_call(functools.partial(keep_kernel, **sizes), out_shape=(shape,...  1.29 us
    pallas_call x2, Pallas kernels, rows_of(): pl.pallas_call(functools.partial(rows_kernel, half=half, shards=shards, s...  0.95 us
  transfers between devices with their start and end apart: 17, of which 8 were waited for; matrix products, arithmetic and copies ran while one was open for 1% of the time, Pallas kernels for 10%

profile of v13, /device:TPU:0, one launch (start us, length us, event | category | flops | bytes accessed | tf_op | source)
XLA Modules:
  0.0 38.8 jit_solution(12325249554358338255)
XLA Ops:
  0.6 0.0 copy-start.2
  0.6 0.0 copy-start
  0.7 0.0 copy-start.1
  1.3 3.6 %sums_send.1 = (f32[4,2,64,256]{3,2,1,0:T(8,128)S(1)}, f32[4,2,64,256]{3,2,1,0:T(8,128)S(1)}, bf16[1536,1024]{1,0:T(8,128)(2,1)S(1)}) custom-call(s32[1]{0:T(128)S(6)} %copy.12.live_in.live, s32[12]{0:T(128)} %bids.5, s32[12,128]{1,0:T(8,128)} %bitcast.26, bf16[1536,1024]{1,0:T(8,128)(2,1)} %points.1), custom_call_target="tpu_custom_call" | custom-call | flops 201326592 | bytes 1572864 | tf_op jit(solution)/shard_map/sums_send/pallas_call | solution.py:242
  4.9 0.5 %collective-permute-start = (f32[4,2,64,256]{3,2,1,0:T(8,128)S(1)}, f32[4,2,64,256]{3,2,1,0:T(8,128)S(1)}, u32[]{:S(2)}, u32[]{:S(2)}) collective-permute-start(f32[4,2,64,256]{3,2,1,0:T(8,128)S(1)} %get-tuple-element.28), channel_id=1, source_target_pairs={{0,1},{1,0},{2,3},{3,2},{4,5},{5,4},{6,7},{7,6},{8,9},{9,8},{10,11... | collective-permute-start | bytes 1572872 | tf_op jit(solution)/shard_map/ppermute | solution.py:234
  5.5 0.1 collective-permute-start.8
  5.5 0.0 copy-done.2
  5.5 0.0 copy-done
  5.5 0.0 copy-done.1
  5.5 1.3 %sums_keep.1 = (f32[4,2,64,256]{3,2,1,0:T(8,128)S(1)}, f32[4,2,64,256]{3,2,1,0:T(8,128)S(1)}) custom-call(s32[1]{0:T(128)S(6)} %copy.12.live_in.live, s32[12]{0:T(128)S(1)} %copy-done.2, s32[12,128]{1,0:T(8,128)S(1)} %bitcast.27, bf16[128,256]{1,0:T(8,128)(2,1)S(1)} %copy-done.1, bf16[1536,1024]{1,0:T(8,128)(2,1)S(1)} %get-tuple-element.26.points), custom_call_target="tpu_custom_call" | custom-call | flops 201326592 | bytes 1572864 | tf_op jit(solution)/shard_map/sums_keep/pallas_call | solution.py:259
  6.8 0.2 collective-permute-done.crossed
  7.0 0.2 fusion.5
  7.2 3.9 %collective-permute-start.3 = (s16[2,64,256]{2,1,0:T(8,128)(2,1)S(1)}, s16[2,64,256]{2,1,0:T(8,128)(2,1)S(1)}, u32[]{:S(2)}, u32[]{:S(2)}) collective-permute-start(s16[2,64,256]{2,1,0:T(8,128)(2,1)S(1)} %get-tuple-element.53), channel_id=1, source_target_pairs={{0,6},{1,7},{2,4},{3,5},{4,2},{5,3},{6,0},{7,1},{8,14},{9,15},{10,... | collective-permute-start | bytes 196616 | tf_op jit(solution)/shard_map/ppermute | solution.py:234
  11.1 0.4 %collective-permute-start.2 = (s16[2,64,256]{2,1,0:T(8,128)(2,1)S(1)}, s16[2,64,256]{2,1,0:T(8,128)(2,1)S(1)}, u32[]{:S(2)}, u32[]{:S(2)}) collective-permute-start(s16[2,64,256]{2,1,0:T(8,128)(2,1)S(1)} %get-tuple-element.54), channel_id=1, source_target_pairs={{0,4},{1,5},{2,6},{3,7},{4,0},{5,1},{6,2},{7,3},{8,12},{9,13},{10,... | collective-permute-start | bytes 196616 | tf_op jit(solution)/shard_map/ppermute | solution.py:234
  11.6 0.2 collective-permute-start.1
  11.8 0.0 collective-permute-done.8.crossed
  11.8 0.2 fusion.11
  12.0 2.9 %collective-permute-start.11 = (s16[2,64,256]{2,1,0:T(8,128)(2,1)S(1)}, s16[2,64,256]{2,1,0:T(8,128)(2,1)S(1)}, u32[]{:S(2)}, u32[]{:S(2)}) collective-permute-start(s16[2,64,256]{2,1,0:T(8,128)(2,1)S(1)} %get-tuple-element.50), channel_id=1, source_target_pairs={{0,6},{1,7},{2,4},{3,5},{4,2},{5,3},{6,0},{7,1},{8,14},{9,15},{10,... | collective-permute-start | bytes 196616 | tf_op jit(solution)/shard_map/ppermute | solution.py:234
  14.9 0.4 %collective-permute-start.10 = (s16[2,64,256]{2,1,0:T(8,128)(2,1)S(1)}, s16[2,64,256]{2,1,0:T(8,128)(2,1)S(1)}, u32[]{:S(2)}, u32[]{:S(2)}) collective-permute-start(s16[2,64,256]{2,1,0:T(8,128)(2,1)S(1)} %get-tuple-element.51), channel_id=1, source_target_pairs={{0,4},{1,5},{2,6},{3,7},{4,0},{5,1},{6,2},{7,3},{8,12},{9,13},{10,... | collective-permute-start | bytes 196616 | tf_op jit(solution)/shard_map/ppermute | solution.py:234
  15.4 0.0 collective-permute-done.3.refs_2_
  15.4 0.2 collective-permute-start.9
  15.6 0.1 collective-permute-done.2.refs_1_
  15.7 0.9 %collective-permute-done.1.refs_0_ = s16[2,64,256]{2,1,0:T(8,128)(2,1)S(1)} collective-permute-done((s16[2,64,256]{2,1,0:T(8,128)(2,1)S(1)}, s16[2,64,256]{2,1,0:T(8,128)(2,1)S(1)}, u32[]{:S(2)}, u32[]{:S(2)}) %collective-permute-start.1) | collective-permute-done | bytes 65568 | tf_op jit(solution)/shard_map/ppermute | solution.py:234
  16.5 0.2 mix0.1
  16.7 2.7 %collective-permute-start.4 = (s16[2,64,256]{2,1,0:T(8,128)(2,1)S(1)}, s16[2,64,256]{2,1,0:T(8,128)(2,1)S(1)}, u32[]{:S(2)}, u32[]{:S(2)}) collective-permute-start(s16[2,64,256]{2,1,0:T(8,128)(2,1)S(1)} %get-tuple-element.30), channel_id=1, source_target_pairs={{0,8},{1,9},{2,10},{3,11},{4,12},{5,13},{6,14},{7,15},{8,0},{9,1},... | collective-permute-start | bytes 196616 | tf_op jit(solution)/shard_map/ppermute | solution.py:234
  19.4 0.0 collective-permute-done.11.refs_2_
  19.4 0.2 collective-permute-done.10.refs_1_
  19.6 0.1 collective-permute-done.9.refs_0_
  19.6 0.2 mix1.1
  19.8 2.7 %collective-permute-start.12 = (s16[2,64,256]{2,1,0:T(8,128)(2,1)S(1)}, s16[2,64,256]{2,1,0:T(8,128)(2,1)S(1)}, u32[]{:S(2)}, u32[]{:S(2)}) collective-permute-start(s16[2,64,256]{2,1,0:T(8,128)(2,1)S(1)} %get-tuple-element.40), channel_id=1, source_target_pairs={{0,8},{1,9},{2,10},{3,11},{4,12},{5,13},{6,14},{7,15},{8,0},{9,1},... | collective-permute-start | bytes 196616 | tf_op jit(solution)/shard_map/ppermute | solution.py:234
  22.5 0.0 collective-permute-done.4.there
  22.5 0.1 finish0.1
  22.6 0.8 %collective-permute-start.5 = (s16[2,64,256]{2,1,0:T(8,128)(2,1)S(1)}, s16[2,64,256]{2,1,0:T(8,128)(2,1)S(1)}, u32[]{:S(2)}, u32[]{:S(2)}) collective-permute-start(s16[2,64,256]{2,1,0:T(8,128)(2,1)S(1)} %get-tuple-element.32), channel_id=1, source_target_pairs={{0,2},{1,3},{2,0},{3,1},{4,6},{5,7},{6,4},{7,5},{8,10},{9,11},{10,... | collective-permute-start | bytes 196616 | tf_op jit(solution)/shard_map/ppermute | solution.py:234
  23.4 1.7 %collective-permute-done.12.there = s16[2,64,256]{2,1,0:T(8,128)(2,1)S(1)} collective-permute-done((s16[2,64,256]{2,1,0:T(8,128)(2,1)S(1)}, s16[2,64,256]{2,1,0:T(8,128)(2,1)S(1)}, u32[]{:S(2)}, u32[]{:S(2)}) %collective-permute-start.12) | collective-permute-done | bytes 65568 | tf_op jit(solution)/shard_map/ppermute | solution.py:234
  25.0 0.1 finish1.1
  25.1 1.7 %collective-permute-start.15 = (s16[2,64,256]{2,1,0:T(8,128)(2,1)S(1)}, s16[2,64,256]{2,1,0:T(8,128)(2,1)S(1)}, u32[]{:S(2)}, u32[]{:S(2)}) collective-permute-start(s16[2,64,256]{2,1,0:T(8,128)(2,1)S(1)} %get-tuple-element.42), channel_id=1, source_target_pairs={{0,6},{1,7},{2,4},{3,5},{4,2},{5,3},{6,0},{7,1},{8,14},{9,15},{10,... | collective-permute-start | bytes 196616 | tf_op jit(solution)/shard_map/ppermute | solution.py:234
  26.9 0.4 %collective-permute-start.14 = (s16[2,64,256]{2,1,0:T(8,128)(2,1)S(1)}, s16[2,64,256]{2,1,0:T(8,128)(2,1)S(1)}, u32[]{:S(2)}, u32[]{:S(2)}) collective-permute-start(s16[2,64,256]{2,1,0:T(8,128)(2,1)S(1)} %get-tuple-element.42), channel_id=1, source_target_pairs={{0,4},{1,5},{2,6},{3,7},{4,0},{5,1},{6,2},{7,3},{8,12},{9,13},{10,... | collective-permute-start | bytes 196616 | tf_op jit(solution)/shard_map/ppermute | solution.py:234
  27.3 1.4 %collective-permute-start.13 = (s16[2,64,256]{2,1,0:T(8,128)(2,1)S(1)}, s16[2,64,256]{2,1,0:T(8,128)(2,1)S(1)}, u32[]{:S(2)}, u32[]{:S(2)}) collective-permute-start(s16[2,64,256]{2,1,0:T(8,128)(2,1)S(1)} %get-tuple-element.42), channel_id=1, source_target_pairs={{0,2},{1,3},{2,0},{3,1},{4,6},{5,7},{6,4},{7,5},{8,10},{9,11},{10,... | collective-permute-start | bytes 196616 | tf_op jit(solution)/shard_map/ppermute | solution.py:234
  28.7 0.0 collective-permute-done.5
  28.7 1.6 %collective-permute-start.6 = (s16[4,64,256]{2,1,0:T(8,128)(2,1)S(1)}, s16[4,64,256]{2,1,0:T(8,128)(2,1)S(1)}, u32[]{:S(2)}, u32[]{:S(2)}) collective-permute-start(s16[4,64,256]{2,1,0:T(8,128)(2,1)S(1)} %pad_add_fusion), channel_id=1, source_target_pairs={{0,4},{1,5},{2,6},{3,7},{4,0},{5,1},{6,2},{7,3},{8,12},{9,13},{10,... | collective-permute-start | bytes 393224 | tf_op jit(solution)/shard_map/ppermute | solution.py:234
  30.4 1.3 %collective-permute-done.13 = s16[2,64,256]{2,1,0:T(8,128)(2,1)S(1)} collective-permute-done((s16[2,64,256]{2,1,0:T(8,128)(2,1)S(1)}, s16[2,64,256]{2,1,0:T(8,128)(2,1)S(1)}, u32[]{:S(2)}, u32[]{:S(2)}) %collective-permute-start.13) | collective-permute-done | bytes 65568 | tf_op jit(solution)/shard_map/ppermute | solution.py:234
  31.7 0.0 collective-permute-done.14
  31.7 0.0 collective-permute-done.15
  31.7 0.1 collective-permute-start.16
  31.8 2.0 %collective-permute-done.6 = s16[4,64,256]{2,1,0:T(8,128)(2,1)S(1)} collective-permute-done((s16[4,64,256]{2,1,0:T(8,128)(2,1)S(1)}, s16[4,64,256]{2,1,0:T(8,128)(2,1)S(1)}, u32[]{:S(2)}, u32[]{:S(2)}) %collective-permute-start.6) | collective-permute-done | bytes 131104 | tf_op jit(solution)/shard_map/ppermute | solution.py:234
  33.8 0.1 collective-permute-start.7
  33.9 0.0 collective-permute-done.16.far
  33.9 0.5 %rows1.1 = (bf16[64,256]{1,0:T(8,128)(2,1)S(1)}, bf16[256,1024]{1,0:T(8,128)(2,1)S(1)}) custom-call(f32[64,256]{1,0:T(8,128)S(1)} %get-tuple-element.41.own, s16[8,64,256]{2,1,0:T(8,128)(2,1)S(1)} %constant_dynamic-update-slice_fusion.3.near, s16[8,64,256]{2,1,0:T(8,128)(2,1)S(1)} %collective-permute-done.16.far), custom_call_target="tpu_custom_call" | custom-call | tf_op jit(solution)/shard_map/rows1/pallas_call | solution.py:308
  34.4 1.7 %scores1.1 = (f32[12,128]{1,0:T(8,128)S(1)}, f32[12,128]{1,0:T(8,128)S(1)}) custom-call(s32[12]{0:T(128)S(1)} %copy-done.2, s32[12,128]{1,0:T(8,128)S(1)} %bitcast.28, bf16[1536,1024]{1,0:T(8,128)(2,1)S(1)} %get-tuple-element.26.points, bf16[256,1024]{1,0:T(8,128)(2,1)S(1)} %get-tuple-element.43.cents), custom_call_target="tpu_custom_call" | custom-call | flops 805306368 | bytes 3145728 | tf_op jit(solution)/shard_map/scores1/pallas_call | solution.py:323
  36.0 0.0 collective-permute-done.7.far
  36.0 0.5 %rows0.1 = (bf16[64,256]{1,0:T(8,128)(2,1)S(1)}, bf16[256,1024]{1,0:T(8,128)(2,1)S(1)}) custom-call(f32[64,256]{1,0:T(8,128)S(1)} %get-tuple-element.31.own, s16[8,64,256]{2,1,0:T(8,128)(2,1)S(1)} %constant_dynamic-update-slice_fusion.near, s16[8,64,256]{2,1,0:T(8,128)(2,1)S(1)} %collective-permute-done.7.far), custom_call_target="tpu_custom_call" | custom-call | tf_op jit(solution)/shard_map/rows0/pallas_call | solution.py:308
  36.5 2.3 %scores0.1 = (bf16[128,256]{1,0:T(8,128)(2,1)}, f32[12,128]{1,0:T(8,128)}) custom-call(s32[12]{0:T(128)S(1)} %copy-done.2, s32[12,128]{1,0:T(8,128)S(1)} %bitcast.29, bf16[1536,1024]{1,0:T(8,128)(2,1)S(1)} %get-tuple-element.26.points, bf16[256,1024]{1,0:T(8,128)(2,1)S(1)} %get-tuple-element.33.cents, f32[12,128]{1,0:T(8,128)S(1)} %get-tuple-element.44.refs_0_, ...), custom_call_target="tpu_custom_call" | custom-call | flops 805306368 | bytes 3145728 | tf_op jit(solution)/shard_map/scores0/pallas_call | solution.py:323
  (8 shorter events, 0.1 us)
Async XLA Ops:
  0.6 4.9 %copy-start.2 = (s32[12]{0:T(128)S(1)}, s32[12]{0:T(128)}, u32[]{:S(2)}) copy-start(s32[12]{0:T(128)} %bids.5) | copy-start | bytes 148
  0.6 4.9 %copy-start = (s32[1536]{0:T(1024)S(1)}, s32[1536]{0:T(1024)}, u32[]{:S(2)}) copy-start(s32[1536]{0:T(1024)} %param.7) | copy-start | bytes 18436
  0.7 4.9 %copy-start.1 = (bf16[128,256]{1,0:T(8,128)(2,1)S(1)}, bf16[128,256]{1,0:T(8,128)(2,1)}, u32[]{:S(2)}) copy-start(bf16[128,256]{1,0:T(8,128)(2,1)} %old.1) | copy-start | bytes 196612
  4.9 2.1 %collective-permute-start = (f32[4,2,64,256]{3,2,1,0:T(8,128)S(1)}, f32[4,2,64,256]{3,2,1,0:T(8,128)S(1)}, u32[]{:S(2)}, u32[]{:S(2)}) collective-permute-start(f32[4,2,64,256]{3,2,1,0:T(8,128)S(1)} %get-tuple-element.28), channel_id=1, source_target_pairs={{0,1},{1,0},{2,3},{3,2},{4,5},{5,4},{6,7},{7,6},{8,9},{9,8},{10,11... | collective-permute-start | bytes 1572872 | tf_op jit(solution)/shard_map/ppermute | solution.py:234
  5.5 6.3 %collective-permute-start.8 = (f32[4,2,64,256]{3,2,1,0:T(8,128)S(1)}, f32[4,2,64,256]{3,2,1,0:T(8,128)S(1)}, u32[]{:S(2)}, u32[]{:S(2)}) collective-permute-start(f32[4,2,64,256]{3,2,1,0:T(8,128)S(1)} %get-tuple-element.36), channel_id=1, source_target_pairs={{0,1},{1,0},{2,3},{3,2},{4,5},{5,4},{6,7},{7,6},{8,9},{9,8},{10,11... | collective-permute-start | bytes 1572872 | tf_op jit(solution)/shard_map/ppermute | solution.py:234
  7.2 8.2 %collective-permute-start.3 = (s16[2,64,256]{2,1,0:T(8,128)(2,1)S(1)}, s16[2,64,256]{2,1,0:T(8,128)(2,1)S(1)}, u32[]{:S(2)}, u32[]{:S(2)}) collective-permute-start(s16[2,64,256]{2,1,0:T(8,128)(2,1)S(1)} %get-tuple-element.53), channel_id=1, source_target_pairs={{0,6},{1,7},{2,4},{3,5},{4,2},{5,3},{6,0},{7,1},{8,14},{9,15},{10,... | collective-permute-start | bytes 196616 | tf_op jit(solution)/shard_map/ppermute | solution.py:234
  11.1 4.5 %collective-permute-start.2 = (s16[2,64,256]{2,1,0:T(8,128)(2,1)S(1)}, s16[2,64,256]{2,1,0:T(8,128)(2,1)S(1)}, u32[]{:S(2)}, u32[]{:S(2)}) collective-permute-start(s16[2,64,256]{2,1,0:T(8,128)(2,1)S(1)} %get-tuple-element.54), channel_id=1, source_target_pairs={{0,4},{1,5},{2,6},{3,7},{4,0},{5,1},{6,2},{7,3},{8,12},{9,13},{10,... | collective-permute-start | bytes 196616 | tf_op jit(solution)/shard_map/ppermute | solution.py:234
  11.6 5.0 %collective-permute-start.1 = (s16[2,64,256]{2,1,0:T(8,128)(2,1)S(1)}, s16[2,64,256]{2,1,0:T(8,128)(2,1)S(1)}, u32[]{:S(2)}, u32[]{:S(2)}) collective-permute-start(s16[2,64,256]{2,1,0:T(8,128)(2,1)S(1)} %get-tuple-element.55), channel_id=1, source_target_pairs={{0,2},{1,3},{2,0},{3,1},{4,6},{5,7},{6,4},{7,5},{8,10},{9,11},{10,... | collective-permute-start | bytes 196616 | tf_op jit(solution)/shard_map/ppermute | solution.py:234
  12.0 7.4 %collective-permute-start.11 = (s16[2,64,256]{2,1,0:T(8,128)(2,1)S(1)}, s16[2,64,256]{2,1,0:T(8,128)(2,1)S(1)}, u32[]{:S(2)}, u32[]{:S(2)}) collective-permute-start(s16[2,64,256]{2,1,0:T(8,128)(2,1)S(1)} %get-tuple-element.50), channel_id=1, source_target_pairs={{0,6},{1,7},{2,4},{3,5},{4,2},{5,3},{6,0},{7,1},{8,14},{9,15},{10,... | collective-permute-start | bytes 196616 | tf_op jit(solution)/shard_map/ppermute | solution.py:234
  14.9 4.7 %collective-permute-start.10 = (s16[2,64,256]{2,1,0:T(8,128)(2,1)S(1)}, s16[2,64,256]{2,1,0:T(8,128)(2,1)S(1)}, u32[]{:S(2)}, u32[]{:S(2)}) collective-permute-start(s16[2,64,256]{2,1,0:T(8,128)(2,1)S(1)} %get-tuple-element.51), channel_id=1, source_target_pairs={{0,4},{1,5},{2,6},{3,7},{4,0},{5,1},{6,2},{7,3},{8,12},{9,13},{10,... | collective-permute-start | bytes 196616 | tf_op jit(solution)/shard_map/ppermute | solution.py:234
  15.4 4.3 %collective-permute-start.9 = (s16[2,64,256]{2,1,0:T(8,128)(2,1)S(1)}, s16[2,64,256]{2,1,0:T(8,128)(2,1)S(1)}, u32[]{:S(2)}, u32[]{:S(2)}) collective-permute-start(s16[2,64,256]{2,1,0:T(8,128)(2,1)S(1)} %get-tuple-element.52), channel_id=1, source_target_pairs={{0,2},{1,3},{2,0},{3,1},{4,6},{5,7},{6,4},{7,5},{8,10},{9,11},{10,... | collective-permute-start | bytes 196616 | tf_op jit(solution)/shard_map/ppermute | solution.py:234
  16.7 5.7 %collective-permute-start.4 = (s16[2,64,256]{2,1,0:T(8,128)(2,1)S(1)}, s16[2,64,256]{2,1,0:T(8,128)(2,1)S(1)}, u32[]{:S(2)}, u32[]{:S(2)}) collective-permute-start(s16[2,64,256]{2,1,0:T(8,128)(2,1)S(1)} %get-tuple-element.30), channel_id=1, source_target_pairs={{0,8},{1,9},{2,10},{3,11},{4,12},{5,13},{6,14},{7,15},{8,0},{9,1},... | collective-permute-start | bytes 196616 | tf_op jit(solution)/shard_map/ppermute | solution.py:234
  19.8 5.2 %collective-permute-start.12 = (s16[2,64,256]{2,1,0:T(8,128)(2,1)S(1)}, s16[2,64,256]{2,1,0:T(8,128)(2,1)S(1)}, u32[]{:S(2)}, u32[]{:S(2)}) collective-permute-start(s16[2,64,256]{2,1,0:T(8,128)(2,1)S(1)} %get-tuple-element.40), channel_id=1, source_target_pairs={{0,8},{1,9},{2,10},{3,11},{4,12},{5,13},{6,14},{7,15},{8,0},{9,1},... | collective-permute-start | bytes 196616 | tf_op jit(solution)/shard_map/ppermute | solution.py:234
  22.6 6.1 %collective-permute-start.5 = (s16[2,64,256]{2,1,0:T(8,128)(2,1)S(1)}, s16[2,64,256]{2,1,0:T(8,128)(2,1)S(1)}, u32[]{:S(2)}, u32[]{:S(2)}) collective-permute-start(s16[2,64,256]{2,1,0:T(8,128)(2,1)S(1)} %get-tuple-element.32), channel_id=1, source_target_pairs={{0,2},{1,3},{2,0},{3,1},{4,6},{5,7},{6,4},{7,5},{8,10},{9,11},{10,... | collective-permute-start | bytes 196616 | tf_op jit(solution)/shard_map/ppermute | solution.py:234
  25.1 6.5 %collective-permute-start.15 = (s16[2,64,256]{2,1,0:T(8,128)(2,1)S(1)}, s16[2,64,256]{2,1,0:T(8,128)(2,1)S(1)}, u32[]{:S(2)}, u32[]{:S(2)}) collective-permute-start(s16[2,64,256]{2,1,0:T(8,128)(2,1)S(1)} %get-tuple-element.42), channel_id=1, source_target_pairs={{0,6},{1,7},{2,4},{3,5},{4,2},{5,3},{6,0},{7,1},{8,14},{9,15},{10,... | collective-permute-start | bytes 196616 | tf_op jit(solution)/shard_map/ppermute | solution.py:234
  26.9 4.8 %collective-permute-start.14 = (s16[2,64,256]{2,1,0:T(8,128)(2,1)S(1)}, s16[2,64,256]{2,1,0:T(8,128)(2,1)S(1)}, u32[]{:S(2)}, u32[]{:S(2)}) collective-permute-start(s16[2,64,256]{2,1,0:T(8,128)(2,1)S(1)} %get-tuple-element.42), channel_id=1, source_target_pairs={{0,4},{1,5},{2,6},{3,7},{4,0},{5,1},{6,2},{7,3},{8,12},{9,13},{10,... | collective-permute-start | bytes 196616 | tf_op jit(solution)/shard_map/ppermute | solution.py:234
  27.3 4.4 %collective-permute-start.13 = (s16[2,64,256]{2,1,0:T(8,128)(2,1)S(1)}, s16[2,64,256]{2,1,0:T(8,128)(2,1)S(1)}, u32[]{:S(2)}, u32[]{:S(2)}) collective-permute-start(s16[2,64,256]{2,1,0:T(8,128)(2,1)S(1)} %get-tuple-element.42), channel_id=1, source_target_pairs={{0,2},{1,3},{2,0},{3,1},{4,6},{5,7},{6,4},{7,5},{8,10},{9,11},{10,... | collective-permute-start | bytes 196616 | tf_op jit(solution)/shard_map/ppermute | solution.py:234
  28.7 5.0 %collective-permute-start.6 = (s16[4,64,256]{2,1,0:T(8,128)(2,1)S(1)}, s16[4,64,256]{2,1,0:T(8,128)(2,1)S(1)}, u32[]{:S(2)}, u32[]{:S(2)}) collective-permute-start(s16[4,64,256]{2,1,0:T(8,128)(2,1)S(1)} %pad_add_fusion), channel_id=1, source_target_pairs={{0,4},{1,5},{2,6},{3,7},{4,0},{5,1},{6,2},{7,3},{8,12},{9,13},{10,... | collective-permute-start | bytes 393224 | tf_op jit(solution)/shard_map/ppermute | solution.py:234
  31.7 2.2 %collective-permute-start.16 = (s16[8,64,256]{2,1,0:T(8,128)(2,1)S(1)}, s16[8,64,256]{2,1,0:T(8,128)(2,1)S(1)}, u32[]{:S(2)}, u32[]{:S(2)}) collective-permute-start(s16[8,64,256]{2,1,0:T(8,128)(2,1)S(1)} %constant_dynamic-update-slice_fusion.3.near), channel_id=1, source_target_pairs={{0,1},{1,0},{2,3},{3,2},{4,5},{5,4},{6,7},{7,6},{8,9},{9,8},{10,11... | collective-permute-start | bytes 786440 | tf_op jit(solution)/shard_map/ppermute | solution.py:234
  33.8 2.2 %collective-permute-start.7 = (s16[8,64,256]{2,1,0:T(8,128)(2,1)S(1)}, s16[8,64,256]{2,1,0:T(8,128)(2,1)S(1)}, u32[]{:S(2)}, u32[]{:S(2)}) collective-permute-start(s16[8,64,256]{2,1,0:T(8,128)(2,1)S(1)} %constant_dynamic-update-slice_fusion.near), channel_id=1, source_target_pairs={{0,1},{1,0},{2,3},{3,2},{4,5},{5,4},{6,7},{7,6},{8,9},{9,8},{10,11... | collective-permute-start | bytes 786440 | tf_op jit(solution)/shard_map/ppermute | solution.py:234

commit v14 on v11

--- a/solution.py
+++ b/solution.py
@@ -75,7 +75,7 @@
 
 
 def send_kernel(
-    live_in, bids_in, slots_in, points, first_half, second_half, held, live, bids, slots, small, arrived, *, blocks, group, shards, subs, width
+    live_in, bids_in, slots_in, points, first_half, second_half, held, live, bids, slots, small, arrived, *, blocks, parts, shards, subs, width
 ):
     sub, shard = lax.axis_index("sub"), lax.axis_index("shard")
     firsts = [
@@ -85,18 +85,20 @@
     ]
     for copy in firsts:
         copy.start()
-    copies = []
-    for first in range(0, blocks, group):
-        span = pl.ds(first * SLOT, group * SLOT)
-        copies.append(pltpu.make_async_copy(points.at[span], held.at[span], arrived.at[first // group]))
-        copies[-1].start(priority=(first // group) % 2)
+    copies = {}
+    first = 0
+    for part, count in enumerate(parts):
+        span = pl.ds(first * SLOT, count * SLOT)
+        copies[first] = pltpu.make_async_copy(points.at[span], held.at[span], arrived.at[part])
+        copies[first].start(priority=part % 2)
+        first += count
     for sums in (first_half, second_half):
         sums[...] = jnp.zeros_like(sums)
     for copy in firsts:
         copy.wait()
     for block in range(blocks):
-        if block % group == 0:
-            copies[block // group].wait()
+        if block in copies:
+            copies[block].wait()
         span = slice(block * SLOT, (block + 1) * SLOT)
         add_block(
             (first_half, second_half),
@@ -148,18 +150,26 @@
     code[1] = encode(mine[1] + decode(there[0], rate), rate)
 
 
-def rows_kernel(own, near, far, fresh, cents, *, half, shards, subs, rows, width, rate):
+def rows_kernel(own, *refs, shards, subs, rows, width, rate):
     chips = near_group(subs, shards)
     sub, shard = lax.axis_index("sub"), lax.axis_index("shard")
     bits = late_bits(shards)
     late_count = 1 << len(bits)
     half_rows = rows // 2
+    fresh, cents = refs[-2:]
+    count = (len(refs) - 2) // 2
+    near, far = refs[:count], refs[count : 2 * count]
+
+    def piece_of(blocks, piece):
+        each = blocks[0].shape[0]
+        return decode(blocks[piece // each][piece % each], rate)
+
     for over_shard in range(shards):
         parts = []
         for over_sub in range(0, subs, 2):
             piece = chips.index((over_sub, over_shard % 2)) * late_count + late_place(bits, over_shard)
-            parts.append((sub ^ over_sub, decode(near[piece], rate)))
-            parts.append((sub ^ 1 ^ over_sub, decode(far[piece], rate)))
+            parts.append((sub ^ over_sub, piece_of(near, piece)))
+            parts.append((sub ^ 1 ^ over_sub, piece_of(far, piece)))
         squares = sum(jnp.sum(part * part, axis=1, keepdims=True) for _, part in parts)
         scale = lax.rsqrt(squares + norm_eps)
         row = pl.ds(pl.multiple_of((shard ^ over_shard) * half_rows, half_rows), half_rows)
@@ -222,6 +232,7 @@
     bits = late_bits(shards)
     late = 1 << len(bits)
     group = 2 if blocks % 2 == 0 else 1
+    parts = [count for count in (blocks // 2, blocks // 3, blocks - blocks // 2 - blocks // 3) if count]
     limit = pltpu.CompilerParams(vmem_limit_bytes=8 * MIB + 4 * total * feat_width)
     smem = pl.BlockSpec(memory_space=pltpu.SMEM)
     vmem = pl.BlockSpec(memory_space=pltpu.VMEM)
@@ -241,7 +252,7 @@
     cost = pl.CostEstimate(flops=row_count * SLOT * feat_width, bytes_accessed=row_count * feat_width, transcendentals=0)
     sizes = dict(blocks=blocks, shards=shards, subs=subs, width=width)
     *send, held = pl.pallas_call(
-        functools.partial(send_kernel, group=group, **sizes),
+        functools.partial(send_kernel, parts=parts, **sizes),
         out_shape=(shape, shape, jax.ShapeDtypeStruct(points.shape, points.dtype)),
         in_specs=[hbm] * 4,
         out_specs=(vmem, vmem, vmem),
@@ -250,7 +261,7 @@
             pltpu.SMEM((blocks,), jnp.int32),
             pltpu.VMEM((blocks, SLOT), jnp.int32),
             pltpu.SemaphoreType.DMA((3,)),
-            pltpu.SemaphoreType.DMA((blocks // group,)),
+            pltpu.SemaphoreType.DMA((len(parts),)),
         ],
         compiler_params=limit,
         cost_estimate=cost,
@@ -308,7 +319,7 @@
     def rows_of(half, own, near, far):
         return pl.pallas_call(
             functools.partial(
-                rows_kernel, half=half, shards=shards, subs=subs, rows=rows, width=width, rate=rate
+                rows_kernel, shards=shards, subs=subs, rows=rows, width=width, rate=rate
             ),
             out_shape=(
                 jax.ShapeDtypeStruct((half_rows, width), jnp.bfloat16),
@@ -316,7 +327,7 @@
             ),
             compiler_params=limit,
             name=f"rows{half}",
-        )(own, near, far)
+        )(own, *near, *far)
 
     def scores(half, last, cents, *earlier):
         line = jax.ShapeDtypeStruct((blocks, SLOT), jnp.float32)
@@ -346,11 +357,11 @@
     own, codes = (first_own, second_own), (first_code, second_code)
     near = jnp.concatenate([codes[0], swap(codes[0], 2, 0)])
     near = [jnp.concatenate([near, swap(near, 0, 1)])]
-    near.append(jnp.concatenate([codes[1]] + [swap(codes[1], *chip) for chip in chips[1:]]))
-    far = [swap(block, 1, 0) for block in near]
-    second_fresh, second_rows = rows_of(1, own[1], near[1], far[1])
+    blocks_near = [codes[1]] + [swap(codes[1], *chip) for chip in chips[1:]]
+    second_fresh, second_rows = rows_of(1, own[1], blocks_near, [swap(block, 1, 0) for block in blocks_near])
     mine, rival = scores(1, False, second_rows)
-    first_fresh, first_rows = rows_of(0, own[0], near[0], far[0])
+    first_near = after(near[0], second_fresh)
+    first_fresh, first_rows = rows_of(0, own[0], [first_near], [swap(first_near, 1, 0)])
     fresh, margin = scores(0, True, first_rows, mine, rival, first_fresh, second_fresh)
     return fresh, margin.reshape(row_count)
 

time: 38.2 us -> 37.5 us (0.982)
  waiting for transfers between devices: 6.25 us -> 5.41 us
  starting transfers between devices: 20.2 us -> 20.8 us
    ppermute x17 -> x20, waiting for transfers between devices: 6.25 us -> 5.41 us  [swap(): return lax.ppermute(value, ('shard', 'sub'), pairs)]
    ppermute x17 -> x20, starting transfers between devices: 20.2 us -> 20.8 us  [swap(): return lax.ppermute(value, ('shard', 'sub'), pairs)]
  transfers between devices with their start and end apart: 17 -> 20, of which waited for: 8 -> 12; matrix products, arithmetic and copies ran while one was open for 1% -> 1% of each run, Pallas kernels for 11% -> 11%
where the time goes in v14:
time: 37.5 us; the launch traced here: 37.4 us
  starting transfers between devices  20.8 us (55%)
  Pallas kernels  9.24 us (25%)
  waiting for transfers between devices  5.41 us (14%)
  between operations  1.42 us (4%)
  other arithmetic  0.44 us (1%)
    ppermute x20, starting transfers between devices, swap(): return lax.ppermute(value, ('shard', 'sub'), pairs)  20.8 us
    ppermute x20, waiting for transfers between devices, swap(): return lax.ppermute(value, ('shard', 'sub'), pairs)  5.41 us
    pallas_call x2, Pallas kernels, scores(): pl.pallas_call(functools.partial(score_kernel, half=half, last=last, bloc...  3.98 us
    pallas_call x1, Pallas kernels, local(): pl.pallas_call(functools.partial(send_kernel, parts=parts, **sizes), out_...  2.45 us
    pallas_call x1, Pallas kernels, local(): pl.pallas_call(functools.partial(keep_kernel, **sizes), out_shape=(shape,...  1.28 us
    pallas_call x2, Pallas kernels, rows_of(): pl.pallas_call(functools.partial(rows_kernel, shards=shards, subs=subs, r...  0.95 us
  transfers between devices with their start and end apart: 20, of which 12 were waited for; matrix products, arithmetic and copies ran while one was open for 1% of the time, Pallas kernels for 11%

profile of v14, /device:TPU:0, one launch (start us, length us, event | category | flops | bytes accessed | tf_op | source)
XLA Modules:
  0.0 37.4 jit_solution(8476337308947944058)
XLA Ops:
  0.6 0.0 copy-start.2
  0.6 0.0 copy-start
  0.7 0.0 copy-start.1
  1.3 2.4 %sums_send.1 = (f32[4,2,64,256]{3,2,1,0:T(8,128)S(1)}, f32[4,2,64,256]{3,2,1,0:T(8,128)S(1)}, bf16[1536,1024]{1,0:T(8,128)(2,1)S(1)}) custom-call(s32[1]{0:T(128)S(6)} %copy.7.live_in.live, s32[12]{0:T(128)} %bids.5, s32[12,128]{1,0:T(8,128)} %bitcast.26, bf16[1536,1024]{1,0:T(8,128)(2,1)} %points.1), custom_call_target="tpu_custom_call" | custom-call | flops 201326592 | bytes 1572864 | tf_op jit(solution)/shard_map/sums_send/pallas_call | solution.py:254
  3.8 0.5 %collective-permute-start = (f32[4,2,64,256]{3,2,1,0:T(8,128)S(1)}, f32[4,2,64,256]{3,2,1,0:T(8,128)S(1)}, u32[]{:S(2)}, u32[]{:S(2)}) collective-permute-start(f32[4,2,64,256]{3,2,1,0:T(8,128)S(1)} %get-tuple-element.29), channel_id=1, source_target_pairs={{0,1},{1,0},{2,3},{3,2},{4,5},{5,4},{6,7},{7,6},{8,9},{9,8},{10,11... | collective-permute-start | bytes 1572872 | tf_op jit(solution)/shard_map/ppermute | solution.py:246
  4.3 0.1 collective-permute-start.7
  4.4 0.0 copy-done.2
  4.4 0.0 copy-done
  4.4 0.0 copy-done.1
  4.4 1.3 %sums_keep.1 = (f32[4,2,64,256]{3,2,1,0:T(8,128)S(1)}, f32[4,2,64,256]{3,2,1,0:T(8,128)S(1)}) custom-call(s32[1]{0:T(128)S(6)} %copy.7.live_in.live, s32[12]{0:T(128)S(1)} %copy-done.2, s32[12,128]{1,0:T(8,128)S(1)} %bitcast.27, bf16[128,256]{1,0:T(8,128)(2,1)S(1)} %copy-done.1, bf16[1536,1024]{1,0:T(8,128)(2,1)S(1)} %get-tuple-element.27.points), custom_call_target="tpu_custom_call" | custom-call | flops 201326592 | bytes 1572864 | tf_op jit(solution)/shard_map/sums_keep/pallas_call | solution.py:271
  5.7 0.2 collective-permute-done.crossed
  5.9 0.2 fusion.5
  6.1 3.9 %collective-permute-start.3 = (s16[2,64,256]{2,1,0:T(8,128)(2,1)S(1)}, s16[2,64,256]{2,1,0:T(8,128)(2,1)S(1)}, u32[]{:S(2)}, u32[]{:S(2)}) collective-permute-start(s16[2,64,256]{2,1,0:T(8,128)(2,1)S(1)} %get-tuple-element.55), channel_id=1, source_target_pairs={{0,6},{1,7},{2,4},{3,5},{4,2},{5,3},{6,0},{7,1},{8,14},{9,15},{10,... | collective-permute-start | bytes 196616 | tf_op jit(solution)/shard_map/ppermute | solution.py:246
  10.0 0.4 %collective-permute-start.2 = (s16[2,64,256]{2,1,0:T(8,128)(2,1)S(1)}, s16[2,64,256]{2,1,0:T(8,128)(2,1)S(1)}, u32[]{:S(2)}, u32[]{:S(2)}) collective-permute-start(s16[2,64,256]{2,1,0:T(8,128)(2,1)S(1)} %get-tuple-element.56), channel_id=1, source_target_pairs={{0,4},{1,5},{2,6},{3,7},{4,0},{5,1},{6,2},{7,3},{8,12},{9,13},{10,... | collective-permute-start | bytes 196616 | tf_op jit(solution)/shard_map/ppermute | solution.py:246
  10.4 0.2 collective-permute-start.1
  10.6 0.0 collective-permute-done.7.crossed
  10.6 0.2 fusion.11
  10.9 2.9 %collective-permute-start.10 = (s16[2,64,256]{2,1,0:T(8,128)(2,1)S(1)}, s16[2,64,256]{2,1,0:T(8,128)(2,1)S(1)}, u32[]{:S(2)}, u32[]{:S(2)}) collective-permute-start(s16[2,64,256]{2,1,0:T(8,128)(2,1)S(1)} %get-tuple-element.52), channel_id=1, source_target_pairs={{0,6},{1,7},{2,4},{3,5},{4,2},{5,3},{6,0},{7,1},{8,14},{9,15},{10,... | collective-permute-start | bytes 196616 | tf_op jit(solution)/shard_map/ppermute | solution.py:246
  13.8 0.4 %collective-permute-start.9 = (s16[2,64,256]{2,1,0:T(8,128)(2,1)S(1)}, s16[2,64,256]{2,1,0:T(8,128)(2,1)S(1)}, u32[]{:S(2)}, u32[]{:S(2)}) collective-permute-start(s16[2,64,256]{2,1,0:T(8,128)(2,1)S(1)} %get-tuple-element.53), channel_id=1, source_target_pairs={{0,4},{1,5},{2,6},{3,7},{4,0},{5,1},{6,2},{7,3},{8,12},{9,13},{10,... | collective-permute-start | bytes 196616 | tf_op jit(solution)/shard_map/ppermute | solution.py:246
  14.2 0.0 collective-permute-done.3.refs_2_
  14.2 0.2 collective-permute-start.8
  14.5 0.1 collective-permute-done.2.refs_1_
  14.5 0.9 %collective-permute-done.1.refs_0_ = s16[2,64,256]{2,1,0:T(8,128)(2,1)S(1)} collective-permute-done((s16[2,64,256]{2,1,0:T(8,128)(2,1)S(1)}, s16[2,64,256]{2,1,0:T(8,128)(2,1)S(1)}, u32[]{:S(2)}, u32[]{:S(2)}) %collective-permute-start.1) | collective-permute-done | bytes 65568 | tf_op jit(solution)/shard_map/ppermute | solution.py:246
  15.4 0.2 mix0.1
  15.6 2.7 %collective-permute-start.4 = (s16[2,64,256]{2,1,0:T(8,128)(2,1)S(1)}, s16[2,64,256]{2,1,0:T(8,128)(2,1)S(1)}, u32[]{:S(2)}, u32[]{:S(2)}) collective-permute-start(s16[2,64,256]{2,1,0:T(8,128)(2,1)S(1)} %get-tuple-element.31), channel_id=1, source_target_pairs={{0,8},{1,9},{2,10},{3,11},{4,12},{5,13},{6,14},{7,15},{8,0},{9,1},... | collective-permute-start | bytes 196616 | tf_op jit(solution)/shard_map/ppermute | solution.py:246
  18.3 0.0 collective-permute-done.10.refs_2_
  18.3 0.2 collective-permute-done.9.refs_1_
  18.4 0.1 collective-permute-done.8.refs_0_
  18.5 0.2 mix1.1
  18.7 2.7 %collective-permute-start.11 = (s16[2,64,256]{2,1,0:T(8,128)(2,1)S(1)}, s16[2,64,256]{2,1,0:T(8,128)(2,1)S(1)}, u32[]{:S(2)}, u32[]{:S(2)}) collective-permute-start(s16[2,64,256]{2,1,0:T(8,128)(2,1)S(1)} %get-tuple-element.40), channel_id=1, source_target_pairs={{0,8},{1,9},{2,10},{3,11},{4,12},{5,13},{6,14},{7,15},{8,0},{9,1},... | collective-permute-start | bytes 196616 | tf_op jit(solution)/shard_map/ppermute | solution.py:246
  21.3 0.0 collective-permute-done.4.there
  21.3 0.1 finish0.1
  21.4 0.8 %collective-permute-start.5 = (s16[2,64,256]{2,1,0:T(8,128)(2,1)S(1)}, s16[2,64,256]{2,1,0:T(8,128)(2,1)S(1)}, u32[]{:S(2)}, u32[]{:S(2)}) collective-permute-start(s16[2,64,256]{2,1,0:T(8,128)(2,1)S(1)} %get-tuple-element.33), channel_id=1, source_target_pairs={{0,2},{1,3},{2,0},{3,1},{4,6},{5,7},{6,4},{7,5},{8,10},{9,11},{10,... | collective-permute-start | bytes 196616 | tf_op jit(solution)/shard_map/ppermute | solution.py:246
  22.2 1.7 %collective-permute-done.11.there = s16[2,64,256]{2,1,0:T(8,128)(2,1)S(1)} collective-permute-done((s16[2,64,256]{2,1,0:T(8,128)(2,1)S(1)}, s16[2,64,256]{2,1,0:T(8,128)(2,1)S(1)}, u32[]{:S(2)}, u32[]{:S(2)}) %collective-permute-start.11) | collective-permute-done | bytes 65568 | tf_op jit(solution)/shard_map/ppermute | solution.py:246
  23.9 0.1 finish1.1
  24.0 1.7 %collective-permute-start.14 = (s16[2,64,256]{2,1,0:T(8,128)(2,1)S(1)}, s16[2,64,256]{2,1,0:T(8,128)(2,1)S(1)}, u32[]{:S(2)}, u32[]{:S(2)}) collective-permute-start(s16[2,64,256]{2,1,0:T(8,128)(2,1)S(1)} %get-tuple-element.42.refs_0_), channel_id=1, source_target_pairs={{0,6},{1,7},{2,4},{3,5},{4,2},{5,3},{6,0},{7,1},{8,14},{9,15},{10,... | collective-permute-start | bytes 196616 | tf_op jit(solution)/shard_map/ppermute | solution.py:246
  25.7 0.5 %collective-permute-start.13 = (s16[2,64,256]{2,1,0:T(8,128)(2,1)S(1)}, s16[2,64,256]{2,1,0:T(8,128)(2,1)S(1)}, u32[]{:S(2)}, u32[]{:S(2)}) collective-permute-start(s16[2,64,256]{2,1,0:T(8,128)(2,1)S(1)} %get-tuple-element.42.refs_0_), channel_id=1, source_target_pairs={{0,4},{1,5},{2,6},{3,7},{4,0},{5,1},{6,2},{7,3},{8,12},{9,13},{10,... | collective-permute-start | bytes 196616 | tf_op jit(solution)/shard_map/ppermute | solution.py:246
  26.2 1.4 %collective-permute-start.12 = (s16[2,64,256]{2,1,0:T(8,128)(2,1)S(1)}, s16[2,64,256]{2,1,0:T(8,128)(2,1)S(1)}, u32[]{:S(2)}, u32[]{:S(2)}) collective-permute-start(s16[2,64,256]{2,1,0:T(8,128)(2,1)S(1)} %get-tuple-element.42.refs_0_), channel_id=1, source_target_pairs={{0,2},{1,3},{2,0},{3,1},{4,6},{5,7},{6,4},{7,5},{8,10},{9,11},{10,... | collective-permute-start | bytes 196616 | tf_op jit(solution)/shard_map/ppermute | solution.py:246
  27.6 0.0 collective-permute-done.5
  27.6 1.6 %collective-permute-start.6 = (s16[4,64,256]{2,1,0:T(8,128)(2,1)S(1)}, s16[4,64,256]{2,1,0:T(8,128)(2,1)S(1)}, u32[]{:S(2)}, u32[]{:S(2)}) collective-permute-start(s16[4,64,256]{2,1,0:T(8,128)(2,1)S(1)} %pad_add_fusion.1), channel_id=1, source_target_pairs={{0,4},{1,5},{2,6},{3,7},{4,0},{5,1},{6,2},{7,3},{8,12},{9,13},{10,... | collective-permute-start | bytes 393224 | tf_op jit(solution)/shard_map/ppermute | solution.py:246
  29.2 0.0 collective-permute-start.15
  29.2 0.7 %collective-permute-done.14.refs_3_ = s16[2,64,256]{2,1,0:T(8,128)(2,1)S(1)} collective-permute-done((s16[2,64,256]{2,1,0:T(8,128)(2,1)S(1)}, s16[2,64,256]{2,1,0:T(8,128)(2,1)S(1)}, u32[]{:S(2)}, u32[]{:S(2)}) %collective-permute-start.14) | collective-permute-done | bytes 65568 | tf_op jit(solution)/shard_map/ppermute | solution.py:246
  29.9 0.0 collective-permute-start.18
  29.9 0.6 %collective-permute-done.13.refs_2_ = s16[2,64,256]{2,1,0:T(8,128)(2,1)S(1)} collective-permute-done((s16[2,64,256]{2,1,0:T(8,128)(2,1)S(1)}, s16[2,64,256]{2,1,0:T(8,128)(2,1)S(1)}, u32[]{:S(2)}, u32[]{:S(2)}) %collective-permute-start.13) | collective-permute-done | bytes 65568 | tf_op jit(solution)/shard_map/ppermute | solution.py:246
  30.5 0.0 collective-permute-start.17
  30.5 0.0 collective-permute-done.12.refs_1_
  30.5 0.5 %collective-permute-start.16 = (s16[2,64,256]{2,1,0:T(8,128)(2,1)S(1)}, s16[2,64,256]{2,1,0:T(8,128)(2,1)S(1)}, u32[]{:S(2)}, u32[]{:S(2)}) collective-permute-start(s16[2,64,256]{2,1,0:T(8,128)(2,1)S(1)} %collective-permute-done.12.refs_1_), channel_id=1, source_target_pairs={{0,1},{1,0},{2,3},{3,2},{4,5},{5,4},{6,7},{7,6},{8,9},{9,8},{10,11... | collective-permute-start | bytes 196616 | tf_op jit(solution)/shard_map/ppermute | solution.py:246
  31.0 0.0 collective-permute-done.15.refs_4_
  31.0 0.2 collective-permute-done.18.refs_7_
  31.2 0.6 %collective-permute-done.17.refs_6_ = s16[2,64,256]{2,1,0:T(8,128)(2,1)S(1)} collective-permute-done((s16[2,64,256]{2,1,0:T(8,128)(2,1)S(1)}, s16[2,64,256]{2,1,0:T(8,128)(2,1)S(1)}, u32[]{:S(2)}, u32[]{:S(2)}) %collective-permute-start.17) | collective-permute-done | bytes 65568 | tf_op jit(solution)/shard_map/ppermute | solution.py:246
  31.8 0.2 collective-permute-done.16.refs_5_
  31.9 0.5 %rows1.1 = (bf16[64,256]{1,0:T(8,128)(2,1)S(1)}, bf16[256,1024]{1,0:T(8,128)(2,1)S(1)}) custom-call(f32[64,256]{1,0:T(8,128)S(1)} %get-tuple-element.41.own, s16[2,64,256]{2,1,0:T(8,128)(2,1)S(1)} %get-tuple-element.42.refs_0_, s16[2,64,256]{2,1,0:T(8,128)(2,1)S(1)} %collective-permute-done.12.refs_1_, ...), custom_call_target="tpu_custom_call" | custom-call | tf_op jit(solution)/shard_map/rows1/pallas_call | solution.py:320
  32.4 0.2 collective-permute-done.6
  32.6 0.2 collective-permute-start.19
  32.9 1.7 %scores1.1 = (f32[12,128]{1,0:T(8,128)S(1)}, f32[12,128]{1,0:T(8,128)S(1)}) custom-call(s32[12]{0:T(128)S(1)} %copy-done.2, s32[12,128]{1,0:T(8,128)S(1)} %bitcast.28, bf16[1536,1024]{1,0:T(8,128)(2,1)S(1)} %get-tuple-element.27.points, bf16[256,1024]{1,0:T(8,128)(2,1)S(1)} %get-tuple-element.46.cents), custom_call_target="tpu_custom_call" | custom-call | flops 805306368 | bytes 3145728 | tf_op jit(solution)/shard_map/scores1/pallas_call | solution.py:335
  34.5 0.0 collective-permute-done.19.refs_1_
  34.5 0.5 %rows0.1 = (bf16[64,256]{1,0:T(8,128)(2,1)S(1)}, bf16[256,1024]{1,0:T(8,128)(2,1)S(1)}) custom-call(f32[64,256]{1,0:T(8,128)S(1)} %get-tuple-element.32.own, s16[8,64,256]{2,1,0:T(8,128)(2,1)S(1)} %pad_add_fusion.refs_0_, s16[8,64,256]{2,1,0:T(8,128)(2,1)S(1)} %collective-permute-done.19.refs_1_), custom_call_target="tpu_custom_call" | custom-call | tf_op jit(solution)/shard_map/rows0/pallas_call | solution.py:320
  35.0 2.3 %scores0.1 = (bf16[128,256]{1,0:T(8,128)(2,1)}, f32[12,128]{1,0:T(8,128)}) custom-call(s32[12]{0:T(128)S(1)} %copy-done.2, s32[12,128]{1,0:T(8,128)S(1)} %bitcast.29, bf16[1536,1024]{1,0:T(8,128)(2,1)S(1)} %get-tuple-element.27.points, bf16[256,1024]{1,0:T(8,128)(2,1)S(1)} %get-tuple-element.45.cents, f32[12,128]{1,0:T(8,128)S(1)} %get-tuple-element.47.refs_0_, ...), custom_call_target="tpu_custom_call" | custom-call | flops 805306368 | bytes 3145728 | tf_op jit(solution)/shard_map/scores0/pallas_call | solution.py:335
  (2 shorter events, 0.0 us)
Async XLA Ops:
  0.6 3.8 %copy-start.2 = (s32[12]{0:T(128)S(1)}, s32[12]{0:T(128)}, u32[]{:S(2)}) copy-start(s32[12]{0:T(128)} %bids.5) | copy-start | bytes 148
  0.6 3.8 %copy-start = (s32[1536]{0:T(1024)S(1)}, s32[1536]{0:T(1024)}, u32[]{:S(2)}) copy-start(s32[1536]{0:T(1024)} %param.7) | copy-start | bytes 18436
  0.7 3.8 %copy-start.1 = (bf16[128,256]{1,0:T(8,128)(2,1)S(1)}, bf16[128,256]{1,0:T(8,128)(2,1)}, u32[]{:S(2)}) copy-start(bf16[128,256]{1,0:T(8,128)(2,1)} %old.1) | copy-start | bytes 196612
  3.8 2.1 %collective-permute-start = (f32[4,2,64,256]{3,2,1,0:T(8,128)S(1)}, f32[4,2,64,256]{3,2,1,0:T(8,128)S(1)}, u32[]{:S(2)}, u32[]{:S(2)}) collective-permute-start(f32[4,2,64,256]{3,2,1,0:T(8,128)S(1)} %get-tuple-element.29), channel_id=1, source_target_pairs={{0,1},{1,0},{2,3},{3,2},{4,5},{5,4},{6,7},{7,6},{8,9},{9,8},{10,11... | collective-permute-start | bytes 1572872 | tf_op jit(solution)/shard_map/ppermute | solution.py:246
  4.3 6.3 %collective-permute-start.7 = (f32[4,2,64,256]{3,2,1,0:T(8,128)S(1)}, f32[4,2,64,256]{3,2,1,0:T(8,128)S(1)}, u32[]{:S(2)}, u32[]{:S(2)}) collective-permute-start(f32[4,2,64,256]{3,2,1,0:T(8,128)S(1)} %get-tuple-element.36), channel_id=1, source_target_pairs={{0,1},{1,0},{2,3},{3,2},{4,5},{5,4},{6,7},{7,6},{8,9},{9,8},{10,11... | collective-permute-start | bytes 1572872 | tf_op jit(solution)/shard_map/ppermute | solution.py:246
  6.1 8.2 %collective-permute-start.3 = (s16[2,64,256]{2,1,0:T(8,128)(2,1)S(1)}, s16[2,64,256]{2,1,0:T(8,128)(2,1)S(1)}, u32[]{:S(2)}, u32[]{:S(2)}) collective-permute-start(s16[2,64,256]{2,1,0:T(8,128)(2,1)S(1)} %get-tuple-element.55), channel_id=1, source_target_pairs={{0,6},{1,7},{2,4},{3,5},{4,2},{5,3},{6,0},{7,1},{8,14},{9,15},{10,... | collective-permute-start | bytes 196616 | tf_op jit(solution)/shard_map/ppermute | solution.py:246
  10.0 4.5 %collective-permute-start.2 = (s16[2,64,256]{2,1,0:T(8,128)(2,1)S(1)}, s16[2,64,256]{2,1,0:T(8,128)(2,1)S(1)}, u32[]{:S(2)}, u32[]{:S(2)}) collective-permute-start(s16[2,64,256]{2,1,0:T(8,128)(2,1)S(1)} %get-tuple-element.56), channel_id=1, source_target_pairs={{0,4},{1,5},{2,6},{3,7},{4,0},{5,1},{6,2},{7,3},{8,12},{9,13},{10,... | collective-permute-start | bytes 196616 | tf_op jit(solution)/shard_map/ppermute | solution.py:246
  10.4 5.0 %collective-permute-start.1 = (s16[2,64,256]{2,1,0:T(8,128)(2,1)S(1)}, s16[2,64,256]{2,1,0:T(8,128)(2,1)S(1)}, u32[]{:S(2)}, u32[]{:S(2)}) collective-permute-start(s16[2,64,256]{2,1,0:T(8,128)(2,1)S(1)} %get-tuple-element.57), channel_id=1, source_target_pairs={{0,2},{1,3},{2,0},{3,1},{4,6},{5,7},{6,4},{7,5},{8,10},{9,11},{10,... | collective-permute-start | bytes 196616 | tf_op jit(solution)/shard_map/ppermute | solution.py:246
  10.9 7.4 %collective-permute-start.10 = (s16[2,64,256]{2,1,0:T(8,128)(2,1)S(1)}, s16[2,64,256]{2,1,0:T(8,128)(2,1)S(1)}, u32[]{:S(2)}, u32[]{:S(2)}) collective-permute-start(s16[2,64,256]{2,1,0:T(8,128)(2,1)S(1)} %get-tuple-element.52), channel_id=1, source_target_pairs={{0,6},{1,7},{2,4},{3,5},{4,2},{5,3},{6,0},{7,1},{8,14},{9,15},{10,... | collective-permute-start | bytes 196616 | tf_op jit(solution)/shard_map/ppermute | solution.py:246
  13.8 4.7 %collective-permute-start.9 = (s16[2,64,256]{2,1,0:T(8,128)(2,1)S(1)}, s16[2,64,256]{2,1,0:T(8,128)(2,1)S(1)}, u32[]{:S(2)}, u32[]{:S(2)}) collective-permute-start(s16[2,64,256]{2,1,0:T(8,128)(2,1)S(1)} %get-tuple-element.53), channel_id=1, source_target_pairs={{0,4},{1,5},{2,6},{3,7},{4,0},{5,1},{6,2},{7,3},{8,12},{9,13},{10,... | collective-permute-start | bytes 196616 | tf_op jit(solution)/shard_map/ppermute | solution.py:246
  14.2 4.3 %collective-permute-start.8 = (s16[2,64,256]{2,1,0:T(8,128)(2,1)S(1)}, s16[2,64,256]{2,1,0:T(8,128)(2,1)S(1)}, u32[]{:S(2)}, u32[]{:S(2)}) collective-permute-start(s16[2,64,256]{2,1,0:T(8,128)(2,1)S(1)} %get-tuple-element.54), channel_id=1, source_target_pairs={{0,2},{1,3},{2,0},{3,1},{4,6},{5,7},{6,4},{7,5},{8,10},{9,11},{10,... | collective-permute-start | bytes 196616 | tf_op jit(solution)/shard_map/ppermute | solution.py:246
  15.6 5.7 %collective-permute-start.4 = (s16[2,64,256]{2,1,0:T(8,128)(2,1)S(1)}, s16[2,64,256]{2,1,0:T(8,128)(2,1)S(1)}, u32[]{:S(2)}, u32[]{:S(2)}) collective-permute-start(s16[2,64,256]{2,1,0:T(8,128)(2,1)S(1)} %get-tuple-element.31), channel_id=1, source_target_pairs={{0,8},{1,9},{2,10},{3,11},{4,12},{5,13},{6,14},{7,15},{8,0},{9,1},... | collective-permute-start | bytes 196616 | tf_op jit(solution)/shard_map/ppermute | solution.py:246
  18.7 5.2 %collective-permute-start.11 = (s16[2,64,256]{2,1,0:T(8,128)(2,1)S(1)}, s16[2,64,256]{2,1,0:T(8,128)(2,1)S(1)}, u32[]{:S(2)}, u32[]{:S(2)}) collective-permute-start(s16[2,64,256]{2,1,0:T(8,128)(2,1)S(1)} %get-tuple-element.40), channel_id=1, source_target_pairs={{0,8},{1,9},{2,10},{3,11},{4,12},{5,13},{6,14},{7,15},{8,0},{9,1},... | collective-permute-start | bytes 196616 | tf_op jit(solution)/shard_map/ppermute | solution.py:246
  21.4 6.1 %collective-permute-start.5 = (s16[2,64,256]{2,1,0:T(8,128)(2,1)S(1)}, s16[2,64,256]{2,1,0:T(8,128)(2,1)S(1)}, u32[]{:S(2)}, u32[]{:S(2)}) collective-permute-start(s16[2,64,256]{2,1,0:T(8,128)(2,1)S(1)} %get-tuple-element.33), channel_id=1, source_target_pairs={{0,2},{1,3},{2,0},{3,1},{4,6},{5,7},{6,4},{7,5},{8,10},{9,11},{10,... | collective-permute-start | bytes 196616 | tf_op jit(solution)/shard_map/ppermute | solution.py:246
  24.0 5.9 %collective-permute-start.14 = (s16[2,64,256]{2,1,0:T(8,128)(2,1)S(1)}, s16[2,64,256]{2,1,0:T(8,128)(2,1)S(1)}, u32[]{:S(2)}, u32[]{:S(2)}) collective-permute-start(s16[2,64,256]{2,1,0:T(8,128)(2,1)S(1)} %get-tuple-element.42.refs_0_), channel_id=1, source_target_pairs={{0,6},{1,7},{2,4},{3,5},{4,2},{5,3},{6,0},{7,1},{8,14},{9,15},{10,... | collective-permute-start | bytes 196616 | tf_op jit(solution)/shard_map/ppermute | solution.py:246
  25.7 4.8 %collective-permute-start.13 = (s16[2,64,256]{2,1,0:T(8,128)(2,1)S(1)}, s16[2,64,256]{2,1,0:T(8,128)(2,1)S(1)}, u32[]{:S(2)}, u32[]{:S(2)}) collective-permute-start(s16[2,64,256]{2,1,0:T(8,128)(2,1)S(1)} %get-tuple-element.42.refs_0_), channel_id=1, source_target_pairs={{0,4},{1,5},{2,6},{3,7},{4,0},{5,1},{6,2},{7,3},{8,12},{9,13},{10,... | collective-permute-start | bytes 196616 | tf_op jit(solution)/shard_map/ppermute | solution.py:246
  26.2 4.4 %collective-permute-start.12 = (s16[2,64,256]{2,1,0:T(8,128)(2,1)S(1)}, s16[2,64,256]{2,1,0:T(8,128)(2,1)S(1)}, u32[]{:S(2)}, u32[]{:S(2)}) collective-permute-start(s16[2,64,256]{2,1,0:T(8,128)(2,1)S(1)} %get-tuple-element.42.refs_0_), channel_id=1, source_target_pairs={{0,2},{1,3},{2,0},{3,1},{4,6},{5,7},{6,4},{7,5},{8,10},{9,11},{10,... | collective-permute-start | bytes 196616 | tf_op jit(solution)/shard_map/ppermute | solution.py:246
  27.6 5.0 %collective-permute-start.6 = (s16[4,64,256]{2,1,0:T(8,128)(2,1)S(1)}, s16[4,64,256]{2,1,0:T(8,128)(2,1)S(1)}, u32[]{:S(2)}, u32[]{:S(2)}) collective-permute-start(s16[4,64,256]{2,1,0:T(8,128)(2,1)S(1)} %pad_add_fusion.1), channel_id=1, source_target_pairs={{0,4},{1,5},{2,6},{3,7},{4,0},{5,1},{6,2},{7,3},{8,12},{9,13},{10,... | collective-permute-start | bytes 393224 | tf_op jit(solution)/shard_map/ppermute | solution.py:246
  29.2 1.8 %collective-permute-start.15 = (s16[2,64,256]{2,1,0:T(8,128)(2,1)S(1)}, s16[2,64,256]{2,1,0:T(8,128)(2,1)S(1)}, u32[]{:S(2)}, u32[]{:S(2)}) collective-permute-start(s16[2,64,256]{2,1,0:T(8,128)(2,1)S(1)} %get-tuple-element.42.refs_0_), channel_id=1, source_target_pairs={{0,1},{1,0},{2,3},{3,2},{4,5},{5,4},{6,7},{7,6},{8,9},{9,8},{10,11... | collective-permute-start | bytes 196616 | tf_op jit(solution)/shard_map/ppermute | solution.py:246
  29.9 1.3 %collective-permute-start.18 = (s16[2,64,256]{2,1,0:T(8,128)(2,1)S(1)}, s16[2,64,256]{2,1,0:T(8,128)(2,1)S(1)}, u32[]{:S(2)}, u32[]{:S(2)}) collective-permute-start(s16[2,64,256]{2,1,0:T(8,128)(2,1)S(1)} %collective-permute-done.14.refs_3_), channel_id=1, source_target_pairs={{0,1},{1,0},{2,3},{3,2},{4,5},{5,4},{6,7},{7,6},{8,9},{9,8},{10,11... | collective-permute-start | bytes 196616 | tf_op jit(solution)/shard_map/ppermute | solution.py:246
  30.5 1.3 %collective-permute-start.17 = (s16[2,64,256]{2,1,0:T(8,128)(2,1)S(1)}, s16[2,64,256]{2,1,0:T(8,128)(2,1)S(1)}, u32[]{:S(2)}, u32[]{:S(2)}) collective-permute-start(s16[2,64,256]{2,1,0:T(8,128)(2,1)S(1)} %collective-permute-done.13.refs_2_), channel_id=1, source_target_pairs={{0,1},{1,0},{2,3},{3,2},{4,5},{5,4},{6,7},{7,6},{8,9},{9,8},{10,11... | collective-permute-start | bytes 196616 | tf_op jit(solution)/shard_map/ppermute | solution.py:246
  30.5 1.4 %collective-permute-start.16 = (s16[2,64,256]{2,1,0:T(8,128)(2,1)S(1)}, s16[2,64,256]{2,1,0:T(8,128)(2,1)S(1)}, u32[]{:S(2)}, u32[]{:S(2)}) collective-permute-start(s16[2,64,256]{2,1,0:T(8,128)(2,1)S(1)} %collective-permute-done.12.refs_1_), channel_id=1, source_target_pairs={{0,1},{1,0},{2,3},{3,2},{4,5},{5,4},{6,7},{7,6},{8,9},{9,8},{10,11... | collective-permute-start | bytes 196616 | tf_op jit(solution)/shard_map/ppermute | solution.py:246
  32.6 1.9 %collective-permute-start.19 = (s16[8,64,256]{2,1,0:T(8,128)(2,1)S(1)}, s16[8,64,256]{2,1,0:T(8,128)(2,1)S(1)}, u32[]{:S(2)}, u32[]{:S(2)}) collective-permute-start(s16[8,64,256]{2,1,0:T(8,128)(2,1)S(1)} %pad_add_fusion.refs_0_), channel_id=1, source_target_pairs={{0,1},{1,0},{2,3},{3,2},{4,5},{5,4},{6,7},{7,6},{8,9},{9,8},{10,11... | collective-permute-start | bytes 786440 | tf_op jit(solution)/shard_map/ppermute | solution.py:246

commit v15 on v14

--- a/solution.py
+++ b/solution.py
@@ -181,9 +181,15 @@
 
 def score_kernel(bids, slots, points, cents, *refs, half, last, blocks, shards, rows, group):
     if last:
-        mine_in, rival_in, fresh_first, fresh_second, fresh, margin = refs
+        mine_in, rival_in, fresh_first, fresh_second, fresh_out, margin_out, fresh, margin, written = refs
         fresh[: rows // 2] = fresh_first[...]
         fresh[rows // 2 :] = fresh_second[...]
+        cut = (blocks - 1) // 8 * 8
+        spans = [slice(0, cut), slice(cut, blocks)] if cut else [slice(0, blocks)]
+        writes = [pltpu.make_async_copy(fresh, fresh_out, written.at[0])]
+        for index, span in enumerate(spans):
+            writes.append(pltpu.make_async_copy(margin.at[span], margin_out.at[span], written.at[index + 1]))
+        writes[0].start()
     else:
         mine_out, rival_out = refs
     half_rows = rows // 2
@@ -212,9 +218,15 @@
             rival = jnp.max(rivals, axis=0, keepdims=True)
             if last:
                 margin[line, :] = (mine_in[line, :] + mine) - jnp.maximum(rival_in[line, :], rival)
+                for span, write in zip(spans, writes[1:]):
+                    if at + 1 == span.stop:
+                        write.start()
             else:
                 mine_out[line, :] = mine
                 rival_out[line, :] = rival
+    if last:
+        for write in writes:
+            write.wait()
 
 
 def local(points, block_ids, slot_ids, live_blocks, old_centroids):
@@ -338,7 +350,14 @@
             ),
             out_shape=(fresh, line) if last else (line, line),
             in_specs=[smem] + [vmem] * (3 + len(earlier)),
-            out_specs=(vmem, vmem),
+            out_specs=(hbm, hbm) if last else (vmem, vmem),
+            scratch_shapes=[
+                pltpu.VMEM((rows, width), jnp.bfloat16),
+                pltpu.VMEM((blocks, SLOT), jnp.float32),
+                pltpu.SemaphoreType.DMA((3,)),
+            ]
+            if last
+            else [],
             compiler_params=limit,
             cost_estimate=pl.CostEstimate(
                 flops=row_count * total * feat_width,

time: 37.5 us -> 37.5 us (level)
  no operation moved by 1% of the time
where the time goes in v15:
time: 37.5 us; the launch traced here: 37.4 us
  starting transfers between devices  20.8 us (55%)
  Pallas kernels  9.24 us (25%)
  waiting for transfers between devices  5.41 us (14%)
  between operations  1.42 us (4%)
  other arithmetic  0.44 us (1%)
    ppermute x20, starting transfers between devices, swap(): return lax.ppermute(value, ('shard', 'sub'), pairs)  20.8 us
    ppermute x20, waiting for transfers between devices, swap(): return lax.ppermute(value, ('shard', 'sub'), pairs)  5.41 us
    pallas_call x2, Pallas kernels, scores(): pl.pallas_call(functools.partial(score_kernel, half=half, last=last, bloc...  3.98 us
    pallas_call x1, Pallas kernels, local(): pl.pallas_call(functools.partial(send_kernel, parts=parts, **sizes), out_...  2.45 us
    pallas_call x1, Pallas kernels, local(): pl.pallas_call(functools.partial(keep_kernel, **sizes), out_shape=(shape,...  1.28 us
    pallas_call x2, Pallas kernels, rows_of(): pl.pallas_call(functools.partial(rows_kernel, shards=shards, subs=subs, r...  0.95 us
  transfers between devices with their start and end apart: 20, of which 12 were waited for; matrix products, arithmetic and copies ran while one was open for 1% of the time, Pallas kernels for 11%

profile of v15, /device:TPU:0, one launch (start us, length us, event | category | flops | bytes accessed | tf_op | source)
XLA Modules:
  0.0 37.4 jit_solution(13115535324205209049)
XLA Ops:
  0.6 0.0 copy-start.2
  0.6 0.0 copy-start
  0.7 0.0 copy-start.1
  1.3 2.4 %sums_send.1 = (f32[4,2,64,256]{3,2,1,0:T(8,128)S(1)}, f32[4,2,64,256]{3,2,1,0:T(8,128)S(1)}, bf16[1536,1024]{1,0:T(8,128)(2,1)S(1)}) custom-call(s32[1]{0:T(128)S(6)} %copy.7.live_in.live, s32[12]{0:T(128)} %bids.5, s32[12,128]{1,0:T(8,128)} %bitcast.26, bf16[1536,1024]{1,0:T(8,128)(2,1)} %points.1), custom_call_target="tpu_custom_call" | custom-call | flops 201326592 | bytes 1572864 | tf_op jit(solution)/shard_map/sums_send/pallas_call | solution.py:266
  3.8 0.5 %collective-permute-start = (f32[4,2,64,256]{3,2,1,0:T(8,128)S(1)}, f32[4,2,64,256]{3,2,1,0:T(8,128)S(1)}, u32[]{:S(2)}, u32[]{:S(2)}) collective-permute-start(f32[4,2,64,256]{3,2,1,0:T(8,128)S(1)} %get-tuple-element.29), channel_id=1, source_target_pairs={{0,1},{1,0},{2,3},{3,2},{4,5},{5,4},{6,7},{7,6},{8,9},{9,8},{10,11... | collective-permute-start | bytes 1572872 | tf_op jit(solution)/shard_map/ppermute | solution.py:258
  4.3 0.1 collective-permute-start.7
  4.4 0.0 copy-done.2
  4.4 0.0 copy-done
  4.4 0.0 copy-done.1
  4.4 1.3 %sums_keep.1 = (f32[4,2,64,256]{3,2,1,0:T(8,128)S(1)}, f32[4,2,64,256]{3,2,1,0:T(8,128)S(1)}) custom-call(s32[1]{0:T(128)S(6)} %copy.7.live_in.live, s32[12]{0:T(128)S(1)} %copy-done.2, s32[12,128]{1,0:T(8,128)S(1)} %bitcast.27, bf16[128,256]{1,0:T(8,128)(2,1)S(1)} %copy-done.1, bf16[1536,1024]{1,0:T(8,128)(2,1)S(1)} %get-tuple-element.27.points), custom_call_target="tpu_custom_call" | custom-call | flops 201326592 | bytes 1572864 | tf_op jit(solution)/shard_map/sums_keep/pallas_call | solution.py:283
  5.7 0.2 collective-permute-done.crossed
  5.9 0.2 fusion.5
  6.1 3.9 %collective-permute-start.3 = (s16[2,64,256]{2,1,0:T(8,128)(2,1)S(1)}, s16[2,64,256]{2,1,0:T(8,128)(2,1)S(1)}, u32[]{:S(2)}, u32[]{:S(2)}) collective-permute-start(s16[2,64,256]{2,1,0:T(8,128)(2,1)S(1)} %get-tuple-element.55), channel_id=1, source_target_pairs={{0,6},{1,7},{2,4},{3,5},{4,2},{5,3},{6,0},{7,1},{8,14},{9,15},{10,... | collective-permute-start | bytes 196616 | tf_op jit(solution)/shard_map/ppermute | solution.py:258
  10.0 0.4 %collective-permute-start.2 = (s16[2,64,256]{2,1,0:T(8,128)(2,1)S(1)}, s16[2,64,256]{2,1,0:T(8,128)(2,1)S(1)}, u32[]{:S(2)}, u32[]{:S(2)}) collective-permute-start(s16[2,64,256]{2,1,0:T(8,128)(2,1)S(1)} %get-tuple-element.56), channel_id=1, source_target_pairs={{0,4},{1,5},{2,6},{3,7},{4,0},{5,1},{6,2},{7,3},{8,12},{9,13},{10,... | collective-permute-start | bytes 196616 | tf_op jit(solution)/shard_map/ppermute | solution.py:258
  10.4 0.2 collective-permute-start.1
  10.6 0.0 collective-permute-done.7.crossed
  10.6 0.2 fusion.11
  10.9 2.9 %collective-permute-start.10 = (s16[2,64,256]{2,1,0:T(8,128)(2,1)S(1)}, s16[2,64,256]{2,1,0:T(8,128)(2,1)S(1)}, u32[]{:S(2)}, u32[]{:S(2)}) collective-permute-start(s16[2,64,256]{2,1,0:T(8,128)(2,1)S(1)} %get-tuple-element.52), channel_id=1, source_target_pairs={{0,6},{1,7},{2,4},{3,5},{4,2},{5,3},{6,0},{7,1},{8,14},{9,15},{10,... | collective-permute-start | bytes 196616 | tf_op jit(solution)/shard_map/ppermute | solution.py:258
  13.8 0.4 %collective-permute-start.9 = (s16[2,64,256]{2,1,0:T(8,128)(2,1)S(1)}, s16[2,64,256]{2,1,0:T(8,128)(2,1)S(1)}, u32[]{:S(2)}, u32[]{:S(2)}) collective-permute-start(s16[2,64,256]{2,1,0:T(8,128)(2,1)S(1)} %get-tuple-element.53), channel_id=1, source_target_pairs={{0,4},{1,5},{2,6},{3,7},{4,0},{5,1},{6,2},{7,3},{8,12},{9,13},{10,... | collective-permute-start | bytes 196616 | tf_op jit(solution)/shard_map/ppermute | solution.py:258
  14.2 0.0 collective-permute-done.3.refs_2_
  14.2 0.2 collective-permute-start.8
  14.5 0.1 collective-permute-done.2.refs_1_
  14.5 0.9 %collective-permute-done.1.refs_0_ = s16[2,64,256]{2,1,0:T(8,128)(2,1)S(1)} collective-permute-done((s16[2,64,256]{2,1,0:T(8,128)(2,1)S(1)}, s16[2,64,256]{2,1,0:T(8,128)(2,1)S(1)}, u32[]{:S(2)}, u32[]{:S(2)}) %collective-permute-start.1) | collective-permute-done | bytes 65568 | tf_op jit(solution)/shard_map/ppermute | solution.py:258
  15.4 0.2 mix0.1
  15.6 2.7 %collective-permute-start.4 = (s16[2,64,256]{2,1,0:T(8,128)(2,1)S(1)}, s16[2,64,256]{2,1,0:T(8,128)(2,1)S(1)}, u32[]{:S(2)}, u32[]{:S(2)}) collective-permute-start(s16[2,64,256]{2,1,0:T(8,128)(2,1)S(1)} %get-tuple-element.31), channel_id=1, source_target_pairs={{0,8},{1,9},{2,10},{3,11},{4,12},{5,13},{6,14},{7,15},{8,0},{9,1},... | collective-permute-start | bytes 196616 | tf_op jit(solution)/shard_map/ppermute | solution.py:258
  18.3 0.0 collective-permute-done.10.refs_2_
  18.3 0.2 collective-permute-done.9.refs_1_
  18.4 0.1 collective-permute-done.8.refs_0_
  18.5 0.2 mix1.1
  18.7 2.7 %collective-permute-start.11 = (s16[2,64,256]{2,1,0:T(8,128)(2,1)S(1)}, s16[2,64,256]{2,1,0:T(8,128)(2,1)S(1)}, u32[]{:S(2)}, u32[]{:S(2)}) collective-permute-start(s16[2,64,256]{2,1,0:T(8,128)(2,1)S(1)} %get-tuple-element.40), channel_id=1, source_target_pairs={{0,8},{1,9},{2,10},{3,11},{4,12},{5,13},{6,14},{7,15},{8,0},{9,1},... | collective-permute-start | bytes 196616 | tf_op jit(solution)/shard_map/ppermute | solution.py:258
  21.3 0.0 collective-permute-done.4.there
  21.3 0.1 finish0.1
  21.4 0.8 %collective-permute-start.5 = (s16[2,64,256]{2,1,0:T(8,128)(2,1)S(1)}, s16[2,64,256]{2,1,0:T(8,128)(2,1)S(1)}, u32[]{:S(2)}, u32[]{:S(2)}) collective-permute-start(s16[2,64,256]{2,1,0:T(8,128)(2,1)S(1)} %get-tuple-element.33), channel_id=1, source_target_pairs={{0,2},{1,3},{2,0},{3,1},{4,6},{5,7},{6,4},{7,5},{8,10},{9,11},{10,... | collective-permute-start | bytes 196616 | tf_op jit(solution)/shard_map/ppermute | solution.py:258
  22.2 1.7 %collective-permute-done.11.there = s16[2,64,256]{2,1,0:T(8,128)(2,1)S(1)} collective-permute-done((s16[2,64,256]{2,1,0:T(8,128)(2,1)S(1)}, s16[2,64,256]{2,1,0:T(8,128)(2,1)S(1)}, u32[]{:S(2)}, u32[]{:S(2)}) %collective-permute-start.11) | collective-permute-done | bytes 65568 | tf_op jit(solution)/shard_map/ppermute | solution.py:258
  23.9 0.1 finish1.1
  24.0 1.7 %collective-permute-start.14 = (s16[2,64,256]{2,1,0:T(8,128)(2,1)S(1)}, s16[2,64,256]{2,1,0:T(8,128)(2,1)S(1)}, u32[]{:S(2)}, u32[]{:S(2)}) collective-permute-start(s16[2,64,256]{2,1,0:T(8,128)(2,1)S(1)} %get-tuple-element.42.refs_0_), channel_id=1, source_target_pairs={{0,6},{1,7},{2,4},{3,5},{4,2},{5,3},{6,0},{7,1},{8,14},{9,15},{10,... | collective-permute-start | bytes 196616 | tf_op jit(solution)/shard_map/ppermute | solution.py:258
  25.7 0.5 %collective-permute-start.13 = (s16[2,64,256]{2,1,0:T(8,128)(2,1)S(1)}, s16[2,64,256]{2,1,0:T(8,128)(2,1)S(1)}, u32[]{:S(2)}, u32[]{:S(2)}) collective-permute-start(s16[2,64,256]{2,1,0:T(8,128)(2,1)S(1)} %get-tuple-element.42.refs_0_), channel_id=1, source_target_pairs={{0,4},{1,5},{2,6},{3,7},{4,0},{5,1},{6,2},{7,3},{8,12},{9,13},{10,... | collective-permute-start | bytes 196616 | tf_op jit(solution)/shard_map/ppermute | solution.py:258
  26.2 1.4 %collective-permute-start.12 = (s16[2,64,256]{2,1,0:T(8,128)(2,1)S(1)}, s16[2,64,256]{2,1,0:T(8,128)(2,1)S(1)}, u32[]{:S(2)}, u32[]{:S(2)}) collective-permute-start(s16[2,64,256]{2,1,0:T(8,128)(2,1)S(1)} %get-tuple-element.42.refs_0_), channel_id=1, source_target_pairs={{0,2},{1,3},{2,0},{3,1},{4,6},{5,7},{6,4},{7,5},{8,10},{9,11},{10,... | collective-permute-start | bytes 196616 | tf_op jit(solution)/shard_map/ppermute | solution.py:258
  27.6 0.0 collective-permute-done.5
  27.6 1.6 %collective-permute-start.6 = (s16[4,64,256]{2,1,0:T(8,128)(2,1)S(1)}, s16[4,64,256]{2,1,0:T(8,128)(2,1)S(1)}, u32[]{:S(2)}, u32[]{:S(2)}) collective-permute-start(s16[4,64,256]{2,1,0:T(8,128)(2,1)S(1)} %pad_add_fusion.1), channel_id=1, source_target_pairs={{0,4},{1,5},{2,6},{3,7},{4,0},{5,1},{6,2},{7,3},{8,12},{9,13},{10,... | collective-permute-start | bytes 393224 | tf_op jit(solution)/shard_map/ppermute | solution.py:258
  29.2 0.0 collective-permute-start.15
  29.2 0.7 %collective-permute-done.14.refs_3_ = s16[2,64,256]{2,1,0:T(8,128)(2,1)S(1)} collective-permute-done((s16[2,64,256]{2,1,0:T(8,128)(2,1)S(1)}, s16[2,64,256]{2,1,0:T(8,128)(2,1)S(1)}, u32[]{:S(2)}, u32[]{:S(2)}) %collective-permute-start.14) | collective-permute-done | bytes 65568 | tf_op jit(solution)/shard_map/ppermute | solution.py:258
  29.9 0.0 collective-permute-start.18
  29.9 0.6 %collective-permute-done.13.refs_2_ = s16[2,64,256]{2,1,0:T(8,128)(2,1)S(1)} collective-permute-done((s16[2,64,256]{2,1,0:T(8,128)(2,1)S(1)}, s16[2,64,256]{2,1,0:T(8,128)(2,1)S(1)}, u32[]{:S(2)}, u32[]{:S(2)}) %collective-permute-start.13) | collective-permute-done | bytes 65568 | tf_op jit(solution)/shard_map/ppermute | solution.py:258
  30.5 0.0 collective-permute-start.17
  30.5 0.0 collective-permute-done.12.refs_1_
  30.5 0.5 %collective-permute-start.16 = (s16[2,64,256]{2,1,0:T(8,128)(2,1)S(1)}, s16[2,64,256]{2,1,0:T(8,128)(2,1)S(1)}, u32[]{:S(2)}, u32[]{:S(2)}) collective-permute-start(s16[2,64,256]{2,1,0:T(8,128)(2,1)S(1)} %collective-permute-done.12.refs_1_), channel_id=1, source_target_pairs={{0,1},{1,0},{2,3},{3,2},{4,5},{5,4},{6,7},{7,6},{8,9},{9,8},{10,11... | collective-permute-start | bytes 196616 | tf_op jit(solution)/shard_map/ppermute | solution.py:258
  31.0 0.0 collective-permute-done.15.refs_4_
  31.0 0.2 collective-permute-done.18.refs_7_
  31.2 0.6 %collective-permute-done.17.refs_6_ = s16[2,64,256]{2,1,0:T(8,128)(2,1)S(1)} collective-permute-done((s16[2,64,256]{2,1,0:T(8,128)(2,1)S(1)}, s16[2,64,256]{2,1,0:T(8,128)(2,1)S(1)}, u32[]{:S(2)}, u32[]{:S(2)}) %collective-permute-start.17) | collective-permute-done | bytes 65568 | tf_op jit(solution)/shard_map/ppermute | solution.py:258
  31.8 0.2 collective-permute-done.16.refs_5_
  31.9 0.5 %rows1.1 = (bf16[64,256]{1,0:T(8,128)(2,1)S(1)}, bf16[256,1024]{1,0:T(8,128)(2,1)S(1)}) custom-call(f32[64,256]{1,0:T(8,128)S(1)} %get-tuple-element.41.own, s16[2,64,256]{2,1,0:T(8,128)(2,1)S(1)} %get-tuple-element.42.refs_0_, s16[2,64,256]{2,1,0:T(8,128)(2,1)S(1)} %collective-permute-done.12.refs_1_, ...), custom_call_target="tpu_custom_call" | custom-call | tf_op jit(solution)/shard_map/rows1/pallas_call | solution.py:332
  32.4 0.2 collective-permute-done.6
  32.6 0.2 collective-permute-start.19
  32.9 1.7 %scores1.1 = (f32[12,128]{1,0:T(8,128)S(1)}, f32[12,128]{1,0:T(8,128)S(1)}) custom-call(s32[12]{0:T(128)S(1)} %copy-done.2, s32[12,128]{1,0:T(8,128)S(1)} %bitcast.28, bf16[1536,1024]{1,0:T(8,128)(2,1)S(1)} %get-tuple-element.27.points, bf16[256,1024]{1,0:T(8,128)(2,1)S(1)} %get-tuple-element.46.cents), custom_call_target="tpu_custom_call" | custom-call | flops 805306368 | bytes 3145728 | tf_op jit(solution)/shard_map/scores1/pallas_call | solution.py:347
  34.5 0.0 collective-permute-done.19.refs_1_
  34.5 0.5 %rows0.1 = (bf16[64,256]{1,0:T(8,128)(2,1)S(1)}, bf16[256,1024]{1,0:T(8,128)(2,1)S(1)}) custom-call(f32[64,256]{1,0:T(8,128)S(1)} %get-tuple-element.32.own, s16[8,64,256]{2,1,0:T(8,128)(2,1)S(1)} %pad_add_fusion.refs_0_, s16[8,64,256]{2,1,0:T(8,128)(2,1)S(1)} %collective-permute-done.19.refs_1_), custom_call_target="tpu_custom_call" | custom-call | tf_op jit(solution)/shard_map/rows0/pallas_call | solution.py:332
  35.0 2.3 %scores0.1 = (bf16[128,256]{1,0:T(8,128)(2,1)}, f32[12,128]{1,0:T(8,128)}) custom-call(s32[12]{0:T(128)S(1)} %copy-done.2, s32[12,128]{1,0:T(8,128)S(1)} %bitcast.29, bf16[1536,1024]{1,0:T(8,128)(2,1)S(1)} %get-tuple-element.27.points, bf16[256,1024]{1,0:T(8,128)(2,1)S(1)} %get-tuple-element.45.cents, f32[12,128]{1,0:T(8,128)S(1)} %get-tuple-element.47.refs_0_, ...), custom_call_target="tpu_custom_call" | custom-call | flops 805306368 | bytes 3145728 | tf_op jit(solution)/shard_map/scores0/pallas_call | solution.py:347
  (2 shorter events, 0.0 us)
Async XLA Ops:
  0.6 3.8 %copy-start.2 = (s32[12]{0:T(128)S(1)}, s32[12]{0:T(128)}, u32[]{:S(2)}) copy-start(s32[12]{0:T(128)} %bids.5) | copy-start | bytes 148
  0.6 3.8 %copy-start = (s32[1536]{0:T(1024)S(1)}, s32[1536]{0:T(1024)}, u32[]{:S(2)}) copy-start(s32[1536]{0:T(1024)} %param.7) | copy-start | bytes 18436
  0.7 3.8 %copy-start.1 = (bf16[128,256]{1,0:T(8,128)(2,1)S(1)}, bf16[128,256]{1,0:T(8,128)(2,1)}, u32[]{:S(2)}) copy-start(bf16[128,256]{1,0:T(8,128)(2,1)} %old.1) | copy-start | bytes 196612
  3.8 2.1 %collective-permute-start = (f32[4,2,64,256]{3,2,1,0:T(8,128)S(1)}, f32[4,2,64,256]{3,2,1,0:T(8,128)S(1)}, u32[]{:S(2)}, u32[]{:S(2)}) collective-permute-start(f32[4,2,64,256]{3,2,1,0:T(8,128)S(1)} %get-tuple-element.29), channel_id=1, source_target_pairs={{0,1},{1,0},{2,3},{3,2},{4,5},{5,4},{6,7},{7,6},{8,9},{9,8},{10,11... | collective-permute-start | bytes 1572872 | tf_op jit(solution)/shard_map/ppermute | solution.py:258
  4.3 6.3 %collective-permute-start.7 = (f32[4,2,64,256]{3,2,1,0:T(8,128)S(1)}, f32[4,2,64,256]{3,2,1,0:T(8,128)S(1)}, u32[]{:S(2)}, u32[]{:S(2)}) collective-permute-start(f32[4,2,64,256]{3,2,1,0:T(8,128)S(1)} %get-tuple-element.36), channel_id=1, source_target_pairs={{0,1},{1,0},{2,3},{3,2},{4,5},{5,4},{6,7},{7,6},{8,9},{9,8},{10,11... | collective-permute-start | bytes 1572872 | tf_op jit(solution)/shard_map/ppermute | solution.py:258
  6.1 8.2 %collective-permute-start.3 = (s16[2,64,256]{2,1,0:T(8,128)(2,1)S(1)}, s16[2,64,256]{2,1,0:T(8,128)(2,1)S(1)}, u32[]{:S(2)}, u32[]{:S(2)}) collective-permute-start(s16[2,64,256]{2,1,0:T(8,128)(2,1)S(1)} %get-tuple-element.55), channel_id=1, source_target_pairs={{0,6},{1,7},{2,4},{3,5},{4,2},{5,3},{6,0},{7,1},{8,14},{9,15},{10,... | collective-permute-start | bytes 196616 | tf_op jit(solution)/shard_map/ppermute | solution.py:258
  10.0 4.5 %collective-permute-start.2 = (s16[2,64,256]{2,1,0:T(8,128)(2,1)S(1)}, s16[2,64,256]{2,1,0:T(8,128)(2,1)S(1)}, u32[]{:S(2)}, u32[]{:S(2)}) collective-permute-start(s16[2,64,256]{2,1,0:T(8,128)(2,1)S(1)} %get-tuple-element.56), channel_id=1, source_target_pairs={{0,4},{1,5},{2,6},{3,7},{4,0},{5,1},{6,2},{7,3},{8,12},{9,13},{10,... | collective-permute-start | bytes 196616 | tf_op jit(solution)/shard_map/ppermute | solution.py:258
  10.4 5.0 %collective-permute-start.1 = (s16[2,64,256]{2,1,0:T(8,128)(2,1)S(1)}, s16[2,64,256]{2,1,0:T(8,128)(2,1)S(1)}, u32[]{:S(2)}, u32[]{:S(2)}) collective-permute-start(s16[2,64,256]{2,1,0:T(8,128)(2,1)S(1)} %get-tuple-element.57), channel_id=1, source_target_pairs={{0,2},{1,3},{2,0},{3,1},{4,6},{5,7},{6,4},{7,5},{8,10},{9,11},{10,... | collective-permute-start | bytes 196616 | tf_op jit(solution)/shard_map/ppermute | solution.py:258
  10.9 7.4 %collective-permute-start.10 = (s16[2,64,256]{2,1,0:T(8,128)(2,1)S(1)}, s16[2,64,256]{2,1,0:T(8,128)(2,1)S(1)}, u32[]{:S(2)}, u32[]{:S(2)}) collective-permute-start(s16[2,64,256]{2,1,0:T(8,128)(2,1)S(1)} %get-tuple-element.52), channel_id=1, source_target_pairs={{0,6},{1,7},{2,4},{3,5},{4,2},{5,3},{6,0},{7,1},{8,14},{9,15},{10,... | collective-permute-start | bytes 196616 | tf_op jit(solution)/shard_map/ppermute | solution.py:258
  13.8 4.7 %collective-permute-start.9 = (s16[2,64,256]{2,1,0:T(8,128)(2,1)S(1)}, s16[2,64,256]{2,1,0:T(8,128)(2,1)S(1)}, u32[]{:S(2)}, u32[]{:S(2)}) collective-permute-start(s16[2,64,256]{2,1,0:T(8,128)(2,1)S(1)} %get-tuple-element.53), channel_id=1, source_target_pairs={{0,4},{1,5},{2,6},{3,7},{4,0},{5,1},{6,2},{7,3},{8,12},{9,13},{10,... | collective-permute-start | bytes 196616 | tf_op jit(solution)/shard_map/ppermute | solution.py:258
  14.2 4.3 %collective-permute-start.8 = (s16[2,64,256]{2,1,0:T(8,128)(2,1)S(1)}, s16[2,64,256]{2,1,0:T(8,128)(2,1)S(1)}, u32[]{:S(2)}, u32[]{:S(2)}) collective-permute-start(s16[2,64,256]{2,1,0:T(8,128)(2,1)S(1)} %get-tuple-element.54), channel_id=1, source_target_pairs={{0,2},{1,3},{2,0},{3,1},{4,6},{5,7},{6,4},{7,5},{8,10},{9,11},{10,... | collective-permute-start | bytes 196616 | tf_op jit(solution)/shard_map/ppermute | solution.py:258
  15.6 5.7 %collective-permute-start.4 = (s16[2,64,256]{2,1,0:T(8,128)(2,1)S(1)}, s16[2,64,256]{2,1,0:T(8,128)(2,1)S(1)}, u32[]{:S(2)}, u32[]{:S(2)}) collective-permute-start(s16[2,64,256]{2,1,0:T(8,128)(2,1)S(1)} %get-tuple-element.31), channel_id=1, source_target_pairs={{0,8},{1,9},{2,10},{3,11},{4,12},{5,13},{6,14},{7,15},{8,0},{9,1},... | collective-permute-start | bytes 196616 | tf_op jit(solution)/shard_map/ppermute | solution.py:258
  18.7 5.2 %collective-permute-start.11 = (s16[2,64,256]{2,1,0:T(8,128)(2,1)S(1)}, s16[2,64,256]{2,1,0:T(8,128)(2,1)S(1)}, u32[]{:S(2)}, u32[]{:S(2)}) collective-permute-start(s16[2,64,256]{2,1,0:T(8,128)(2,1)S(1)} %get-tuple-element.40), channel_id=1, source_target_pairs={{0,8},{1,9},{2,10},{3,11},{4,12},{5,13},{6,14},{7,15},{8,0},{9,1},... | collective-permute-start | bytes 196616 | tf_op jit(solution)/shard_map/ppermute | solution.py:258
  21.4 6.1 %collective-permute-start.5 = (s16[2,64,256]{2,1,0:T(8,128)(2,1)S(1)}, s16[2,64,256]{2,1,0:T(8,128)(2,1)S(1)}, u32[]{:S(2)}, u32[]{:S(2)}) collective-permute-start(s16[2,64,256]{2,1,0:T(8,128)(2,1)S(1)} %get-tuple-element.33), channel_id=1, source_target_pairs={{0,2},{1,3},{2,0},{3,1},{4,6},{5,7},{6,4},{7,5},{8,10},{9,11},{10,... | collective-permute-start | bytes 196616 | tf_op jit(solution)/shard_map/ppermute | solution.py:258
  24.0 5.9 %collective-permute-start.14 = (s16[2,64,256]{2,1,0:T(8,128)(2,1)S(1)}, s16[2,64,256]{2,1,0:T(8,128)(2,1)S(1)}, u32[]{:S(2)}, u32[]{:S(2)}) collective-permute-start(s16[2,64,256]{2,1,0:T(8,128)(2,1)S(1)} %get-tuple-element.42.refs_0_), channel_id=1, source_target_pairs={{0,6},{1,7},{2,4},{3,5},{4,2},{5,3},{6,0},{7,1},{8,14},{9,15},{10,... | collective-permute-start | bytes 196616 | tf_op jit(solution)/shard_map/ppermute | solution.py:258
  25.7 4.8 %collective-permute-start.13 = (s16[2,64,256]{2,1,0:T(8,128)(2,1)S(1)}, s16[2,64,256]{2,1,0:T(8,128)(2,1)S(1)}, u32[]{:S(2)}, u32[]{:S(2)}) collective-permute-start(s16[2,64,256]{2,1,0:T(8,128)(2,1)S(1)} %get-tuple-element.42.refs_0_), channel_id=1, source_target_pairs={{0,4},{1,5},{2,6},{3,7},{4,0},{5,1},{6,2},{7,3},{8,12},{9,13},{10,... | collective-permute-start | bytes 196616 | tf_op jit(solution)/shard_map/ppermute | solution.py:258
  26.2 4.4 %collective-permute-start.12 = (s16[2,64,256]{2,1,0:T(8,128)(2,1)S(1)}, s16[2,64,256]{2,1,0:T(8,128)(2,1)S(1)}, u32[]{:S(2)}, u32[]{:S(2)}) collective-permute-start(s16[2,64,256]{2,1,0:T(8,128)(2,1)S(1)} %get-tuple-element.42.refs_0_), channel_id=1, source_target_pairs={{0,2},{1,3},{2,0},{3,1},{4,6},{5,7},{6,4},{7,5},{8,10},{9,11},{10,... | collective-permute-start | bytes 196616 | tf_op jit(solution)/shard_map/ppermute | solution.py:258
  27.6 5.0 %collective-permute-start.6 = (s16[4,64,256]{2,1,0:T(8,128)(2,1)S(1)}, s16[4,64,256]{2,1,0:T(8,128)(2,1)S(1)}, u32[]{:S(2)}, u32[]{:S(2)}) collective-permute-start(s16[4,64,256]{2,1,0:T(8,128)(2,1)S(1)} %pad_add_fusion.1), channel_id=1, source_target_pairs={{0,4},{1,5},{2,6},{3,7},{4,0},{5,1},{6,2},{7,3},{8,12},{9,13},{10,... | collective-permute-start | bytes 393224 | tf_op jit(solution)/shard_map/ppermute | solution.py:258
  29.2 1.8 %collective-permute-start.15 = (s16[2,64,256]{2,1,0:T(8,128)(2,1)S(1)}, s16[2,64,256]{2,1,0:T(8,128)(2,1)S(1)}, u32[]{:S(2)}, u32[]{:S(2)}) collective-permute-start(s16[2,64,256]{2,1,0:T(8,128)(2,1)S(1)} %get-tuple-element.42.refs_0_), channel_id=1, source_target_pairs={{0,1},{1,0},{2,3},{3,2},{4,5},{5,4},{6,7},{7,6},{8,9},{9,8},{10,11... | collective-permute-start | bytes 196616 | tf_op jit(solution)/shard_map/ppermute | solution.py:258
  29.9 1.3 %collective-permute-start.18 = (s16[2,64,256]{2,1,0:T(8,128)(2,1)S(1)}, s16[2,64,256]{2,1,0:T(8,128)(2,1)S(1)}, u32[]{:S(2)}, u32[]{:S(2)}) collective-permute-start(s16[2,64,256]{2,1,0:T(8,128)(2,1)S(1)} %collective-permute-done.14.refs_3_), channel_id=1, source_target_pairs={{0,1},{1,0},{2,3},{3,2},{4,5},{5,4},{6,7},{7,6},{8,9},{9,8},{10,11... | collective-permute-start | bytes 196616 | tf_op jit(solution)/shard_map/ppermute | solution.py:258
  30.5 1.3 %collective-permute-start.17 = (s16[2,64,256]{2,1,0:T(8,128)(2,1)S(1)}, s16[2,64,256]{2,1,0:T(8,128)(2,1)S(1)}, u32[]{:S(2)}, u32[]{:S(2)}) collective-permute-start(s16[2,64,256]{2,1,0:T(8,128)(2,1)S(1)} %collective-permute-done.13.refs_2_), channel_id=1, source_target_pairs={{0,1},{1,0},{2,3},{3,2},{4,5},{5,4},{6,7},{7,6},{8,9},{9,8},{10,11... | collective-permute-start | bytes 196616 | tf_op jit(solution)/shard_map/ppermute | solution.py:258
  30.5 1.4 %collective-permute-start.16 = (s16[2,64,256]{2,1,0:T(8,128)(2,1)S(1)}, s16[2,64,256]{2,1,0:T(8,128)(2,1)S(1)}, u32[]{:S(2)}, u32[]{:S(2)}) collective-permute-start(s16[2,64,256]{2,1,0:T(8,128)(2,1)S(1)} %collective-permute-done.12.refs_1_), channel_id=1, source_target_pairs={{0,1},{1,0},{2,3},{3,2},{4,5},{5,4},{6,7},{7,6},{8,9},{9,8},{10,11... | collective-permute-start | bytes 196616 | tf_op jit(solution)/shard_map/ppermute | solution.py:258
  32.6 1.9 %collective-permute-start.19 = (s16[8,64,256]{2,1,0:T(8,128)(2,1)S(1)}, s16[8,64,256]{2,1,0:T(8,128)(2,1)S(1)}, u32[]{:S(2)}, u32[]{:S(2)}) collective-permute-start(s16[8,64,256]{2,1,0:T(8,128)(2,1)S(1)} %pad_add_fusion.refs_0_), channel_id=1, source_target_pairs={{0,1},{1,0},{2,3},{3,2},{4,5},{5,4},{6,7},{7,6},{8,9},{9,8},{10,11... | collective-permute-start | bytes 786440 | tf_op jit(solution)/shard_map/ppermute | solution.py:258

commit v16 on v14

--- a/solution.py
+++ b/solution.py
@@ -355,9 +355,11 @@
     first_own, first_code = finish(0, *first)
     second_own, second_code = finish(1, *second, first_code)
     own, codes = (first_own, second_own), (first_code, second_code)
-    near = jnp.concatenate([codes[0], swap(codes[0], 2, 0)])
-    near = [jnp.concatenate([near, swap(near, 0, 1)])]
-    blocks_near = [codes[1]] + [swap(codes[1], *chip) for chip in chips[1:]]
+    by_x = swap(codes[0], 2, 0)
+    by_z = swap(codes[0], 0, 1)
+    near = [jnp.concatenate([codes[0], by_x, by_z, swap(by_x, 0, 1)])]
+    ready = [codes[1], codes[1], codes[1]]
+    blocks_near = [codes[1]] + [swap(code, *chip) for code, chip in zip(ready, chips[1:])]
     second_fresh, second_rows = rows_of(1, own[1], blocks_near, [swap(block, 1, 0) for block in blocks_near])
     mine, rival = scores(1, False, second_rows)
     first_near = after(near[0], second_fresh)

time: 37.5 us -> 38.3 us (1.021)
  starting transfers between devices: 20.8 us -> 22.8 us
  waiting for transfers between devices: 5.41 us -> 4.19 us
    ppermute x20 -> x21, starting transfers between devices: 20.8 us -> 22.8 us  [swap(): return lax.ppermute(value, ('shard', 'sub'), pairs)]
    ppermute x20 -> x21, waiting for transfers between devices: 5.41 us -> 4.19 us  [swap(): return lax.ppermute(value, ('shard', 'sub'), pairs)]
  transfers between devices with their start and end apart: 20 -> 21, of which waited for: 12 -> 10; matrix products, arithmetic and copies ran while one was open for 1% -> 1% of each run, Pallas kernels for 11% -> 9%
where the time goes in v16:
time: 38.3 us; the launch traced here: 38.1 us
  starting transfers between devices  22.8 us (60%)
  Pallas kernels  9.29 us (24%)
  waiting for transfers between devices  4.19 us (11%)
  between operations  1.44 us (4%)
  other arithmetic  0.43 us (1%)
    ppermute x21, starting transfers between devices, swap(): return lax.ppermute(value, ('shard', 'sub'), pairs)  22.8 us
    ppermute x21, waiting for transfers between devices, swap(): return lax.ppermute(value, ('shard', 'sub'), pairs)  4.19 us
    pallas_call x2, Pallas kernels, scores(): pl.pallas_call(functools.partial(score_kernel, half=half, last=last, bloc...  4.03 us
    pallas_call x1, Pallas kernels, local(): pl.pallas_call(functools.partial(send_kernel, parts=parts, **sizes), out_...  2.45 us
    pallas_call x1, Pallas kernels, local(): pl.pallas_call(functools.partial(keep_kernel, **sizes), out_shape=(shape,...  1.28 us
    pallas_call x2, Pallas kernels, rows_of(): pl.pallas_call(functools.partial(rows_kernel, shards=shards, subs=subs, r...  0.95 us
  transfers between devices with their start and end apart: 21, of which 10 were waited for; matrix products, arithmetic and copies ran while one was open for 1% of the time, Pallas kernels for 9%

profile of v16, /device:TPU:0, one launch (start us, length us, event | category | flops | bytes accessed | tf_op | source)
XLA Modules:
  0.0 38.1 jit_solution(15569603629440972221)
XLA Ops:
  0.6 0.0 copy-start.2
  0.6 0.0 copy-start
  0.7 0.0 copy-start.1
  1.3 2.4 %sums_send.1 = (f32[4,2,64,256]{3,2,1,0:T(8,128)S(1)}, f32[4,2,64,256]{3,2,1,0:T(8,128)S(1)}, bf16[1536,1024]{1,0:T(8,128)(2,1)S(1)}) custom-call(s32[1]{0:T(128)S(6)} %copy.7.live_in.live, s32[12]{0:T(128)} %bids.5, s32[12,128]{1,0:T(8,128)} %bitcast.26, bf16[1536,1024]{1,0:T(8,128)(2,1)} %points.1), custom_call_target="tpu_custom_call" | custom-call | flops 201326592 | bytes 1572864 | tf_op jit(solution)/shard_map/sums_send/pallas_call | solution.py:254
  3.8 0.5 %collective-permute-start = (f32[4,2,64,256]{3,2,1,0:T(8,128)S(1)}, f32[4,2,64,256]{3,2,1,0:T(8,128)S(1)}, u32[]{:S(2)}, u32[]{:S(2)}) collective-permute-start(f32[4,2,64,256]{3,2,1,0:T(8,128)S(1)} %get-tuple-element.29), channel_id=1, source_target_pairs={{0,1},{1,0},{2,3},{3,2},{4,5},{5,4},{6,7},{7,6},{8,9},{9,8},{10,11... | collective-permute-start | bytes 1572872 | tf_op jit(solution)/shard_map/ppermute | solution.py:246
  4.3 0.1 collective-permute-start.8
  4.4 0.0 copy-done.2
  4.4 0.0 copy-done
  4.4 0.0 copy-done.1
  4.4 1.3 %sums_keep.1 = (f32[4,2,64,256]{3,2,1,0:T(8,128)S(1)}, f32[4,2,64,256]{3,2,1,0:T(8,128)S(1)}) custom-call(s32[1]{0:T(128)S(6)} %copy.7.live_in.live, s32[12]{0:T(128)S(1)} %copy-done.2, s32[12,128]{1,0:T(8,128)S(1)} %bitcast.27, bf16[128,256]{1,0:T(8,128)(2,1)S(1)} %copy-done.1, bf16[1536,1024]{1,0:T(8,128)(2,1)S(1)} %get-tuple-element.27.points), custom_call_target="tpu_custom_call" | custom-call | flops 201326592 | bytes 1572864 | tf_op jit(solution)/shard_map/sums_keep/pallas_call | solution.py:271
  5.7 0.2 collective-permute-done.crossed
  5.9 0.2 fusion.5
  6.1 3.9 %collective-permute-start.3 = (s16[2,64,256]{2,1,0:T(8,128)(2,1)S(1)}, s16[2,64,256]{2,1,0:T(8,128)(2,1)S(1)}, u32[]{:S(2)}, u32[]{:S(2)}) collective-permute-start(s16[2,64,256]{2,1,0:T(8,128)(2,1)S(1)} %get-tuple-element.55), channel_id=1, source_target_pairs={{0,6},{1,7},{2,4},{3,5},{4,2},{5,3},{6,0},{7,1},{8,14},{9,15},{10,... | collective-permute-start | bytes 196616 | tf_op jit(solution)/shard_map/ppermute | solution.py:246
  10.0 0.4 %collective-permute-start.2 = (s16[2,64,256]{2,1,0:T(8,128)(2,1)S(1)}, s16[2,64,256]{2,1,0:T(8,128)(2,1)S(1)}, u32[]{:S(2)}, u32[]{:S(2)}) collective-permute-start(s16[2,64,256]{2,1,0:T(8,128)(2,1)S(1)} %get-tuple-element.56), channel_id=1, source_target_pairs={{0,4},{1,5},{2,6},{3,7},{4,0},{5,1},{6,2},{7,3},{8,12},{9,13},{10,... | collective-permute-start | bytes 196616 | tf_op jit(solution)/shard_map/ppermute | solution.py:246
  10.4 0.2 collective-permute-start.1
  10.6 0.0 collective-permute-done.8.crossed
  10.6 0.2 fusion.11
  10.9 2.9 %collective-permute-start.11 = (s16[2,64,256]{2,1,0:T(8,128)(2,1)S(1)}, s16[2,64,256]{2,1,0:T(8,128)(2,1)S(1)}, u32[]{:S(2)}, u32[]{:S(2)}) collective-permute-start(s16[2,64,256]{2,1,0:T(8,128)(2,1)S(1)} %get-tuple-element.52), channel_id=1, source_target_pairs={{0,6},{1,7},{2,4},{3,5},{4,2},{5,3},{6,0},{7,1},{8,14},{9,15},{10,... | collective-permute-start | bytes 196616 | tf_op jit(solution)/shard_map/ppermute | solution.py:246
  13.8 0.4 %collective-permute-start.10 = (s16[2,64,256]{2,1,0:T(8,128)(2,1)S(1)}, s16[2,64,256]{2,1,0:T(8,128)(2,1)S(1)}, u32[]{:S(2)}, u32[]{:S(2)}) collective-permute-start(s16[2,64,256]{2,1,0:T(8,128)(2,1)S(1)} %get-tuple-element.53), channel_id=1, source_target_pairs={{0,4},{1,5},{2,6},{3,7},{4,0},{5,1},{6,2},{7,3},{8,12},{9,13},{10,... | collective-permute-start | bytes 196616 | tf_op jit(solution)/shard_map/ppermute | solution.py:246
  14.2 0.0 collective-permute-done.3.refs_2_
  14.2 0.2 collective-permute-start.9
  14.5 0.1 collective-permute-done.2.refs_1_
  14.5 0.9 %collective-permute-done.1.refs_0_ = s16[2,64,256]{2,1,0:T(8,128)(2,1)S(1)} collective-permute-done((s16[2,64,256]{2,1,0:T(8,128)(2,1)S(1)}, s16[2,64,256]{2,1,0:T(8,128)(2,1)S(1)}, u32[]{:S(2)}, u32[]{:S(2)}) %collective-permute-start.1) | collective-permute-done | bytes 65568 | tf_op jit(solution)/shard_map/ppermute | solution.py:246
  15.4 0.2 mix0.1
  15.6 2.7 %collective-permute-start.4 = (s16[2,64,256]{2,1,0:T(8,128)(2,1)S(1)}, s16[2,64,256]{2,1,0:T(8,128)(2,1)S(1)}, u32[]{:S(2)}, u32[]{:S(2)}) collective-permute-start(s16[2,64,256]{2,1,0:T(8,128)(2,1)S(1)} %get-tuple-element.31), channel_id=1, source_target_pairs={{0,8},{1,9},{2,10},{3,11},{4,12},{5,13},{6,14},{7,15},{8,0},{9,1},... | collective-permute-start | bytes 196616 | tf_op jit(solution)/shard_map/ppermute | solution.py:246
  18.3 0.0 collective-permute-done.11.refs_2_
  18.3 0.2 collective-permute-done.10.refs_1_
  18.4 0.1 collective-permute-done.9.refs_0_
  18.5 0.2 mix1.1
  18.7 2.7 %collective-permute-start.12 = (s16[2,64,256]{2,1,0:T(8,128)(2,1)S(1)}, s16[2,64,256]{2,1,0:T(8,128)(2,1)S(1)}, u32[]{:S(2)}, u32[]{:S(2)}) collective-permute-start(s16[2,64,256]{2,1,0:T(8,128)(2,1)S(1)} %get-tuple-element.40), channel_id=1, source_target_pairs={{0,8},{1,9},{2,10},{3,11},{4,12},{5,13},{6,14},{7,15},{8,0},{9,1},... | collective-permute-start | bytes 196616 | tf_op jit(solution)/shard_map/ppermute | solution.py:246
  21.3 0.0 collective-permute-done.4.there
  21.3 0.1 finish0.1
  21.4 0.8 %collective-permute-start.5 = (s16[2,64,256]{2,1,0:T(8,128)(2,1)S(1)}, s16[2,64,256]{2,1,0:T(8,128)(2,1)S(1)}, u32[]{:S(2)}, u32[]{:S(2)}) collective-permute-start(s16[2,64,256]{2,1,0:T(8,128)(2,1)S(1)} %get-tuple-element.33), channel_id=1, source_target_pairs={{0,2},{1,3},{2,0},{3,1},{4,6},{5,7},{6,4},{7,5},{8,10},{9,11},{10,... | collective-permute-start | bytes 196616 | tf_op jit(solution)/shard_map/ppermute | solution.py:246
  22.2 2.0 %collective-permute-start.6 = (s16[2,64,256]{2,1,0:T(8,128)(2,1)S(1)}, s16[2,64,256]{2,1,0:T(8,128)(2,1)S(1)}, u32[]{:S(2)}, u32[]{:S(2)}) collective-permute-start(s16[2,64,256]{2,1,0:T(8,128)(2,1)S(1)} %get-tuple-element.33), channel_id=1, source_target_pairs={{0,4},{1,5},{2,6},{3,7},{4,0},{5,1},{6,2},{7,3},{8,12},{9,13},{10,... | collective-permute-start | bytes 196616 | tf_op jit(solution)/shard_map/ppermute | solution.py:246
  24.3 0.0 collective-permute-done.12.there
  24.3 0.1 finish1.1
  24.4 1.7 %collective-permute-start.15 = (s16[2,64,256]{2,1,0:T(8,128)(2,1)S(1)}, s16[2,64,256]{2,1,0:T(8,128)(2,1)S(1)}, u32[]{:S(2)}, u32[]{:S(2)}) collective-permute-start(s16[2,64,256]{2,1,0:T(8,128)(2,1)S(1)} %get-tuple-element.42.refs_0_), channel_id=1, source_target_pairs={{0,6},{1,7},{2,4},{3,5},{4,2},{5,3},{6,0},{7,1},{8,14},{9,15},{10,... | collective-permute-start | bytes 196616 | tf_op jit(solution)/shard_map/ppermute | solution.py:246
  26.1 1.3 %collective-permute-start.14 = (s16[2,64,256]{2,1,0:T(8,128)(2,1)S(1)}, s16[2,64,256]{2,1,0:T(8,128)(2,1)S(1)}, u32[]{:S(2)}, u32[]{:S(2)}) collective-permute-start(s16[2,64,256]{2,1,0:T(8,128)(2,1)S(1)} %get-tuple-element.42.refs_0_), channel_id=1, source_target_pairs={{0,4},{1,5},{2,6},{3,7},{4,0},{5,1},{6,2},{7,3},{8,12},{9,13},{10,... | collective-permute-start | bytes 196616 | tf_op jit(solution)/shard_map/ppermute | solution.py:246
  27.4 0.6 %collective-permute-start.13 = (s16[2,64,256]{2,1,0:T(8,128)(2,1)S(1)}, s16[2,64,256]{2,1,0:T(8,128)(2,1)S(1)}, u32[]{:S(2)}, u32[]{:S(2)}) collective-permute-start(s16[2,64,256]{2,1,0:T(8,128)(2,1)S(1)} %get-tuple-element.42.refs_0_), channel_id=1, source_target_pairs={{0,2},{1,3},{2,0},{3,1},{4,6},{5,7},{6,4},{7,5},{8,10},{9,11},{10,... | collective-permute-start | bytes 196616 | tf_op jit(solution)/shard_map/ppermute | solution.py:246
  27.9 0.0 collective-permute-done.5
  27.9 1.7 %collective-permute-start.7 = (s16[2,64,256]{2,1,0:T(8,128)(2,1)S(1)}, s16[2,64,256]{2,1,0:T(8,128)(2,1)S(1)}, u32[]{:S(2)}, u32[]{:S(2)}) collective-permute-start(s16[2,64,256]{2,1,0:T(8,128)(2,1)S(1)} %collective-permute-done.5), channel_id=1, source_target_pairs={{0,4},{1,5},{2,6},{3,7},{4,0},{5,1},{6,2},{7,3},{8,12},{9,13},{10,... | collective-permute-start | bytes 196616 | tf_op jit(solution)/shard_map/ppermute | solution.py:246
  29.7 0.0 collective-permute-done.6
  29.7 0.0 collective-permute-start.16
  29.7 0.4 collective-permute-done.15.refs_3_
  30.0 0.2 collective-permute-start.19
  30.2 0.2 collective-permute-done.14.refs_2_
  30.4 0.2 collective-permute-start.18
  30.5 1.1 %collective-permute-done.13.refs_1_ = s16[2,64,256]{2,1,0:T(8,128)(2,1)S(1)} collective-permute-done((s16[2,64,256]{2,1,0:T(8,128)(2,1)S(1)}, s16[2,64,256]{2,1,0:T(8,128)(2,1)S(1)}, u32[]{:S(2)}, u32[]{:S(2)}) %collective-permute-start.13) | collective-permute-done | bytes 65568 | tf_op jit(solution)/shard_map/ppermute | solution.py:246
  31.6 0.0 collective-permute-start.17
  31.6 0.6 %collective-permute-done.7 = s16[2,64,256]{2,1,0:T(8,128)(2,1)S(1)} collective-permute-done((s16[2,64,256]{2,1,0:T(8,128)(2,1)S(1)}, s16[2,64,256]{2,1,0:T(8,128)(2,1)S(1)}, u32[]{:S(2)}, u32[]{:S(2)}) %collective-permute-start.7) | collective-permute-done | bytes 65568 | tf_op jit(solution)/shard_map/ppermute | solution.py:246
  32.2 0.0 collective-permute-done.16.refs_4_
  32.2 0.0 collective-permute-done.19.refs_7_
  32.3 0.0 collective-permute-done.18.refs_6_
  32.3 0.6 %collective-permute-done.17.refs_5_ = s16[2,64,256]{2,1,0:T(8,128)(2,1)S(1)} collective-permute-done((s16[2,64,256]{2,1,0:T(8,128)(2,1)S(1)}, s16[2,64,256]{2,1,0:T(8,128)(2,1)S(1)}, u32[]{:S(2)}, u32[]{:S(2)}) %collective-permute-start.17) | collective-permute-done | bytes 65568 | tf_op jit(solution)/shard_map/ppermute | solution.py:246
  32.9 0.5 %rows1.1 = (bf16[64,256]{1,0:T(8,128)(2,1)S(1)}, bf16[256,1024]{1,0:T(8,128)(2,1)S(1)}) custom-call(f32[64,256]{1,0:T(8,128)S(1)} %get-tuple-element.41.own, s16[2,64,256]{2,1,0:T(8,128)(2,1)S(1)} %get-tuple-element.42.refs_0_, s16[2,64,256]{2,1,0:T(8,128)(2,1)S(1)} %collective-permute-done.13.refs_1_, ...), custom_call_target="tpu_custom_call" | custom-call | tf_op jit(solution)/shard_map/rows1/pallas_call | solution.py:320
  33.4 0.2 collective-permute-start.20
  33.6 1.7 %scores1.1 = (f32[12,128]{1,0:T(8,128)S(1)}, f32[12,128]{1,0:T(8,128)S(1)}) custom-call(s32[12]{0:T(128)S(1)} %copy-done.2, s32[12,128]{1,0:T(8,128)S(1)} %bitcast.28, bf16[1536,1024]{1,0:T(8,128)(2,1)S(1)} %get-tuple-element.27.points, bf16[256,1024]{1,0:T(8,128)(2,1)S(1)} %get-tuple-element.46.cents), custom_call_target="tpu_custom_call" | custom-call | flops 805306368 | bytes 3145728 | tf_op jit(solution)/shard_map/scores1/pallas_call | solution.py:335
  35.3 0.0 collective-permute-done.20.refs_1_
  35.3 0.5 %rows0.1 = (bf16[64,256]{1,0:T(8,128)(2,1)S(1)}, bf16[256,1024]{1,0:T(8,128)(2,1)S(1)}) custom-call(f32[64,256]{1,0:T(8,128)S(1)} %get-tuple-element.32.own, s16[8,64,256]{2,1,0:T(8,128)(2,1)S(1)} %pad_add_fusion.refs_0_, s16[8,64,256]{2,1,0:T(8,128)(2,1)S(1)} %collective-permute-done.20.refs_1_), custom_call_target="tpu_custom_call" | custom-call | tf_op jit(solution)/shard_map/rows0/pallas_call | solution.py:320
  35.8 2.3 %scores0.1 = (bf16[128,256]{1,0:T(8,128)(2,1)}, f32[12,128]{1,0:T(8,128)}) custom-call(s32[12]{0:T(128)S(1)} %copy-done.2, s32[12,128]{1,0:T(8,128)S(1)} %bitcast.29, bf16[1536,1024]{1,0:T(8,128)(2,1)S(1)} %get-tuple-element.27.points, bf16[256,1024]{1,0:T(8,128)(2,1)S(1)} %get-tuple-element.45.cents, f32[12,128]{1,0:T(8,128)S(1)} %get-tuple-element.47.refs_0_, ...), custom_call_target="tpu_custom_call" | custom-call | flops 805306368 | bytes 3145728 | tf_op jit(solution)/shard_map/scores0/pallas_call | solution.py:335
  (1 shorter events, 0.0 us)
Async XLA Ops:
  0.6 3.8 %copy-start.2 = (s32[12]{0:T(128)S(1)}, s32[12]{0:T(128)}, u32[]{:S(2)}) copy-start(s32[12]{0:T(128)} %bids.5) | copy-start | bytes 148
  0.6 3.8 %copy-start = (s32[1536]{0:T(1024)S(1)}, s32[1536]{0:T(1024)}, u32[]{:S(2)}) copy-start(s32[1536]{0:T(1024)} %param.7) | copy-start | bytes 18436
  0.7 3.8 %copy-start.1 = (bf16[128,256]{1,0:T(8,128)(2,1)S(1)}, bf16[128,256]{1,0:T(8,128)(2,1)}, u32[]{:S(2)}) copy-start(bf16[128,256]{1,0:T(8,128)(2,1)} %old.1) | copy-start | bytes 196612
  3.8 2.1 %collective-permute-start = (f32[4,2,64,256]{3,2,1,0:T(8,128)S(1)}, f32[4,2,64,256]{3,2,1,0:T(8,128)S(1)}, u32[]{:S(2)}, u32[]{:S(2)}) collective-permute-start(f32[4,2,64,256]{3,2,1,0:T(8,128)S(1)} %get-tuple-element.29), channel_id=1, source_target_pairs={{0,1},{1,0},{2,3},{3,2},{4,5},{5,4},{6,7},{7,6},{8,9},{9,8},{10,11... | collective-permute-start | bytes 1572872 | tf_op jit(solution)/shard_map/ppermute | solution.py:246
  4.3 6.3 %collective-permute-start.8 = (f32[4,2,64,256]{3,2,1,0:T(8,128)S(1)}, f32[4,2,64,256]{3,2,1,0:T(8,128)S(1)}, u32[]{:S(2)}, u32[]{:S(2)}) collective-permute-start(f32[4,2,64,256]{3,2,1,0:T(8,128)S(1)} %get-tuple-element.36), channel_id=1, source_target_pairs={{0,1},{1,0},{2,3},{3,2},{4,5},{5,4},{6,7},{7,6},{8,9},{9,8},{10,11... | collective-permute-start | bytes 1572872 | tf_op jit(solution)/shard_map/ppermute | solution.py:246
  6.1 8.2 %collective-permute-start.3 = (s16[2,64,256]{2,1,0:T(8,128)(2,1)S(1)}, s16[2,64,256]{2,1,0:T(8,128)(2,1)S(1)}, u32[]{:S(2)}, u32[]{:S(2)}) collective-permute-start(s16[2,64,256]{2,1,0:T(8,128)(2,1)S(1)} %get-tuple-element.55), channel_id=1, source_target_pairs={{0,6},{1,7},{2,4},{3,5},{4,2},{5,3},{6,0},{7,1},{8,14},{9,15},{10,... | collective-permute-start | bytes 196616 | tf_op jit(solution)/shard_map/ppermute | solution.py:246
  10.0 4.5 %collective-permute-start.2 = (s16[2,64,256]{2,1,0:T(8,128)(2,1)S(1)}, s16[2,64,256]{2,1,0:T(8,128)(2,1)S(1)}, u32[]{:S(2)}, u32[]{:S(2)}) collective-permute-start(s16[2,64,256]{2,1,0:T(8,128)(2,1)S(1)} %get-tuple-element.56), channel_id=1, source_target_pairs={{0,4},{1,5},{2,6},{3,7},{4,0},{5,1},{6,2},{7,3},{8,12},{9,13},{10,... | collective-permute-start | bytes 196616 | tf_op jit(solution)/shard_map/ppermute | solution.py:246
  10.4 5.0 %collective-permute-start.1 = (s16[2,64,256]{2,1,0:T(8,128)(2,1)S(1)}, s16[2,64,256]{2,1,0:T(8,128)(2,1)S(1)}, u32[]{:S(2)}, u32[]{:S(2)}) collective-permute-start(s16[2,64,256]{2,1,0:T(8,128)(2,1)S(1)} %get-tuple-element.57), channel_id=1, source_target_pairs={{0,2},{1,3},{2,0},{3,1},{4,6},{5,7},{6,4},{7,5},{8,10},{9,11},{10,... | collective-permute-start | bytes 196616 | tf_op jit(solution)/shard_map/ppermute | solution.py:246
  10.9 7.4 %collective-permute-start.11 = (s16[2,64,256]{2,1,0:T(8,128)(2,1)S(1)}, s16[2,64,256]{2,1,0:T(8,128)(2,1)S(1)}, u32[]{:S(2)}, u32[]{:S(2)}) collective-permute-start(s16[2,64,256]{2,1,0:T(8,128)(2,1)S(1)} %get-tuple-element.52), channel_id=1, source_target_pairs={{0,6},{1,7},{2,4},{3,5},{4,2},{5,3},{6,0},{7,1},{8,14},{9,15},{10,... | collective-permute-start | bytes 196616 | tf_op jit(solution)/shard_map/ppermute | solution.py:246
  13.8 4.7 %collective-permute-start.10 = (s16[2,64,256]{2,1,0:T(8,128)(2,1)S(1)}, s16[2,64,256]{2,1,0:T(8,128)(2,1)S(1)}, u32[]{:S(2)}, u32[]{:S(2)}) collective-permute-start(s16[2,64,256]{2,1,0:T(8,128)(2,1)S(1)} %get-tuple-element.53), channel_id=1, source_target_pairs={{0,4},{1,5},{2,6},{3,7},{4,0},{5,1},{6,2},{7,3},{8,12},{9,13},{10,... | collective-permute-start | bytes 196616 | tf_op jit(solution)/shard_map/ppermute | solution.py:246
  14.2 4.3 %collective-permute-start.9 = (s16[2,64,256]{2,1,0:T(8,128)(2,1)S(1)}, s16[2,64,256]{2,1,0:T(8,128)(2,1)S(1)}, u32[]{:S(2)}, u32[]{:S(2)}) collective-permute-start(s16[2,64,256]{2,1,0:T(8,128)(2,1)S(1)} %get-tuple-element.54), channel_id=1, source_target_pairs={{0,2},{1,3},{2,0},{3,1},{4,6},{5,7},{6,4},{7,5},{8,10},{9,11},{10,... | collective-permute-start | bytes 196616 | tf_op jit(solution)/shard_map/ppermute | solution.py:246
  15.6 5.7 %collective-permute-start.4 = (s16[2,64,256]{2,1,0:T(8,128)(2,1)S(1)}, s16[2,64,256]{2,1,0:T(8,128)(2,1)S(1)}, u32[]{:S(2)}, u32[]{:S(2)}) collective-permute-start(s16[2,64,256]{2,1,0:T(8,128)(2,1)S(1)} %get-tuple-element.31), channel_id=1, source_target_pairs={{0,8},{1,9},{2,10},{3,11},{4,12},{5,13},{6,14},{7,15},{8,0},{9,1},... | collective-permute-start | bytes 196616 | tf_op jit(solution)/shard_map/ppermute | solution.py:246
  18.7 5.6 %collective-permute-start.12 = (s16[2,64,256]{2,1,0:T(8,128)(2,1)S(1)}, s16[2,64,256]{2,1,0:T(8,128)(2,1)S(1)}, u32[]{:S(2)}, u32[]{:S(2)}) collective-permute-start(s16[2,64,256]{2,1,0:T(8,128)(2,1)S(1)} %get-tuple-element.40), channel_id=1, source_target_pairs={{0,8},{1,9},{2,10},{3,11},{4,12},{5,13},{6,14},{7,15},{8,0},{9,1},... | collective-permute-start | bytes 196616 | tf_op jit(solution)/shard_map/ppermute | solution.py:246
  21.4 6.5 %collective-permute-start.5 = (s16[2,64,256]{2,1,0:T(8,128)(2,1)S(1)}, s16[2,64,256]{2,1,0:T(8,128)(2,1)S(1)}, u32[]{:S(2)}, u32[]{:S(2)}) collective-permute-start(s16[2,64,256]{2,1,0:T(8,128)(2,1)S(1)} %get-tuple-element.33), channel_id=1, source_target_pairs={{0,2},{1,3},{2,0},{3,1},{4,6},{5,7},{6,4},{7,5},{8,10},{9,11},{10,... | collective-permute-start | bytes 196616 | tf_op jit(solution)/shard_map/ppermute | solution.py:246
  22.2 7.4 %collective-permute-start.6 = (s16[2,64,256]{2,1,0:T(8,128)(2,1)S(1)}, s16[2,64,256]{2,1,0:T(8,128)(2,1)S(1)}, u32[]{:S(2)}, u32[]{:S(2)}) collective-permute-start(s16[2,64,256]{2,1,0:T(8,128)(2,1)S(1)} %get-tuple-element.33), channel_id=1, source_target_pairs={{0,4},{1,5},{2,6},{3,7},{4,0},{5,1},{6,2},{7,3},{8,12},{9,13},{10,... | collective-permute-start | bytes 196616 | tf_op jit(solution)/shard_map/ppermute | solution.py:246
  24.4 5.6 %collective-permute-start.15 = (s16[2,64,256]{2,1,0:T(8,128)(2,1)S(1)}, s16[2,64,256]{2,1,0:T(8,128)(2,1)S(1)}, u32[]{:S(2)}, u32[]{:S(2)}) collective-permute-start(s16[2,64,256]{2,1,0:T(8,128)(2,1)S(1)} %get-tuple-element.42.refs_0_), channel_id=1, source_target_pairs={{0,6},{1,7},{2,4},{3,5},{4,2},{5,3},{6,0},{7,1},{8,14},{9,15},{10,... | collective-permute-start | bytes 196616 | tf_op jit(solution)/shard_map/ppermute | solution.py:246
  26.1 4.3 %collective-permute-start.14 = (s16[2,64,256]{2,1,0:T(8,128)(2,1)S(1)}, s16[2,64,256]{2,1,0:T(8,128)(2,1)S(1)}, u32[]{:S(2)}, u32[]{:S(2)}) collective-permute-start(s16[2,64,256]{2,1,0:T(8,128)(2,1)S(1)} %get-tuple-element.42.refs_0_), channel_id=1, source_target_pairs={{0,4},{1,5},{2,6},{3,7},{4,0},{5,1},{6,2},{7,3},{8,12},{9,13},{10,... | collective-permute-start | bytes 196616 | tf_op jit(solution)/shard_map/ppermute | solution.py:246
  27.4 4.3 %collective-permute-start.13 = (s16[2,64,256]{2,1,0:T(8,128)(2,1)S(1)}, s16[2,64,256]{2,1,0:T(8,128)(2,1)S(1)}, u32[]{:S(2)}, u32[]{:S(2)}) collective-permute-start(s16[2,64,256]{2,1,0:T(8,128)(2,1)S(1)} %get-tuple-element.42.refs_0_), channel_id=1, source_target_pairs={{0,2},{1,3},{2,0},{3,1},{4,6},{5,7},{6,4},{7,5},{8,10},{9,11},{10,... | collective-permute-start | bytes 196616 | tf_op jit(solution)/shard_map/ppermute | solution.py:246
  27.9 4.3 %collective-permute-start.7 = (s16[2,64,256]{2,1,0:T(8,128)(2,1)S(1)}, s16[2,64,256]{2,1,0:T(8,128)(2,1)S(1)}, u32[]{:S(2)}, u32[]{:S(2)}) collective-permute-start(s16[2,64,256]{2,1,0:T(8,128)(2,1)S(1)} %collective-permute-done.5), channel_id=1, source_target_pairs={{0,4},{1,5},{2,6},{3,7},{4,0},{5,1},{6,2},{7,3},{8,12},{9,13},{10,... | collective-permute-start | bytes 196616 | tf_op jit(solution)/shard_map/ppermute | solution.py:246
  29.7 2.6 %collective-permute-start.16 = (s16[2,64,256]{2,1,0:T(8,128)(2,1)S(1)}, s16[2,64,256]{2,1,0:T(8,128)(2,1)S(1)}, u32[]{:S(2)}, u32[]{:S(2)}) collective-permute-start(s16[2,64,256]{2,1,0:T(8,128)(2,1)S(1)} %get-tuple-element.42.refs_0_), channel_id=1, source_target_pairs={{0,1},{1,0},{2,3},{3,2},{4,5},{5,4},{6,7},{7,6},{8,9},{9,8},{10,11... | collective-permute-start | bytes 196616 | tf_op jit(solution)/shard_map/ppermute | solution.py:246
  30.0 2.2 %collective-permute-start.19 = (s16[2,64,256]{2,1,0:T(8,128)(2,1)S(1)}, s16[2,64,256]{2,1,0:T(8,128)(2,1)S(1)}, u32[]{:S(2)}, u32[]{:S(2)}) collective-permute-start(s16[2,64,256]{2,1,0:T(8,128)(2,1)S(1)} %collective-permute-done.15.refs_3_), channel_id=1, source_target_pairs={{0,1},{1,0},{2,3},{3,2},{4,5},{5,4},{6,7},{7,6},{8,9},{9,8},{10,11... | collective-permute-start | bytes 196616 | tf_op jit(solution)/shard_map/ppermute | solution.py:246
  30.4 1.9 %collective-permute-start.18 = (s16[2,64,256]{2,1,0:T(8,128)(2,1)S(1)}, s16[2,64,256]{2,1,0:T(8,128)(2,1)S(1)}, u32[]{:S(2)}, u32[]{:S(2)}) collective-permute-start(s16[2,64,256]{2,1,0:T(8,128)(2,1)S(1)} %collective-permute-done.14.refs_2_), channel_id=1, source_target_pairs={{0,1},{1,0},{2,3},{3,2},{4,5},{5,4},{6,7},{7,6},{8,9},{9,8},{10,11... | collective-permute-start | bytes 196616 | tf_op jit(solution)/shard_map/ppermute | solution.py:246
  31.6 1.3 %collective-permute-start.17 = (s16[2,64,256]{2,1,0:T(8,128)(2,1)S(1)}, s16[2,64,256]{2,1,0:T(8,128)(2,1)S(1)}, u32[]{:S(2)}, u32[]{:S(2)}) collective-permute-start(s16[2,64,256]{2,1,0:T(8,128)(2,1)S(1)} %collective-permute-done.13.refs_1_), channel_id=1, source_target_pairs={{0,1},{1,0},{2,3},{3,2},{4,5},{5,4},{6,7},{7,6},{8,9},{9,8},{10,11... | collective-permute-start | bytes 196616 | tf_op jit(solution)/shard_map/ppermute | solution.py:246
  33.4 1.9 %collective-permute-start.20 = (s16[8,64,256]{2,1,0:T(8,128)(2,1)S(1)}, s16[8,64,256]{2,1,0:T(8,128)(2,1)S(1)}, u32[]{:S(2)}, u32[]{:S(2)}) collective-permute-start(s16[8,64,256]{2,1,0:T(8,128)(2,1)S(1)} %pad_add_fusion.refs_0_), channel_id=1, source_target_pairs={{0,1},{1,0},{2,3},{3,2},{4,5},{5,4},{6,7},{7,6},{8,9},{9,8},{10,11... | collective-permute-start | bytes 786440 | tf_op jit(solution)/shard_map/ppermute | solution.py:246

commit v17 on v14

--- a/solution.py
+++ b/solution.py
@@ -88,17 +88,21 @@
     copies = {}
     first = 0
     for part, count in enumerate(parts):
-        span = pl.ds(first * SLOT, count * SLOT)
-        copies[first] = pltpu.make_async_copy(points.at[span], held.at[span], arrived.at[part])
-        copies[first].start(priority=part % 2)
+        copies[first] = []
+        half = count * SLOT // 2
+        for side in range(2):
+            span = pl.ds(first * SLOT + side * half, half)
+            copy = pltpu.make_async_copy(points.at[span], held.at[span], arrived.at[2 * part + side])
+            copy.start(priority=side)
+            copies[first].append(copy)
         first += count
     for sums in (first_half, second_half):
         sums[...] = jnp.zeros_like(sums)
     for copy in firsts:
         copy.wait()
     for block in range(blocks):
-        if block in copies:
-            copies[block].wait()
+        for copy in copies.get(block, ()):
+            copy.wait()
         span = slice(block * SLOT, (block + 1) * SLOT)
         add_block(
             (first_half, second_half),
@@ -232,7 +236,8 @@
     bits = late_bits(shards)
     late = 1 << len(bits)
     group = 2 if blocks % 2 == 0 else 1
-    parts = [count for count in (blocks // 2, blocks // 3, blocks - blocks // 2 - blocks // 3) if count]
+    third = blocks // 3
+    parts = [count for count in (third, blocks - 2 * third + 1, third - 1) if count > 0]
     limit = pltpu.CompilerParams(vmem_limit_bytes=8 * MIB + 4 * total * feat_width)
     smem = pl.BlockSpec(memory_space=pltpu.SMEM)
     vmem = pl.BlockSpec(memory_space=pltpu.VMEM)
@@ -261,7 +266,7 @@
             pltpu.SMEM((blocks,), jnp.int32),
             pltpu.VMEM((blocks, SLOT), jnp.int32),
             pltpu.SemaphoreType.DMA((3,)),
-            pltpu.SemaphoreType.DMA((len(parts),)),
+            pltpu.SemaphoreType.DMA((2 * len(parts),)),
         ],
         compiler_params=limit,
         cost_estimate=cost,

time: 37.5 us -> 37.6 us (level)
  no operation moved by 1% of the time
where the time goes in v17:
time: 37.6 us; the launch traced here: 37.4 us
  starting transfers between devices  20.8 us (55%)
  Pallas kernels  9.3 us (25%)
  waiting for transfers between devices  5.41 us (14%)
  between operations  1.42 us (4%)
  other arithmetic  0.44 us (1%)
    ppermute x20, starting transfers between devices, swap(): return lax.ppermute(value, ('shard', 'sub'), pairs)  20.8 us
    ppermute x20, waiting for transfers between devices, swap(): return lax.ppermute(value, ('shard', 'sub'), pairs)  5.41 us
    pallas_call x2, Pallas kernels, scores(): pl.pallas_call(functools.partial(score_kernel, half=half, last=last, bloc...  3.97 us
    pallas_call x1, Pallas kernels, local(): pl.pallas_call(functools.partial(send_kernel, parts=parts, **sizes), out_...  2.51 us
    pallas_call x1, Pallas kernels, local(): pl.pallas_call(functools.partial(keep_kernel, **sizes), out_shape=(shape,...  1.29 us
    pallas_call x2, Pallas kernels, rows_of(): pl.pallas_call(functools.partial(rows_kernel, shards=shards, subs=subs, r...  0.95 us
  transfers between devices with their start and end apart: 20, of which 12 were waited for; matrix products, arithmetic and copies ran while one was open for 1% of the time, Pallas kernels for 11%

profile of v17, /device:TPU:0, one launch (start us, length us, event | category | flops | bytes accessed | tf_op | source)
XLA Modules:
  0.0 37.4 jit_solution(8061834542815827320)
XLA Ops:
  0.6 0.0 copy-start.2
  0.6 0.0 copy-start
  0.7 0.0 copy-start.1
  1.3 2.5 %sums_send.1 = (f32[4,2,64,256]{3,2,1,0:T(8,128)S(1)}, f32[4,2,64,256]{3,2,1,0:T(8,128)S(1)}, bf16[1536,1024]{1,0:T(8,128)(2,1)S(1)}) custom-call(s32[1]{0:T(128)S(6)} %copy.7.live_in.live, s32[12]{0:T(128)} %bids.5, s32[12,128]{1,0:T(8,128)} %bitcast.26, bf16[1536,1024]{1,0:T(8,128)(2,1)} %points.1), custom_call_target="tpu_custom_call" | custom-call | flops 201326592 | bytes 1572864 | tf_op jit(solution)/shard_map/sums_send/pallas_call | solution.py:259
  3.9 0.5 %collective-permute-start = (f32[4,2,64,256]{3,2,1,0:T(8,128)S(1)}, f32[4,2,64,256]{3,2,1,0:T(8,128)S(1)}, u32[]{:S(2)}, u32[]{:S(2)}) collective-permute-start(f32[4,2,64,256]{3,2,1,0:T(8,128)S(1)} %get-tuple-element.29), channel_id=1, source_target_pairs={{0,1},{1,0},{2,3},{3,2},{4,5},{5,4},{6,7},{7,6},{8,9},{9,8},{10,11... | collective-permute-start | bytes 1572872 | tf_op jit(solution)/shard_map/ppermute | solution.py:251
  4.4 0.1 collective-permute-start.7
  4.5 0.0 copy-done.2
  4.5 0.0 copy-done
  4.5 0.0 copy-done.1
  4.5 1.3 %sums_keep.1 = (f32[4,2,64,256]{3,2,1,0:T(8,128)S(1)}, f32[4,2,64,256]{3,2,1,0:T(8,128)S(1)}) custom-call(s32[1]{0:T(128)S(6)} %copy.7.live_in.live, s32[12]{0:T(128)S(1)} %copy-done.2, s32[12,128]{1,0:T(8,128)S(1)} %bitcast.27, bf16[128,256]{1,0:T(8,128)(2,1)S(1)} %copy-done.1, bf16[1536,1024]{1,0:T(8,128)(2,1)S(1)} %get-tuple-element.27.points), custom_call_target="tpu_custom_call" | custom-call | flops 201326592 | bytes 1572864 | tf_op jit(solution)/shard_map/sums_keep/pallas_call | solution.py:276
  5.8 0.2 collective-permute-done.crossed
  5.9 0.2 fusion.5
  6.1 3.9 %collective-permute-start.3 = (s16[2,64,256]{2,1,0:T(8,128)(2,1)S(1)}, s16[2,64,256]{2,1,0:T(8,128)(2,1)S(1)}, u32[]{:S(2)}, u32[]{:S(2)}) collective-permute-start(s16[2,64,256]{2,1,0:T(8,128)(2,1)S(1)} %get-tuple-element.55), channel_id=1, source_target_pairs={{0,6},{1,7},{2,4},{3,5},{4,2},{5,3},{6,0},{7,1},{8,14},{9,15},{10,... | collective-permute-start | bytes 196616 | tf_op jit(solution)/shard_map/ppermute | solution.py:251
  10.1 0.4 %collective-permute-start.2 = (s16[2,64,256]{2,1,0:T(8,128)(2,1)S(1)}, s16[2,64,256]{2,1,0:T(8,128)(2,1)S(1)}, u32[]{:S(2)}, u32[]{:S(2)}) collective-permute-start(s16[2,64,256]{2,1,0:T(8,128)(2,1)S(1)} %get-tuple-element.56), channel_id=1, source_target_pairs={{0,4},{1,5},{2,6},{3,7},{4,0},{5,1},{6,2},{7,3},{8,12},{9,13},{10,... | collective-permute-start | bytes 196616 | tf_op jit(solution)/shard_map/ppermute | solution.py:251
  10.5 0.2 collective-permute-start.1
  10.7 0.0 collective-permute-done.7.crossed
  10.7 0.2 fusion.11
  10.9 2.9 %collective-permute-start.10 = (s16[2,64,256]{2,1,0:T(8,128)(2,1)S(1)}, s16[2,64,256]{2,1,0:T(8,128)(2,1)S(1)}, u32[]{:S(2)}, u32[]{:S(2)}) collective-permute-start(s16[2,64,256]{2,1,0:T(8,128)(2,1)S(1)} %get-tuple-element.52), channel_id=1, source_target_pairs={{0,6},{1,7},{2,4},{3,5},{4,2},{5,3},{6,0},{7,1},{8,14},{9,15},{10,... | collective-permute-start | bytes 196616 | tf_op jit(solution)/shard_map/ppermute | solution.py:251
  13.8 0.4 %collective-permute-start.9 = (s16[2,64,256]{2,1,0:T(8,128)(2,1)S(1)}, s16[2,64,256]{2,1,0:T(8,128)(2,1)S(1)}, u32[]{:S(2)}, u32[]{:S(2)}) collective-permute-start(s16[2,64,256]{2,1,0:T(8,128)(2,1)S(1)} %get-tuple-element.53), channel_id=1, source_target_pairs={{0,4},{1,5},{2,6},{3,7},{4,0},{5,1},{6,2},{7,3},{8,12},{9,13},{10,... | collective-permute-start | bytes 196616 | tf_op jit(solution)/shard_map/ppermute | solution.py:251
  14.3 0.0 collective-permute-done.3.refs_2_
  14.3 0.2 collective-permute-start.8
  14.5 0.1 collective-permute-done.2.refs_1_
  14.6 0.9 %collective-permute-done.1.refs_0_ = s16[2,64,256]{2,1,0:T(8,128)(2,1)S(1)} collective-permute-done((s16[2,64,256]{2,1,0:T(8,128)(2,1)S(1)}, s16[2,64,256]{2,1,0:T(8,128)(2,1)S(1)}, u32[]{:S(2)}, u32[]{:S(2)}) %collective-permute-start.1) | collective-permute-done | bytes 65568 | tf_op jit(solution)/shard_map/ppermute | solution.py:251
  15.5 0.2 mix0.1
  15.7 2.7 %collective-permute-start.4 = (s16[2,64,256]{2,1,0:T(8,128)(2,1)S(1)}, s16[2,64,256]{2,1,0:T(8,128)(2,1)S(1)}, u32[]{:S(2)}, u32[]{:S(2)}) collective-permute-start(s16[2,64,256]{2,1,0:T(8,128)(2,1)S(1)} %get-tuple-element.31), channel_id=1, source_target_pairs={{0,8},{1,9},{2,10},{3,11},{4,12},{5,13},{6,14},{7,15},{8,0},{9,1},... | collective-permute-start | bytes 196616 | tf_op jit(solution)/shard_map/ppermute | solution.py:251
  18.3 0.0 collective-permute-done.10.refs_2_
  18.3 0.2 collective-permute-done.9.refs_1_
  18.5 0.1 collective-permute-done.8.refs_0_
  18.5 0.2 mix1.1
  18.7 2.7 %collective-permute-start.11 = (s16[2,64,256]{2,1,0:T(8,128)(2,1)S(1)}, s16[2,64,256]{2,1,0:T(8,128)(2,1)S(1)}, u32[]{:S(2)}, u32[]{:S(2)}) collective-permute-start(s16[2,64,256]{2,1,0:T(8,128)(2,1)S(1)} %get-tuple-element.40), channel_id=1, source_target_pairs={{0,8},{1,9},{2,10},{3,11},{4,12},{5,13},{6,14},{7,15},{8,0},{9,1},... | collective-permute-start | bytes 196616 | tf_op jit(solution)/shard_map/ppermute | solution.py:251
  21.4 0.0 collective-permute-done.4.there
  21.4 0.1 finish0.1
  21.5 0.8 %collective-permute-start.5 = (s16[2,64,256]{2,1,0:T(8,128)(2,1)S(1)}, s16[2,64,256]{2,1,0:T(8,128)(2,1)S(1)}, u32[]{:S(2)}, u32[]{:S(2)}) collective-permute-start(s16[2,64,256]{2,1,0:T(8,128)(2,1)S(1)} %get-tuple-element.33), channel_id=1, source_target_pairs={{0,2},{1,3},{2,0},{3,1},{4,6},{5,7},{6,4},{7,5},{8,10},{9,11},{10,... | collective-permute-start | bytes 196616 | tf_op jit(solution)/shard_map/ppermute | solution.py:251
  22.3 1.7 %collective-permute-done.11.there = s16[2,64,256]{2,1,0:T(8,128)(2,1)S(1)} collective-permute-done((s16[2,64,256]{2,1,0:T(8,128)(2,1)S(1)}, s16[2,64,256]{2,1,0:T(8,128)(2,1)S(1)}, u32[]{:S(2)}, u32[]{:S(2)}) %collective-permute-start.11) | collective-permute-done | bytes 65568 | tf_op jit(solution)/shard_map/ppermute | solution.py:251
  24.0 0.1 finish1.1
  24.1 1.7 %collective-permute-start.14 = (s16[2,64,256]{2,1,0:T(8,128)(2,1)S(1)}, s16[2,64,256]{2,1,0:T(8,128)(2,1)S(1)}, u32[]{:S(2)}, u32[]{:S(2)}) collective-permute-start(s16[2,64,256]{2,1,0:T(8,128)(2,1)S(1)} %get-tuple-element.42.refs_0_), channel_id=1, source_target_pairs={{0,6},{1,7},{2,4},{3,5},{4,2},{5,3},{6,0},{7,1},{8,14},{9,15},{10,... | collective-permute-start | bytes 196616 | tf_op jit(solution)/shard_map/ppermute | solution.py:251
  25.8 0.5 %collective-permute-start.13 = (s16[2,64,256]{2,1,0:T(8,128)(2,1)S(1)}, s16[2,64,256]{2,1,0:T(8,128)(2,1)S(1)}, u32[]{:S(2)}, u32[]{:S(2)}) collective-permute-start(s16[2,64,256]{2,1,0:T(8,128)(2,1)S(1)} %get-tuple-element.42.refs_0_), channel_id=1, source_target_pairs={{0,4},{1,5},{2,6},{3,7},{4,0},{5,1},{6,2},{7,3},{8,12},{9,13},{10,... | collective-permute-start | bytes 196616 | tf_op jit(solution)/shard_map/ppermute | solution.py:251
  26.2 1.4 %collective-permute-start.12 = (s16[2,64,256]{2,1,0:T(8,128)(2,1)S(1)}, s16[2,64,256]{2,1,0:T(8,128)(2,1)S(1)}, u32[]{:S(2)}, u32[]{:S(2)}) collective-permute-start(s16[2,64,256]{2,1,0:T(8,128)(2,1)S(1)} %get-tuple-element.42.refs_0_), channel_id=1, source_target_pairs={{0,2},{1,3},{2,0},{3,1},{4,6},{5,7},{6,4},{7,5},{8,10},{9,11},{10,... | collective-permute-start | bytes 196616 | tf_op jit(solution)/shard_map/ppermute | solution.py:251
  27.6 0.0 collective-permute-done.5
  27.6 1.6 %collective-permute-start.6 = (s16[4,64,256]{2,1,0:T(8,128)(2,1)S(1)}, s16[4,64,256]{2,1,0:T(8,128)(2,1)S(1)}, u32[]{:S(2)}, u32[]{:S(2)}) collective-permute-start(s16[4,64,256]{2,1,0:T(8,128)(2,1)S(1)} %pad_add_fusion.1), channel_id=1, source_target_pairs={{0,4},{1,5},{2,6},{3,7},{4,0},{5,1},{6,2},{7,3},{8,12},{9,13},{10,... | collective-permute-start | bytes 393224 | tf_op jit(solution)/shard_map/ppermute | solution.py:251
  29.3 0.0 collective-permute-start.15
  29.3 0.7 %collective-permute-done.14.refs_3_ = s16[2,64,256]{2,1,0:T(8,128)(2,1)S(1)} collective-permute-done((s16[2,64,256]{2,1,0:T(8,128)(2,1)S(1)}, s16[2,64,256]{2,1,0:T(8,128)(2,1)S(1)}, u32[]{:S(2)}, u32[]{:S(2)}) %collective-permute-start.14) | collective-permute-done | bytes 65568 | tf_op jit(solution)/shard_map/ppermute | solution.py:251
  30.0 0.0 collective-permute-start.18
  30.0 0.6 %collective-permute-done.13.refs_2_ = s16[2,64,256]{2,1,0:T(8,128)(2,1)S(1)} collective-permute-done((s16[2,64,256]{2,1,0:T(8,128)(2,1)S(1)}, s16[2,64,256]{2,1,0:T(8,128)(2,1)S(1)}, u32[]{:S(2)}, u32[]{:S(2)}) %collective-permute-start.13) | collective-permute-done | bytes 65568 | tf_op jit(solution)/shard_map/ppermute | solution.py:251
  30.6 0.0 collective-permute-start.17
  30.6 0.0 collective-permute-done.12.refs_1_
  30.6 0.5 %collective-permute-start.16 = (s16[2,64,256]{2,1,0:T(8,128)(2,1)S(1)}, s16[2,64,256]{2,1,0:T(8,128)(2,1)S(1)}, u32[]{:S(2)}, u32[]{:S(2)}) collective-permute-start(s16[2,64,256]{2,1,0:T(8,128)(2,1)S(1)} %collective-permute-done.12.refs_1_), channel_id=1, source_target_pairs={{0,1},{1,0},{2,3},{3,2},{4,5},{5,4},{6,7},{7,6},{8,9},{9,8},{10,11... | collective-permute-start | bytes 196616 | tf_op jit(solution)/shard_map/ppermute | solution.py:251
  31.1 0.0 collective-permute-done.15.refs_4_
  31.1 0.2 collective-permute-done.18.refs_7_
  31.3 0.6 %collective-permute-done.17.refs_6_ = s16[2,64,256]{2,1,0:T(8,128)(2,1)S(1)} collective-permute-done((s16[2,64,256]{2,1,0:T(8,128)(2,1)S(1)}, s16[2,64,256]{2,1,0:T(8,128)(2,1)S(1)}, u32[]{:S(2)}, u32[]{:S(2)}) %collective-permute-start.17) | collective-permute-done | bytes 65568 | tf_op jit(solution)/shard_map/ppermute | solution.py:251
  31.8 0.2 collective-permute-done.16.refs_5_
  32.0 0.5 %rows1.1 = (bf16[64,256]{1,0:T(8,128)(2,1)S(1)}, bf16[256,1024]{1,0:T(8,128)(2,1)S(1)}) custom-call(f32[64,256]{1,0:T(8,128)S(1)} %get-tuple-element.41.own, s16[2,64,256]{2,1,0:T(8,128)(2,1)S(1)} %get-tuple-element.42.refs_0_, s16[2,64,256]{2,1,0:T(8,128)(2,1)S(1)} %collective-permute-done.12.refs_1_, ...), custom_call_target="tpu_custom_call" | custom-call | tf_op jit(solution)/shard_map/rows1/pallas_call | solution.py:325
  32.5 0.2 collective-permute-done.6
  32.7 0.2 collective-permute-start.19
  32.9 1.7 %scores1.1 = (f32[12,128]{1,0:T(8,128)S(1)}, f32[12,128]{1,0:T(8,128)S(1)}) custom-call(s32[12]{0:T(128)S(1)} %copy-done.2, s32[12,128]{1,0:T(8,128)S(1)} %bitcast.28, bf16[1536,1024]{1,0:T(8,128)(2,1)S(1)} %get-tuple-element.27.points, bf16[256,1024]{1,0:T(8,128)(2,1)S(1)} %get-tuple-element.46.cents), custom_call_target="tpu_custom_call" | custom-call | flops 805306368 | bytes 3145728 | tf_op jit(solution)/shard_map/scores1/pallas_call | solution.py:340
  34.6 0.0 collective-permute-done.19.refs_1_
  34.6 0.5 %rows0.1 = (bf16[64,256]{1,0:T(8,128)(2,1)S(1)}, bf16[256,1024]{1,0:T(8,128)(2,1)S(1)}) custom-call(f32[64,256]{1,0:T(8,128)S(1)} %get-tuple-element.32.own, s16[8,64,256]{2,1,0:T(8,128)(2,1)S(1)} %pad_add_fusion.refs_0_, s16[8,64,256]{2,1,0:T(8,128)(2,1)S(1)} %collective-permute-done.19.refs_1_), custom_call_target="tpu_custom_call" | custom-call | tf_op jit(solution)/shard_map/rows0/pallas_call | solution.py:325
  35.1 2.3 %scores0.1 = (bf16[128,256]{1,0:T(8,128)(2,1)}, f32[12,128]{1,0:T(8,128)}) custom-call(s32[12]{0:T(128)S(1)} %copy-done.2, s32[12,128]{1,0:T(8,128)S(1)} %bitcast.29, bf16[1536,1024]{1,0:T(8,128)(2,1)S(1)} %get-tuple-element.27.points, bf16[256,1024]{1,0:T(8,128)(2,1)S(1)} %get-tuple-element.45.cents, f32[12,128]{1,0:T(8,128)S(1)} %get-tuple-element.47.refs_0_, ...), custom_call_target="tpu_custom_call" | custom-call | flops 805306368 | bytes 3145728 | tf_op jit(solution)/shard_map/scores0/pallas_call | solution.py:340
  (2 shorter events, 0.0 us)
Async XLA Ops:
  0.6 3.8 %copy-start.2 = (s32[12]{0:T(128)S(1)}, s32[12]{0:T(128)}, u32[]{:S(2)}) copy-start(s32[12]{0:T(128)} %bids.5) | copy-start | bytes 148
  0.6 3.8 %copy-start = (s32[1536]{0:T(1024)S(1)}, s32[1536]{0:T(1024)}, u32[]{:S(2)}) copy-start(s32[1536]{0:T(1024)} %param.7) | copy-start | bytes 18436
  0.7 3.8 %copy-start.1 = (bf16[128,256]{1,0:T(8,128)(2,1)S(1)}, bf16[128,256]{1,0:T(8,128)(2,1)}, u32[]{:S(2)}) copy-start(bf16[128,256]{1,0:T(8,128)(2,1)} %old.1) | copy-start | bytes 196612
  3.9 2.1 %collective-permute-start = (f32[4,2,64,256]{3,2,1,0:T(8,128)S(1)}, f32[4,2,64,256]{3,2,1,0:T(8,128)S(1)}, u32[]{:S(2)}, u32[]{:S(2)}) collective-permute-start(f32[4,2,64,256]{3,2,1,0:T(8,128)S(1)} %get-tuple-element.29), channel_id=1, source_target_pairs={{0,1},{1,0},{2,3},{3,2},{4,5},{5,4},{6,7},{7,6},{8,9},{9,8},{10,11... | collective-permute-start | bytes 1572872 | tf_op jit(solution)/shard_map/ppermute | solution.py:251
  4.4 6.3 %collective-permute-start.7 = (f32[4,2,64,256]{3,2,1,0:T(8,128)S(1)}, f32[4,2,64,256]{3,2,1,0:T(8,128)S(1)}, u32[]{:S(2)}, u32[]{:S(2)}) collective-permute-start(f32[4,2,64,256]{3,2,1,0:T(8,128)S(1)} %get-tuple-element.36), channel_id=1, source_target_pairs={{0,1},{1,0},{2,3},{3,2},{4,5},{5,4},{6,7},{7,6},{8,9},{9,8},{10,11... | collective-permute-start | bytes 1572872 | tf_op jit(solution)/shard_map/ppermute | solution.py:251
  6.1 8.2 %collective-permute-start.3 = (s16[2,64,256]{2,1,0:T(8,128)(2,1)S(1)}, s16[2,64,256]{2,1,0:T(8,128)(2,1)S(1)}, u32[]{:S(2)}, u32[]{:S(2)}) collective-permute-start(s16[2,64,256]{2,1,0:T(8,128)(2,1)S(1)} %get-tuple-element.55), channel_id=1, source_target_pairs={{0,6},{1,7},{2,4},{3,5},{4,2},{5,3},{6,0},{7,1},{8,14},{9,15},{10,... | collective-permute-start | bytes 196616 | tf_op jit(solution)/shard_map/ppermute | solution.py:251
  10.1 4.5 %collective-permute-start.2 = (s16[2,64,256]{2,1,0:T(8,128)(2,1)S(1)}, s16[2,64,256]{2,1,0:T(8,128)(2,1)S(1)}, u32[]{:S(2)}, u32[]{:S(2)}) collective-permute-start(s16[2,64,256]{2,1,0:T(8,128)(2,1)S(1)} %get-tuple-element.56), channel_id=1, source_target_pairs={{0,4},{1,5},{2,6},{3,7},{4,0},{5,1},{6,2},{7,3},{8,12},{9,13},{10,... | collective-permute-start | bytes 196616 | tf_op jit(solution)/shard_map/ppermute | solution.py:251
  10.5 5.0 %collective-permute-start.1 = (s16[2,64,256]{2,1,0:T(8,128)(2,1)S(1)}, s16[2,64,256]{2,1,0:T(8,128)(2,1)S(1)}, u32[]{:S(2)}, u32[]{:S(2)}) collective-permute-start(s16[2,64,256]{2,1,0:T(8,128)(2,1)S(1)} %get-tuple-element.57), channel_id=1, source_target_pairs={{0,2},{1,3},{2,0},{3,1},{4,6},{5,7},{6,4},{7,5},{8,10},{9,11},{10,... | collective-permute-start | bytes 196616 | tf_op jit(solution)/shard_map/ppermute | solution.py:251
  10.9 7.4 %collective-permute-start.10 = (s16[2,64,256]{2,1,0:T(8,128)(2,1)S(1)}, s16[2,64,256]{2,1,0:T(8,128)(2,1)S(1)}, u32[]{:S(2)}, u32[]{:S(2)}) collective-permute-start(s16[2,64,256]{2,1,0:T(8,128)(2,1)S(1)} %get-tuple-element.52), channel_id=1, source_target_pairs={{0,6},{1,7},{2,4},{3,5},{4,2},{5,3},{6,0},{7,1},{8,14},{9,15},{10,... | collective-permute-start | bytes 196616 | tf_op jit(solution)/shard_map/ppermute | solution.py:251
  13.8 4.7 %collective-permute-start.9 = (s16[2,64,256]{2,1,0:T(8,128)(2,1)S(1)}, s16[2,64,256]{2,1,0:T(8,128)(2,1)S(1)}, u32[]{:S(2)}, u32[]{:S(2)}) collective-permute-start(s16[2,64,256]{2,1,0:T(8,128)(2,1)S(1)} %get-tuple-element.53), channel_id=1, source_target_pairs={{0,4},{1,5},{2,6},{3,7},{4,0},{5,1},{6,2},{7,3},{8,12},{9,13},{10,... | collective-permute-start | bytes 196616 | tf_op jit(solution)/shard_map/ppermute | solution.py:251
  14.3 4.3 %collective-permute-start.8 = (s16[2,64,256]{2,1,0:T(8,128)(2,1)S(1)}, s16[2,64,256]{2,1,0:T(8,128)(2,1)S(1)}, u32[]{:S(2)}, u32[]{:S(2)}) collective-permute-start(s16[2,64,256]{2,1,0:T(8,128)(2,1)S(1)} %get-tuple-element.54), channel_id=1, source_target_pairs={{0,2},{1,3},{2,0},{3,1},{4,6},{5,7},{6,4},{7,5},{8,10},{9,11},{10,... | collective-permute-start | bytes 196616 | tf_op jit(solution)/shard_map/ppermute | solution.py:251
  15.7 5.7 %collective-permute-start.4 = (s16[2,64,256]{2,1,0:T(8,128)(2,1)S(1)}, s16[2,64,256]{2,1,0:T(8,128)(2,1)S(1)}, u32[]{:S(2)}, u32[]{:S(2)}) collective-permute-start(s16[2,64,256]{2,1,0:T(8,128)(2,1)S(1)} %get-tuple-element.31), channel_id=1, source_target_pairs={{0,8},{1,9},{2,10},{3,11},{4,12},{5,13},{6,14},{7,15},{8,0},{9,1},... | collective-permute-start | bytes 196616 | tf_op jit(solution)/shard_map/ppermute | solution.py:251
  18.7 5.2 %collective-permute-start.11 = (s16[2,64,256]{2,1,0:T(8,128)(2,1)S(1)}, s16[2,64,256]{2,1,0:T(8,128)(2,1)S(1)}, u32[]{:S(2)}, u32[]{:S(2)}) collective-permute-start(s16[2,64,256]{2,1,0:T(8,128)(2,1)S(1)} %get-tuple-element.40), channel_id=1, source_target_pairs={{0,8},{1,9},{2,10},{3,11},{4,12},{5,13},{6,14},{7,15},{8,0},{9,1},... | collective-permute-start | bytes 196616 | tf_op jit(solution)/shard_map/ppermute | solution.py:251
  21.5 6.1 %collective-permute-start.5 = (s16[2,64,256]{2,1,0:T(8,128)(2,1)S(1)}, s16[2,64,256]{2,1,0:T(8,128)(2,1)S(1)}, u32[]{:S(2)}, u32[]{:S(2)}) collective-permute-start(s16[2,64,256]{2,1,0:T(8,128)(2,1)S(1)} %get-tuple-element.33), channel_id=1, source_target_pairs={{0,2},{1,3},{2,0},{3,1},{4,6},{5,7},{6,4},{7,5},{8,10},{9,11},{10,... | collective-permute-start | bytes 196616 | tf_op jit(solution)/shard_map/ppermute | solution.py:251
  24.1 5.9 %collective-permute-start.14 = (s16[2,64,256]{2,1,0:T(8,128)(2,1)S(1)}, s16[2,64,256]{2,1,0:T(8,128)(2,1)S(1)}, u32[]{:S(2)}, u32[]{:S(2)}) collective-permute-start(s16[2,64,256]{2,1,0:T(8,128)(2,1)S(1)} %get-tuple-element.42.refs_0_), channel_id=1, source_target_pairs={{0,6},{1,7},{2,4},{3,5},{4,2},{5,3},{6,0},{7,1},{8,14},{9,15},{10,... | collective-permute-start | bytes 196616 | tf_op jit(solution)/shard_map/ppermute | solution.py:251
  25.8 4.8 %collective-permute-start.13 = (s16[2,64,256]{2,1,0:T(8,128)(2,1)S(1)}, s16[2,64,256]{2,1,0:T(8,128)(2,1)S(1)}, u32[]{:S(2)}, u32[]{:S(2)}) collective-permute-start(s16[2,64,256]{2,1,0:T(8,128)(2,1)S(1)} %get-tuple-element.42.refs_0_), channel_id=1, source_target_pairs={{0,4},{1,5},{2,6},{3,7},{4,0},{5,1},{6,2},{7,3},{8,12},{9,13},{10,... | collective-permute-start | bytes 196616 | tf_op jit(solution)/shard_map/ppermute | solution.py:251
  26.2 4.4 %collective-permute-start.12 = (s16[2,64,256]{2,1,0:T(8,128)(2,1)S(1)}, s16[2,64,256]{2,1,0:T(8,128)(2,1)S(1)}, u32[]{:S(2)}, u32[]{:S(2)}) collective-permute-start(s16[2,64,256]{2,1,0:T(8,128)(2,1)S(1)} %get-tuple-element.42.refs_0_), channel_id=1, source_target_pairs={{0,2},{1,3},{2,0},{3,1},{4,6},{5,7},{6,4},{7,5},{8,10},{9,11},{10,... | collective-permute-start | bytes 196616 | tf_op jit(solution)/shard_map/ppermute | solution.py:251
  27.6 5.0 %collective-permute-start.6 = (s16[4,64,256]{2,1,0:T(8,128)(2,1)S(1)}, s16[4,64,256]{2,1,0:T(8,128)(2,1)S(1)}, u32[]{:S(2)}, u32[]{:S(2)}) collective-permute-start(s16[4,64,256]{2,1,0:T(8,128)(2,1)S(1)} %pad_add_fusion.1), channel_id=1, source_target_pairs={{0,4},{1,5},{2,6},{3,7},{4,0},{5,1},{6,2},{7,3},{8,12},{9,13},{10,... | collective-permute-start | bytes 393224 | tf_op jit(solution)/shard_map/ppermute | solution.py:251
  29.3 1.8 %collective-permute-start.15 = (s16[2,64,256]{2,1,0:T(8,128)(2,1)S(1)}, s16[2,64,256]{2,1,0:T(8,128)(2,1)S(1)}, u32[]{:S(2)}, u32[]{:S(2)}) collective-permute-start(s16[2,64,256]{2,1,0:T(8,128)(2,1)S(1)} %get-tuple-element.42.refs_0_), channel_id=1, source_target_pairs={{0,1},{1,0},{2,3},{3,2},{4,5},{5,4},{6,7},{7,6},{8,9},{9,8},{10,11... | collective-permute-start | bytes 196616 | tf_op jit(solution)/shard_map/ppermute | solution.py:251
  30.0 1.3 %collective-permute-start.18 = (s16[2,64,256]{2,1,0:T(8,128)(2,1)S(1)}, s16[2,64,256]{2,1,0:T(8,128)(2,1)S(1)}, u32[]{:S(2)}, u32[]{:S(2)}) collective-permute-start(s16[2,64,256]{2,1,0:T(8,128)(2,1)S(1)} %collective-permute-done.14.refs_3_), channel_id=1, source_target_pairs={{0,1},{1,0},{2,3},{3,2},{4,5},{5,4},{6,7},{7,6},{8,9},{9,8},{10,11... | collective-permute-start | bytes 196616 | tf_op jit(solution)/shard_map/ppermute | solution.py:251
  30.6 1.3 %collective-permute-start.17 = (s16[2,64,256]{2,1,0:T(8,128)(2,1)S(1)}, s16[2,64,256]{2,1,0:T(8,128)(2,1)S(1)}, u32[]{:S(2)}, u32[]{:S(2)}) collective-permute-start(s16[2,64,256]{2,1,0:T(8,128)(2,1)S(1)} %collective-permute-done.13.refs_2_), channel_id=1, source_target_pairs={{0,1},{1,0},{2,3},{3,2},{4,5},{5,4},{6,7},{7,6},{8,9},{9,8},{10,11... | collective-permute-start | bytes 196616 | tf_op jit(solution)/shard_map/ppermute | solution.py:251
  30.6 1.4 %collective-permute-start.16 = (s16[2,64,256]{2,1,0:T(8,128)(2,1)S(1)}, s16[2,64,256]{2,1,0:T(8,128)(2,1)S(1)}, u32[]{:S(2)}, u32[]{:S(2)}) collective-permute-start(s16[2,64,256]{2,1,0:T(8,128)(2,1)S(1)} %collective-permute-done.12.refs_1_), channel_id=1, source_target_pairs={{0,1},{1,0},{2,3},{3,2},{4,5},{5,4},{6,7},{7,6},{8,9},{9,8},{10,11... | collective-permute-start | bytes 196616 | tf_op jit(solution)/shard_map/ppermute | solution.py:251
  32.7 1.9 %collective-permute-start.19 = (s16[8,64,256]{2,1,0:T(8,128)(2,1)S(1)}, s16[8,64,256]{2,1,0:T(8,128)(2,1)S(1)}, u32[]{:S(2)}, u32[]{:S(2)}) collective-permute-start(s16[8,64,256]{2,1,0:T(8,128)(2,1)S(1)} %pad_add_fusion.refs_0_), channel_id=1, source_target_pairs={{0,1},{1,0},{2,3},{3,2},{4,5},{5,4},{6,7},{7,6},{8,9},{9,8},{10,11... | collective-permute-start | bytes 786440 | tf_op jit(solution)/shard_map/ppermute | solution.py:251

commit v18 on v14

--- a/solution.py
+++ b/solution.py
@@ -39,10 +39,9 @@
 
 
 def near_group(subs, shards):
-    group = [(0, 0)]
+    group = [(0, 0), (0, 1)]
     for bit in bits_of(subs)[1:]:
         group = group + [(sub ^ bit, shard) for sub, shard in group]
-    group = group + [(sub, shard ^ 1) for sub, shard in group]
     return group
 
 
@@ -355,8 +354,8 @@
     first_own, first_code = finish(0, *first)
     second_own, second_code = finish(1, *second, first_code)
     own, codes = (first_own, second_own), (first_code, second_code)
-    near = jnp.concatenate([codes[0], swap(codes[0], 2, 0)])
-    near = [jnp.concatenate([near, swap(near, 0, 1)])]
+    near = jnp.concatenate([codes[0], swap(codes[0], 0, 1)])
+    near = [jnp.concatenate([near, swap(near, 2, 0)])]
     blocks_near = [codes[1]] + [swap(codes[1], *chip) for chip in chips[1:]]
     second_fresh, second_rows = rows_of(1, own[1], blocks_near, [swap(block, 1, 0) for block in blocks_near])
     mine, rival = scores(1, False, second_rows)

time: 37.5 us -> 38.9 us (1.037)
  Pallas kernels: 9.24 us -> 10 us
  waiting for transfers between devices: 5.41 us -> 6.04 us
    ppermute x20, waiting for transfers between devices: 5.41 us -> 6.04 us  [swap(): return lax.ppermute(value, ('shard', 'sub'), pairs)]
    pallas_call x1, Pallas kernels: 1.28 us -> 1.77 us  [local(): pl.pallas_call(functools.partial(keep_kernel, **sizes), out_shape=(shape,...]
  transfers between devices with their start and end apart: 20 -> 20, of which waited for: 12 -> 8; matrix products, arithmetic and copies ran while one was open for 1% -> 1% of each run, Pallas kernels for 11% -> 12%
where the time goes in v18:
time: 38.9 us; the launch traced here: 38.7 us
  starting transfers between devices  20.8 us (53%)
  Pallas kernels  10 us (26%)
  waiting for transfers between devices  6.04 us (16%)
  between operations  1.44 us (4%)
  other arithmetic  0.44 us (1%)
    ppermute x20, starting transfers between devices, swap(): return lax.ppermute(value, ('shard', 'sub'), pairs)  20.8 us
    ppermute x20, waiting for transfers between devices, swap(): return lax.ppermute(value, ('shard', 'sub'), pairs)  6.04 us
    pallas_call x2, Pallas kernels, scores(): pl.pallas_call(functools.partial(score_kernel, half=half, last=last, bloc...  3.98 us
    pallas_call x1, Pallas kernels, local(): pl.pallas_call(functools.partial(send_kernel, parts=parts, **sizes), out_...  2.73 us
    pallas_call x1, Pallas kernels, local(): pl.pallas_call(functools.partial(keep_kernel, **sizes), out_shape=(shape,...  1.77 us
    pallas_call x2, Pallas kernels, rows_of(): pl.pallas_call(functools.partial(rows_kernel, shards=shards, subs=subs, r...  0.95 us
  transfers between devices with their start and end apart: 20, of which 8 were waited for; matrix products, arithmetic and copies ran while one was open for 1% of the time, Pallas kernels for 12%

profile of v18, /device:TPU:0, one launch (start us, length us, event | category | flops | bytes accessed | tf_op | source)
XLA Modules:
  0.0 38.7 jit_solution(543591750791198976)
XLA Ops:
  0.6 0.0 copy-start.2
  0.6 0.0 copy-start
  0.7 0.0 copy-start.1
  1.3 2.7 %sums_send.1 = (f32[4,2,64,256]{3,2,1,0:T(8,128)S(1)}, f32[4,2,64,256]{3,2,1,0:T(8,128)S(1)}, bf16[1536,1024]{1,0:T(8,128)(2,1)S(1)}) custom-call(s32[1]{0:T(128)S(6)} %copy.7.live_in.live, s32[12]{0:T(128)} %bids.5, s32[12,128]{1,0:T(8,128)} %bitcast.26, bf16[1536,1024]{1,0:T(8,128)(2,1)} %points.1), custom_call_target="tpu_custom_call" | custom-call | flops 201326592 | bytes 1572864 | tf_op jit(solution)/shard_map/sums_send/pallas_call | solution.py:253
  4.1 0.5 %collective-permute-start = (f32[4,2,64,256]{3,2,1,0:T(8,128)S(1)}, f32[4,2,64,256]{3,2,1,0:T(8,128)S(1)}, u32[]{:S(2)}, u32[]{:S(2)}) collective-permute-start(f32[4,2,64,256]{3,2,1,0:T(8,128)S(1)} %get-tuple-element.29), channel_id=1, source_target_pairs={{0,1},{1,0},{2,3},{3,2},{4,5},{5,4},{6,7},{7,6},{8,9},{9,8},{10,11... | collective-permute-start | bytes 1572872 | tf_op jit(solution)/shard_map/ppermute | solution.py:245
  4.6 0.1 collective-permute-start.7
  4.7 0.0 copy-done.2
  4.7 0.0 copy-done
  4.7 0.0 copy-done.1
  4.7 1.8 %sums_keep.1 = (f32[4,2,64,256]{3,2,1,0:T(8,128)S(1)}, f32[4,2,64,256]{3,2,1,0:T(8,128)S(1)}) custom-call(s32[1]{0:T(128)S(6)} %copy.7.live_in.live, s32[12]{0:T(128)S(1)} %copy-done.2, s32[12,128]{1,0:T(8,128)S(1)} %bitcast.27, bf16[128,256]{1,0:T(8,128)(2,1)S(1)} %copy-done.1, bf16[1536,1024]{1,0:T(8,128)(2,1)S(1)} %get-tuple-element.27.points), custom_call_target="tpu_custom_call" | custom-call | flops 201326592 | bytes 1572864 | tf_op jit(solution)/shard_map/sums_keep/pallas_call | solution.py:270
  6.5 0.0 collective-permute-done.crossed
  6.5 0.2 fusion.5
  6.7 4.0 %collective-permute-start.3 = (s16[2,64,256]{2,1,0:T(8,128)(2,1)S(1)}, s16[2,64,256]{2,1,0:T(8,128)(2,1)S(1)}, u32[]{:S(2)}, u32[]{:S(2)}) collective-permute-start(s16[2,64,256]{2,1,0:T(8,128)(2,1)S(1)} %get-tuple-element.55), channel_id=1, source_target_pairs={{0,6},{1,7},{2,4},{3,5},{4,2},{5,3},{6,0},{7,1},{8,14},{9,15},{10,... | collective-permute-start | bytes 196616 | tf_op jit(solution)/shard_map/ppermute | solution.py:245
  10.7 0.5 %collective-permute-start.2 = (s16[2,64,256]{2,1,0:T(8,128)(2,1)S(1)}, s16[2,64,256]{2,1,0:T(8,128)(2,1)S(1)}, u32[]{:S(2)}, u32[]{:S(2)}) collective-permute-start(s16[2,64,256]{2,1,0:T(8,128)(2,1)S(1)} %get-tuple-element.56), channel_id=1, source_target_pairs={{0,2},{1,3},{2,0},{3,1},{4,6},{5,7},{6,4},{7,5},{8,10},{9,11},{10,... | collective-permute-start | bytes 196616 | tf_op jit(solution)/shard_map/ppermute | solution.py:245
  11.2 0.1 collective-permute-start.1
  11.3 0.0 collective-permute-done.7.crossed
  11.3 0.2 fusion.11
  11.5 2.9 %collective-permute-start.10 = (s16[2,64,256]{2,1,0:T(8,128)(2,1)S(1)}, s16[2,64,256]{2,1,0:T(8,128)(2,1)S(1)}, u32[]{:S(2)}, u32[]{:S(2)}) collective-permute-start(s16[2,64,256]{2,1,0:T(8,128)(2,1)S(1)} %get-tuple-element.52), channel_id=1, source_target_pairs={{0,6},{1,7},{2,4},{3,5},{4,2},{5,3},{6,0},{7,1},{8,14},{9,15},{10,... | collective-permute-start | bytes 196616 | tf_op jit(solution)/shard_map/ppermute | solution.py:245
  14.4 0.5 %collective-permute-start.9 = (s16[2,64,256]{2,1,0:T(8,128)(2,1)S(1)}, s16[2,64,256]{2,1,0:T(8,128)(2,1)S(1)}, u32[]{:S(2)}, u32[]{:S(2)}) collective-permute-start(s16[2,64,256]{2,1,0:T(8,128)(2,1)S(1)} %get-tuple-element.53), channel_id=1, source_target_pairs={{0,2},{1,3},{2,0},{3,1},{4,6},{5,7},{6,4},{7,5},{8,10},{9,11},{10,... | collective-permute-start | bytes 196616 | tf_op jit(solution)/shard_map/ppermute | solution.py:245
  15.0 0.0 collective-permute-done.3.refs_2_
  15.0 0.2 collective-permute-start.8
  15.2 0.0 collective-permute-done.2.refs_1_
  15.2 0.9 %collective-permute-done.1.refs_0_ = s16[2,64,256]{2,1,0:T(8,128)(2,1)S(1)} collective-permute-done((s16[2,64,256]{2,1,0:T(8,128)(2,1)S(1)}, s16[2,64,256]{2,1,0:T(8,128)(2,1)S(1)}, u32[]{:S(2)}, u32[]{:S(2)}) %collective-permute-start.1) | collective-permute-done | bytes 65568 | tf_op jit(solution)/shard_map/ppermute | solution.py:245
  16.1 0.2 mix0.1
  16.3 2.7 %collective-permute-start.4 = (s16[2,64,256]{2,1,0:T(8,128)(2,1)S(1)}, s16[2,64,256]{2,1,0:T(8,128)(2,1)S(1)}, u32[]{:S(2)}, u32[]{:S(2)}) collective-permute-start(s16[2,64,256]{2,1,0:T(8,128)(2,1)S(1)} %get-tuple-element.31), channel_id=1, source_target_pairs={{0,8},{1,9},{2,10},{3,11},{4,12},{5,13},{6,14},{7,15},{8,0},{9,1},... | collective-permute-start | bytes 196616 | tf_op jit(solution)/shard_map/ppermute | solution.py:245
  19.0 0.0 collective-permute-done.10.refs_2_
  19.0 0.0 collective-permute-done.9.refs_1_
  19.0 0.3 collective-permute-done.8.refs_0_
  19.2 0.2 mix1.1
  19.4 2.7 %collective-permute-start.11 = (s16[2,64,256]{2,1,0:T(8,128)(2,1)S(1)}, s16[2,64,256]{2,1,0:T(8,128)(2,1)S(1)}, u32[]{:S(2)}, u32[]{:S(2)}) collective-permute-start(s16[2,64,256]{2,1,0:T(8,128)(2,1)S(1)} %get-tuple-element.40), channel_id=1, source_target_pairs={{0,8},{1,9},{2,10},{3,11},{4,12},{5,13},{6,14},{7,15},{8,0},{9,1},... | collective-permute-start | bytes 196616 | tf_op jit(solution)/shard_map/ppermute | solution.py:245
  22.1 1.4 %collective-permute-done.4.there = s16[2,64,256]{2,1,0:T(8,128)(2,1)S(1)} collective-permute-done((s16[2,64,256]{2,1,0:T(8,128)(2,1)S(1)}, s16[2,64,256]{2,1,0:T(8,128)(2,1)S(1)}, u32[]{:S(2)}, u32[]{:S(2)}) %collective-permute-start.4) | collective-permute-done | bytes 65568 | tf_op jit(solution)/shard_map/ppermute | solution.py:245
  23.5 0.1 finish0.1
  23.6 0.1 collective-permute-start.5
  23.7 1.7 %collective-permute-done.11.there = s16[2,64,256]{2,1,0:T(8,128)(2,1)S(1)} collective-permute-done((s16[2,64,256]{2,1,0:T(8,128)(2,1)S(1)}, s16[2,64,256]{2,1,0:T(8,128)(2,1)S(1)}, u32[]{:S(2)}, u32[]{:S(2)}) %collective-permute-start.11) | collective-permute-done | bytes 65568 | tf_op jit(solution)/shard_map/ppermute | solution.py:245
  25.4 0.1 finish1.1
  25.5 1.3 %collective-permute-start.14 = (s16[2,64,256]{2,1,0:T(8,128)(2,1)S(1)}, s16[2,64,256]{2,1,0:T(8,128)(2,1)S(1)}, u32[]{:S(2)}, u32[]{:S(2)}) collective-permute-start(s16[2,64,256]{2,1,0:T(8,128)(2,1)S(1)} %get-tuple-element.42.refs_0_), channel_id=1, source_target_pairs={{0,6},{1,7},{2,4},{3,5},{4,2},{5,3},{6,0},{7,1},{8,14},{9,15},{10,... | collective-permute-start | bytes 196616 | tf_op jit(solution)/shard_map/ppermute | solution.py:245
  26.8 0.6 %collective-permute-start.13 = (s16[2,64,256]{2,1,0:T(8,128)(2,1)S(1)}, s16[2,64,256]{2,1,0:T(8,128)(2,1)S(1)}, u32[]{:S(2)}, u32[]{:S(2)}) collective-permute-start(s16[2,64,256]{2,1,0:T(8,128)(2,1)S(1)} %get-tuple-element.42.refs_0_), channel_id=1, source_target_pairs={{0,2},{1,3},{2,0},{3,1},{4,6},{5,7},{6,4},{7,5},{8,10},{9,11},{10,... | collective-permute-start | bytes 196616 | tf_op jit(solution)/shard_map/ppermute | solution.py:245
  27.3 1.7 %collective-permute-start.12 = (s16[2,64,256]{2,1,0:T(8,128)(2,1)S(1)}, s16[2,64,256]{2,1,0:T(8,128)(2,1)S(1)}, u32[]{:S(2)}, u32[]{:S(2)}) collective-permute-start(s16[2,64,256]{2,1,0:T(8,128)(2,1)S(1)} %get-tuple-element.42.refs_0_), channel_id=1, source_target_pairs={{0,4},{1,5},{2,6},{3,7},{4,0},{5,1},{6,2},{7,3},{8,12},{9,13},{10,... | collective-permute-start | bytes 196616 | tf_op jit(solution)/shard_map/ppermute | solution.py:245
  29.0 0.0 collective-permute-done.5
  29.0 1.8 %collective-permute-start.6 = (s16[4,64,256]{2,1,0:T(8,128)(2,1)S(1)}, s16[4,64,256]{2,1,0:T(8,128)(2,1)S(1)}, u32[]{:S(2)}, u32[]{:S(2)}) collective-permute-start(s16[4,64,256]{2,1,0:T(8,128)(2,1)S(1)} %pad_add_fusion.1), channel_id=1, source_target_pairs={{0,2},{1,3},{2,0},{3,1},{4,6},{5,7},{6,4},{7,5},{8,10},{9,11},{10,... | collective-permute-start | bytes 393224 | tf_op jit(solution)/shard_map/ppermute | solution.py:245
  30.8 0.0 collective-permute-start.15
  30.8 0.0 collective-permute-done.14.refs_3_
  30.8 0.5 %collective-permute-start.18 = (s16[2,64,256]{2,1,0:T(8,128)(2,1)S(1)}, s16[2,64,256]{2,1,0:T(8,128)(2,1)S(1)}, u32[]{:S(2)}, u32[]{:S(2)}) collective-permute-start(s16[2,64,256]{2,1,0:T(8,128)(2,1)S(1)} %collective-permute-done.14.refs_3_), channel_id=1, source_target_pairs={{0,1},{1,0},{2,3},{3,2},{4,5},{5,4},{6,7},{7,6},{8,9},{9,8},{10,11... | collective-permute-start | bytes 196616 | tf_op jit(solution)/shard_map/ppermute | solution.py:245
  31.3 0.5 %collective-permute-done.13.refs_2_ = s16[2,64,256]{2,1,0:T(8,128)(2,1)S(1)} collective-permute-done((s16[2,64,256]{2,1,0:T(8,128)(2,1)S(1)}, s16[2,64,256]{2,1,0:T(8,128)(2,1)S(1)}, u32[]{:S(2)}, u32[]{:S(2)}) %collective-permute-start.13) | collective-permute-done | bytes 65568 | tf_op jit(solution)/shard_map/ppermute | solution.py:245
  31.9 0.0 collective-permute-start.17
  31.9 0.0 collective-permute-done.12.refs_1_
  31.9 0.5 %collective-permute-start.16 = (s16[2,64,256]{2,1,0:T(8,128)(2,1)S(1)}, s16[2,64,256]{2,1,0:T(8,128)(2,1)S(1)}, u32[]{:S(2)}, u32[]{:S(2)}) collective-permute-start(s16[2,64,256]{2,1,0:T(8,128)(2,1)S(1)} %collective-permute-done.12.refs_1_), channel_id=1, source_target_pairs={{0,1},{1,0},{2,3},{3,2},{4,5},{5,4},{6,7},{7,6},{8,9},{9,8},{10,11... | collective-permute-start | bytes 196616 | tf_op jit(solution)/shard_map/ppermute | solution.py:245
  32.4 0.0 collective-permute-done.15.refs_4_
  32.4 0.0 collective-permute-done.18.refs_7_
  32.4 0.7 %collective-permute-done.17.refs_6_ = s16[2,64,256]{2,1,0:T(8,128)(2,1)S(1)} collective-permute-done((s16[2,64,256]{2,1,0:T(8,128)(2,1)S(1)}, s16[2,64,256]{2,1,0:T(8,128)(2,1)S(1)}, u32[]{:S(2)}, u32[]{:S(2)}) %collective-permute-start.17) | collective-permute-done | bytes 65568 | tf_op jit(solution)/shard_map/ppermute | solution.py:245
  33.1 0.2 collective-permute-done.16.refs_5_
  33.3 0.5 %rows1.1 = (bf16[64,256]{1,0:T(8,128)(2,1)S(1)}, bf16[256,1024]{1,0:T(8,128)(2,1)S(1)}) custom-call(f32[64,256]{1,0:T(8,128)S(1)} %get-tuple-element.41.own, s16[2,64,256]{2,1,0:T(8,128)(2,1)S(1)} %get-tuple-element.42.refs_0_, s16[2,64,256]{2,1,0:T(8,128)(2,1)S(1)} %collective-permute-done.12.refs_1_, ...), custom_call_target="tpu_custom_call" | custom-call | tf_op jit(solution)/shard_map/rows1/pallas_call | solution.py:319
  33.8 0.3 collective-permute-done.6
  34.1 0.1 collective-permute-start.19
  34.2 1.7 %scores1.1 = (f32[12,128]{1,0:T(8,128)S(1)}, f32[12,128]{1,0:T(8,128)S(1)}) custom-call(s32[12]{0:T(128)S(1)} %copy-done.2, s32[12,128]{1,0:T(8,128)S(1)} %bitcast.28, bf16[1536,1024]{1,0:T(8,128)(2,1)S(1)} %get-tuple-element.27.points, bf16[256,1024]{1,0:T(8,128)(2,1)S(1)} %get-tuple-element.46.cents), custom_call_target="tpu_custom_call" | custom-call | flops 805306368 | bytes 3145728 | tf_op jit(solution)/shard_map/scores1/pallas_call | solution.py:334
  35.9 0.0 collective-permute-done.19.refs_1_
  35.9 0.5 %rows0.1 = (bf16[64,256]{1,0:T(8,128)(2,1)S(1)}, bf16[256,1024]{1,0:T(8,128)(2,1)S(1)}) custom-call(f32[64,256]{1,0:T(8,128)S(1)} %get-tuple-element.32.own, s16[8,64,256]{2,1,0:T(8,128)(2,1)S(1)} %pad_add_fusion.refs_0_, s16[8,64,256]{2,1,0:T(8,128)(2,1)S(1)} %collective-permute-done.19.refs_1_), custom_call_target="tpu_custom_call" | custom-call | tf_op jit(solution)/shard_map/rows0/pallas_call | solution.py:319
  36.4 2.3 %scores0.1 = (bf16[128,256]{1,0:T(8,128)(2,1)}, f32[12,128]{1,0:T(8,128)}) custom-call(s32[12]{0:T(128)S(1)} %copy-done.2, s32[12,128]{1,0:T(8,128)S(1)} %bitcast.29, bf16[1536,1024]{1,0:T(8,128)(2,1)S(1)} %get-tuple-element.27.points, bf16[256,1024]{1,0:T(8,128)(2,1)S(1)} %get-tuple-element.45.cents, f32[12,128]{1,0:T(8,128)S(1)} %get-tuple-element.47.refs_0_, ...), custom_call_target="tpu_custom_call" | custom-call | flops 805306368 | bytes 3145728 | tf_op jit(solution)/shard_map/scores0/pallas_call | solution.py:334
  (2 shorter events, 0.0 us)
Async XLA Ops:
  0.6 4.0 %copy-start.2 = (s32[12]{0:T(128)S(1)}, s32[12]{0:T(128)}, u32[]{:S(2)}) copy-start(s32[12]{0:T(128)} %bids.5) | copy-start | bytes 148
  0.6 4.0 %copy-start = (s32[1536]{0:T(1024)S(1)}, s32[1536]{0:T(1024)}, u32[]{:S(2)}) copy-start(s32[1536]{0:T(1024)} %param.7) | copy-start | bytes 18436
  0.7 4.0 %copy-start.1 = (bf16[128,256]{1,0:T(8,128)(2,1)S(1)}, bf16[128,256]{1,0:T(8,128)(2,1)}, u32[]{:S(2)}) copy-start(bf16[128,256]{1,0:T(8,128)(2,1)} %old.1) | copy-start | bytes 196612
  4.1 2.4 %collective-permute-start = (f32[4,2,64,256]{3,2,1,0:T(8,128)S(1)}, f32[4,2,64,256]{3,2,1,0:T(8,128)S(1)}, u32[]{:S(2)}, u32[]{:S(2)}) collective-permute-start(f32[4,2,64,256]{3,2,1,0:T(8,128)S(1)} %get-tuple-element.29), channel_id=1, source_target_pairs={{0,1},{1,0},{2,3},{3,2},{4,5},{5,4},{6,7},{7,6},{8,9},{9,8},{10,11... | collective-permute-start | bytes 1572872 | tf_op jit(solution)/shard_map/ppermute | solution.py:245
  4.6 6.7 %collective-permute-start.7 = (f32[4,2,64,256]{3,2,1,0:T(8,128)S(1)}, f32[4,2,64,256]{3,2,1,0:T(8,128)S(1)}, u32[]{:S(2)}, u32[]{:S(2)}) collective-permute-start(f32[4,2,64,256]{3,2,1,0:T(8,128)S(1)} %get-tuple-element.36), channel_id=1, source_target_pairs={{0,1},{1,0},{2,3},{3,2},{4,5},{5,4},{6,7},{7,6},{8,9},{9,8},{10,11... | collective-permute-start | bytes 1572872 | tf_op jit(solution)/shard_map/ppermute | solution.py:245
  6.7 8.3 %collective-permute-start.3 = (s16[2,64,256]{2,1,0:T(8,128)(2,1)S(1)}, s16[2,64,256]{2,1,0:T(8,128)(2,1)S(1)}, u32[]{:S(2)}, u32[]{:S(2)}) collective-permute-start(s16[2,64,256]{2,1,0:T(8,128)(2,1)S(1)} %get-tuple-element.55), channel_id=1, source_target_pairs={{0,6},{1,7},{2,4},{3,5},{4,2},{5,3},{6,0},{7,1},{8,14},{9,15},{10,... | collective-permute-start | bytes 196616 | tf_op jit(solution)/shard_map/ppermute | solution.py:245
  10.7 4.5 %collective-permute-start.2 = (s16[2,64,256]{2,1,0:T(8,128)(2,1)S(1)}, s16[2,64,256]{2,1,0:T(8,128)(2,1)S(1)}, u32[]{:S(2)}, u32[]{:S(2)}) collective-permute-start(s16[2,64,256]{2,1,0:T(8,128)(2,1)S(1)} %get-tuple-element.56), channel_id=1, source_target_pairs={{0,2},{1,3},{2,0},{3,1},{4,6},{5,7},{6,4},{7,5},{8,10},{9,11},{10,... | collective-permute-start | bytes 196616 | tf_op jit(solution)/shard_map/ppermute | solution.py:245
  11.2 4.9 %collective-permute-start.1 = (s16[2,64,256]{2,1,0:T(8,128)(2,1)S(1)}, s16[2,64,256]{2,1,0:T(8,128)(2,1)S(1)}, u32[]{:S(2)}, u32[]{:S(2)}) collective-permute-start(s16[2,64,256]{2,1,0:T(8,128)(2,1)S(1)} %get-tuple-element.57), channel_id=1, source_target_pairs={{0,4},{1,5},{2,6},{3,7},{4,0},{5,1},{6,2},{7,3},{8,12},{9,13},{10,... | collective-permute-start | bytes 196616 | tf_op jit(solution)/shard_map/ppermute | solution.py:245
  11.5 7.4 %collective-permute-start.10 = (s16[2,64,256]{2,1,0:T(8,128)(2,1)S(1)}, s16[2,64,256]{2,1,0:T(8,128)(2,1)S(1)}, u32[]{:S(2)}, u32[]{:S(2)}) collective-permute-start(s16[2,64,256]{2,1,0:T(8,128)(2,1)S(1)} %get-tuple-element.52), channel_id=1, source_target_pairs={{0,6},{1,7},{2,4},{3,5},{4,2},{5,3},{6,0},{7,1},{8,14},{9,15},{10,... | collective-permute-start | bytes 196616 | tf_op jit(solution)/shard_map/ppermute | solution.py:245
  14.4 4.5 %collective-permute-start.9 = (s16[2,64,256]{2,1,0:T(8,128)(2,1)S(1)}, s16[2,64,256]{2,1,0:T(8,128)(2,1)S(1)}, u32[]{:S(2)}, u32[]{:S(2)}) collective-permute-start(s16[2,64,256]{2,1,0:T(8,128)(2,1)S(1)} %get-tuple-element.53), channel_id=1, source_target_pairs={{0,2},{1,3},{2,0},{3,1},{4,6},{5,7},{6,4},{7,5},{8,10},{9,11},{10,... | collective-permute-start | bytes 196616 | tf_op jit(solution)/shard_map/ppermute | solution.py:245
  15.0 4.3 %collective-permute-start.8 = (s16[2,64,256]{2,1,0:T(8,128)(2,1)S(1)}, s16[2,64,256]{2,1,0:T(8,128)(2,1)S(1)}, u32[]{:S(2)}, u32[]{:S(2)}) collective-permute-start(s16[2,64,256]{2,1,0:T(8,128)(2,1)S(1)} %get-tuple-element.54), channel_id=1, source_target_pairs={{0,4},{1,5},{2,6},{3,7},{4,0},{5,1},{6,2},{7,3},{8,12},{9,13},{10,... | collective-permute-start | bytes 196616 | tf_op jit(solution)/shard_map/ppermute | solution.py:245
  16.3 7.2 %collective-permute-start.4 = (s16[2,64,256]{2,1,0:T(8,128)(2,1)S(1)}, s16[2,64,256]{2,1,0:T(8,128)(2,1)S(1)}, u32[]{:S(2)}, u32[]{:S(2)}) collective-permute-start(s16[2,64,256]{2,1,0:T(8,128)(2,1)S(1)} %get-tuple-element.31), channel_id=1, source_target_pairs={{0,8},{1,9},{2,10},{3,11},{4,12},{5,13},{6,14},{7,15},{8,0},{9,1},... | collective-permute-start | bytes 196616 | tf_op jit(solution)/shard_map/ppermute | solution.py:245
  19.4 5.9 %collective-permute-start.11 = (s16[2,64,256]{2,1,0:T(8,128)(2,1)S(1)}, s16[2,64,256]{2,1,0:T(8,128)(2,1)S(1)}, u32[]{:S(2)}, u32[]{:S(2)}) collective-permute-start(s16[2,64,256]{2,1,0:T(8,128)(2,1)S(1)} %get-tuple-element.40), channel_id=1, source_target_pairs={{0,8},{1,9},{2,10},{3,11},{4,12},{5,13},{6,14},{7,15},{8,0},{9,1},... | collective-permute-start | bytes 196616 | tf_op jit(solution)/shard_map/ppermute | solution.py:245
  23.6 5.4 %collective-permute-start.5 = (s16[2,64,256]{2,1,0:T(8,128)(2,1)S(1)}, s16[2,64,256]{2,1,0:T(8,128)(2,1)S(1)}, u32[]{:S(2)}, u32[]{:S(2)}) collective-permute-start(s16[2,64,256]{2,1,0:T(8,128)(2,1)S(1)} %get-tuple-element.33), channel_id=1, source_target_pairs={{0,4},{1,5},{2,6},{3,7},{4,0},{5,1},{6,2},{7,3},{8,12},{9,13},{10,... | collective-permute-start | bytes 196616 | tf_op jit(solution)/shard_map/ppermute | solution.py:245
  25.5 5.4 %collective-permute-start.14 = (s16[2,64,256]{2,1,0:T(8,128)(2,1)S(1)}, s16[2,64,256]{2,1,0:T(8,128)(2,1)S(1)}, u32[]{:S(2)}, u32[]{:S(2)}) collective-permute-start(s16[2,64,256]{2,1,0:T(8,128)(2,1)S(1)} %get-tuple-element.42.refs_0_), channel_id=1, source_target_pairs={{0,6},{1,7},{2,4},{3,5},{4,2},{5,3},{6,0},{7,1},{8,14},{9,15},{10,... | collective-permute-start | bytes 196616 | tf_op jit(solution)/shard_map/ppermute | solution.py:245
  26.8 5.1 %collective-permute-start.13 = (s16[2,64,256]{2,1,0:T(8,128)(2,1)S(1)}, s16[2,64,256]{2,1,0:T(8,128)(2,1)S(1)}, u32[]{:S(2)}, u32[]{:S(2)}) collective-permute-start(s16[2,64,256]{2,1,0:T(8,128)(2,1)S(1)} %get-tuple-element.42.refs_0_), channel_id=1, source_target_pairs={{0,2},{1,3},{2,0},{3,1},{4,6},{5,7},{6,4},{7,5},{8,10},{9,11},{10,... | collective-permute-start | bytes 196616 | tf_op jit(solution)/shard_map/ppermute | solution.py:245
  27.3 4.5 %collective-permute-start.12 = (s16[2,64,256]{2,1,0:T(8,128)(2,1)S(1)}, s16[2,64,256]{2,1,0:T(8,128)(2,1)S(1)}, u32[]{:S(2)}, u32[]{:S(2)}) collective-permute-start(s16[2,64,256]{2,1,0:T(8,128)(2,1)S(1)} %get-tuple-element.42.refs_0_), channel_id=1, source_target_pairs={{0,4},{1,5},{2,6},{3,7},{4,0},{5,1},{6,2},{7,3},{8,12},{9,13},{10,... | collective-permute-start | bytes 196616 | tf_op jit(solution)/shard_map/ppermute | solution.py:245
  29.0 5.0 %collective-permute-start.6 = (s16[4,64,256]{2,1,0:T(8,128)(2,1)S(1)}, s16[4,64,256]{2,1,0:T(8,128)(2,1)S(1)}, u32[]{:S(2)}, u32[]{:S(2)}) collective-permute-start(s16[4,64,256]{2,1,0:T(8,128)(2,1)S(1)} %pad_add_fusion.1), channel_id=1, source_target_pairs={{0,2},{1,3},{2,0},{3,1},{4,6},{5,7},{6,4},{7,5},{8,10},{9,11},{10,... | collective-permute-start | bytes 393224 | tf_op jit(solution)/shard_map/ppermute | solution.py:245
  30.8 1.6 %collective-permute-start.15 = (s16[2,64,256]{2,1,0:T(8,128)(2,1)S(1)}, s16[2,64,256]{2,1,0:T(8,128)(2,1)S(1)}, u32[]{:S(2)}, u32[]{:S(2)}) collective-permute-start(s16[2,64,256]{2,1,0:T(8,128)(2,1)S(1)} %get-tuple-element.42.refs_0_), channel_id=1, source_target_pairs={{0,1},{1,0},{2,3},{3,2},{4,5},{5,4},{6,7},{7,6},{8,9},{9,8},{10,11... | collective-permute-start | bytes 196616 | tf_op jit(solution)/shard_map/ppermute | solution.py:245
  30.8 1.6 %collective-permute-start.18 = (s16[2,64,256]{2,1,0:T(8,128)(2,1)S(1)}, s16[2,64,256]{2,1,0:T(8,128)(2,1)S(1)}, u32[]{:S(2)}, u32[]{:S(2)}) collective-permute-start(s16[2,64,256]{2,1,0:T(8,128)(2,1)S(1)} %collective-permute-done.14.refs_3_), channel_id=1, source_target_pairs={{0,1},{1,0},{2,3},{3,2},{4,5},{5,4},{6,7},{7,6},{8,9},{9,8},{10,11... | collective-permute-start | bytes 196616 | tf_op jit(solution)/shard_map/ppermute | solution.py:245
  31.9 1.3 %collective-permute-start.17 = (s16[2,64,256]{2,1,0:T(8,128)(2,1)S(1)}, s16[2,64,256]{2,1,0:T(8,128)(2,1)S(1)}, u32[]{:S(2)}, u32[]{:S(2)}) collective-permute-start(s16[2,64,256]{2,1,0:T(8,128)(2,1)S(1)} %collective-permute-done.13.refs_2_), channel_id=1, source_target_pairs={{0,1},{1,0},{2,3},{3,2},{4,5},{5,4},{6,7},{7,6},{8,9},{9,8},{10,11... | collective-permute-start | bytes 196616 | tf_op jit(solution)/shard_map/ppermute | solution.py:245
  31.9 1.4 %collective-permute-start.16 = (s16[2,64,256]{2,1,0:T(8,128)(2,1)S(1)}, s16[2,64,256]{2,1,0:T(8,128)(2,1)S(1)}, u32[]{:S(2)}, u32[]{:S(2)}) collective-permute-start(s16[2,64,256]{2,1,0:T(8,128)(2,1)S(1)} %collective-permute-done.12.refs_1_), channel_id=1, source_target_pairs={{0,1},{1,0},{2,3},{3,2},{4,5},{5,4},{6,7},{7,6},{8,9},{9,8},{10,11... | collective-permute-start | bytes 196616 | tf_op jit(solution)/shard_map/ppermute | solution.py:245
  34.1 1.8 %collective-permute-start.19 = (s16[8,64,256]{2,1,0:T(8,128)(2,1)S(1)}, s16[8,64,256]{2,1,0:T(8,128)(2,1)S(1)}, u32[]{:S(2)}, u32[]{:S(2)}) collective-permute-start(s16[8,64,256]{2,1,0:T(8,128)(2,1)S(1)} %pad_add_fusion.refs_0_), channel_id=1, source_target_pairs={{0,1},{1,0},{2,3},{3,2},{4,5},{5,4},{6,7},{7,6},{8,9},{9,8},{10,11... | collective-permute-start | bytes 786440 | tf_op jit(solution)/shard_map/ppermute | solution.py:245
